TPU v7x, 32 devices: a whole 2x2x4 slice. The times are simulated.
32 devices in a mesh: outer: 2 (over core), inner: 16 (over z, y, x).
Axes of the slice: x: 2, y: 2, z: 4, core: 2. Of those that a mesh axis runs over, the one named last changes fastest.
Arguments:
- cotangent: bfloat16 [4096, 2048], P(('outer', 'inner')), may hold values from -1.5 to 1.5
- hidden: bfloat16 [4096, 8, 384], P(('outer', 'inner')), may hold values from -6 to 6
- probs: float32 [4096, 8], P(('outer', 'inner')), may hold values from 0.02 to 0.5
- expert_ids: int32 [4096, 8], P(('outer', 'inner')), may hold values from 0 to 63, all different within a row; in each aligned block of 128 rows (0 to 127, 128 to 255, ...) at most 24 rows name the same one
- secondary: bfloat16 [384, 64, 2048], P(None, 'inner'), may hold values from -0.3125 to 0.3125
- weight: float32 [384, 64, 2048], P('outer', 'inner'), may hold values from -0.3125 to 0.3125
- moment1: float32 [384, 64, 2048], P('outer', 'inner'), may hold values from -4 to 4
- moment2: float32 [384, 64, 2048], P('outer', 'inner'), may hold values from 0.05 to 2
Outputs:
- d_hidden: bfloat16 [4096, 8, 384], P(('outer', 'inner'))
- d_probs: float32 [4096, 8], P(('outer', 'inner'))
- new_weight: float32 [384, 64, 2048], P('outer', 'inner')
- new_moment1: float32 [384, 64, 2048], P('outer', 'inner')
- new_moment2: float32 [384, 64, 2048], P('outer', 'inner')
- new_secondary: bfloat16 [384, 64, 2048], P(None, 'inner')
Inputs may be any that keep to these rules, and one draw needn't show every extreme that they name: `expert_ids`: each token names 8 different experts. Among the 1024 choices of the rows of one device (aligned blocks of 128 tokens), no expert is named more than 24 times, a bound that some block reaches.
All inputs are finite; a program needn't handle non-finite values.
Results may differ from a plain program's by a relative error of at most 0.0085.
Values may be sent and summed in bfloat16 or wider, within the bound.
No kernel may reach another device: no remote copies, remote signals or barrier semaphores. Data moves between devices by JAX's collectives and lax.ppermute only.
A program may use at most 128 MiB of HBM per device.

v0:
```python
import jax
import jax.numpy as jnp
from jax import lax
from jax.sharding import PartitionSpec as P

EXPERTS = 64
CAP = 24


beta_one = 0.9
beta_two = 0.95
adam_epsilon = 1e-08
learn_rate = 0.003
decay_rate = 0.1
bias_one = 1.0 - 0.9**20
bias_two = 1.0 - 0.95**20


def slot_targets(flat_ids):
    count = flat_ids.shape[0]
    block = 128
    blocks = count // block
    onehot = (jnp.arange(EXPERTS, dtype=jnp.int32)[:, None] == flat_ids[None, :]).astype(
        jnp.bfloat16
    )
    tiles = onehot.reshape(EXPERTS, blocks, block)
    lower = (jnp.arange(block)[:, None] < jnp.arange(block)[None, :]).astype(jnp.bfloat16)
    within = jnp.einsum("ebk,kj->ebj", tiles, lower, preferred_element_type=jnp.float32)
    totals = jnp.sum(tiles.astype(jnp.float32), axis=2)
    small = (jnp.arange(blocks)[:, None] < jnp.arange(blocks)[None, :]).astype(jnp.float32)
    before = jnp.dot(totals, small, precision=lax.Precision.HIGHEST)
    ranking = (within + before[..., None]).reshape(EXPERTS, count)
    position = jnp.sum(ranking * onehot.astype(jnp.float32), axis=0).astype(jnp.int32)
    return flat_ids * CAP + position


def local(cotangent, hidden, probs, expert_ids, secondary, weight, moment1, moment2):
    token_count = cotangent.shape[0]
    top_k = expert_ids.shape[1]
    hidden_width = hidden.shape[2]
    feature_width = cotangent.shape[1]
    local_experts = secondary.shape[1]
    group_size = lax.axis_size("inner")
    choice_count = token_count * top_k
    target = slot_targets(expert_ids.reshape(choice_count))
    all_slots = jnp.arange(EXPERTS * CAP, dtype=jnp.int32)
    matches = (all_slots[:, None] == target[None, :]).astype(jnp.bfloat16)
    weighted = (
        (probs[..., None] * hidden.astype(jnp.float32))
        .astype(jnp.bfloat16)
        .reshape(choice_count, hidden_width)
    )
    w_send = jnp.dot(matches, weighted, preferred_element_type=jnp.float32).astype(jnp.bfloat16)
    w_send = w_send.reshape(group_size, local_experts, CAP, hidden_width)
    all_cot, all_ids = (
        lax.all_gather(cotangent, "inner", axis=0, tiled=True),
        lax.all_gather(expert_ids, "inner", axis=0, tiled=True),
    )
    w_recv = lax.all_to_all(w_send, "inner", split_axis=0, concat_axis=0, tiled=True)
    source_ids = all_ids.reshape(group_size, choice_count)
    source_target = jax.vmap(slot_targets)(source_ids)
    offset = lax.axis_index("inner") * (local_experts * CAP)
    mine_slots = offset + jnp.arange(local_experts * CAP, dtype=jnp.int32)
    mine_match = (mine_slots[None, :, None] == source_target[:, None, :]).astype(jnp.bfloat16)
    token_match = jnp.sum(
        mine_match.reshape(group_size, local_experts * CAP, token_count, top_k), axis=3
    )
    cot_blocks = all_cot.reshape(group_size, token_count, feature_width)
    d_recv = jnp.einsum(
        "jst,jtd->jsd", token_match, cot_blocks, preferred_element_type=jnp.float32
    ).astype(jnp.bfloat16)
    d_recv = d_recv.reshape(group_size, local_experts, CAP, feature_width)
    grads = jnp.einsum(
        "jlcd,hld->jlch", d_recv, secondary, preferred_element_type=jnp.float32
    ).astype(jnp.bfloat16)
    grad = lax.psum_scatter(
        jnp.einsum("jlch,jlcd->hld", w_recv, d_recv, preferred_element_type=jnp.float32).astype(
            jnp.bfloat16
        ),
        "outer",
        scatter_dimension=0,
        tiled=True,
    ).astype(jnp.float32)
    back = lax.all_to_all(grads, "inner", split_axis=0, concat_axis=0, tiled=True)
    back = back.reshape(group_size * local_experts * CAP, hidden_width)
    g_rows = back[target].astype(jnp.float32).reshape(token_count, top_k, hidden_width)
    d_hidden = (probs[..., None] * g_rows).astype(jnp.bfloat16)
    d_probs = jnp.sum(hidden.astype(jnp.float32) * g_rows, axis=-1)
    new_moment1 = beta_one * moment1 + (1.0 - beta_one) * grad
    new_moment2 = beta_two * moment2 + (1.0 - beta_two) * grad * grad
    update = (
        new_moment1 / bias_one / (jnp.sqrt(new_moment2 / bias_two) + adam_epsilon)
        + decay_rate * weight
    )
    new_weight = weight - learn_rate * update
    new_secondary = lax.all_gather(new_weight.astype(jnp.bfloat16), "outer", axis=0, tiled=True)
    return (d_hidden, d_probs, new_weight, new_moment1, new_moment2, new_secondary)


def solution(mesh):
    in_specs = (
        P(("outer", "inner"), None),
        P(("outer", "inner"), None, None),
        P(("outer", "inner"), None),
        P(("outer", "inner"), None),
        P(None, "inner", None),
        P("outer", "inner", None),
        P("outer", "inner", None),
        P("outer", "inner", None),
    )
    out_specs = (
        P(("outer", "inner"), None, None),
        P(("outer", "inner"), None),
        P("outer", "inner", None),
        P("outer", "inner", None),
        P("outer", "inner", None),
        P(None, "inner", None),
    )
    return jax.shard_map(local, mesh=mesh, in_specs=in_specs, out_specs=out_specs, check_vma=False)
```

profile of v0, /device:TPU:0, one launch (start us, length us, event | category | flops | bytes accessed | tf_op | source)
XLA Modules:
  0.0 294.9 jit_solution(15799601330153429941)
XLA Ops:
  7.2 0.0 all-gather.3.cloned.1.call-start
  7.2 0.7 all-gather.3.cloned.1.call-update
  7.9 0.8 copy.97
  8.7 0.7 broadcast_multiply_fusion
  9.4 0.1 copy.96
  9.5 0.1 mul.111
  9.6 0.8 copy.87
  10.4 0.1 eq.71
  10.5 0.1 convert_reduce_fusion.1
  10.6 0.1 fusion.38
  10.7 0.2 fusion.28
  11.0 0.0 copy-start.1
  11.0 4.0 %fusion.12 = bf16[1536,384]{1,0:T(8,128)(2,1)} fusion(s32[1024]{0:T(1024)S(1)} %bitcast_add_fusion.1, bf16[128,8,384]{2,1,0:T(8,128)(2,1)} %param.9, f32[128,8]{1,0:T(8,128)S(1)} %copy.87), kind=kOutput, calls=%fused_computation.23 | convolution fusion | flops 1211301888 | bytes 1974272 | tf_op jit(solution)/shard_map/dot_general | solution.py:53
  15.0 8.3 %all-to-all-start.1 = ((bf16[16,4,24,384]{3,2,1,0:T(8,128)(2,1)}), bf16[16,4,24,384]{3,2,1,0:T(8,128)(2,1)S(1)}, u32[]{:S(2)}, u32[]{:S(2)}) async-start(bf16[16,4,24,384]{3,2,1,0:T(8,128)(2,1)} %bitcast.17), calls=%async_computation.1 | async-start | bytes 2359296 | tf_op jit(solution)/shard_map/all_to_all | solution.py:59
  23.3 0.0 all-reduce.3.cloned.1.call-start
  23.4 0.0 copy-done.1
  23.4 64.7 %all_gather.9 = s32[2048,8]{0,1:T(8,128)S(1)} all-gather(s32[128,8]{0,1:T(8,128)S(1)} %copy-done.1), channel_id=1, replica_groups=mesh['outer'=2,'inner'=16] {'inner'}, dimensions={0}, use_global_device_ids=true | all-gather | bytes 69632 | tf_op jit(solution)/shard_map/all_gather | solution.py:57
  88.1 0.3 copy.88
  88.4 0.5 eq.65
  88.9 1.2 convert_reduce_fusion
  90.1 0.4 fusion.40
  90.5 1.6 fusion.7
  92.1 0.2 copy.91
  92.3 0.2 copy.92
  92.6 2.7 fusion.10
  95.3 49.3 %all-gather.3.cloned.1.call-done = bf16[2048,2048]{1,0:T(8,128)(2,1)} async-done(((bf16[128,2048]{1,0:T(8,128)(2,1)}), bf16[2048,2048]{1,0:T(8,128)(2,1)}) %all-gather.3.cloned.1.call-update) | async-done | bytes 8388624 | tf_op jit(solution)/shard_map/all_gather | solution.py:56
  144.6 7.9 %convolution_convert_fusion = bf16[16,96,2048]{2,1,0:T(8,128)(2,1)} fusion(bf16[16,96,128]{2,1,0:T(8,128)(2,1)S(1)} %fusion.10, bf16[16,128,2048]{2,1,0:T(8,128)(2,1)} %bitcast.46), kind=kOutput, calls=%fused_computation.16 | convolution fusion | flops 808452096 | bytes 15073280 | tf_op jit(solution)/shard_map/jst,jtd->jsd/dot_general | solution.py:69
  152.5 0.0 all-to-all-done.1
  152.5 9.5 %fusion.2 = bf16[384,4,2048]{0,2,1:T(8,128)(2,1)} fusion(bf16[16,4,24,2048]{3,2,1,0:T(8,128)(2,1)} %bitcast.47, bf16[16,4,24,384]{3,2,1,0:T(8,128)(2,1)S(1)} %all-to-all-done.1), kind=kOutput, calls=%fused_computation.6 | convolution fusion | flops 2419064832 | bytes 13762560 | tf_op jit(solution)/shard_map/jlch,jlcd->hld/dot_general | solution.py:77
  162.0 11.2 %copy.100 = bf16[384,4,2048]{2,1,0:T(4,128)(2,1)} copy(bf16[384,4,2048]{0,2,1:T(8,128)(2,1)} %fusion.2) | data formatting | bytes 12582912 | tf_op jit(solution)/shard_map/convert_element_type | solution.py:77
  173.2 0.0 copy-start.2
  173.2 0.0 all-reduce.3.cloned.1.call-update
  173.2 0.0 all-gather.5.cloned.1.call-start
  173.3 0.6 copy-done.2
  173.9 0.6 dynamic-slice
  175.1 28.5 %all-reduce.3.cloned.1.call-done = bf16[384,4,2048]{2,1,0:T(4,128)(2,1)} async-done(((bf16[384,4,2048]{2,1,0:T(4,128)(2,1)}), bf16[384,4,2048]{2,1,0:T(4,128)(2,1)}) %all-reduce.3.cloned.1.call-update) | async-done | bytes 6291472
  203.6 21.1 %fusion.42 = (bf16[192,4,2048]{2,1,0:T(4,128)(2,1)}, f32[192,4,2048]{2,1,0:T(4,128)}, f32[192,4,2048]{2,1,0:T(4,128)}, f32[192,4,2048]{2,1,0:T(4,128)}) fusion(f32[192,4,2048]{2,1,0:T(4,128)} %param.13, bf16[384,4,2048]{2,1,0:T(4,128)(2,1)} %all-reduce.3.cloned.1.call-done, u32[]{:T(128)S(6)} %multiply.3, f32[192,4,2048]{2,1,0:T(4,128)} %param.14, ...), kind=kLoop, calls=%fused_computation.55 | loop fusion | flops 26738688 | bytes 44040196 | tf_op jit(solution)/shard_map/convert_element_type | solution.py:96
  224.7 0.0 all-gather.5.cloned.1.call-update
  224.7 14.0 %fusion.22 = bf16[16,4,24,384]{3,2,0,1:T(8,128)(2,1)S(1)} fusion(bf16[384,4,2048,1]{2,1,0,3:T(4,128)(2,1)} %bitcast.52, bf16[16,4,24,2048]{3,2,1,0:T(8,128)(2,1)} %bitcast.48), kind=kOutput, calls=%fused_computation.32 | convolution fusion | flops 2416508928 | bytes 13762560 | tf_op jit(solution)/shard_map/jlcd,hld->jlch/dot_general | solution.py:73
  238.7 0.0 copy-start
  238.8 1.1 copy.95
  239.9 6.8 %all-to-all-start = ((bf16[16,4,24,384]{3,2,1,0:T(8,128)(2,1)}), bf16[16,4,24,384]{3,2,1,0:T(8,128)(2,1)S(1)}, u32[]{:S(2)}, u32[]{:S(2)}) async-start(bf16[16,4,24,384]{3,2,1,0:T(8,128)(2,1)} %copy.95), calls=%async_computation | async-start | bytes 2359296 | tf_op jit(solution)/shard_map/all_to_all | solution.py:84
  246.7 0.1 mul.105
  246.8 27.0 %all-to-all-done = bf16[16,4,24,384]{3,2,1,0:T(8,128)(2,1)S(1)} async-done(((bf16[16,4,24,384]{3,2,1,0:T(8,128)(2,1)}), bf16[16,4,24,384]{3,2,1,0:T(8,128)(2,1)S(1)}, u32[]{:S(2)}, u32[]{:S(2)}) %all-to-all-start) | async-done | bytes 1179680 | tf_op jit(solution)/shard_map/all_to_all | solution.py:84
  273.8 3.9 %gather_fusion = bf16[1024,384]{1,0:T(8,128)(2,1)S(1)} fusion(bf16[1536,384]{1,0:T(8,128)(2,1)S(1)} %bitcast.45, s32[1024]{0:T(1024)S(1)} %broadcast_clamp_fusion), kind=kCustom, calls=%fused_computation | custom fusion | bytes 1576960 | tf_op jit(solution)/shard_map/gather | solution.py:86
  277.7 0.0 copy-done
  277.8 1.3 fusion.16
  279.0 0.7 copy.101
  279.7 0.0 all-gather.5.cloned.1.call-done
  279.7 8.7 %copy.123 = bf16[384,4,2048]{2,1,0:T(4,128)(2,1)} copy(bf16[384,4,2048]{2,1,0:T(4,128)(2,1)} %all-gather.5.cloned.1.call-done) | data formatting | bytes 12582912
  (7 shorter events, 0.1 us)
Async XLA Ops:
  7.2 137.5 %all-gather.3.cloned.1.call-start = ((), (), s32[]{:S(2)}) async-start(), calls=%async_computation.2 | async-start | bytes 8912896 | tf_op jit(solution)/shard_map/all_gather | solution.py:56
  11.0 12.4 %copy-start.1 = (s32[128,8]{0,1:T(8,128)S(1)}, s32[128,8]{0,1:T(8,128)}, u32[]{:S(2)}) copy-start(s32[128,8]{0,1:T(8,128)} %param.11) | copy-start | bytes 12292
  15.0 137.5 %all-to-all-start.1 = ((bf16[16,4,24,384]{3,2,1,0:T(8,128)(2,1)}), bf16[16,4,24,384]{3,2,1,0:T(8,128)(2,1)S(1)}, u32[]{:S(2)}, u32[]{:S(2)}) async-start(bf16[16,4,24,384]{3,2,1,0:T(8,128)(2,1)} %bitcast.17), calls=%async_computation.1 | async-start | bytes 2359296 | tf_op jit(solution)/shard_map/all_to_all | solution.py:59
  23.3 180.3 %all-reduce.3.cloned.1.call-start = ((), (), s32[]{:S(2)}) async-start(), calls=%async_computation.4 | async-start | bytes 12582912
  173.2 0.7 copy-start.2
  173.2 106.5 %all-gather.5.cloned.1.call-start = ((), (), s32[]{:S(2)}) async-start(), calls=%async_computation.3 | async-start | bytes 9437184 | tf_op jit(solution)/shard_map/all_gather | solution.py:96
  238.7 39.0 %copy-start = (bf16[128,8,384]{2,1,0:T(8,128)(2,1)S(1)}, bf16[128,8,384]{2,1,0:T(8,128)(2,1)}, u32[]{:S(2)}) copy-start(bf16[128,8,384]{2,1,0:T(8,128)(2,1)} %param.9) | copy-start | bytes 2359300
  239.9 33.9 %all-to-all-start = ((bf16[16,4,24,384]{3,2,1,0:T(8,128)(2,1)}), bf16[16,4,24,384]{3,2,1,0:T(8,128)(2,1)S(1)}, u32[]{:S(2)}, u32[]{:S(2)}) async-start(bf16[16,4,24,384]{3,2,1,0:T(8,128)(2,1)} %copy.95), calls=%async_computation | async-start | bytes 2359296 | tf_op jit(solution)/shard_map/all_to_all | solution.py:84
Sparse Core Ops, SparseCore 0:
  10.8 133.8 all-gather.2
  173.3 30.2 all-reduce.2
  224.8 17.9 all-gather.4
where the time goes:
time: 296 us; the launch traced here: 295 us
  waiting for transfers between devices  106 us (36%)
  blocking collectives  64.7 us (22%)
  matrix products  37.8 us (13%)
  local copies, waits for them, and re-layouts  29.9 us (10%)
  other arithmetic  27.1 us (9%)
  starting transfers between devices  15.2 us (5%)
  between operations  14.6 us (5%)
    all_gather x1, blocking collectives, local(): lax.all_gather(expert_ids, 'inner', axis=0, tiled=True)  64.7 us
    all_gather x1, waiting for transfers between devices, local(): lax.all_gather(cotangent, 'inner', axis=0, tiled=True)  49.3 us
    unnamed x4, waiting for transfers between devices  29.3 us
    all_to_all x1, waiting for transfers between devices, local(): lax.all_to_all(grads, 'inner', split_axis=0, concat_axis=0, tiled=True)  27 us
    convert_element_type x1, other arithmetic, local(): new_weight.astype(jnp.bfloat16)  21.1 us
    dot_general x1, matrix products, local(): jnp.einsum('jlcd,hld->jlch', d_recv, secondary, preferred_element_type=jn...  14 us
    unnamed x11, local copies, waits for them, and re-layouts  12.1 us
    convert_element_type x1, local copies, waits for them, and re-layouts, local(): jnp.einsum('jlch,jlcd->hld', w_recv, d_recv, preferred_element_type=jnp.f...  11.2 us
  transfers between devices with their start and end apart: 5, of which 3 were waited for; matrix products, arithmetic and copies ran while one was open for 15% of the time, Pallas kernels for 0%

commit v1 on v0

v1 whole, which is shorter than its diff:
```python
import functools

import jax
import jax.numpy as jnp
from jax import lax
from jax.experimental import pallas as pl
from jax.experimental.pallas import tpu as pltpu
from jax.sharding import PartitionSpec as P

EXPERTS = 64
CAP = 24
LANES = 128
MIB = 1 << 20


beta_one = 0.9
beta_two = 0.95
adam_epsilon = 1e-08
learn_rate = 0.003
decay_rate = 0.1
bias_one = 1.0 - 0.9**20
bias_two = 1.0 - 0.95**20

KERNEL_VMEM = 56 * MIB
ANY = pl.BlockSpec(memory_space=pl.ANY)


def slot_targets(flat_ids):
    count = flat_ids.shape[0]
    block = 128
    blocks = count // block
    onehot = (jnp.arange(EXPERTS, dtype=jnp.int32)[:, None] == flat_ids[None, :]).astype(
        jnp.bfloat16
    )
    tiles = onehot.reshape(EXPERTS, blocks, block)
    lower = (jnp.arange(block)[:, None] < jnp.arange(block)[None, :]).astype(jnp.bfloat16)
    within = jnp.einsum("ebk,kj->ebj", tiles, lower, preferred_element_type=jnp.float32)
    totals = jnp.sum(tiles.astype(jnp.float32), axis=2)
    small = (jnp.arange(blocks)[:, None] < jnp.arange(blocks)[None, :]).astype(jnp.float32)
    before = jnp.dot(totals, small, precision=lax.Precision.HIGHEST)
    ranking = (within + before[..., None]).reshape(EXPERTS, count)
    position = jnp.sum(ranking * onehot.astype(jnp.float32), axis=0).astype(jnp.int32)
    return flat_ids * CAP + position


def line_ring(length):
    return [0] + list(range(1, length, 2)) + list(range(2, length, 2))[::-1]


def ring_place(plane, length):
    return jnp.where(plane % 2 == 1, (plane + 1) // 2, (length - plane // 2) % length)


def ring_plane(place, length):
    up = 2 * place - 1
    down = 2 * (length - place)
    return jnp.where(place == 0, 0, jnp.where(up < length, up, down))


def step_perm(size, steps, flip):
    ring = line_ring(size // 4)
    after = {at: ring[(i + steps) % len(ring)] for i, at in enumerate(ring)}
    return [(i, after[i // 4] * 4 + (i % 4 ^ flip)) for i in range(size)]


def source_order(size):
    me = lax.axis_index("inner")
    length = size // 4
    steps = jnp.arange(length, dtype=jnp.int32)
    flips = jnp.arange(4, dtype=jnp.int32)
    at = ring_plane((ring_place(me // 4, length) - steps) % length, length)
    return (at[:, None] * 4 + (me % 4 ^ flips)[None, :]).reshape(size)


def gather_groups(shard, size):
    half = shard.shape[0] // 2
    length = size // 4

    def move(block, steps, flip):
        return lax.ppermute(block, "inner", step_perm(size, steps, flip))

    own, here, by_x, by_y = shard, None, None, None
    for k in range(length + 1):
        moving = {}
        if k < length - 1:
            moving["own"] = move(own, 1, 0)
        if k < length:
            moving["x"] = move(own, 0, 1)
            moving["y"] = move(own, 0, 2)
        if k > 0:
            moving["low"] = move(by_x[:half], 0, 2)
            moving["high"] = move(by_y[half:], 0, 1)
        moved = yield moving
        if k > 0:
            yield (here, by_x, by_y, moved["low"], moved["high"])
        else:
            yield None
        here, own = own, moved.get("own")
        by_x, by_y = moved.get("x"), moved.get("y")


def grads_kernel(order, match, a, x, y, low, high, by_expert, *refs):
    d_out, g_all, match_in, rows, weights, d_rows, grads, sems = refs[-8:]
    experts, width, features = by_expert.shape
    count = d_out.shape[0] // experts
    pieces = (a, x, y, low, high)
    loads, at = [], 0
    for piece in pieces:
        loads.append((piece, rows.at[pl.ds(at, piece.shape[0])]))
        at += piece.shape[0]
    loads.append((match, match_in))
    loads += [(by_expert.at[e], weights.at[e]) for e in range(experts)]
    loads = [pltpu.make_async_copy(s, d, sems.at[i]) for i, (s, d) in enumerate(loads)]
    for load in loads:
        load.start()
    for load in loads[:6]:
        load.wait()
    step = min(512, features)
    for at in range(0, features, step):
        d_rows[:, at : at + step] = jnp.dot(
            match_in[...], rows[:, at : at + step], preferred_element_type=jnp.float32
        ).astype(jnp.bfloat16)
    first = 6 + experts
    stores = [pltpu.make_async_copy(d_rows, d_out, sems.at[first])]
    stores[0].start()
    parts = []
    for e in range(experts):
        loads[6 + e].wait()
        parts.append(
            lax.dot_general(
                d_rows[e * count : (e + 1) * count],
                weights[e],
                (((1,), (1,)), ((), ())),
                preferred_element_type=jnp.float32,
            )
        )
    for c in range(4):
        mine = [p[c * CAP : (c + 1) * CAP] for p in parts]
        grads[c] = jnp.concatenate(mine, axis=0).astype(jnp.bfloat16)
        store = pltpu.make_async_copy(grads.at[c], g_all.at[order[c]], sems.at[first + 1 + c])
        store.start()
        stores.append(store)
    for store in stores:
        store.wait()


def chunk_grads(order, match, part, by_expert, g_all, size):
    experts, width, features = by_expert.shape
    count, tokens = match.shape
    before = [] if g_all is None else [g_all]
    return pl.pallas_call(
        grads_kernel,
        out_shape=(
            jax.ShapeDtypeStruct((count, features), jnp.bfloat16),
            jax.ShapeDtypeStruct((size, experts * CAP, width), jnp.bfloat16),
        ),
        in_specs=[pl.BlockSpec(memory_space=pltpu.SMEM)] + [ANY] * (7 + len(before)),
        out_specs=(ANY, ANY),
        scratch_shapes=[
            pltpu.VMEM((count, tokens), jnp.bfloat16),
            pltpu.VMEM((tokens, features), jnp.bfloat16),
            pltpu.VMEM(by_expert.shape, jnp.bfloat16),
            pltpu.VMEM((count, features), jnp.bfloat16),
            pltpu.VMEM((4, experts * CAP, width), jnp.bfloat16),
            pltpu.SemaphoreType.DMA((11 + experts,)),
        ],
        input_output_aliases={8: 1} if before else {},
        compiler_params=pltpu.CompilerParams(vmem_limit_bytes=KERNEL_VMEM),
        cost_estimate=pl.CostEstimate(
            flops=2 * count * features * (tokens + width),
            bytes_accessed=2 * (by_expert.size + 2 * tokens * features),
            transcendentals=0,
        ),
    )(order, match, *part, by_expert, *before)


def partial_kernel(weighted, *refs):
    blocks, (out, w_in, rows, sums, sems) = refs[:-5], refs[-5:]
    experts, _, features = out.shape
    count = blocks[0].shape[0] // experts
    first = pltpu.make_async_copy(weighted, w_in, sems.at[0])
    first.start()
    loads = []
    for e in range(experts):
        for k, block in enumerate(blocks):
            loads.append(
                pltpu.make_async_copy(
                    block.at[pl.ds(e * count, count)],
                    rows.at[e, pl.ds(k * count, count)],
                    sems.at[len(loads) + 1],
                )
            )
            loads[-1].start()
    first.wait()
    stores = []
    step = min(1024, features)
    for e in range(experts):
        for load in loads[e * len(blocks) : (e + 1) * len(blocks)]:
            load.wait()
        for at in range(0, features, step):
            sums[e, :, at : at + step] = jnp.dot(
                w_in[e], rows[e, :, at : at + step], preferred_element_type=jnp.float32
            ).astype(jnp.bfloat16)
        store = pltpu.make_async_copy(sums.at[e], out.at[e], sems.at[len(loads) + 1 + e])
        store.start()
        stores.append(store)
    for store in stores:
        store.wait()


def partial_rows(weighted, blocks):
    experts, rows, slots = weighted.shape
    features = blocks[0].shape[1]
    return pl.pallas_call(
        partial_kernel,
        out_shape=jax.ShapeDtypeStruct((experts, rows, features), jnp.bfloat16),
        in_specs=[ANY] * (1 + len(blocks)),
        out_specs=ANY,
        scratch_shapes=[
            pltpu.VMEM(weighted.shape, jnp.bfloat16),
            pltpu.VMEM((experts, slots, features), jnp.bfloat16),
            pltpu.VMEM((experts, rows, features), jnp.bfloat16),
            pltpu.SemaphoreType.DMA((experts * (len(blocks) + 1) + 1,)),
        ],
        compiler_params=pltpu.CompilerParams(vmem_limit_bytes=KERNEL_VMEM),
        cost_estimate=pl.CostEstimate(
            flops=2 * weighted.size * features,
            bytes_accessed=2 * (experts * rows + experts * slots) * features,
            transcendentals=0,
        ),
    )(weighted, *blocks)


def adam_kernel(count, at, *refs):
    del at
    partials, (w, m1, m2, new_w, new_m1, new_m2, copy, full, grad) = refs[:count], refs[count:]
    experts, rows, features = partials[0].shape
    tiles = features // LANES
    for e in range(experts):
        total = partials[0][e].astype(jnp.float32)
        for part in partials[1:]:
            total = total + part[e].astype(jnp.float32)
        for t in range(tiles):
            grad[pl.ds(t * experts + e, rows, stride=tiles * experts), :] = total[
                :, t * LANES : (t + 1) * LANES
            ]
    g = grad[...]
    one = beta_one * m1[...] + (1.0 - beta_one) * g
    two = beta_two * m2[...] + (1.0 - beta_two) * g * g
    new_m1[...] = one
    new_m2[...] = two
    old = w[...]
    update = one * (1.0 / bias_one) / (jnp.sqrt(two * (1.0 / bias_two)) + adam_epsilon)
    new = old - learn_rate * (update + decay_rate * old)
    new_w[...] = new
    copy[...] = new.astype(jnp.bfloat16)
    full[...] = new.astype(jnp.bfloat16)


def adam_rows(at, partials, w, m1, m2, total_rows):
    experts, rows, features = partials[0].shape
    block = 16
    steps = rows // block
    flat = block * experts * features // LANES
    count = len(partials)
    part = pl.BlockSpec((experts, block, features), lambda i, at: (0, i, 0))
    line = pl.BlockSpec((flat, LANES), lambda i, at: (i, 0))
    placed = pl.BlockSpec((flat, LANES), lambda i, at: (at[0] * steps + i, 0))
    return pl.pallas_call(
        functools.partial(adam_kernel, count),
        grid_spec=pltpu.PrefetchScalarGridSpec(
            num_scalar_prefetch=1,
            grid=(steps,),
            in_specs=[part] * count + [line] * 3,
            out_specs=[line] * 4 + [placed],
            scratch_shapes=[pltpu.VMEM((flat, LANES), jnp.float32)],
        ),
        out_shape=[jax.ShapeDtypeStruct(w.shape, jnp.float32)] * 3
        + [
            jax.ShapeDtypeStruct(w.shape, jnp.bfloat16),
            jax.ShapeDtypeStruct((total_rows, LANES), jnp.bfloat16),
        ],
        compiler_params=pltpu.CompilerParams(vmem_limit_bytes=KERNEL_VMEM),
        cost_estimate=pl.CostEstimate(
            flops=20 * w.size, bytes_accessed=32 * w.size, transcendentals=2 * w.size
        ),
    )(at, *partials, w, m1, m2)


def place_kernel(owner, got, full, out):
    del owner, full
    out[...] = got[...]


def place_rows(owner, got, full):
    block = min(got.shape[0], 3072)
    steps = got.shape[0] // block
    return pl.pallas_call(
        place_kernel,
        grid_spec=pltpu.PrefetchScalarGridSpec(
            num_scalar_prefetch=1,
            grid=(steps,),
            in_specs=[pl.BlockSpec((block, LANES), lambda i, at: (i, 0)), ANY],
            out_specs=pl.BlockSpec((block, LANES), lambda i, at: (at[0] * steps + i, 0)),
        ),
        out_shape=jax.ShapeDtypeStruct(full.shape, full.dtype),
        input_output_aliases={2: 0},
        compiler_params=pltpu.CompilerParams(vmem_limit_bytes=KERNEL_VMEM),
        cost_estimate=pl.CostEstimate(flops=0, bytes_accessed=4 * got.size, transcendentals=0),
    )(owner, got, full)


def finish_kernel(target, probs, hidden, rows, d_hidden, d_probs):
    choices, width = hidden.shape
    slots = rows.shape[0]
    places = lax.broadcasted_iota(jnp.int32, (choices, slots), 1)
    onehot = jnp.where(places == target[...], 1.0, 0.0).astype(jnp.bfloat16)
    g = jnp.dot(onehot, rows[...], preferred_element_type=jnp.float32)
    d_hidden[...] = (probs[...] * g).astype(jnp.bfloat16)
    d_probs[...] = lax.dot_general(
        jnp.ones((8, width), jnp.float32),
        hidden[...].astype(jnp.float32) * g,
        (((1,), (1,)), ((), ())),
        precision=lax.Precision.HIGHEST,
        preferred_element_type=jnp.float32,
    )


def finish(target, probs, hidden, back):
    choices, width = hidden.shape
    slots = back.shape[0]
    step = 256
    column = pl.BlockSpec((step, 1), lambda i: (i, 0))
    block = pl.BlockSpec((step, width), lambda i: (i, 0))
    return pl.pallas_call(
        finish_kernel,
        grid=(choices // step,),
        out_shape=(
            jax.ShapeDtypeStruct((choices, width), jnp.bfloat16),
            jax.ShapeDtypeStruct((8, choices), jnp.float32),
        ),
        in_specs=[column, column, block, pl.BlockSpec((slots, width), lambda i: (0, 0))],
        out_specs=(block, pl.BlockSpec((8, step), lambda i: (0, i))),
        compiler_params=pltpu.CompilerParams(vmem_limit_bytes=KERNEL_VMEM),
        cost_estimate=pl.CostEstimate(
            flops=2 * choices * slots * width, bytes_accessed=8 * hidden.size, transcendentals=0
        ),
    )(target, probs, hidden, back)


def lane_view(array):
    h, e, d = array.shape
    return array.reshape(h, e, d // LANES, LANES).transpose(0, 2, 1, 3).reshape(-1, LANES)


def lane_unview(rows, shape):
    h, e, d = shape
    return rows.reshape(h, d // LANES, e, LANES).transpose(0, 2, 1, 3).reshape(shape)


def local(cotangent, hidden, probs, expert_ids, secondary, weight, moment1, moment2):
    token_count = cotangent.shape[0]
    top_k = expert_ids.shape[1]
    hidden_width = hidden.shape[2]
    experts = secondary.shape[1]
    size = lax.axis_size("inner")
    length = size // 4
    outer_size = lax.axis_size("outer")
    outer_at = lax.axis_index("outer")
    choices = token_count * top_k
    slots = experts * CAP
    rows = weight.shape[0]

    flat_ids = expert_ids.reshape(choices)
    target = slot_targets(flat_ids)
    all_slots = jnp.arange(EXPERTS * CAP, dtype=jnp.int32)
    matches = (all_slots[:, None] == target[None, :]).astype(jnp.bfloat16)
    weighted = (
        (probs[..., None] * hidden.astype(jnp.float32))
        .astype(jnp.bfloat16)
        .reshape(choices, hidden_width)
    )
    w_send = jnp.dot(matches, weighted, preferred_element_type=jnp.float32).astype(jnp.bfloat16)
    w_send = w_send.reshape(size, slots, hidden_width)
    number = (jnp.arange(choices, dtype=jnp.int32) // top_k + 1).astype(jnp.bfloat16)
    token_at = jnp.dot(matches, number[:, None], preferred_element_type=jnp.float32)
    token_at = token_at.astype(jnp.bfloat16).reshape(size, 1, slots)
    token_at = jnp.pad(token_at, ((0, 0), (0, 7), (0, hidden_width - slots)))
    w_send = jnp.concatenate([w_send, token_at], axis=1)
    by_expert = jnp.transpose(secondary, (1, 0, 2))
    columns = (target[:, None], probs.reshape(choices, 1))
    order = source_order(size).reshape(length, 4)
    g_all = None

    def prepare(w_recv):
        w_recv = jnp.take(w_recv, order.reshape(size), axis=0)
        slot_token = w_recv[:, slots, :slots].astype(jnp.int32).reshape(length, 4, experts, CAP)
        first = token_count * jnp.arange(4, dtype=jnp.int32)[None, :, None, None] - 1
        slot_row = jnp.where(slot_token > 0, slot_token + first, -1)
        slot_row = slot_row.transpose(0, 2, 1, 3).reshape(length, 4 * slots)
        tokens = jnp.arange(4 * token_count, dtype=jnp.int32)
        match = [(slot_row[k][:, None] == tokens).astype(jnp.bfloat16) for k in range(length)]
        w_slots = w_recv[:, :slots].reshape(size, experts, CAP, hidden_width)
        w_slots = w_slots.transpose(1, 3, 0, 2).reshape(experts, hidden_width, size * CAP)
        owners = [
            lax.dynamic_slice_in_dim(w_slots, (outer_at + r) % outer_size * rows, rows, 1)
            for r in range(outer_size)
        ]
        return match, owners

    groups = gather_groups(cotangent, size)
    parts, d_rows = [], []
    for k in range(length + 1):
        moving = next(groups)
        if k == 0:
            moving, w_send = lax.optimization_barrier((moving, w_send))
            w_recv = lax.all_to_all(w_send, "inner", split_axis=0, concat_axis=0, tiled=True)
        elif k == 1:
            moving, by_expert, columns = lax.optimization_barrier((moving, by_expert, columns))
        elif k >= 3:
            if k == 3:
                match, owners = prepare(w_recv)
            for j in (k - 3,) if k < length else (k - 3, k - 2):
                d_chunk, g_all = chunk_grads(order[j], match[j], parts[j], by_expert, g_all, size)
                d_rows.append(d_chunk)
            moving, d_rows, g_all, match, owners = lax.optimization_barrier(
                (moving, d_rows, g_all, match, owners)
            )
        part = groups.send(moving)
        if part is not None:
            parts.append(part)
    last = length - 1
    d_chunk, g_all = chunk_grads(order[last], match[last], parts[last], by_expert, g_all, size)
    d_rows.append(d_chunk)
    back = lax.all_to_all(g_all, "inner", split_axis=0, concat_axis=0, tiled=True)

    def outer_perm(steps):
        return [(i, (i + steps) % outer_size) for i in range(outer_size)]

    partials = []
    for r in range(1, outer_size):
        sent = partial_rows(owners[r], d_rows)
        partials.append(lax.ppermute(sent, "outer", outer_perm(r)))
    partials.append(partial_rows(owners[0], d_rows))

    new_weight, new_moment1, new_moment2, copy, full = adam_rows(
        outer_at.astype(jnp.int32)[None],
        partials,
        lane_view(weight),
        lane_view(moment1),
        lane_view(moment2),
        secondary.size // LANES,
    )
    for r in range(1, outer_size):
        got = lax.ppermute(copy, "outer", outer_perm(r))
        owner = (outer_at + outer_size - r) % outer_size
        full = place_rows(owner.astype(jnp.int32)[None], got, full)

    d_hidden, d_probs = finish(
        *columns,
        hidden.reshape(choices, hidden_width),
        back.reshape(size * slots, hidden_width),
    )
    return (
        d_hidden.reshape(hidden.shape),
        d_probs[0].reshape(probs.shape),
        lane_unview(new_weight, weight.shape),
        lane_unview(new_moment1, weight.shape),
        lane_unview(new_moment2, weight.shape),
        lane_unview(full, secondary.shape),
    )


def solution(mesh):
    in_specs = (
        P(("outer", "inner"), None),
        P(("outer", "inner"), None, None),
        P(("outer", "inner"), None),
        P(("outer", "inner"), None),
        P(None, "inner", None),
        P("outer", "inner", None),
        P("outer", "inner", None),
        P("outer", "inner", None),
    )
    out_specs = (
        P(("outer", "inner"), None, None),
        P(("outer", "inner"), None),
        P("outer", "inner", None),
        P("outer", "inner", None),
        P("outer", "inner", None),
        P(None, "inner", None),
    )
    return jax.shard_map(local, mesh=mesh, in_specs=in_specs, out_specs=out_specs, check_vma=False)
```

time: 296 us -> 214 us (0.72)
  Pallas kernels: 0 us -> 72.5 us
  blocking collectives: 64.7 us -> 0 us
  waiting for transfers between devices: 106 us -> 64.5 us
  matrix products: 37.8 us -> 4.52 us
  other arithmetic: 27.1 us -> 6.85 us
  starting transfers between devices: 15.2 us -> 34.1 us
  between operations: 14.6 us -> 1.11 us
    pallas_call x0 -> x9, Pallas kernels: none -> 72.5 us  [the longest x4 28.2 us: chunk_grads(): pl.pallas_call(grads_kernel, out_shape=(jax.ShapeDtypeStruct((count, feat...]
    all_gather x1 -> x0, blocking collectives: 64.7 us -> none  [local(): lax.all_gather(expert_ids, 'inner', axis=0, tiled=True)]
    all_gather x2 -> x0, waiting for transfers between devices: 49.3 us -> none  [the longest x1 49.3 us: local(): lax.all_gather(cotangent, 'inner', axis=0, tiled=True)]
    ppermute x0 -> x21, waiting for transfers between devices: none -> 38.4 us  [the longest x19 37.5 us: move(): return lax.ppermute(block, 'inner', step_perm(size, steps, flip))]
    dot_general x3 -> x1, matrix products: 31.4 us -> 1.15 us  [local(): jnp.dot(matches, number[:, None], preferred_element_type=jnp.float32)]
    unnamed x4 -> x0, waiting for transfers between devices: 29.3 us -> none
    ppermute x0 -> x21, starting transfers between devices: none -> 24.2 us  [the longest x19 24 us: move(): return lax.ppermute(block, 'inner', step_perm(size, steps, flip))]
    convert_element_type x1 -> x6, other arithmetic: 21.1 us -> 3.6 us  [the longest x4 3.56 us: prepare(): (slot_row[k][:, None] == tokens).astype(jnp.bfloat16)]
  transfers between devices with their start and end apart: 5 -> 23, of which waited for: 3 -> 9; matrix products, arithmetic and copies ran while one was open for 15% -> 17% of each run, Pallas kernels for 0% -> 16%
where the time goes in v1:
time: 214 us; the launch traced here: 213 us
  Pallas kernels  72.5 us (34%)
  waiting for transfers between devices  64.5 us (30%)
  starting transfers between devices  34.1 us (16%)
  local copies, waits for them, and re-layouts  29 us (14%)
  other arithmetic  6.85 us (3%)
  matrix products  4.52 us (2%)
    ppermute x19, waiting for transfers between devices, move(): return lax.ppermute(block, 'inner', step_perm(size, steps, flip))  37.5 us
    pallas_call x4, Pallas kernels, chunk_grads(): pl.pallas_call(grads_kernel, out_shape=(jax.ShapeDtypeStruct((count, feat...  28.2 us
    all_to_all x1, waiting for transfers between devices, local(): lax.all_to_all(g_all, 'inner', split_axis=0, concat_axis=0, tiled=True)  26.1 us
    ppermute x19, starting transfers between devices, move(): return lax.ppermute(block, 'inner', step_perm(size, steps, flip))  24 us
    pallas_call x1, Pallas kernels, adam_rows(): pl.pallas_call(functools.partial(adam_kernel, count), grid_spec=pltpu.Pre...  22.8 us
    unnamed x30, local copies, waits for them, and re-layouts  14 us
    pallas_call x2, Pallas kernels, partial_rows(): pl.pallas_call(partial_kernel, out_shape=jax.ShapeDtypeStruct((experts, r...  9.86 us
    pallas_call x1, Pallas kernels, finish(): pl.pallas_call(finish_kernel, grid=(choices // step,), out_shape=(jax.Sha...  7.49 us
  transfers between devices with their start and end apart: 23, of which 9 were waited for; matrix products, arithmetic and copies ran while one was open for 17% of the time, Pallas kernels for 16%

profile of v1, /device:TPU:0, one launch (start us, length us, event | category | flops | bytes accessed | tf_op | source)
XLA Modules:
  0.0 212.6 jit_solution(4087597742617898743)
XLA Ops:
  0.6 3.0 %collective-permute-start.1 = (bf16[128,2048]{1,0:T(8,128)(2,1)}, bf16[128,2048]{1,0:T(8,128)(2,1)S(1)}, u32[]{:S(2)}, u32[]{:S(2)}) collective-permute-start(bf16[128,2048]{1,0:T(8,128)(2,1)} %a.1), channel_id=1, source_target_pairs={{0,1},{1,0},{2,3},{3,2},{4,5},{5,4},{6,7},{7,6},{8,9},{9,8},{10,11... | collective-permute-start | bytes 1572872 | tf_op jit(solution)/shard_map/ppermute | solution.py:80
  3.6 1.6 collective-permute-start
  5.2 1.5 collective-permute-start.2
  6.7 0.7 broadcast_multiply_fusion
  7.4 0.8 copy.32
  9.0 1.2 fusion.9
  10.4 3.0 %fusion.4 = bf16[1536,384]{1,0:T(8,128)(2,1)S(1)} fusion(s32[1024]{0:T(1024)S(1)} %bitcast_add_fusion, bf16[128,8,384]{2,1,0:T(8,128)(2,1)} %param.9, f32[128,8]{1,0:T(8,128)S(1)} %copy.34), kind=kOutput, calls=%fused_computation.7 | convolution fusion | flops 1211301888 | bytes 1974272 | tf_op jit(solution)/shard_map/dot_general | solution.py:383
  13.4 1.2 fusion.6
  14.6 1.2 collective-permute-done.1.x
  15.8 2.5 %collective-permute-done.a = bf16[128,2048]{1,0:T(8,128)(2,1)} collective-permute-done((bf16[128,2048]{1,0:T(8,128)(2,1)}, bf16[128,2048]{1,0:T(8,128)(2,1)}, u32[]{:S(2)}, u32[]{:S(2)}) %collective-permute-start) | collective-permute-done | bytes 524320 | tf_op jit(solution)/shard_map/ppermute | solution.py:80
  18.3 0.3 collective-permute-done.2.y
  18.5 5.7 %all-to-all-start = ((bf16[16,104,384]{2,1,0:T(8,128)(2,1)}), bf16[16,104,384]{2,1,0:T(8,128)(2,1)S(1)}, u32[]{:S(2)}, u32[]{:S(2)}) async-start(bf16[16,104,384]{2,1,0:T(8,128)(2,1)} %fusion.6), calls=%async_computation | async-start | bytes 2555904 | tf_op jit(solution)/shard_map/all_to_all | solution.py:417
  24.3 1.9 collective-permute-start.7
  26.2 1.5 collective-permute-start.6
  27.7 1.5 collective-permute-start.5
  29.9 8.9 %copy.61 = bf16[384,4,2048]{2,0,1:T(8,128)(2,1)} copy(bf16[384,4,2048]{2,1,0:T(4,128)(2,1)} %param.12) | data formatting | bytes 12582912 | tf_op args[4]
  38.8 0.8 add.148.target
  39.7 0.6 collective-permute-start.4
  40.4 0.6 collective-permute-start.3
  40.9 14.9 %collective-permute-done.4.low = bf16[64,2048]{1,0:T(8,128)(2,1)S(1)} collective-permute-done((bf16[64,2048]{1,0:T(8,128)(2,1)S(1)}, bf16[64,2048]{1,0:T(8,128)(2,1)S(1)}, u32[]{:S(2)}, u32[]{:S(2)}) %collective-permute-start.4) | collective-permute-done | bytes 262176 | tf_op jit(solution)/shard_map/ppermute | solution.py:80
  55.8 9.2 %collective-permute-done.5.a = bf16[128,2048]{1,0:T(8,128)(2,1)} collective-permute-done((bf16[128,2048]{1,0:T(8,128)(2,1)}, bf16[128,2048]{1,0:T(8,128)(2,1)}, u32[]{:S(2)}, u32[]{:S(2)}) %collective-permute-start.5) | collective-permute-done | bytes 524320 | tf_op jit(solution)/shard_map/ppermute | solution.py:80
  65.0 1.5 collective-permute-start.10
  66.6 2.1 collective-permute-start.8
  68.7 0.6 slice_bitcast_fusion
  69.2 1.7 slice.76
  70.9 1.7 slice.77
  72.6 0.6 collective-permute-start.18
  73.1 7.0 %collective-permute-done.10.x = bf16[128,2048]{1,0:T(8,128)(2,1)S(1)} collective-permute-done((bf16[128,2048]{1,0:T(8,128)(2,1)}, bf16[128,2048]{1,0:T(8,128)(2,1)S(1)}, u32[]{:S(2)}, u32[]{:S(2)}) %collective-permute-start.10) | collective-permute-done | bytes 524320 | tf_op jit(solution)/shard_map/ppermute | solution.py:80
  80.2 0.8 slice.83
  80.9 2.1 collective-permute-start.11
  83.1 1.5 collective-permute-start.13
  84.6 0.8 slice.82
  85.3 0.8 gather_fusion
  86.9 0.9 fusion.13.match
  87.8 0.9 fusion.14.match
  88.7 0.9 fusion.15.match
  89.9 0.8 constant_dynamic-slice_fusion
  90.6 2.4 %collective-permute-done.11.low = bf16[64,2048]{1,0:T(8,128)(2,1)} collective-permute-done((bf16[64,2048]{1,0:T(8,128)(2,1)}, bf16[64,2048]{1,0:T(8,128)(2,1)}, u32[]{:S(2)}, u32[]{:S(2)}) %collective-permute-start.11) | collective-permute-done | bytes 262176 | tf_op jit(solution)/shard_map/ppermute | solution.py:80
  93.1 0.6 collective-permute-start.9
  93.6 7.0 %shard_map.127 = (bf16[384,2048]{1,0:T(8,128)(2,1)}, bf16[16,96,384]{2,1,0:T(8,128)(2,1)}) custom-call(s32[4]{0:T(128)} %get-tuple-element.120.order, bf16[384,512]{1,0:T(8,128)(2,1)} %fusion.13.match, bf16[128,2048]{1,0:T(8,128)(2,1)} %a.1, bf16[128,2048]{1,0:T(8,128)(2,1)} %copy-done.1, bf16[128,2048]{1,0:T(8,128)(2,1)} %copy-done.2, ...), custom_call_target="tpu_custom_call" | custom-call | flops 1409286144 | bytes 10485760 | tf_op jit(solution)/shard_map/pallas_call | solution.py:151
  100.7 1.1 copy.57.weighted
  101.8 1.1 copy.56.weighted
  102.9 0.9 fusion.16.match
  103.8 1.1 slice.73
  104.9 1.0 slice.74
  105.9 2.1 collective-permute-start.16
  107.9 1.5 collective-permute-start.15
  109.4 7.0 %shard_map.128 = (bf16[384,2048]{1,0:T(8,128)(2,1)}, bf16[16,96,384]{2,1,0:T(8,128)(2,1)}) custom-call(s32[4]{0:T(128)} %get-tuple-element.119.order, bf16[384,512]{1,0:T(8,128)(2,1)} %fusion.14.match, bf16[128,2048]{1,0:T(8,128)(2,1)} %collective-permute-done.a, bf16[128,2048]{1,0:T(8,128)(2,1)} %collective-permute-done.6.x, ...), custom_call_target="tpu_custom_call", output_to_operand_aliasing={{1}: (8, {})} | custom-call | flops 1409286144 | bytes 10485760 | tf_op jit(solution)/shard_map/pallas_call | solution.py:151
  116.4 7.0 %shard_map.129 = (bf16[384,2048]{1,0:T(8,128)(2,1)}, bf16[16,96,384]{2,1,0:T(8,128)(2,1)}) custom-call(s32[4]{0:T(128)} %get-tuple-element.118.order, bf16[384,512]{1,0:T(8,128)(2,1)} %fusion.15.match, bf16[128,2048]{1,0:T(8,128)(2,1)} %collective-permute-done.5.a, bf16[128,2048]{1,0:T(8,128)(2,1)} %copy-done.3, ...), custom_call_target="tpu_custom_call", output_to_operand_aliasing={{1}: (8, {})} | custom-call | flops 1409286144 | bytes 10485760 | tf_op jit(solution)/shard_map/pallas_call | solution.py:151
  123.5 0.7 copy-done.9
  124.2 7.2 %shard_map.130 = (bf16[384,2048]{1,0:T(8,128)(2,1)}, bf16[16,96,384]{2,1,0:T(8,128)(2,1)}) custom-call(s32[4]{0:T(128)} %get-tuple-element.121.order, bf16[384,512]{1,0:T(8,128)(2,1)} %fusion.16.match, bf16[128,2048]{1,0:T(8,128)(2,1)} %collective-permute-done.12.a, bf16[128,2048]{1,0:T(8,128)(2,1)} %collective-permute-done.13.x, ...), custom_call_target="tpu_custom_call", output_to_operand_aliasing={{1}: (8, {})} | custom-call | flops 1409286144 | bytes 10485760 | tf_op jit(solution)/shard_map/pallas_call | solution.py:151
  131.4 4.9 %shard_map.132 = bf16[4,192,2048]{2,1,0:T(8,128)(2,1)} custom-call(bf16[4,192,384]{2,1,0:T(8,128)(2,1)} %copy.57.weighted, bf16[384,2048]{1,0:T(8,128)(2,1)} %get-tuple-element.90.refs_0_, bf16[384,2048]{1,0:T(8,128)(2,1)} %get-tuple-element.91.refs_1_, bf16[384,2048]{1,0:T(8,128)(2,1)} %get-tuple-element.92.refs_2_, bf16[384,2048]{1,0:T(8,128)(2,1)} %get-tuple-element.93.refs_3_), custom_call_target="tpu_custom_call" | custom-call | flops 1207959552 | bytes 9437184 | tf_op jit(solution)/shard_map/pallas_call | solution.py:214
  136.4 4.9 %shard_map.133.refs_1_ = bf16[4,192,2048]{2,1,0:T(8,128)(2,1)} custom-call(bf16[4,192,384]{2,1,0:T(8,128)(2,1)} %copy.56.weighted, bf16[384,2048]{1,0:T(8,128)(2,1)} %get-tuple-element.90.refs_0_, bf16[384,2048]{1,0:T(8,128)(2,1)} %get-tuple-element.91.refs_1_, bf16[384,2048]{1,0:T(8,128)(2,1)} %get-tuple-element.92.refs_2_, ...), custom_call_target="tpu_custom_call" | custom-call | flops 1207959552 | bytes 9437184 | tf_op jit(solution)/shard_map/pallas_call | solution.py:214
  141.4 0.9 collective-permute-done.19.refs_0_
  142.3 1.7 copy-done
  144.0 22.8 %shard_map.134 = (f32[12288,128]{1,0:T(8,128)}, f32[12288,128]{1,0:T(8,128)}, f32[12288,128]{1,0:T(8,128)}, bf16[12288,128]{1,0:T(8,128)(2,1)}, bf16[24576,128]{1,0:T(8,128)(2,1)}) custom-call(s32[1]{0:T(128)} %bitcast.18.at, bf16[4,192,2048]{2,1,0:T(8,128)(2,1)} %copy-done, bf16[4,192,2048]{2,1,0:T(8,128)(2,1)} %shard_map.133.refs_1_, ...), custom_call_target="tpu_custom_call" | custom-call | flops 31457280 | bytes 50331648 | tf_op jit(solution)/shard_map/pallas_call | solution.py:269
  166.9 4.3 %all-to-all-start.1 = ((bf16[16,96,384]{2,1,0:T(8,128)(2,1)}), bf16[16,96,384]{2,1,0:T(8,128)(2,1)S(1)}, u32[]{:S(2)}, u32[]{:S(2)}) async-start(bf16[16,96,384]{2,1,0:T(8,128)(2,1)} %get-tuple-element.86), calls=%async_computation.1 | async-start | bytes 2359296 | tf_op jit(solution)/shard_map/all_to_all | solution.py:435
  171.2 1.1 copy.46.probs
  172.2 26.1 %all-to-all-done.1 = bf16[16,96,384]{2,1,0:T(8,128)(2,1)S(1)} async-done(((bf16[16,96,384]{2,1,0:T(8,128)(2,1)}), bf16[16,96,384]{2,1,0:T(8,128)(2,1)S(1)}, u32[]{:S(2)}, u32[]{:S(2)}) %all-to-all-start.1) | async-done | bytes 1179680 | tf_op jit(solution)/shard_map/all_to_all | solution.py:435
  198.3 1.0 copy-done.5
  199.4 7.5 %shard_map.131 = (bf16[1024,384]{1,0:T(8,128)(2,1)}, f32[8,1024]{1,0:T(8,128)}) custom-call(s32[1024,1]{1,0:T(8,128)} %add.148.target, f32[1024,1]{1,0:T(8,128)} %copy.46.probs, bf16[1024,384]{1,0:T(8,128)(2,1)} %bitcast.87, bf16[1536,384]{1,0:T(8,128)(2,1)} %bitcast.81), custom_call_target="tpu_custom_call" | custom-call | flops 1207959552 | bytes 3145728 | tf_op jit(solution)/shard_map/pallas_call | solution.py:335
  206.8 0.8 slice_reduce_fusion
  207.7 0.7 copy.54
  208.4 4.2 %shard_map.135 = bf16[24576,128]{1,0:T(8,128)(2,1)} custom-call(s32[1]{0:T(128)} %bitcast.37.owner, bf16[12288,128]{1,0:T(8,128)(2,1)} %collective-permute-done.20.got, bf16[24576,128]{1,0:T(8,128)(2,1)} %get-tuple-element.99.full), custom_call_target="tpu_custom_call", output_to_operand_aliasing={{}: (2, {})} | custom-call | bytes 6291456 | tf_op jit(solution)/shard_map/pallas_call | solution.py:298
  (79 shorter events, 3.3 us)
Async XLA Ops:
  0.6 9.6 %copy-start.12 = (f32[128,8]{0,1:T(8,128)S(1)}, f32[128,8]{0,1:T(8,128)}, u32[]{:S(2)}) copy-start(f32[128,8]{0,1:T(8,128)} %param.10) | copy-start | bytes 12292
  0.6 15.1 %collective-permute-start.1 = (bf16[128,2048]{1,0:T(8,128)(2,1)}, bf16[128,2048]{1,0:T(8,128)(2,1)S(1)}, u32[]{:S(2)}, u32[]{:S(2)}) collective-permute-start(bf16[128,2048]{1,0:T(8,128)(2,1)} %a.1), channel_id=1, source_target_pairs={{0,1},{1,0},{2,3},{3,2},{4,5},{5,4},{6,7},{7,6},{8,9},{9,8},{10,11... | collective-permute-start | bytes 1572872 | tf_op jit(solution)/shard_map/ppermute | solution.py:80
  3.6 14.6 %collective-permute-start = (bf16[128,2048]{1,0:T(8,128)(2,1)}, bf16[128,2048]{1,0:T(8,128)(2,1)}, u32[]{:S(2)}, u32[]{:S(2)}) collective-permute-start(bf16[128,2048]{1,0:T(8,128)(2,1)} %a.1), channel_id=1, source_target_pairs={{0,4},{1,5},{2,6},{3,7},{4,12},{5,13},{6,14},{7,15},{8,0},{9,1},{1... | collective-permute-start | bytes 1572872 | tf_op jit(solution)/shard_map/ppermute | solution.py:80
  5.2 13.3 %collective-permute-start.2 = (bf16[128,2048]{1,0:T(8,128)(2,1)}, bf16[128,2048]{1,0:T(8,128)(2,1)S(1)}, u32[]{:S(2)}, u32[]{:S(2)}) collective-permute-start(bf16[128,2048]{1,0:T(8,128)(2,1)} %a.1), channel_id=1, source_target_pairs={{0,2},{1,3},{2,0},{3,1},{4,6},{5,7},{6,4},{7,5},{8,10},{9,11},{10,... | collective-permute-start | bytes 1572872 | tf_op jit(solution)/shard_map/ppermute | solution.py:80
  15.8 23.9 %copy-start.1 = (bf16[128,2048]{1,0:T(8,128)(2,1)}, bf16[128,2048]{1,0:T(8,128)(2,1)S(1)}, u32[]{:S(2)}) copy-start(bf16[128,2048]{1,0:T(8,128)(2,1)S(1)} %collective-permute-done.1.x) | copy-start | bytes 1572868
  18.5 21.1 %copy-start.2 = (bf16[128,2048]{1,0:T(8,128)(2,1)}, bf16[128,2048]{1,0:T(8,128)(2,1)S(1)}, u32[]{:S(2)}) copy-start(bf16[128,2048]{1,0:T(8,128)(2,1)S(1)} %collective-permute-done.2.y) | copy-start | bytes 1572868
  18.5 66.8 %all-to-all-start = ((bf16[16,104,384]{2,1,0:T(8,128)(2,1)}), bf16[16,104,384]{2,1,0:T(8,128)(2,1)S(1)}, u32[]{:S(2)}, u32[]{:S(2)}) async-start(bf16[16,104,384]{2,1,0:T(8,128)(2,1)} %fusion.6), calls=%async_computation | async-start | bytes 2555904 | tf_op jit(solution)/shard_map/all_to_all | solution.py:417
  24.3 31.5 %collective-permute-start.7 = (bf16[128,2048]{1,0:T(8,128)(2,1)}, bf16[128,2048]{1,0:T(8,128)(2,1)}, u32[]{:S(2)}, u32[]{:S(2)}) collective-permute-start(bf16[128,2048]{1,0:T(8,128)(2,1)} %collective-permute-done.a), channel_id=1, source_target_pairs={{0,2},{1,3},{2,0},{3,1},{4,6},{5,7},{6,4},{7,5},{8,10},{9,11},{10,... | collective-permute-start | bytes 1572872 | tf_op jit(solution)/shard_map/ppermute | solution.py:80
  26.2 29.6 %collective-permute-start.6 = (bf16[128,2048]{1,0:T(8,128)(2,1)}, bf16[128,2048]{1,0:T(8,128)(2,1)}, u32[]{:S(2)}, u32[]{:S(2)}) collective-permute-start(bf16[128,2048]{1,0:T(8,128)(2,1)} %collective-permute-done.a), channel_id=1, source_target_pairs={{0,1},{1,0},{2,3},{3,2},{4,5},{5,4},{6,7},{7,6},{8,9},{9,8},{10,11... | collective-permute-start | bytes 1572872 | tf_op jit(solution)/shard_map/ppermute | solution.py:80
  27.7 37.4 %collective-permute-start.5 = (bf16[128,2048]{1,0:T(8,128)(2,1)}, bf16[128,2048]{1,0:T(8,128)(2,1)}, u32[]{:S(2)}, u32[]{:S(2)}) collective-permute-start(bf16[128,2048]{1,0:T(8,128)(2,1)} %collective-permute-done.a), channel_id=1, source_target_pairs={{0,4},{1,5},{2,6},{3,7},{4,12},{5,13},{6,14},{7,15},{8,0},{9,1},{1... | collective-permute-start | bytes 1572872 | tf_op jit(solution)/shard_map/ppermute | solution.py:80
  39.7 16.1 %collective-permute-start.4 = (bf16[64,2048]{1,0:T(8,128)(2,1)S(1)}, bf16[64,2048]{1,0:T(8,128)(2,1)S(1)}, u32[]{:S(2)}, u32[]{:S(2)}) collective-permute-start(bf16[64,2048]{1,0:T(8,128)(2,1)S(1)} %slice.62), channel_id=1, source_target_pairs={{0,2},{1,3},{2,0},{3,1},{4,6},{5,7},{6,4},{7,5},{8,10},{9,11},{10,... | collective-permute-start | bytes 786440 | tf_op jit(solution)/shard_map/ppermute | solution.py:80
  40.4 15.5 %collective-permute-start.3 = (bf16[64,2048]{1,0:T(8,128)(2,1)S(1)}, bf16[64,2048]{1,0:T(8,128)(2,1)S(1)}, u32[]{:S(2)}, u32[]{:S(2)}) collective-permute-start(bf16[64,2048]{1,0:T(8,128)(2,1)S(1)} %slice.61), channel_id=1, source_target_pairs={{0,1},{1,0},{2,3},{3,2},{4,5},{5,4},{6,7},{7,6},{8,9},{9,8},{10,11... | collective-permute-start | bytes 786440 | tf_op jit(solution)/shard_map/ppermute | solution.py:80
  55.8 9.2 %copy-start.6 = (bf16[64,2048]{1,0:T(8,128)(2,1)}, bf16[64,2048]{1,0:T(8,128)(2,1)S(1)}, u32[]{:S(2)}) copy-start(bf16[64,2048]{1,0:T(8,128)(2,1)S(1)} %collective-permute-done.4.low) | copy-start | bytes 786436
  55.8 9.2 %copy-start.7 = (bf16[64,2048]{1,0:T(8,128)(2,1)}, bf16[64,2048]{1,0:T(8,128)(2,1)S(1)}, u32[]{:S(2)}) copy-start(bf16[64,2048]{1,0:T(8,128)(2,1)S(1)} %collective-permute-done.3.high) | copy-start | bytes 786436
  65.0 18.0 %collective-permute-start.12 = (bf16[128,2048]{1,0:T(8,128)(2,1)}, bf16[128,2048]{1,0:T(8,128)(2,1)}, u32[]{:S(2)}, u32[]{:S(2)}) collective-permute-start(bf16[128,2048]{1,0:T(8,128)(2,1)} %collective-permute-done.5.a), channel_id=1, source_target_pairs={{0,4},{1,5},{2,6},{3,7},{4,12},{5,13},{6,14},{7,15},{8,0},{9,1},{1... | collective-permute-start | bytes 1572872 | tf_op jit(solution)/shard_map/ppermute | solution.py:80
  65.0 15.1 %collective-permute-start.10 = (bf16[128,2048]{1,0:T(8,128)(2,1)}, bf16[128,2048]{1,0:T(8,128)(2,1)S(1)}, u32[]{:S(2)}, u32[]{:S(2)}) collective-permute-start(bf16[128,2048]{1,0:T(8,128)(2,1)} %collective-permute-done.5.a), channel_id=1, source_target_pairs={{0,1},{1,0},{2,3},{3,2},{4,5},{5,4},{6,7},{7,6},{8,9},{9,8},{10,11... | collective-permute-start | bytes 1572872 | tf_op jit(solution)/shard_map/ppermute | solution.py:80
  66.6 16.5 %collective-permute-start.8 = (bf16[128,2048]{1,0:T(8,128)(2,1)}, bf16[128,2048]{1,0:T(8,128)(2,1)S(1)}, u32[]{:S(2)}, u32[]{:S(2)}) collective-permute-start(bf16[128,2048]{1,0:T(8,128)(2,1)} %collective-permute-done.5.a), channel_id=1, source_target_pairs={{0,2},{1,3},{2,0},{3,1},{4,6},{5,7},{6,4},{7,5},{8,10},{9,11},{10,... | collective-permute-start | bytes 1572872 | tf_op jit(solution)/shard_map/ppermute | solution.py:80
  72.6 36.8 %collective-permute-start.18 = (bf16[64,2048]{1,0:T(8,128)(2,1)}, bf16[64,2048]{1,0:T(8,128)(2,1)}, u32[]{:S(2)}, u32[]{:S(2)}) collective-permute-start(bf16[64,2048]{1,0:T(8,128)(2,1)} %slice.77), channel_id=1, source_target_pairs={{0,1},{1,0},{2,3},{3,2},{4,5},{5,4},{6,7},{7,6},{8,9},{9,8},{10,11... | collective-permute-start | bytes 786440 | tf_op jit(solution)/shard_map/ppermute | solution.py:80
  73.1 36.3 %collective-permute-start.17 = (bf16[64,2048]{1,0:T(8,128)(2,1)}, bf16[64,2048]{1,0:T(8,128)(2,1)}, u32[]{:S(2)}, u32[]{:S(2)}) collective-permute-start(bf16[64,2048]{1,0:T(8,128)(2,1)} %slice.76), channel_id=1, source_target_pairs={{0,2},{1,3},{2,0},{3,1},{4,6},{5,7},{6,4},{7,5},{8,10},{9,11},{10,... | collective-permute-start | bytes 786440 | tf_op jit(solution)/shard_map/ppermute | solution.py:80
  80.2 6.0 %copy-start.3 = (bf16[128,2048]{1,0:T(8,128)(2,1)}, bf16[128,2048]{1,0:T(8,128)(2,1)S(1)}, u32[]{:S(2)}) copy-start(bf16[128,2048]{1,0:T(8,128)(2,1)S(1)} %collective-permute-done.10.x) | copy-start | bytes 1572868
  80.9 12.1 %collective-permute-start.11 = (bf16[64,2048]{1,0:T(8,128)(2,1)}, bf16[64,2048]{1,0:T(8,128)(2,1)}, u32[]{:S(2)}, u32[]{:S(2)}) collective-permute-start(bf16[64,2048]{1,0:T(8,128)(2,1)} %slice.83), channel_id=1, source_target_pairs={{0,2},{1,3},{2,0},{3,1},{4,6},{5,7},{6,4},{7,5},{8,10},{9,11},{10,... | collective-permute-start | bytes 786440 | tf_op jit(solution)/shard_map/ppermute | solution.py:80
  83.0 20.8 %collective-permute-start.14 = (bf16[128,2048]{1,0:T(8,128)(2,1)}, bf16[128,2048]{1,0:T(8,128)(2,1)}, u32[]{:S(2)}, u32[]{:S(2)}) collective-permute-start(bf16[128,2048]{1,0:T(8,128)(2,1)} %collective-permute-done.12.a), channel_id=1, source_target_pairs={{0,2},{1,3},{2,0},{3,1},{4,6},{5,7},{6,4},{7,5},{8,10},{9,11},{10,... | collective-permute-start | bytes 1572872 | tf_op jit(solution)/shard_map/ppermute | solution.py:80
  83.1 1.5 copy-start.4
  83.1 20.8 %collective-permute-start.13 = (bf16[128,2048]{1,0:T(8,128)(2,1)}, bf16[128,2048]{1,0:T(8,128)(2,1)}, u32[]{:S(2)}, u32[]{:S(2)}) collective-permute-start(bf16[128,2048]{1,0:T(8,128)(2,1)} %collective-permute-done.12.a), channel_id=1, source_target_pairs={{0,1},{1,0},{2,3},{3,2},{4,5},{5,4},{6,7},{7,6},{8,9},{9,8},{10,11... | collective-permute-start | bytes 1572872 | tf_op jit(solution)/shard_map/ppermute | solution.py:80
  89.9 3.2 %copy-start.11 = (bf16[64,2048]{1,0:T(8,128)(2,1)S(1)}, bf16[64,2048]{1,0:T(8,128)(2,1)}, u32[]{:S(2)}) copy-start(bf16[64,2048]{1,0:T(8,128)(2,1)} %slice.82) | copy-start | bytes 786436
  93.1 10.7 %collective-permute-start.9 = (bf16[64,2048]{1,0:T(8,128)(2,1)S(1)}, bf16[64,2048]{1,0:T(8,128)(2,1)S(1)}, u32[]{:S(2)}, u32[]{:S(2)}) collective-permute-start(bf16[64,2048]{1,0:T(8,128)(2,1)S(1)} %copy-done.11), channel_id=1, source_target_pairs={{0,1},{1,0},{2,3},{3,2},{4,5},{5,4},{6,7},{7,6},{8,9},{9,8},{10,11... | collective-permute-start | bytes 786440 | tf_op jit(solution)/shard_map/ppermute | solution.py:80
  103.8 12.6 %copy-start.8 = (bf16[64,2048]{1,0:T(8,128)(2,1)}, bf16[64,2048]{1,0:T(8,128)(2,1)S(1)}, u32[]{:S(2)}) copy-start(bf16[64,2048]{1,0:T(8,128)(2,1)S(1)} %collective-permute-done.9.high) | copy-start | bytes 786436
  105.9 17.5 %collective-permute-start.16 = (bf16[64,2048]{1,0:T(8,128)(2,1)S(1)}, bf16[64,2048]{1,0:T(8,128)(2,1)S(1)}, u32[]{:S(2)}, u32[]{:S(2)}) collective-permute-start(bf16[64,2048]{1,0:T(8,128)(2,1)S(1)} %slice.74), channel_id=1, source_target_pairs={{0,2},{1,3},{2,0},{3,1},{4,6},{5,7},{6,4},{7,5},{8,10},{9,11},{10,... | collective-permute-start | bytes 786440 | tf_op jit(solution)/shard_map/ppermute | solution.py:80
  107.9 15.5 %collective-permute-start.15 = (bf16[64,2048]{1,0:T(8,128)(2,1)S(1)}, bf16[64,2048]{1,0:T(8,128)(2,1)S(1)}, u32[]{:S(2)}, u32[]{:S(2)}) collective-permute-start(bf16[64,2048]{1,0:T(8,128)(2,1)S(1)} %slice.73), channel_id=1, source_target_pairs={{0,1},{1,0},{2,3},{3,2},{4,5},{5,4},{6,7},{7,6},{8,9},{9,8},{10,11... | collective-permute-start | bytes 786440 | tf_op jit(solution)/shard_map/ppermute | solution.py:80
  123.4 0.7 copy-start.9
  123.4 0.8 copy-start.10
  136.3 5.9 %collective-permute-start.19 = (bf16[4,192,2048]{2,1,0:T(8,128)(2,1)}, bf16[4,192,2048]{2,1,0:T(8,128)(2,1)S(1)}, u32[]{:S(2)}, u32[]{:S(2)}) collective-permute-start(bf16[4,192,2048]{2,1,0:T(8,128)(2,1)} %shard_map.132), channel_id=1, source_target_pairs={{0,16},{16,0},{1,17},{17,1},{2,18},{18,2},{3,19},{19,3},{4,20},{20... | collective-permute-start | bytes 9437192 | tf_op jit(solution)/shard_map/ppermute | solution.py:443
  142.3 1.7 copy-start
  166.8 41.6 %collective-permute-start.20 = (bf16[12288,128]{1,0:T(8,128)(2,1)}, bf16[12288,128]{1,0:T(8,128)(2,1)}, u32[]{:S(2)}, u32[]{:S(2)}) collective-permute-start(bf16[12288,128]{1,0:T(8,128)(2,1)} %get-tuple-element.98), channel_id=1, source_target_pairs={{0,16},{16,0},{1,17},{17,1},{2,18},{18,2},{3,19},{19,3},{4,20},{20... | collective-permute-start | bytes 9437192 | tf_op jit(solution)/shard_map/ppermute | solution.py:455
  166.9 31.4 %all-to-all-start.1 = ((bf16[16,96,384]{2,1,0:T(8,128)(2,1)}), bf16[16,96,384]{2,1,0:T(8,128)(2,1)S(1)}, u32[]{:S(2)}, u32[]{:S(2)}) async-start(bf16[16,96,384]{2,1,0:T(8,128)(2,1)} %get-tuple-element.86), calls=%async_computation.1 | async-start | bytes 2359296 | tf_op jit(solution)/shard_map/all_to_all | solution.py:435
  198.3 1.0 copy-start.5

commit v2 on v0

v2 whole, which is shorter than its diff:
```python
import functools
import math

import jax
import jax.numpy as jnp
from jax import lax
from jax.experimental import pallas as pl
from jax.experimental.pallas import tpu as pltpu
from jax.sharding import PartitionSpec as P

EXPERTS = 64
CAP = 24
TOP = 8
LANES = 128
MIB = 1 << 20


beta_one = 0.9
beta_two = 0.95
adam_epsilon = 1e-08
learn_rate = 0.003
decay_rate = 0.1
bias_one = 1.0 - 0.9**20
bias_two = 1.0 - 0.95**20

HBM = pl.BlockSpec(memory_space=pltpu.HBM)
INSIDE = pl.BlockSpec(memory_space=pltpu.VMEM)


def slot_targets(flat_ids):
    count = flat_ids.shape[0]
    block = 128
    blocks = count // block
    onehot = (jnp.arange(EXPERTS, dtype=jnp.int32)[:, None] == flat_ids[None, :]).astype(
        jnp.bfloat16
    )
    tiles = onehot.reshape(EXPERTS, blocks, block)
    lower = (jnp.arange(block)[:, None] < jnp.arange(block)[None, :]).astype(jnp.bfloat16)
    within = jnp.einsum("ebk,kj->ebj", tiles, lower, preferred_element_type=jnp.float32)
    totals = jnp.sum(tiles.astype(jnp.float32), axis=2)
    small = (jnp.arange(blocks)[:, None] < jnp.arange(blocks)[None, :]).astype(jnp.float32)
    before = jnp.dot(totals, small, precision=lax.Precision.HIGHEST)
    ranking = (within + before[..., None]).reshape(EXPERTS, count)
    position = jnp.sum(ranking * onehot.astype(jnp.float32), axis=0).astype(jnp.int32)
    return flat_ids * CAP + position


def line_ring(length):
    return [0] + list(range(1, length, 2)) + list(range(2, length, 2))[::-1]


def ring_place(plane, length):
    return jnp.where(plane % 2 == 1, (plane + 1) // 2, (length - plane // 2) % length)


def ring_plane(place, length):
    up = 2 * place - 1
    down = 2 * (length - place)
    return jnp.where(place == 0, 0, jnp.where(up < length, up, down))


def step_perm(size, steps, flip):
    ring = line_ring(size // 4)
    after = {at: ring[(i + steps) % len(ring)] for i, at in enumerate(ring)}
    return [(i, after[i // 4] * 4 + (i % 4 ^ flip)) for i in range(size)]


def source_order(size):
    me = lax.axis_index("inner")
    length = size // 4
    steps = jnp.arange(length, dtype=jnp.int32)
    flips = jnp.arange(4, dtype=jnp.int32)
    at = ring_plane((ring_place(me // 4, length) - steps) % length, length)
    return (at[:, None] * 4 + (me % 4 ^ flips)[None, :]).reshape(size)


def grads_kernel(first, a, x, y, low, high, by_expert, d_out, g_out, *scratch):
    rows, match, d_rows, grads, sems = scratch
    experts, width, features = by_expert.shape
    tokens = rows.shape[0] // 4
    slots = experts * CAP
    pieces = (a, x, y, low, high)
    loads, at = [], 0
    for i, piece in enumerate(pieces):
        place = rows.at[pl.ds(at, piece.shape[0])]
        loads.append(pltpu.make_async_copy(piece, place, sems.at[i]))
        loads[-1].start()
        at += piece.shape[0]
    for load in loads:
        load.wait()

    slot = lax.broadcasted_iota(jnp.int32, (slots, tokens), 0)
    expert = first[0] + slot // CAP
    place = (slot % CAP).astype(jnp.float32)
    expert = expert.astype(jnp.float32)
    earlier = lax.broadcasted_iota(jnp.int32, (tokens, tokens), 0)
    earlier = earlier < lax.broadcasted_iota(jnp.int32, (tokens, tokens), 1)
    earlier = jnp.where(earlier, 1.0, 0.0).astype(jnp.bfloat16)
    hits = []
    for c in range(4):
        ids = rows[c * tokens : (c + 1) * tokens, features:].astype(jnp.float32).T
        named = jnp.zeros((slots, tokens), jnp.float32)
        for k in range(TOP):
            named = jnp.where(expert == ids[k : k + 1], 1.0, named)
        rank = jnp.dot(
            named.astype(jnp.bfloat16), earlier, preferred_element_type=jnp.float32
        )
        hits.append(jnp.where(rank == place, named, 0.0))
    blank = jnp.zeros((CAP, tokens), jnp.float32)
    lines = []
    for e in range(experts):
        for c in range(4):
            line = [blank] * 4
            line[c] = hits[c][e * CAP : (e + 1) * CAP]
            lines.append(jnp.concatenate(line, axis=1))
    match[...] = jnp.concatenate(lines, axis=0).astype(jnp.bfloat16)

    step = min(512, features)
    for at in range(0, features, step):
        d_rows[:, at : at + step] = jnp.dot(
            match[...], rows[:, at : at + step], preferred_element_type=jnp.float32
        ).astype(jnp.bfloat16)
    stores = [pltpu.make_async_copy(d_rows, d_out, sems.at[5])]
    stores[0].start()
    count = 4 * CAP
    found = [
        lax.dot_general(
            d_rows[e * count : (e + 1) * count],
            by_expert[e],
            (((1,), (1,)), ((), ())),
            preferred_element_type=jnp.float32,
        )
        for e in range(experts)
    ]
    for c in range(4):
        mine = [f[c * CAP : (c + 1) * CAP] for f in found]
        grads[c] = jnp.concatenate(mine, axis=0).astype(jnp.bfloat16)
    stores.append(pltpu.make_async_copy(grads, g_out, sems.at[6]))
    stores[1].start()
    for store in stores:
        store.wait()


def chunk_grads(first, part, by_expert):
    experts, width, features = by_expert.shape
    tokens, columns = part[0].shape
    slots = experts * CAP
    return pl.pallas_call(
        grads_kernel,
        out_shape=(
            jax.ShapeDtypeStruct((4 * slots, features), jnp.bfloat16),
            jax.ShapeDtypeStruct((4, slots, width), jnp.bfloat16),
        ),
        in_specs=[pl.BlockSpec(memory_space=pltpu.SMEM)]
        + [HBM] * 5
        + [INSIDE],
        out_specs=(HBM, HBM),
        scratch_shapes=[
            pltpu.VMEM((4 * tokens, columns), jnp.bfloat16),
            pltpu.VMEM((4 * slots, 4 * tokens), jnp.bfloat16),
            pltpu.VMEM((4 * slots, features), jnp.bfloat16),
            pltpu.VMEM((4, slots, width), jnp.bfloat16),
            pltpu.SemaphoreType.DMA((7,)),
        ],
        compiler_params=pltpu.CompilerParams(vmem_limit_bytes=14 * MIB),
        cost_estimate=pl.CostEstimate(
            flops=8 * slots * features * (4 * tokens + width),
            bytes_accessed=8 * (slots + tokens) * features,
            transcendentals=0,
        ),
    )(first, *part, by_expert)


def order_kernel(pieces, *refs):
    arrays, (out, rows, wide, turned, sems) = refs[:-5], refs[-5:]
    size, slots, width = rows.shape
    experts = slots // CAP
    loads = [
        pltpu.make_async_copy(arrays[a].at[i], rows.at[n], sems.at[n])
        for n, (a, i) in enumerate(pieces)
    ]
    for load in loads:
        load.start()
    for n, load in enumerate(loads):
        load.wait()
        wide[n] = rows[n].astype(jnp.float32)
    for e in range(experts):
        mine = [wide[n, e * CAP : (e + 1) * CAP] for n in range(size)]
        turned[e] = jnp.concatenate(mine, axis=0).T.astype(jnp.bfloat16)
    store = pltpu.make_async_copy(turned, out, sems.at[size])
    store.start()
    store.wait()


def order_slots(arrays, pieces):
    slots, width = arrays[0].shape[1:]
    size = len(pieces)
    shape = (slots // CAP, width, size * CAP)
    return pl.pallas_call(
        functools.partial(order_kernel, pieces),
        out_shape=jax.ShapeDtypeStruct(shape, jnp.bfloat16),
        in_specs=[HBM] * len(arrays),
        out_specs=HBM,
        scratch_shapes=[
            pltpu.VMEM((size, slots, width), jnp.bfloat16),
            pltpu.VMEM((size, slots, width), jnp.float32),
            pltpu.VMEM(shape, jnp.bfloat16),
            pltpu.SemaphoreType.DMA((size + 1,)),
        ],
        compiler_params=pltpu.CompilerParams(vmem_limit_bytes=10 * MIB),
        cost_estimate=pl.CostEstimate(
            flops=0, bytes_accessed=8 * size * slots * width, transcendentals=0
        ),
    )(*arrays)


def regroup_kernel(*refs):
    count = len(refs) - 5
    arrays, outs, (held, sems) = refs[:count], refs[count:-2], refs[-2:]
    loads = [
        pltpu.make_async_copy(a.at[pl.ds(1, 3)], held.at[k], sems.at[k])
        for k, a in enumerate(arrays)
    ]
    for load in loads:
        load.start()
    for load in loads:
        load.wait()
    stores = [
        pltpu.make_async_copy(held.at[:, c], out, sems.at[count + c])
        for c, out in enumerate(outs)
    ]
    for store in stores:
        store.start()
    for store in stores:
        store.wait()


def regroup(arrays):
    _, slots, width = arrays[0].shape
    count = len(arrays)
    return pl.pallas_call(
        regroup_kernel,
        out_shape=[jax.ShapeDtypeStruct((count, slots, width), jnp.bfloat16)] * 3,
        in_specs=[HBM] * count,
        out_specs=[HBM] * 3,
        scratch_shapes=[
            pltpu.VMEM((count, 3, slots, width), jnp.bfloat16),
            pltpu.SemaphoreType.DMA((count + 3,)),
        ],
        compiler_params=pltpu.CompilerParams(vmem_limit_bytes=6 * MIB),
        cost_estimate=pl.CostEstimate(
            flops=0, bytes_accessed=12 * count * slots * width, transcendentals=0
        ),
    )(*arrays)


def partial_kernel(owners, weighted, *refs):
    count = owners.shape[0]
    blocks, outs = refs[: -4 - count], refs[-4 - count : -4]
    w_in, rows, sums, sems = refs[-4:]
    experts, width, features = sums.shape
    share = width // count
    slots = blocks[0].shape[0] // experts
    loads = []
    for e in range(experts):
        mine = [(weighted.at[e], w_in.at[e])] + [
            (block.at[pl.ds(e * slots, slots)], rows.at[e, pl.ds(k * slots, slots)])
            for k, block in enumerate(blocks)
        ]
        loads.append(
            [
                pltpu.make_async_copy(source, place, sems.at[e, i])
                for i, (source, place) in enumerate(mine)
            ]
        )
    stores = []
    step = min(1024, features)
    for load in loads[0]:
        load.start()
    for e in range(experts):
        if e + 1 < experts:
            for load in loads[e + 1]:
                load.start()
        for load in loads[e]:
            load.wait()
        for at in range(0, features, step):
            sums[e, :, at : at + step] = jnp.dot(
                w_in[e], rows[e, :, at : at + step], preferred_element_type=jnp.float32
            ).astype(jnp.bfloat16)
        for r, out in enumerate(outs):
            at = pl.multiple_of(owners[r] * share, share)
            store = pltpu.make_async_copy(
                sums.at[e, pl.ds(at, share)], out.at[e], sems.at[e, len(blocks) + 1 + r]
            )
            store.start()
            stores.append(store)
    for store in stores:
        store.wait()


def partial_rows(owners, weighted, blocks):
    experts, width, slots = weighted.shape
    features = blocks[0].shape[1]
    count = owners.shape[0]
    return pl.pallas_call(
        partial_kernel,
        out_shape=[jax.ShapeDtypeStruct((experts, width // count, features), jnp.bfloat16)]
        * count,
        in_specs=[pl.BlockSpec(memory_space=pltpu.SMEM)] + [HBM] * (1 + len(blocks)),
        out_specs=[HBM] * count,
        scratch_shapes=[
            pltpu.VMEM((experts, width, slots), jnp.bfloat16),
            pltpu.VMEM((experts, slots, features), jnp.bfloat16),
            pltpu.VMEM((experts, width, features), jnp.bfloat16),
            pltpu.SemaphoreType.DMA((experts, 1 + len(blocks) + count)),
        ],
        compiler_params=pltpu.CompilerParams(vmem_limit_bytes=20 * MIB),
        cost_estimate=pl.CostEstimate(
            flops=2 * experts * width * slots * features,
            bytes_accessed=2 * experts * (width + slots) * features,
            transcendentals=0,
        ),
    )(owners, weighted, *blocks)


def root_of(x):
    inverse = lax.rsqrt(x)
    root = x * inverse
    return root + 0.5 * inverse * (x - root * root)


def reciprocal(x):
    estimate = pl.reciprocal(x, approx=True)
    return estimate * (2.0 - x * estimate)


def adam_kernel(count, kept, first, at, *refs):
    del at
    partials, (w, m1, m2) = refs[:count], refs[count : count + 3]
    new_w, new_m1, new_m2, full, copy, grad = refs[count + 3 + kept :]
    experts, rows, features = partials[0].shape
    tiles = features // LANES
    for e in range(experts):
        total = partials[0][e].astype(jnp.float32)
        for part in partials[1:]:
            total = total + part[e].astype(jnp.float32)
        for t in range(tiles):
            grad[pl.ds(t * experts + e, rows, stride=tiles * experts), :] = total[
                :, t * LANES : (t + 1) * LANES
            ]
    block = grad.shape[0]
    base = pl.multiple_of((first + pl.program_id(0)) * block, block)
    for start in range(0, block, 128):
        here = slice(start, start + 128)
        there = pl.ds(base + start, 128)
        g = grad[here]
        one = beta_one * m1[there] + (1.0 - beta_one) * g
        two = beta_two * m2[there] + (1.0 - beta_two) * g * g
        new_m1[here] = one
        new_m2[here] = two
        old = w[there]
        root = reciprocal(root_of(two * (1.0 / bias_two)) + adam_epsilon)
        new = old - learn_rate * (one * (1.0 / bias_one) * root + decay_rate * old)
        new_w[here] = new
        copy[here] = new.astype(jnp.bfloat16)
        full[here] = new.astype(jnp.bfloat16)


def adam_rows(at, partials, w, m1, m2, total_rows, before, first, steps):
    experts, rows, features = partials[0].shape
    block = 16
    flat = block * experts * features // LANES
    count, kept = len(partials), len(before)
    whole = rows // block
    part = pl.BlockSpec((experts, block, features), lambda i, at: (0, first + i, 0))
    line = pl.BlockSpec((flat, LANES), lambda i, at: (first + i, 0))
    placed = pl.BlockSpec((flat, LANES), lambda i, at: (at[0] * whole + first + i, 0))
    return pl.pallas_call(
        functools.partial(adam_kernel, count, kept, first),
        grid_spec=pltpu.PrefetchScalarGridSpec(
            num_scalar_prefetch=1,
            grid=(steps,),
            in_specs=[part] * count + [INSIDE] * 3 + [HBM] * kept,
            out_specs=[line] * 3 + [placed, pl.BlockSpec((flat, LANES), lambda i, at: (i, 0))],
            scratch_shapes=[pltpu.VMEM((flat, LANES), jnp.float32)],
        ),
        out_shape=[jax.ShapeDtypeStruct(w.shape, jnp.float32)] * 3
        + [
            jax.ShapeDtypeStruct((total_rows, LANES), jnp.bfloat16),
            jax.ShapeDtypeStruct((steps * flat, LANES), jnp.bfloat16),
        ],
        input_output_aliases={4 + count + i: i for i in range(kept)},
        compiler_params=pltpu.CompilerParams(vmem_limit_bytes=10 * MIB),
        cost_estimate=pl.CostEstimate(
            flops=20 * steps * flat * LANES,
            bytes_accessed=20 * steps * flat * LANES,
            transcendentals=0,
        ),
    )(at, *partials, w, m1, m2, *before)


def place_kernel(cut, at, low, high, full, out):
    del at, full
    here = pl.program_id(0)

    @pl.when(here < cut)
    def _():
        out[...] = low[...]

    @pl.when(here >= cut)
    def _():
        out[...] = high[...]


def place_rows(owner, low, high, full):
    block = math.gcd(low.shape[0], high.shape[0])
    cut = low.shape[0] // block
    steps = cut + high.shape[0] // block
    shape = (block, LANES)
    return pl.pallas_call(
        functools.partial(place_kernel, cut),
        grid_spec=pltpu.PrefetchScalarGridSpec(
            num_scalar_prefetch=1,
            grid=(steps,),
            in_specs=[
                pl.BlockSpec(shape, lambda i, at: (jnp.minimum(i, cut - 1), 0)),
                pl.BlockSpec(shape, lambda i, at: (jnp.maximum(i - cut, 0), 0)),
                HBM,
            ],
            out_specs=pl.BlockSpec(shape, lambda i, at: (at[0] * steps + i, 0)),
        ),
        out_shape=jax.ShapeDtypeStruct(full.shape, full.dtype),
        input_output_aliases={3: 0},
        compiler_params=pltpu.CompilerParams(vmem_limit_bytes=14 * MIB),
        cost_estimate=pl.CostEstimate(
            flops=0, bytes_accessed=4 * (low.size + high.size), transcendentals=0
        ),
    )(owner, low, high, full)


def finish_kernel(pieces, target, probs, hidden, *refs):
    back, (d_hidden, d_probs, rows, states, outs, sums, sems) = refs[:-7], refs[-7:]
    count = back[0].shape[1]
    choices, width = hidden.shape
    slots = rows.shape[0]
    loads = [
        pltpu.make_async_copy(back[a].at[i], rows.at[pl.ds(n * count, count)], sems.at[n])
        for n, (a, i) in enumerate(pieces)
    ]
    loads.append(pltpu.make_async_copy(hidden, states, sems.at[len(pieces)]))
    for load in loads:
        load.start()
    targets, scales = target[...].T, probs[...].T
    for load in loads:
        load.wait()
    ones = jnp.ones((8, width), jnp.bfloat16)
    across = (((1,), (1,)), ((), ()))
    step = 2 * LANES
    stores = []
    for n, at in enumerate(range(0, choices, step)):
        here = slice(at, at + step)

        def column(table):
            return jnp.concatenate([table[:, 2 * n : 2 * n + 1], table[:, 2 * n + 1 : 2 * n + 2]])

        places = lax.broadcasted_iota(jnp.int32, (step, slots), 1)
        onehot = jnp.where(places == column(targets).astype(jnp.int32), 1.0, 0.0)
        g = jnp.dot(onehot.astype(jnp.bfloat16), rows[...], preferred_element_type=jnp.float32)
        outs[here] = (column(scales) * g).astype(jnp.bfloat16)
        stores.append(
            pltpu.make_async_copy(outs.at[here], d_hidden.at[here], sems.at[len(loads) + n])
        )
        stores[n].start()
        product = states[here].astype(jnp.float32) * g
        high = product.astype(jnp.bfloat16)
        low = (product - high.astype(jnp.float32)).astype(jnp.bfloat16)
        sums[:, here] = lax.dot_general(
            ones, high, across, preferred_element_type=jnp.float32
        ) + lax.dot_general(ones, low, across, preferred_element_type=jnp.float32)
    d_probs[...] = sums[...]
    for store in stores:
        store.wait()


def finish(target, probs, hidden, back, pieces):
    choices, width = hidden.shape
    slots = len(pieces) * back[0].shape[1]
    steps = choices // (2 * LANES)
    return pl.pallas_call(
        functools.partial(finish_kernel, pieces),
        out_shape=(
            jax.ShapeDtypeStruct((choices, width), jnp.bfloat16),
            jax.ShapeDtypeStruct((8, choices), jnp.float32),
        ),
        in_specs=[INSIDE, INSIDE] + [HBM] * (1 + len(back)),
        out_specs=(HBM, INSIDE),
        scratch_shapes=[
            pltpu.VMEM((slots, width), jnp.bfloat16),
            pltpu.VMEM((choices, width), jnp.bfloat16),
            pltpu.VMEM((choices, width), jnp.bfloat16),
            pltpu.VMEM((8, choices), jnp.float32),
            pltpu.SemaphoreType.DMA((len(pieces) + 1 + steps,)),
        ],
        compiler_params=pltpu.CompilerParams(vmem_limit_bytes=12 * MIB),
        cost_estimate=pl.CostEstimate(
            flops=2 * choices * slots * width, bytes_accessed=8 * hidden.size, transcendentals=0
        ),
    )(target, probs, hidden, *back)


def lane_view(array):
    h, e, d = array.shape
    return array.reshape(h, e, d // LANES, LANES).transpose(0, 2, 1, 3).reshape(-1, LANES)


def lane_unview(rows, shape):
    h, e, d = shape
    return rows.reshape(h, d // LANES, e, LANES).transpose(0, 2, 1, 3).reshape(shape)


def local(cotangent, hidden, probs, expert_ids, secondary, weight, moment1, moment2):
    token_count = cotangent.shape[0]
    top_k = expert_ids.shape[1]
    hidden_width = hidden.shape[2]
    experts = secondary.shape[1]
    size = lax.axis_size("inner")
    length = size // 4
    outer_size = lax.axis_size("outer")
    outer_at = lax.axis_index("outer")
    me = lax.axis_index("inner")
    choices = token_count * top_k
    slots = experts * CAP
    rows = weight.shape[0]

    flat_ids = expert_ids.reshape(choices)
    target = slot_targets(flat_ids)
    device = flat_ids // experts
    ring_steps = (ring_place(device // 4, length) - ring_place(me // 4, length)) % length
    relative = ring_steps * 4 + (device % 4 ^ me % 4)
    target = (relative - device) * slots + target
    all_slots = jnp.arange(size * slots, dtype=jnp.int32)
    matches = (all_slots[:, None] == target[None, :]).astype(jnp.bfloat16)
    weighted = (
        (probs[..., None] * hidden.astype(jnp.float32))
        .astype(jnp.bfloat16)
        .reshape(choices, hidden_width)
    )
    w_send = jnp.dot(matches, weighted, preferred_element_type=jnp.float32).astype(jnp.bfloat16)
    w_send = w_send.reshape(length, 4, slots, hidden_width)
    columns = tuple(
        v.astype(jnp.float32).reshape(choices // LANES, LANES) for v in (target, probs)
    )
    state = tuple(lane_view(a) for a in (weight, moment1, moment2))

    def move(block, steps, flip):
        return lax.ppermute(block, "inner", step_perm(size, steps, flip))

    tie = lax.optimization_barrier
    last = length - 1
    half = token_count // 2
    first = (me * experts).astype(jnp.int32)[None]
    tags = jnp.pad(expert_ids.astype(jnp.bfloat16), ((0, 0), (0, LANES - top_k)))
    own = jnp.concatenate([cotangent, tags], axis=1)
    by_expert = jnp.transpose(secondary, (1, 0, 2))
    near, parts, w_parts = {}, {}, {}
    d_rows, grads, back = {}, {}, {}

    def add_chunk(j):
        d_rows[j], grads[j] = chunk_grads(first, parts[j], by_expert)

    def flips(arrays):
        return [move(a, 0, c) for c, a in enumerate(arrays, 1)]

    def far(j):
        _, by_x, by_y = near[j]
        return (move(by_x[:half], 0, 2), move(by_y[half:], 0, 1))

    for k in range(length + 1):
        moving = {}
        if k < last:
            moving["own"] = move(own, 1, 0)
        if k < length:
            moving["x"] = move(own, 0, 1)
            moving["y"] = move(own, 0, 2)
        if k > 1:
            moving["far"] = far(k - 1)
        if k == length:
            moving["first"] = far(0)
        if k > 2:
            add_chunk(k - 2)
        if k == 0:
            moving["columns"] = columns
        if k == last - 1:
            moving["weights"] = by_expert
            w_parts[1] = move(w_send[1], 1, 0)
        if k == last:
            for j in range(last, 1, -1):
                w_parts[j] = move(w_send[j], j, 0)
        moving["done"] = (d_rows, grads, w_parts, w_send)
        if k == length:
            last_far = moving.pop("far")
            first_far = moving.pop("first")
        moved = tie(moving)
        d_rows, grads, w_parts, w_send = moved["done"]
        if k == 0:
            columns = moved["columns"]
        if k == last - 1:
            by_expert = moved["weights"]
        if k == last:
            w_parts[0] = w_send[0]
            w_arrays = [w_parts[j] for j in range(length)]
            w_flipped = flips(regroup(w_arrays))
        if 1 < k < length:
            parts[k - 1] = near[k - 1] + moved["far"]
        if k < length:
            near[k] = (own, moved["x"], moved["y"])
        own = moved.get("own")
    parts[last] = near[last] + last_far
    parts[0] = near[0] + first_far
    for j in range(1, last):
        back[j] = move(grads[j], -j, 0)
    add_chunk(last)
    back[last] = move(grads[last], -last, 0)
    add_chunk(0)
    back[0] = grads[0]
    back = [back[j] for j in range(length)]
    pieces = tuple((k, 0) if c == 0 else (length + c - 1, k) for k in range(length) for c in range(4))
    w_slots = order_slots(w_arrays + w_flipped, pieces)
    d_rows, leaving = tie(([d_rows[j] for j in range(length)], regroup(back)))
    flipped = flips(leaving)

    def outer_perm(steps):
        return [(i, (i + steps) % outer_size) for i in range(outer_size)]

    owners = (outer_at + jnp.arange(outer_size, dtype=jnp.int32)) % outer_size
    mine, *sent = partial_rows(owners, w_slots, d_rows)
    partials = [mine] + [
        lax.ppermute(part, "outer", outer_perm(r)) for r, part in enumerate(sent, 1)
    ]
    at = outer_at.astype(jnp.int32)[None]
    total_rows = secondary.size // LANES
    blocks = rows // 16
    cuts = [0, blocks // 2, blocks]
    outs, copies = [], []
    for start, stop in zip(cuts[:-1], cuts[1:]):
        if start:
            partials, flipped = tie((partials, flipped))
        *outs, copy = adam_rows(
            at, partials, *state, total_rows, outs, start, stop - start
        )
        copies.append(copy)
    sent = [
        [lax.ppermute(copy, "outer", outer_perm(r)) for r in range(1, outer_size)]
        for copy in copies
    ]
    new_weight, new_moment1, new_moment2, full = outs
    for r in range(1, outer_size):
        owner = (outer_at + outer_size - r) % outer_size
        full = place_rows(
            owner.astype(jnp.int32)[None], sent[0][r - 1], sent[1][r - 1], full
        )

    d_hidden, d_probs = finish(
        *columns, hidden.reshape(choices, hidden_width), back + flipped, pieces
    )
    return (
        d_hidden.reshape(hidden.shape),
        d_probs[0].reshape(probs.shape),
        lane_unview(new_weight, weight.shape),
        lane_unview(new_moment1, weight.shape),
        lane_unview(new_moment2, weight.shape),
        lane_unview(full, secondary.shape),
    )


def solution(mesh):
    in_specs = (
        P(("outer", "inner"), None),
        P(("outer", "inner"), None, None),
        P(("outer", "inner"), None),
        P(("outer", "inner"), None),
        P(None, "inner", None),
        P("outer", "inner", None),
        P("outer", "inner", None),
        P("outer", "inner", None),
    )
    out_specs = (
        P(("outer", "inner"), None, None),
        P(("outer", "inner"), None),
        P("outer", "inner", None),
        P("outer", "inner", None),
        P("outer", "inner", None),
        P(None, "inner", None),
    )
    return jax.shard_map(local, mesh=mesh, in_specs=in_specs, out_specs=out_specs, check_vma=False)
```

time: 296 us -> 185 us (0.62)
  waiting for transfers between devices: 106 us -> 38.9 us
  blocking collectives: 64.7 us -> 0 us
  Pallas kernels: 0 us -> 57.6 us
  matrix products: 37.8 us -> 3.51 us
  other arithmetic: 27.1 us -> 2.03 us
  starting transfers between devices: 15.2 us -> 39.2 us
  between operations: 14.6 us -> 1.36 us
  local copies, waits for them, and re-layouts: 29.9 us -> 41.4 us
    all_gather x1 -> x0, blocking collectives: 64.7 us -> none  [local(): lax.all_gather(expert_ids, 'inner', axis=0, tiled=True)]
    pallas_call x0 -> x12, Pallas kernels: none -> 57.6 us  [the longest x4 18.7 us: chunk_grads(): pl.pallas_call(grads_kernel, out_shape=(jax.ShapeDtypeStruct((4 * slots,...]
    all_gather x2 -> x0, waiting for transfers between devices: 49.3 us -> none  [the longest x1 49.3 us: local(): lax.all_gather(cotangent, 'inner', axis=0, tiled=True)]
    ppermute x0 -> x34, starting transfers between devices: none -> 39.2 us  [the longest x31 38.6 us: move(): return lax.ppermute(block, 'inner', step_perm(size, steps, flip))]
    ppermute x0 -> x34, waiting for transfers between devices: none -> 38.9 us  [the longest x31 38.9 us: move(): return lax.ppermute(block, 'inner', step_perm(size, steps, flip))]
    dot_general x3 -> x0, matrix products: 31.4 us -> none  [the longest x1 14 us: local(): jnp.einsum('jlcd,hld->jlch', d_recv, secondary, preferred_element_type=jn...]
    unnamed x4 -> x0, waiting for transfers between devices: 29.3 us -> none
    all_to_all x2 -> x0, waiting for transfers between devices: 27 us -> none  [the longest x1 27 us: local(): lax.all_to_all(grads, 'inner', split_axis=0, concat_axis=0, tiled=True)]
  transfers between devices with their start and end apart: 5 -> 34, of which waited for: 3 -> 11; matrix products, arithmetic and copies ran while one was open for 15% -> 8% of each run, Pallas kernels for 0% -> 20%
where the time goes in v2:
time: 185 us; the launch traced here: 184 us
  Pallas kernels  57.6 us (31%)
  local copies, waits for them, and re-layouts  41.4 us (22%)
  starting transfers between devices  39.2 us (21%)
  waiting for transfers between devices  38.9 us (21%)
  matrix products  3.51 us (2%)
  other arithmetic  2.03 us (1%)
    ppermute x31, waiting for transfers between devices, move(): return lax.ppermute(block, 'inner', step_perm(size, steps, flip))  38.9 us
    ppermute x31, starting transfers between devices, move(): return lax.ppermute(block, 'inner', step_perm(size, steps, flip))  38.6 us
    unnamed x106, local copies, waits for them, and re-layouts  37.2 us
    pallas_call x4, Pallas kernels, chunk_grads(): pl.pallas_call(grads_kernel, out_shape=(jax.ShapeDtypeStruct((4 * slots,...  18.7 us
    pallas_call x2, Pallas kernels, adam_rows(): pl.pallas_call(functools.partial(adam_kernel, count, kept, first), grid_s...  14.9 us
    pallas_call x1, Pallas kernels, partial_rows(): pl.pallas_call(partial_kernel, out_shape=[jax.ShapeDtypeStruct((experts,...  8.42 us
    pallas_call x1, Pallas kernels, finish(): pl.pallas_call(functools.partial(finish_kernel, pieces), out_shape=(jax.S...  5.29 us
    pallas_call x2, Pallas kernels, regroup(): pl.pallas_call(regroup_kernel, out_shape=[jax.ShapeDtypeStruct((count, sl...  4.11 us
  transfers between devices with their start and end apart: 34, of which 11 were waited for; matrix products, arithmetic and copies ran while one was open for 8% of the time, Pallas kernels for 20%

profile of v2, /device:TPU:0, one launch (start us, length us, event | category | flops | bytes accessed | tf_op | source)
XLA Modules:
  0.0 184.0 jit_solution(715704379960567752)
XLA Ops:
  1.5 1.1 fusion.9.a
  2.6 3.1 %collective-permute-start = (bf16[128,2176]{1,0:T(8,128)(2,1)S(1)}, bf16[128,2176]{1,0:T(8,128)(2,1)S(1)}, u32[]{:S(2)}, u32[]{:S(2)}) collective-permute-start(bf16[128,2176]{1,0:T(8,128)(2,1)S(1)} %fusion.9.a), channel_id=1, source_target_pairs={{0,4},{1,5},{2,6},{3,7},{4,12},{5,13},{6,14},{7,15},{8,0},{9,1},{1... | collective-permute-start | bytes 1671176 | tf_op jit(solution)/shard_map/ppermute | solution.py:556
  5.6 1.5 collective-permute-start.1
  7.1 1.5 collective-permute-start.2
  10.6 3.2 %fusion.2 = bf16[1536,384]{1,0:T(8,128)(2,1)S(1)} fusion(s32[1024]{0:T(1024)S(1)} %fusion.41, bf16[128,8,384]{2,1,0:T(8,128)(2,1)} %param.9, f32[128,8]{1,0:T(8,128)S(1)} %copy.50), kind=kOutput, calls=%fused_computation.4 | convolution fusion | flops 1211301888 | bytes 1974272 | tf_op jit(solution)/shard_map/dot_general | solution.py:548
  13.7 5.5 %collective-permute-done.a = bf16[128,2176]{1,0:T(8,128)(2,1)S(1)} collective-permute-done((bf16[128,2176]{1,0:T(8,128)(2,1)S(1)}, bf16[128,2176]{1,0:T(8,128)(2,1)S(1)}, u32[]{:S(2)}, u32[]{:S(2)}) %collective-permute-start) | collective-permute-done | bytes 557088 | tf_op jit(solution)/shard_map/ppermute | solution.py:556
  19.7 1.2 collective-permute-done.2.y
  20.9 2.6 %collective-permute-start.5 = (bf16[128,2176]{1,0:T(8,128)(2,1)S(1)}, bf16[128,2176]{1,0:T(8,128)(2,1)S(1)}, u32[]{:S(2)}, u32[]{:S(2)}) collective-permute-start(bf16[128,2176]{1,0:T(8,128)(2,1)S(1)} %collective-permute-done.a), channel_id=1, source_target_pairs={{0,4},{1,5},{2,6},{3,7},{4,12},{5,13},{6,14},{7,15},{8,0},{9,1},{1... | collective-permute-start | bytes 1671176 | tf_op jit(solution)/shard_map/ppermute | solution.py:556
  24.1 1.5 collective-permute-start.7
  25.6 0.8 copy-done.14
  26.4 8.3 %collective-permute-done.5.a = bf16[128,2176]{1,0:T(8,128)(2,1)S(1)} collective-permute-done((bf16[128,2176]{1,0:T(8,128)(2,1)S(1)}, bf16[128,2176]{1,0:T(8,128)(2,1)S(1)}, u32[]{:S(2)}, u32[]{:S(2)}) %collective-permute-start.5) | collective-permute-done | bytes 557088 | tf_op jit(solution)/shard_map/ppermute | solution.py:556
  34.7 1.4 collective-permute-done.6.x
  37.3 1.5 collective-permute-start.9
  38.8 1.6 collective-permute-start.11
  41.4 0.8 copy-done.16
  42.2 1.0 collective-permute-start.8
  44.0 2.7 %collective-permute-done.9.low = bf16[64,2176]{1,0:T(8,128)(2,1)S(1)} collective-permute-done((bf16[64,2176]{1,0:T(8,128)(2,1)S(1)}, bf16[64,2176]{1,0:T(8,128)(2,1)S(1)}, u32[]{:S(2)}, u32[]{:S(2)}) %collective-permute-start.9) | collective-permute-done | bytes 278560 | tf_op jit(solution)/shard_map/ppermute | solution.py:556
  46.7 1.4 collective-permute-start.10
  48.2 6.2 %copy.65 = bf16[384,4,2048]{2,0,1:T(8,128)(2,1)} copy(bf16[384,4,2048]{2,1,0:T(4,128)(2,1)S(1)} %bitcast.83) | data formatting | bytes 12582912 | tf_op args[4]
  54.3 3.4 %collective-permute-done.10.high = bf16[64,2176]{1,0:T(8,128)(2,1)S(1)} collective-permute-done((bf16[64,2176]{1,0:T(8,128)(2,1)S(1)}, bf16[64,2176]{1,0:T(8,128)(2,1)S(1)}, u32[]{:S(2)}, u32[]{:S(2)}) %collective-permute-start.10) | collective-permute-done | bytes 278560 | tf_op jit(solution)/shard_map/ppermute | solution.py:556
  60.2 1.5 collective-permute-start.19
  61.8 0.9 slice_bitcast_fusion.1
  62.7 1.7 collective-permute-start.14
  64.4 1.2 collective-permute-start.15
  66.3 2.4 %collective-permute-done.16.low = bf16[64,2176]{1,0:T(8,128)(2,1)S(1)} collective-permute-done((bf16[64,2176]{1,0:T(8,128)(2,1)S(1)}, bf16[64,2176]{1,0:T(8,128)(2,1)S(1)}, u32[]{:S(2)}, u32[]{:S(2)}) %collective-permute-start.16) | collective-permute-done | bytes 278560 | tf_op jit(solution)/shard_map/ppermute | solution.py:556
  70.0 2.8 %copy-done = bf16[384,4,2048]{2,0,1:T(8,128)(2,1)S(1)} copy-done((bf16[384,4,2048]{2,0,1:T(8,128)(2,1)S(1)}, bf16[384,4,2048]{2,0,1:T(8,128)(2,1)}, u32[]{:S(2)}) %copy-start) | copy-done | bytes 6291480
  72.8 1.1 copy-done.8
  73.9 1.1 copy-done.10
  74.9 1.1 copy-done.15
  76.0 1.0 copy-done.25
  76.9 1.0 copy-done.31
  77.9 4.4 %shard_map.128 = (bf16[384,2048]{1,0:T(8,128)(2,1)S(1)}, bf16[4,96,384]{2,1,0:T(8,128)(2,1)}) custom-call(s32[1]{0:T(128)} %bitcast.5.first, bf16[128,2176]{1,0:T(8,128)(2,1)S(1)} %copy-done.15, bf16[128,2176]{1,0:T(8,128)(2,1)S(1)} %copy-done.8, bf16[128,2176]{1,0:T(8,128)(2,1)S(1)} %copy-done.10, bf16[64,2176]{1,0:T(8,128)(2,1)S(1)} %copy-done.25, ...), custom_call_target="tpu_custom_call" | custom-call | flops 1409286144 | bytes 3670016 | tf_op jit(solution)/shard_map/pallas_call | solution.py:148
  82.3 1.1 copy-done.32
  84.1 1.0 slice.50
  85.1 1.5 collective-permute-start.23
  86.6 1.0 slice_bitcast_fusion.refs_0_
  87.6 2.5 %shard_map.131 = (bf16[4,96,384]{2,1,0:T(8,128)(2,1)S(1)}, bf16[4,96,384]{2,1,0:T(8,128)(2,1)}, bf16[4,96,384]{2,1,0:T(8,128)(2,1)}) custom-call(bf16[4,96,384]{2,1,0:T(8,128)(2,1)S(1)} %slice_bitcast_fusion.refs_0_, bf16[4,96,384]{2,1,0:T(8,128)(2,1)S(1)} %copy-done.12, bf16[4,96,384]{2,1,0:T(8,128)(2,1)} %collective-permute-done.14.refs_2_, ...), custom_call_target="tpu_custom_call" | custom-call | bytes 1769472 | tf_op jit(solution)/shard_map/pallas_call | solution.py:241
  90.8 1.6 collective-permute-start.3
  92.4 1.5 collective-permute-start.4
  94.0 5.3 %shard_map.129 = (bf16[384,2048]{1,0:T(8,128)(2,1)S(1)}, bf16[4,96,384]{2,1,0:T(8,128)(2,1)}) custom-call(s32[1]{0:T(128)} %bitcast.5.first, bf16[128,2176]{1,0:T(8,128)(2,1)S(1)} %copy-done.17, bf16[128,2176]{1,0:T(8,128)(2,1)S(1)} %collective-permute-done.12.x, bf16[128,2176]{1,0:T(8,128)(2,1)S(1)} %collective-permute-done.13.y, ...), custom_call_target="tpu_custom_call" | custom-call | flops 1409286144 | bytes 3670016 | tf_op jit(solution)/shard_map/pallas_call | solution.py:148
  99.2 1.1 copy-done.34
  101.7 5.4 %shard_map.130 = (bf16[384,2048]{1,0:T(8,128)(2,1)S(1)}, bf16[4,96,384]{2,1,0:T(8,128)(2,1)}) custom-call(s32[1]{0:T(128)} %bitcast.5.first, bf16[128,2176]{1,0:T(8,128)(2,1)} %collective-permute-done.11.a, bf16[128,2176]{1,0:T(8,128)(2,1)S(1)} %copy-done.6, bf16[128,2176]{1,0:T(8,128)(2,1)} %collective-permute-done.19.y, ...), custom_call_target="tpu_custom_call" | custom-call | flops 1409286144 | bytes 3670016 | tf_op jit(solution)/shard_map/pallas_call | solution.py:148
  107.1 1.1 copy-done.36
  109.0 2.4 %collective-permute-start.27 = (bf16[4,96,384]{2,1,0:T(8,128)(2,1)}, bf16[4,96,384]{2,1,0:T(8,128)(2,1)}, u32[]{:S(2)}, u32[]{:S(2)}) collective-permute-start(bf16[4,96,384]{2,1,0:T(8,128)(2,1)} %get-tuple-element.116), channel_id=1, source_target_pairs={{0,3},{1,2},{2,1},{3,0},{4,7},{5,6},{6,5},{7,4},{8,11},{9,10},{10,... | collective-permute-start | bytes 884744 | tf_op jit(solution)/shard_map/ppermute | solution.py:556
  112.1 2.2 %collective-permute-start.21 = (bf16[4,96,384]{2,1,0:T(8,128)(2,1)}, bf16[4,96,384]{2,1,0:T(8,128)(2,1)}, u32[]{:S(2)}, u32[]{:S(2)}) collective-permute-start(bf16[4,96,384]{2,1,0:T(8,128)(2,1)} %get-tuple-element.110), channel_id=1, source_target_pairs={{0,12},{1,13},{2,14},{3,15},{4,8},{5,9},{6,10},{7,11},{8,4},{9,5},... | collective-permute-start | bytes 884744 | tf_op jit(solution)/shard_map/ppermute | solution.py:556
  115.0 2.8 %copy-done.1 = bf16[384,4,2048]{2,0,1:T(8,128)(2,1)S(1)} copy-done((bf16[384,4,2048]{2,0,1:T(8,128)(2,1)S(1)}, bf16[384,4,2048]{2,0,1:T(8,128)(2,1)}, u32[]{:S(2)}) %copy-start.1) | copy-done | bytes 6291480
  117.8 1.1 copy-done.4
  118.8 1.0 copy-done.27
  119.8 1.0 copy-done.29
  120.8 3.7 %shard_map.127 = (bf16[384,2048]{1,0:T(8,128)(2,1)S(1)}, bf16[4,96,384]{2,1,0:T(8,128)(2,1)S(1)}) custom-call(s32[1]{0:T(128)} %bitcast.5.first, bf16[128,2176]{1,0:T(8,128)(2,1)S(1)} %fusion.9.a, bf16[128,2176]{1,0:T(8,128)(2,1)S(1)} %collective-permute-done.1.x, bf16[128,2176]{1,0:T(8,128)(2,1)S(1)} %copy-done.4, bf16[64,2176]{1,0:T(8,128)(2,1)S(1)} %copy-done.27, ...), custom_call_target="tpu_custom_call" | custom-call | flops 1409286144 | bytes 3670016 | tf_op jit(solution)/shard_map/pallas_call | solution.py:148
  124.6 3.0 %shard_map.132.weighted = bf16[4,384,384]{2,1,0:T(8,128)(2,1)S(1)} custom-call(bf16[4,96,384]{2,1,0:T(8,128)(2,1)S(1)} %slice_bitcast_fusion.refs_0_, bf16[4,96,384]{2,1,0:T(8,128)(2,1)S(1)} %copy-done.13, bf16[4,96,384]{2,1,0:T(8,128)(2,1)} %collective-permute-done.14.refs_2_, bf16[4,96,384]{2,1,0:T(8,128)(2,1)} %collective-permute-done.15.refs_3_, ...), custom_call_target="tpu_custom_call" | custom-call | bytes 4718592 | tf_op jit(solution)/shard_map/pallas_call | solution.py:199
  127.6 1.6 shard_map.133
  129.2 8.4 %shard_map.134 = (bf16[4,192,2048]{2,1,0:T(8,128)(2,1)S(1)}, bf16[4,192,2048]{2,1,0:T(8,128)(2,1)S(1)}) custom-call(s32[2]{0:T(128)S(1)} %and_select_fusion.owners, bf16[4,384,384]{2,1,0:T(8,128)(2,1)S(1)} %shard_map.132.weighted, bf16[384,2048]{1,0:T(8,128)(2,1)S(1)} %get-tuple-element.124.refs_0_, bf16[384,2048]{1,0:T(8,128)(2,1)S(1)} %copy-done.33, ...), custom_call_target="tpu_custom_call" | custom-call | flops 2415919104 | bytes 12582912 | tf_op jit(solution)/shard_map/pallas_call | solution.py:305
  137.7 1.2 collective-permute-start.29
  139.4 1.8 %collective-permute-start.31 = (bf16[4,96,384]{2,1,0:T(8,128)(2,1)S(1)}, bf16[4,96,384]{2,1,0:T(8,128)(2,1)S(1)}, u32[]{:S(2)}, u32[]{:S(2)}) collective-permute-start(bf16[4,96,384]{2,1,0:T(8,128)(2,1)S(1)} %get-tuple-element.132), channel_id=1, source_target_pairs={{0,3},{1,2},{2,1},{3,0},{4,7},{5,6},{6,5},{7,4},{8,11},{9,10},{10,... | collective-permute-start | bytes 884744 | tf_op jit(solution)/shard_map/ppermute | solution.py:556
  141.3 6.3 %collective-permute-done.29.refs_4_ = bf16[4,96,384]{2,1,0:T(8,128)(2,1)S(1)} collective-permute-done((bf16[4,96,384]{2,1,0:T(8,128)(2,1)S(1)}, bf16[4,96,384]{2,1,0:T(8,128)(2,1)S(1)}, u32[]{:S(2)}, u32[]{:S(2)}) %collective-permute-start.29) | collective-permute-done | bytes 294944 | tf_op jit(solution)/shard_map/ppermute | solution.py:556
  147.6 6.7 %collective-permute-done.30.refs_5_ = bf16[4,96,384]{2,1,0:T(8,128)(2,1)S(1)} collective-permute-done((bf16[4,96,384]{2,1,0:T(8,128)(2,1)S(1)}, bf16[4,96,384]{2,1,0:T(8,128)(2,1)S(1)}, u32[]{:S(2)}, u32[]{:S(2)}) %collective-permute-start.30) | collective-permute-done | bytes 294944 | tf_op jit(solution)/shard_map/ppermute | solution.py:556
  154.4 3.0 %copy-done.2 = f32[192,4,2048]{2,1,0:T(4,128)S(1)} copy-done((f32[192,4,2048]{2,1,0:T(4,128)S(1)}, f32[192,4,2048]{2,1,0:T(4,128)}, u32[]{:S(2)}) %copy-start.2) | copy-done | bytes 6291480
  157.3 7.4 %shard_map.136 = (f32[12288,128]{1,0:T(8,128)}, f32[12288,128]{1,0:T(8,128)}, f32[12288,128]{1,0:T(8,128)}, bf16[24576,128]{1,0:T(8,128)(2,1)}, bf16[6144,128]{1,0:T(8,128)(2,1)}) custom-call(s32[1]{0:T(128)} %bitcast.12.at, bf16[4,192,2048]{2,1,0:T(8,128)(2,1)S(1)} %get-tuple-element.138.refs_0_, bf16[4,192,2048]{2,1,0:T(8,128)(2,1)S(1)} %collective-permute-done.28.refs_1_, ...), custom_call_target="tpu_custom_call" | custom-call | flops 15728640 | bytes 15728640 | tf_op jit(solution)/shard_map/pallas_call | solution.py:378
  164.9 7.5 %shard_map.137 = (f32[12288,128]{1,0:T(8,128)}, f32[12288,128]{1,0:T(8,128)}, f32[12288,128]{1,0:T(8,128)}, bf16[24576,128]{1,0:T(8,128)(2,1)}, bf16[6144,128]{1,0:T(8,128)(2,1)}) custom-call(s32[1]{0:T(128)} %bitcast.12.at, ...), custom_call_target="tpu_custom_call", output_to_operand_aliasing={{0}: (6, {}), {1}: (7, {}), {2}: (8, {}), {3}: (9, {})} | custom-call | flops 15728640 | bytes 15728640 | tf_op jit(solution)/shard_map/pallas_call | solution.py:378
  172.8 1.0 copy-done.40
  173.8 1.0 copy-done.42
  174.7 5.3 %shard_map.135 = (bf16[1024,384]{1,0:T(8,128)(2,1)}, f32[8,1024]{1,0:T(8,128)S(1)}) custom-call(f32[8,128]{1,0:T(8,128)S(1)} %fusion.27.target, f32[8,128]{1,0:T(8,128)S(1)} %reshape.249.probs, bf16[1024,384]{1,0:T(8,128)(2,1)S(1)} %bitcast.77, bf16[4,96,384]{2,1,0:T(8,128)(2,1)S(1)} %copy-done.21, bf16[4,96,384]{2,1,0:T(8,128)(2,1)} %collective-permute-done.20.refs_1_, ...), custom_call_target="tpu_custom_call" | custom-call | flops 1207959552 | bytes 3145728 | tf_op jit(solution)/shard_map/pallas_call | solution.py:489
  180.8 3.2 %shard_map.138 = bf16[24576,128]{1,0:T(8,128)(2,1)} custom-call(s32[1]{0:T(128)} %bitcast.37.at, bf16[6144,128]{1,0:T(8,128)(2,1)} %collective-permute-done.32.low, bf16[6144,128]{1,0:T(8,128)(2,1)S(1)} %collective-permute-done.33.high, bf16[24576,128]{1,0:T(8,128)(2,1)} %get-tuple-element.149.full), custom_call_target="tpu_custom_call", output_to_operand_aliasing={{}: (3, {})} | custom-call | bytes 6291456 | tf_op jit(solution)/shard_map/pallas_call | solution.py:420
  (151 shorter events, 17.9 us)
Async XLA Ops:
  0.6 9.7 %copy-start.44 = (f32[128,8]{0,1:T(8,128)S(1)}, f32[128,8]{0,1:T(8,128)}, u32[]{:S(2)}) copy-start(f32[128,8]{0,1:T(8,128)} %param.10) | copy-start | bytes 12292
  2.6 16.7 %collective-permute-start = (bf16[128,2176]{1,0:T(8,128)(2,1)S(1)}, bf16[128,2176]{1,0:T(8,128)(2,1)S(1)}, u32[]{:S(2)}, u32[]{:S(2)}) collective-permute-start(bf16[128,2176]{1,0:T(8,128)(2,1)S(1)} %fusion.9.a), channel_id=1, source_target_pairs={{0,4},{1,5},{2,6},{3,7},{4,12},{5,13},{6,14},{7,15},{8,0},{9,1},{1... | collective-permute-start | bytes 1671176 | tf_op jit(solution)/shard_map/ppermute | solution.py:556
  5.6 14.1 %collective-permute-start.1 = (bf16[128,2176]{1,0:T(8,128)(2,1)S(1)}, bf16[128,2176]{1,0:T(8,128)(2,1)S(1)}, u32[]{:S(2)}, u32[]{:S(2)}) collective-permute-start(bf16[128,2176]{1,0:T(8,128)(2,1)S(1)} %fusion.9.a), channel_id=1, source_target_pairs={{0,1},{1,0},{2,3},{3,2},{4,5},{5,4},{6,7},{7,6},{8,9},{9,8},{10,11... | collective-permute-start | bytes 1671176 | tf_op jit(solution)/shard_map/ppermute | solution.py:556
  7.1 13.8 %collective-permute-start.2 = (bf16[128,2176]{1,0:T(8,128)(2,1)S(1)}, bf16[128,2176]{1,0:T(8,128)(2,1)S(1)}, u32[]{:S(2)}, u32[]{:S(2)}) collective-permute-start(bf16[128,2176]{1,0:T(8,128)(2,1)S(1)} %fusion.9.a), channel_id=1, source_target_pairs={{0,2},{1,3},{2,0},{3,1},{4,6},{5,7},{6,4},{7,5},{8,10},{9,11},{10,... | collective-permute-start | bytes 1671176 | tf_op jit(solution)/shard_map/ppermute | solution.py:556
  10.5 37.7 %slice-start.4 = ((s8[6291456]{0:T(1024)(128)(4,1)}), s8[4194304]{0:T(1024)(128)(4,1)S(1)}, s32[]{:S(2)}) async-start(s8[6291456]{0:T(1024)(128)(4,1)} %bitcast.82), calls=%async_computation.4 | async-start | bytes 8388608
  10.6 37.6 %slice-start.5 = ((s8[6291456]{0:T(1024)(128)(4,1)}), s8[2097152]{0:T(1024)(128)(4,1)S(1)}, s32[]{:S(2)}) async-start(s8[6291456]{0:T(1024)(128)(4,1)} %bitcast.82), calls=%async_computation.5 | async-start | bytes 4194304
  13.7 48.0 %copy-start.43 = (bf16[1536,384]{1,0:T(8,128)(2,1)}, bf16[1536,384]{1,0:T(8,128)(2,1)S(1)}, u32[]{:S(2)}) copy-start(bf16[1536,384]{1,0:T(8,128)(2,1)S(1)} %fusion.2) | copy-start | bytes 3538948
  20.9 71.5 %copy-start.3 = (bf16[128,2176]{1,0:T(8,128)(2,1)}, bf16[128,2176]{1,0:T(8,128)(2,1)S(1)}, u32[]{:S(2)}) copy-start(bf16[128,2176]{1,0:T(8,128)(2,1)S(1)} %collective-permute-done.2.y) | copy-start | bytes 1671172
  20.9 13.8 %collective-permute-start.5 = (bf16[128,2176]{1,0:T(8,128)(2,1)S(1)}, bf16[128,2176]{1,0:T(8,128)(2,1)S(1)}, u32[]{:S(2)}, u32[]{:S(2)}) collective-permute-start(bf16[128,2176]{1,0:T(8,128)(2,1)S(1)} %collective-permute-done.a), channel_id=1, source_target_pairs={{0,4},{1,5},{2,6},{3,7},{4,12},{5,13},{6,14},{7,15},{8,0},{9,1},{1... | collective-permute-start | bytes 1671176 | tf_op jit(solution)/shard_map/ppermute | solution.py:556
  23.5 12.6 %collective-permute-start.6 = (bf16[128,2176]{1,0:T(8,128)(2,1)S(1)}, bf16[128,2176]{1,0:T(8,128)(2,1)S(1)}, u32[]{:S(2)}, u32[]{:S(2)}) collective-permute-start(bf16[128,2176]{1,0:T(8,128)(2,1)S(1)} %collective-permute-done.a), channel_id=1, source_target_pairs={{0,1},{1,0},{2,3},{3,2},{4,5},{5,4},{6,7},{7,6},{8,9},{9,8},{10,11... | collective-permute-start | bytes 1671176 | tf_op jit(solution)/shard_map/ppermute | solution.py:556
  24.1 12.4 %collective-permute-start.7 = (bf16[128,2176]{1,0:T(8,128)(2,1)S(1)}, bf16[128,2176]{1,0:T(8,128)(2,1)S(1)}, u32[]{:S(2)}, u32[]{:S(2)}) collective-permute-start(bf16[128,2176]{1,0:T(8,128)(2,1)S(1)} %collective-permute-done.a), channel_id=1, source_target_pairs={{0,2},{1,3},{2,0},{3,1},{4,6},{5,7},{6,4},{7,5},{8,10},{9,11},{10,... | collective-permute-start | bytes 1671176 | tf_op jit(solution)/shard_map/ppermute | solution.py:556
  37.3 9.5 %collective-permute-start.9 = (bf16[64,2176]{1,0:T(8,128)(2,1)S(1)}, bf16[64,2176]{1,0:T(8,128)(2,1)S(1)}, u32[]{:S(2)}, u32[]{:S(2)}) collective-permute-start(bf16[64,2176]{1,0:T(8,128)(2,1)S(1)} %slice.42), channel_id=1, source_target_pairs={{0,2},{1,3},{2,0},{3,1},{4,6},{5,7},{6,4},{7,5},{8,10},{9,11},{10,... | collective-permute-start | bytes 835592 | tf_op jit(solution)/shard_map/ppermute | solution.py:556
  38.8 19.7 %collective-permute-start.11 = (bf16[128,2176]{1,0:T(8,128)(2,1)S(1)}, bf16[128,2176]{1,0:T(8,128)(2,1)}, u32[]{:S(2)}, u32[]{:S(2)}) collective-permute-start(bf16[128,2176]{1,0:T(8,128)(2,1)S(1)} %collective-permute-done.5.a), channel_id=1, source_target_pairs={{0,4},{1,5},{2,6},{3,7},{4,12},{5,13},{6,14},{7,15},{8,0},{9,1},{1... | collective-permute-start | bytes 1671176 | tf_op jit(solution)/shard_map/ppermute | solution.py:556
  40.3 18.2 %collective-permute-start.12 = (bf16[128,2176]{1,0:T(8,128)(2,1)S(1)}, bf16[128,2176]{1,0:T(8,128)(2,1)S(1)}, u32[]{:S(2)}, u32[]{:S(2)}) collective-permute-start(bf16[128,2176]{1,0:T(8,128)(2,1)S(1)} %collective-permute-done.5.a), channel_id=1, source_target_pairs={{0,1},{1,0},{2,3},{3,2},{4,5},{5,4},{6,7},{7,6},{8,9},{9,8},{10,11... | collective-permute-start | bytes 1671176 | tf_op jit(solution)/shard_map/ppermute | solution.py:556
  40.9 17.6 %collective-permute-start.13 = (bf16[128,2176]{1,0:T(8,128)(2,1)S(1)}, bf16[128,2176]{1,0:T(8,128)(2,1)S(1)}, u32[]{:S(2)}, u32[]{:S(2)}) collective-permute-start(bf16[128,2176]{1,0:T(8,128)(2,1)S(1)} %collective-permute-done.5.a), channel_id=1, source_target_pairs={{0,2},{1,3},{2,0},{3,1},{4,6},{5,7},{6,4},{7,5},{8,10},{9,11},{10,... | collective-permute-start | bytes 1671176 | tf_op jit(solution)/shard_map/ppermute | solution.py:556
  42.2 16.2 %collective-permute-start.8 = (bf16[4,96,384]{2,1,0:T(8,128)(2,1)S(1)}, bf16[4,96,384]{2,1,0:T(8,128)(2,1)S(1)}, u32[]{:S(2)}, u32[]{:S(2)}) collective-permute-start(bf16[4,96,384]{2,1,0:T(8,128)(2,1)S(1)} %slice_bitcast_fusion.3), channel_id=1, source_target_pairs={{0,4},{1,5},{2,6},{3,7},{4,12},{5,13},{6,14},{7,15},{8,0},{9,1},{1... | collective-permute-start | bytes 884744 | tf_op jit(solution)/shard_map/ppermute | solution.py:556
  46.7 7.6 %copy-start.24 = (bf16[64,2176]{1,0:T(8,128)(2,1)}, bf16[64,2176]{1,0:T(8,128)(2,1)S(1)}, u32[]{:S(2)}) copy-start(bf16[64,2176]{1,0:T(8,128)(2,1)S(1)} %collective-permute-done.9.low) | copy-start | bytes 835588
  46.7 11.0 %collective-permute-start.10 = (bf16[64,2176]{1,0:T(8,128)(2,1)S(1)}, bf16[64,2176]{1,0:T(8,128)(2,1)S(1)}, u32[]{:S(2)}, u32[]{:S(2)}) collective-permute-start(bf16[64,2176]{1,0:T(8,128)(2,1)S(1)} %slice.43), channel_id=1, source_target_pairs={{0,1},{1,0},{2,3},{3,2},{4,5},{5,4},{6,7},{7,6},{8,9},{9,8},{10,11... | collective-permute-start | bytes 835592 | tf_op jit(solution)/shard_map/ppermute | solution.py:556
  59.2 9.6 %collective-permute-start.16 = (bf16[64,2176]{1,0:T(8,128)(2,1)S(1)}, bf16[64,2176]{1,0:T(8,128)(2,1)S(1)}, u32[]{:S(2)}, u32[]{:S(2)}) collective-permute-start(bf16[64,2176]{1,0:T(8,128)(2,1)S(1)} %slice.46), channel_id=1, source_target_pairs={{0,2},{1,3},{2,0},{3,1},{4,6},{5,7},{6,4},{7,5},{8,10},{9,11},{10,... | collective-permute-start | bytes 835592 | tf_op jit(solution)/shard_map/ppermute | solution.py:556
  59.7 23.8 %collective-permute-start.18 = (bf16[128,2176]{1,0:T(8,128)(2,1)}, bf16[128,2176]{1,0:T(8,128)(2,1)S(1)}, u32[]{:S(2)}, u32[]{:S(2)}) collective-permute-start(bf16[128,2176]{1,0:T(8,128)(2,1)} %collective-permute-done.11.a), channel_id=1, source_target_pairs={{0,1},{1,0},{2,3},{3,2},{4,5},{5,4},{6,7},{7,6},{8,9},{9,8},{10,11... | collective-permute-start | bytes 1671176 | tf_op jit(solution)/shard_map/ppermute | solution.py:556
  60.2 23.2 %collective-permute-start.19 = (bf16[128,2176]{1,0:T(8,128)(2,1)}, bf16[128,2176]{1,0:T(8,128)(2,1)}, u32[]{:S(2)}, u32[]{:S(2)}) collective-permute-start(bf16[128,2176]{1,0:T(8,128)(2,1)} %collective-permute-done.11.a), channel_id=1, source_target_pairs={{0,2},{1,3},{2,0},{3,1},{4,6},{5,7},{6,4},{7,5},{8,10},{9,11},{10,... | collective-permute-start | bytes 1671176 | tf_op jit(solution)/shard_map/ppermute | solution.py:556
  62.7 20.8 %collective-permute-start.14 = (bf16[4,96,384]{2,1,0:T(8,128)(2,1)}, bf16[4,96,384]{2,1,0:T(8,128)(2,1)}, u32[]{:S(2)}, u32[]{:S(2)}) collective-permute-start(bf16[4,96,384]{2,1,0:T(8,128)(2,1)} %get-tuple-element.169), channel_id=1, source_target_pairs={{0,12},{1,13},{2,14},{3,15},{4,8},{5,9},{6,10},{7,11},{8,4},{9,5},... | collective-permute-start | bytes 884744 | tf_op jit(solution)/shard_map/ppermute | solution.py:556
  64.4 19.0 %collective-permute-start.15 = (bf16[4,96,384]{2,1,0:T(8,128)(2,1)}, bf16[4,96,384]{2,1,0:T(8,128)(2,1)}, u32[]{:S(2)}, u32[]{:S(2)}) collective-permute-start(bf16[4,96,384]{2,1,0:T(8,128)(2,1)} %get-tuple-element.168), channel_id=1, source_target_pairs={{0,8},{1,9},{2,10},{3,11},{4,0},{5,1},{6,2},{7,3},{8,12},{9,13},{1... | collective-permute-start | bytes 884744 | tf_op jit(solution)/shard_map/ppermute | solution.py:556
  69.5 13.9 %collective-permute-start.17 = (bf16[64,2176]{1,0:T(8,128)(2,1)}, bf16[64,2176]{1,0:T(8,128)(2,1)}, u32[]{:S(2)}, u32[]{:S(2)}) collective-permute-start(bf16[64,2176]{1,0:T(8,128)(2,1)} %slice.47), channel_id=1, source_target_pairs={{0,1},{1,0},{2,3},{3,2},{4,5},{5,4},{6,7},{7,6},{8,9},{9,8},{10,11... | collective-permute-start | bytes 835592 | tf_op jit(solution)/shard_map/ppermute | solution.py:556
  70.0 2.8 %copy-start = (bf16[384,4,2048]{2,0,1:T(8,128)(2,1)S(1)}, bf16[384,4,2048]{2,0,1:T(8,128)(2,1)}, u32[]{:S(2)}) copy-start(bf16[384,4,2048]{2,0,1:T(8,128)(2,1)} %copy.65) | copy-start | bytes 18874372
  82.3 1.1 copy-start.32
  83.4 4.2 %copy-start.12 = (bf16[4,96,384]{2,1,0:T(8,128)(2,1)S(1)}, bf16[4,96,384]{2,1,0:T(8,128)(2,1)}, u32[]{:S(2)}) copy-start(bf16[4,96,384]{2,1,0:T(8,128)(2,1)} %copy-done.11) | copy-start | bytes 884740
  83.4 1.6 copy-start.5
  83.5 16.9 %collective-permute-start.22 = (bf16[64,2176]{1,0:T(8,128)(2,1)S(1)}, bf16[64,2176]{1,0:T(8,128)(2,1)S(1)}, u32[]{:S(2)}, u32[]{:S(2)}) collective-permute-start(bf16[64,2176]{1,0:T(8,128)(2,1)S(1)} %slice.49), channel_id=1, source_target_pairs={{0,2},{1,3},{2,0},{3,1},{4,6},{5,7},{6,4},{7,5},{8,10},{9,11},{10,... | collective-permute-start | bytes 835592 | tf_op jit(solution)/shard_map/ppermute | solution.py:556
  85.1 8.9 %copy-start.17 = (bf16[128,2176]{1,0:T(8,128)(2,1)S(1)}, bf16[128,2176]{1,0:T(8,128)(2,1)}, u32[]{:S(2)}) copy-start(bf16[128,2176]{1,0:T(8,128)(2,1)} %copy-done.16) | copy-start | bytes 1671172
  85.1 8.9 %copy-start.23 = (bf16[64,2176]{1,0:T(8,128)(2,1)S(1)}, bf16[64,2176]{1,0:T(8,128)(2,1)}, u32[]{:S(2)}) copy-start(bf16[64,2176]{1,0:T(8,128)(2,1)} %copy-done.22) | copy-start | bytes 835588
  85.1 16.1 %collective-permute-start.23 = (bf16[64,2176]{1,0:T(8,128)(2,1)S(1)}, bf16[64,2176]{1,0:T(8,128)(2,1)S(1)}, u32[]{:S(2)}, u32[]{:S(2)}) collective-permute-start(bf16[64,2176]{1,0:T(8,128)(2,1)S(1)} %slice.50), channel_id=1, source_target_pairs={{0,1},{1,0},{2,3},{3,2},{4,5},{5,4},{6,7},{7,6},{8,9},{9,8},{10,11... | collective-permute-start | bytes 835592 | tf_op jit(solution)/shard_map/ppermute | solution.py:556
  90.1 24.1 %collective-permute-start.25 = (bf16[4,96,384]{2,1,0:T(8,128)(2,1)S(1)}, bf16[4,96,384]{2,1,0:T(8,128)(2,1)S(1)}, u32[]{:S(2)}, u32[]{:S(2)}) collective-permute-start(bf16[4,96,384]{2,1,0:T(8,128)(2,1)S(1)} %get-tuple-element.114), channel_id=1, source_target_pairs={{0,1},{1,0},{2,3},{3,2},{4,5},{5,4},{6,7},{7,6},{8,9},{9,8},{10,11... | collective-permute-start | bytes 884744 | tf_op jit(solution)/shard_map/ppermute | solution.py:556
  90.8 17.5 %collective-permute-start.3 = (bf16[64,2176]{1,0:T(8,128)(2,1)S(1)}, bf16[64,2176]{1,0:T(8,128)(2,1)S(1)}, u32[]{:S(2)}, u32[]{:S(2)}) collective-permute-start(bf16[64,2176]{1,0:T(8,128)(2,1)S(1)} %slice.39), channel_id=1, source_target_pairs={{0,2},{1,3},{2,0},{3,1},{4,6},{5,7},{6,4},{7,5},{8,10},{9,11},{10,... | collective-permute-start | bytes 835592 | tf_op jit(solution)/shard_map/ppermute | solution.py:556
  92.4 9.3 %copy-start.6 = (bf16[128,2176]{1,0:T(8,128)(2,1)S(1)}, bf16[128,2176]{1,0:T(8,128)(2,1)}, u32[]{:S(2)}) copy-start(bf16[128,2176]{1,0:T(8,128)(2,1)} %copy-done.5) | copy-start | bytes 1671172
  92.4 18.9 %collective-permute-start.4 = (bf16[64,2176]{1,0:T(8,128)(2,1)S(1)}, bf16[64,2176]{1,0:T(8,128)(2,1)S(1)}, u32[]{:S(2)}, u32[]{:S(2)}) collective-permute-start(bf16[64,2176]{1,0:T(8,128)(2,1)S(1)} %slice.40), channel_id=1, source_target_pairs={{0,1},{1,0},{2,3},{3,2},{4,5},{5,4},{6,7},{7,6},{8,9},{9,8},{10,11... | collective-permute-start | bytes 835592 | tf_op jit(solution)/shard_map/ppermute | solution.py:556
  99.2 1.1 copy-start.34
  100.4 27.2 %collective-permute-start.20 = (bf16[4,96,384]{2,1,0:T(8,128)(2,1)}, bf16[4,96,384]{2,1,0:T(8,128)(2,1)}, u32[]{:S(2)}, u32[]{:S(2)}) collective-permute-start(bf16[4,96,384]{2,1,0:T(8,128)(2,1)} %get-tuple-element.109), channel_id=1, source_target_pairs={{0,8},{1,9},{2,10},{3,11},{4,0},{5,1},{6,2},{7,3},{8,12},{9,13},{1... | collective-permute-start | bytes 884744 | tf_op jit(solution)/shard_map/ppermute | solution.py:556
  101.2 23.3 %collective-permute-start.26 = (bf16[4,96,384]{2,1,0:T(8,128)(2,1)}, bf16[4,96,384]{2,1,0:T(8,128)(2,1)}, u32[]{:S(2)}, u32[]{:S(2)}) collective-permute-start(bf16[4,96,384]{2,1,0:T(8,128)(2,1)} %get-tuple-element.115), channel_id=1, source_target_pairs={{0,2},{1,3},{2,0},{3,1},{4,6},{5,7},{6,4},{7,5},{8,10},{9,11},{10,... | collective-permute-start | bytes 884744 | tf_op jit(solution)/shard_map/ppermute | solution.py:556
  101.7 52.6 %slice-start.2 = ((s8[6291456]{0:T(1024)(128)(4,1)}), s8[2097152]{0:T(1024)(128)(4,1)S(1)}, s32[]{:S(2)}) async-start(s8[6291456]{0:T(1024)(128)(4,1)} %bitcast.71), calls=%async_computation.2 | async-start | bytes 4194304
  109.0 15.6 %collective-permute-start.27 = (bf16[4,96,384]{2,1,0:T(8,128)(2,1)}, bf16[4,96,384]{2,1,0:T(8,128)(2,1)}, u32[]{:S(2)}, u32[]{:S(2)}) collective-permute-start(bf16[4,96,384]{2,1,0:T(8,128)(2,1)} %get-tuple-element.116), channel_id=1, source_target_pairs={{0,3},{1,2},{2,1},{3,0},{4,7},{5,6},{6,5},{7,4},{8,11},{9,10},{10,... | collective-permute-start | bytes 884744 | tf_op jit(solution)/shard_map/ppermute | solution.py:556
  112.1 15.5 %collective-permute-start.21 = (bf16[4,96,384]{2,1,0:T(8,128)(2,1)}, bf16[4,96,384]{2,1,0:T(8,128)(2,1)}, u32[]{:S(2)}, u32[]{:S(2)}) collective-permute-start(bf16[4,96,384]{2,1,0:T(8,128)(2,1)} %get-tuple-element.110), channel_id=1, source_target_pairs={{0,12},{1,13},{2,14},{3,15},{4,8},{5,9},{6,10},{7,11},{8,4},{9,5},... | collective-permute-start | bytes 884744 | tf_op jit(solution)/shard_map/ppermute | solution.py:556
  115.0 12.6 %collective-permute-start.24 = (bf16[4,96,384]{2,1,0:T(8,128)(2,1)}, bf16[4,96,384]{2,1,0:T(8,128)(2,1)}, u32[]{:S(2)}, u32[]{:S(2)}) collective-permute-start(bf16[4,96,384]{2,1,0:T(8,128)(2,1)} %get-tuple-element.113), channel_id=1, source_target_pairs={{0,4},{1,5},{2,6},{3,7},{4,12},{5,13},{6,14},{7,15},{8,0},{9,1},{1... | collective-permute-start | bytes 884744 | tf_op jit(solution)/shard_map/ppermute | solution.py:556
  115.0 2.8 %copy-start.1 = (bf16[384,4,2048]{2,0,1:T(8,128)(2,1)S(1)}, bf16[384,4,2048]{2,0,1:T(8,128)(2,1)}, u32[]{:S(2)}) copy-start(bf16[384,4,2048]{2,0,1:T(8,128)(2,1)} %copy.65) | copy-start | bytes 18874372
  120.7 3.8 %copy-start.13 = (bf16[4,96,384]{2,1,0:T(8,128)(2,1)S(1)}, bf16[4,96,384]{2,1,0:T(8,128)(2,1)}, u32[]{:S(2)}) copy-start(bf16[4,96,384]{2,1,0:T(8,128)(2,1)} %copy-done.11) | copy-start | bytes 884740
  120.7 3.8 %copy-start.19 = (bf16[4,96,384]{2,1,0:T(8,128)(2,1)S(1)}, bf16[4,96,384]{2,1,0:T(8,128)(2,1)}, u32[]{:S(2)}) copy-start(bf16[4,96,384]{2,1,0:T(8,128)(2,1)} %copy-done.18) | copy-start | bytes 884740
  120.7 8.4 %copy-start.37 = (bf16[384,2048]{1,0:T(8,128)(2,1)S(1)}, bf16[384,2048]{1,0:T(8,128)(2,1)}, u32[]{:S(2)}) copy-start(bf16[384,2048]{1,0:T(8,128)(2,1)} %copy-done.36) | copy-start | bytes 4718596
  120.7 33.6 %slice-start.3 = ((s8[6291456]{0:T(1024)(128)(4,1)}), s8[4194304]{0:T(1024)(128)(4,1)S(1)}, s32[]{:S(2)}) async-start(s8[6291456]{0:T(1024)(128)(4,1)} %bitcast.71), calls=%async_computation.3 | async-start | bytes 8388608
  124.5 3.1 %copy-start.20 = (bf16[4,96,384]{2,1,0:T(8,128)(2,1)}, bf16[4,96,384]{2,1,0:T(8,128)(2,1)S(1)}, u32[]{:S(2)}) copy-start(bf16[4,96,384]{2,1,0:T(8,128)(2,1)S(1)} %get-tuple-element.89.refs_0_) | copy-start | bytes 884740
  124.5 4.7 %copy-start.33 = (bf16[384,2048]{1,0:T(8,128)(2,1)S(1)}, bf16[384,2048]{1,0:T(8,128)(2,1)}, u32[]{:S(2)}) copy-start(bf16[384,2048]{1,0:T(8,128)(2,1)} %copy-done.32) | copy-start | bytes 4718596
  124.5 4.7 %copy-start.35 = (bf16[384,2048]{1,0:T(8,128)(2,1)S(1)}, bf16[384,2048]{1,0:T(8,128)(2,1)}, u32[]{:S(2)}) copy-start(bf16[384,2048]{1,0:T(8,128)(2,1)} %copy-done.34) | copy-start | bytes 4718596
  124.6 29.8 %slice-start = ((s8[6291456]{0:T(1024)(128)(4,1)}), s8[4194304]{0:T(1024)(128)(4,1)S(1)}, s32[]{:S(2)}) async-start(s8[6291456]{0:T(1024)(128)(4,1)} %bitcast.67), calls=%async_computation | async-start | bytes 8388608
  129.2 25.2 %slice-start.1 = ((s8[6291456]{0:T(1024)(128)(4,1)}), s8[2097152]{0:T(1024)(128)(4,1)S(1)}, s32[]{:S(2)}) async-start(s8[6291456]{0:T(1024)(128)(4,1)} %bitcast.67), calls=%async_computation.1 | async-start | bytes 4194304
  137.6 16.7 %collective-permute-start.28 = (bf16[4,192,2048]{2,1,0:T(8,128)(2,1)S(1)}, bf16[4,192,2048]{2,1,0:T(8,128)(2,1)S(1)}, u32[]{:S(2)}, u32[]{:S(2)}) collective-permute-start(bf16[4,192,2048]{2,1,0:T(8,128)(2,1)S(1)} %get-tuple-element.129), channel_id=1, source_target_pairs={{0,16},{16,0},{1,17},{17,1},{2,18},{18,2},{3,19},{19,3},{4,20},{20... | collective-permute-start | bytes 9437192 | tf_op jit(solution)/shard_map/ppermute | solution.py:638
  137.7 9.9 %collective-permute-start.29 = (bf16[4,96,384]{2,1,0:T(8,128)(2,1)S(1)}, bf16[4,96,384]{2,1,0:T(8,128)(2,1)S(1)}, u32[]{:S(2)}, u32[]{:S(2)}) collective-permute-start(bf16[4,96,384]{2,1,0:T(8,128)(2,1)S(1)} %get-tuple-element.130), channel_id=1, source_target_pairs={{0,1},{1,0},{2,3},{3,2},{4,5},{5,4},{6,7},{7,6},{8,9},{9,8},{10,11... | collective-permute-start | bytes 884744 | tf_op jit(solution)/shard_map/ppermute | solution.py:556
  138.9 15.4 %collective-permute-start.30 = (bf16[4,96,384]{2,1,0:T(8,128)(2,1)S(1)}, bf16[4,96,384]{2,1,0:T(8,128)(2,1)S(1)}, u32[]{:S(2)}, u32[]{:S(2)}) collective-permute-start(bf16[4,96,384]{2,1,0:T(8,128)(2,1)S(1)} %get-tuple-element.131), channel_id=1, source_target_pairs={{0,2},{1,3},{2,0},{3,1},{4,6},{5,7},{6,4},{7,5},{8,10},{9,11},{10,... | collective-permute-start | bytes 884744 | tf_op jit(solution)/shard_map/ppermute | solution.py:556
  139.4 14.9 %collective-permute-start.31 = (bf16[4,96,384]{2,1,0:T(8,128)(2,1)S(1)}, bf16[4,96,384]{2,1,0:T(8,128)(2,1)S(1)}, u32[]{:S(2)}, u32[]{:S(2)}) collective-permute-start(bf16[4,96,384]{2,1,0:T(8,128)(2,1)S(1)} %get-tuple-element.132), channel_id=1, source_target_pairs={{0,3},{1,2},{2,1},{3,0},{4,7},{5,6},{6,5},{7,4},{8,11},{9,10},{10,... | collective-permute-start | bytes 884744 | tf_op jit(solution)/shard_map/ppermute | solution.py:556
  154.3 10.5 %copy-start.39 = (bf16[4,96,384]{2,1,0:T(8,128)(2,1)}, bf16[4,96,384]{2,1,0:T(8,128)(2,1)S(1)}, u32[]{:S(2)}) copy-start(bf16[4,96,384]{2,1,0:T(8,128)(2,1)S(1)} %collective-permute-done.30.refs_5_) | copy-start | bytes 884740
  154.3 10.5 %copy-start.41 = (bf16[4,96,384]{2,1,0:T(8,128)(2,1)}, bf16[4,96,384]{2,1,0:T(8,128)(2,1)S(1)}, u32[]{:S(2)}) copy-start(bf16[4,96,384]{2,1,0:T(8,128)(2,1)S(1)} %collective-permute-done.31.refs_6_) | copy-start | bytes 884740
  154.4 3.0 %copy-start.2 = (f32[192,4,2048]{2,1,0:T(4,128)S(1)}, f32[192,4,2048]{2,1,0:T(4,128)}, u32[]{:S(2)}) copy-start(f32[192,4,2048]{2,1,0:T(4,128)} %param.15) | copy-start | bytes 18874372
  164.8 16.0 %collective-permute-start.32 = (bf16[6144,128]{1,0:T(8,128)(2,1)}, bf16[6144,128]{1,0:T(8,128)(2,1)}, u32[]{:S(2)}, u32[]{:S(2)}) collective-permute-start(bf16[6144,128]{1,0:T(8,128)(2,1)} %get-tuple-element.147), channel_id=1, source_target_pairs={{0,16},{16,0},{1,17},{17,1},{2,18},{18,2},{3,19},{19,3},{4,20},{20... | collective-permute-start | bytes 4718600 | tf_op jit(solution)/shard_map/ppermute | solution.py:653
  164.8 8.0 %copy-start.21 = (bf16[4,96,384]{2,1,0:T(8,128)(2,1)S(1)}, bf16[4,96,384]{2,1,0:T(8,128)(2,1)}, u32[]{:S(2)}) copy-start(bf16[4,96,384]{2,1,0:T(8,128)(2,1)} %copy-done.20) | copy-start | bytes 884740
  164.9 7.9 %copy-start.38 = (bf16[128,8,384]{2,1,0:T(8,128)(2,1)S(1)}, bf16[128,8,384]{2,1,0:T(8,128)(2,1)}, u32[]{:S(2)}) copy-start(bf16[128,8,384]{2,1,0:T(8,128)(2,1)} %param.9) | copy-start | bytes 2359300
  172.4 8.5 %collective-permute-start.33 = (bf16[6144,128]{1,0:T(8,128)(2,1)}, bf16[6144,128]{1,0:T(8,128)(2,1)S(1)}, u32[]{:S(2)}, u32[]{:S(2)}) collective-permute-start(bf16[6144,128]{1,0:T(8,128)(2,1)} %get-tuple-element.148), channel_id=1, source_target_pairs={{0,16},{16,0},{1,17},{17,1},{2,18},{18,2},{3,19},{19,3},{4,20},{20... | collective-permute-start | bytes 4718600 | tf_op jit(solution)/shard_map/ppermute | solution.py:653
  (21 other events, 18.6 us)

commit v3 on v2

--- a/solution.py
+++ b/solution.py
@@ -75,7 +75,7 @@
 
 
 def grads_kernel(first, a, x, y, low, high, by_expert, d_out, g_out, *scratch):
-    rows, match, d_rows, grads, sems = scratch
+    rows, match, d_rows, grads, weights, sems = scratch
     experts, width, features = by_expert.shape
     tokens = rows.shape[0] // 4
     slots = experts * CAP
@@ -88,6 +88,12 @@
         at += piece.shape[0]
     for load in loads:
         load.wait()
+    loads = [
+        pltpu.make_async_copy(by_expert.at[e], weights.at[e], sems.at[7 + e])
+        for e in range(experts)
+    ]
+    for load in loads:
+        load.start()
 
     slot = lax.broadcasted_iota(jnp.int32, (slots, tokens), 0)
     expert = first[0] + slot // CAP
@@ -123,15 +129,17 @@
     stores = [pltpu.make_async_copy(d_rows, d_out, sems.at[5])]
     stores[0].start()
     count = 4 * CAP
-    found = [
-        lax.dot_general(
-            d_rows[e * count : (e + 1) * count],
-            by_expert[e],
-            (((1,), (1,)), ((), ())),
-            preferred_element_type=jnp.float32,
+    found = []
+    for e in range(experts):
+        loads[e].wait()
+        found.append(
+            lax.dot_general(
+                d_rows[e * count : (e + 1) * count],
+                weights[e],
+                (((1,), (1,)), ((), ())),
+                preferred_element_type=jnp.float32,
+            )
         )
-        for e in range(experts)
-    ]
     for c in range(4):
         mine = [f[c * CAP : (c + 1) * CAP] for f in found]
         grads[c] = jnp.concatenate(mine, axis=0).astype(jnp.bfloat16)
@@ -152,17 +160,17 @@
             jax.ShapeDtypeStruct((4, slots, width), jnp.bfloat16),
         ),
         in_specs=[pl.BlockSpec(memory_space=pltpu.SMEM)]
-        + [HBM] * 5
-        + [INSIDE],
+        + [HBM] * 6,
         out_specs=(HBM, HBM),
         scratch_shapes=[
             pltpu.VMEM((4 * tokens, columns), jnp.bfloat16),
             pltpu.VMEM((4 * slots, 4 * tokens), jnp.bfloat16),
             pltpu.VMEM((4 * slots, features), jnp.bfloat16),
             pltpu.VMEM((4, slots, width), jnp.bfloat16),
-            pltpu.SemaphoreType.DMA((7,)),
+            pltpu.VMEM(by_expert.shape, jnp.bfloat16),
+            pltpu.SemaphoreType.DMA((7 + experts,)),
         ],
-        compiler_params=pltpu.CompilerParams(vmem_limit_bytes=14 * MIB),
+        compiler_params=pltpu.CompilerParams(vmem_limit_bytes=56 * MIB),
         cost_estimate=pl.CostEstimate(
             flops=8 * slots * features * (4 * tokens + width),
             bytes_accessed=8 * (slots + tokens) * features,
@@ -247,7 +255,7 @@
             pltpu.VMEM((count, 3, slots, width), jnp.bfloat16),
             pltpu.SemaphoreType.DMA((count + 3,)),
         ],
-        compiler_params=pltpu.CompilerParams(vmem_limit_bytes=6 * MIB),
+        compiler_params=pltpu.CompilerParams(vmem_limit_bytes=10 * MIB),
         cost_estimate=pl.CostEstimate(
             flops=0, bytes_accessed=12 * count * slots * width, transcendentals=0
         ),
@@ -314,7 +322,7 @@
             pltpu.VMEM((experts, width, features), jnp.bfloat16),
             pltpu.SemaphoreType.DMA((experts, 1 + len(blocks) + count)),
         ],
-        compiler_params=pltpu.CompilerParams(vmem_limit_bytes=20 * MIB),
+        compiler_params=pltpu.CompilerParams(vmem_limit_bytes=30 * MIB),
         cost_estimate=pl.CostEstimate(
             flops=2 * experts * width * slots * features,
             bytes_accessed=2 * experts * (width + slots) * features,
@@ -431,7 +439,7 @@
         ),
         out_shape=jax.ShapeDtypeStruct(full.shape, full.dtype),
         input_output_aliases={3: 0},
-        compiler_params=pltpu.CompilerParams(vmem_limit_bytes=14 * MIB),
+        compiler_params=pltpu.CompilerParams(vmem_limit_bytes=12 * MIB),
         cost_estimate=pl.CostEstimate(
             flops=0, bytes_accessed=4 * (low.size + high.size), transcendentals=0
         ),
@@ -571,9 +579,12 @@
     def flips(arrays):
         return [move(a, 0, c) for c, a in enumerate(arrays, 1)]
 
-    def far(j):
+    def halves(j):
         _, by_x, by_y = near[j]
-        return (move(by_x[:half], 0, 2), move(by_y[half:], 0, 1))
+        return (by_x[:half], by_y[half:])
+
+    def far(low, high):
+        return (move(low, 0, 2), move(high, 0, 1))
 
     for k in range(length + 1):
         moving = {}
@@ -583,13 +594,15 @@
             moving["x"] = move(own, 0, 1)
             moving["y"] = move(own, 0, 2)
         if k > 1:
-            moving["far"] = far(k - 1)
+            moving["far"] = far(*halves(k - 1))
         if k == length:
-            moving["first"] = far(0)
+            moving["first"] = far(*first_cut)
         if k > 2:
             add_chunk(k - 2)
         if k == 0:
             moving["columns"] = columns
+        if k == 1:
+            moving["cut"] = halves(0)
         if k == last - 1:
             moving["weights"] = by_expert
             w_parts[1] = move(w_send[1], 1, 0)
@@ -604,6 +617,8 @@
         d_rows, grads, w_parts, w_send = moved["done"]
         if k == 0:
             columns = moved["columns"]
+        if k == 1:
+            first_cut = moved["cut"]
         if k == last - 1:
             by_expert = moved["weights"]
         if k == last:
@@ -627,8 +642,6 @@
     pieces = tuple((k, 0) if c == 0 else (length + c - 1, k) for k in range(length) for c in range(4))
     w_slots = order_slots(w_arrays + w_flipped, pieces)
     d_rows, leaving = tie(([d_rows[j] for j in range(length)], regroup(back)))
-    flipped = flips(leaving)
-
     def outer_perm(steps):
         return [(i, (i + steps) % outer_size) for i in range(outer_size)]
 
@@ -637,6 +650,9 @@
     partials = [mine] + [
         lax.ppermute(part, "outer", outer_perm(r)) for r, part in enumerate(sent, 1)
     ]
+    partials, leaving = tie((partials, leaving))
+    flipped = flips(leaving)
+
     at = outer_at.astype(jnp.int32)[None]
     total_rows = secondary.size // LANES
     blocks = rows // 16

time: 185 us -> 179 us (0.968)
  local copies, waits for them, and re-layouts: 41.4 us -> 24.5 us
  Pallas kernels: 57.6 us -> 65.8 us
  waiting for transfers between devices: 38.9 us -> 42.2 us
    unnamed x106 -> x90, local copies, waits for them, and re-layouts: 37.2 us -> 19.8 us
    pallas_call x4, Pallas kernels: 18.7 us -> 27.6 us  [chunk_grads(): pl.pallas_call(grads_kernel, out_shape=(jax.ShapeDtypeStruct((4 * slots,...]
    ppermute x1, waiting for transfers between devices: 0.01 us -> 5.65 us  [local(): lax.ppermute(part, 'outer', outer_perm(r))]
    ppermute x31, waiting for transfers between devices: 38.9 us -> 36.6 us  [move(): return lax.ppermute(block, 'inner', step_perm(size, steps, flip))]
  transfers between devices with their start and end apart: 34 -> 34, of which waited for: 11 -> 13; matrix products, arithmetic and copies ran while one was open for 8% -> 8% of each run, Pallas kernels for 20% -> 30%
where the time goes in v3:
time: 179 us; the launch traced here: 178 us
  Pallas kernels  65.8 us (37%)
  waiting for transfers between devices  42.2 us (24%)
  starting transfers between devices  40.1 us (22%)
  local copies, waits for them, and re-layouts  24.5 us (14%)
  matrix products  2.23 us (1%)
  other arithmetic  2.1 us (1%)
    ppermute x31, starting transfers between devices, move(): return lax.ppermute(block, 'inner', step_perm(size, steps, flip))  40 us
    ppermute x31, waiting for transfers between devices, move(): return lax.ppermute(block, 'inner', step_perm(size, steps, flip))  36.6 us
    pallas_call x4, Pallas kernels, chunk_grads(): pl.pallas_call(grads_kernel, out_shape=(jax.ShapeDtypeStruct((4 * slots,...  27.6 us
    unnamed x90, local copies, waits for them, and re-layouts  19.8 us
    pallas_call x2, Pallas kernels, adam_rows(): pl.pallas_call(functools.partial(adam_kernel, count, kept, first), grid_s...  14.9 us
    pallas_call x1, Pallas kernels, partial_rows(): pl.pallas_call(partial_kernel, out_shape=[jax.ShapeDtypeStruct((experts,...  8.41 us
    ppermute x1, waiting for transfers between devices, local(): lax.ppermute(part, 'outer', outer_perm(r))  5.65 us
    pallas_call x1, Pallas kernels, finish(): pl.pallas_call(functools.partial(finish_kernel, pieces), out_shape=(jax.S...  5.29 us
  transfers between devices with their start and end apart: 34, of which 13 were waited for; matrix products, arithmetic and copies ran while one was open for 8% of the time, Pallas kernels for 30%

profile of v3, /device:TPU:0, one launch (start us, length us, event | category | flops | bytes accessed | tf_op | source)
XLA Modules:
  0.0 178.2 jit_solution(1713755126450322941)
XLA Ops:
  0.7 0.8 convert_element_type.50
  1.5 1.1 fusion.9.a
  2.6 3.1 %collective-permute-start = (bf16[128,2176]{1,0:T(8,128)(2,1)S(1)}, bf16[128,2176]{1,0:T(8,128)(2,1)}, u32[]{:S(2)}, u32[]{:S(2)}) collective-permute-start(bf16[128,2176]{1,0:T(8,128)(2,1)S(1)} %fusion.9.a), channel_id=1, source_target_pairs={{0,4},{1,5},{2,6},{3,7},{4,12},{5,13},{6,14},{7,15},{8,0},{9,1},{1... | collective-permute-start | bytes 1671176 | tf_op jit(solution)/shard_map/ppermute | solution.py:564
  5.7 1.5 collective-permute-start.1
  7.2 1.5 collective-permute-start.2
  8.7 0.8 copy.48
  10.7 1.9 %fusion.2 = bf16[1536,384]{1,0:T(8,128)(2,1)S(1)} fusion(s32[1024]{0:T(1024)S(1)} %fusion.41, bf16[128,8,384]{2,1,0:T(8,128)(2,1)S(1)} %copy-done.9, f32[128,8]{1,0:T(8,128)S(1)} %copy.50), kind=kOutput, calls=%fused_computation.4 | convolution fusion | flops 1211301888 | bytes 1974272 | tf_op jit(solution)/shard_map/dot_general | solution.py:556
  12.6 6.9 %collective-permute-done.a = bf16[128,2176]{1,0:T(8,128)(2,1)} collective-permute-done((bf16[128,2176]{1,0:T(8,128)(2,1)S(1)}, bf16[128,2176]{1,0:T(8,128)(2,1)}, u32[]{:S(2)}, u32[]{:S(2)}) %collective-permute-start) | collective-permute-done | bytes 557088 | tf_op jit(solution)/shard_map/ppermute | solution.py:564
  19.8 1.2 collective-permute-done.2.y
  21.0 2.6 %collective-permute-start.3 = (bf16[128,2176]{1,0:T(8,128)(2,1)}, bf16[128,2176]{1,0:T(8,128)(2,1)S(1)}, u32[]{:S(2)}, u32[]{:S(2)}) collective-permute-start(bf16[128,2176]{1,0:T(8,128)(2,1)} %collective-permute-done.a), channel_id=1, source_target_pairs={{0,4},{1,5},{2,6},{3,7},{4,12},{5,13},{6,14},{7,15},{8,0},{9,1},{1... | collective-permute-start | bytes 1671176 | tf_op jit(solution)/shard_map/ppermute | solution.py:564
  24.1 1.5 collective-permute-start.5
  25.7 0.7 slice.39
  26.4 0.7 slice.40
  27.1 8.0 %collective-permute-done.3.a = bf16[128,2176]{1,0:T(8,128)(2,1)S(1)} collective-permute-done((bf16[128,2176]{1,0:T(8,128)(2,1)}, bf16[128,2176]{1,0:T(8,128)(2,1)S(1)}, u32[]{:S(2)}, u32[]{:S(2)}) %collective-permute-start.3) | collective-permute-done | bytes 557088 | tf_op jit(solution)/shard_map/ppermute | solution.py:564
  35.1 1.3 collective-permute-done.4.x
  36.4 0.6 collective-permute-done.5.y
  37.1 1.6 collective-permute-start.9
  38.7 1.3 collective-permute-start.11
  41.1 1.0 collective-permute-start.8
  42.1 4.5 %collective-permute-done.9.low = bf16[64,2176]{1,0:T(8,128)(2,1)S(1)} collective-permute-done((bf16[64,2176]{1,0:T(8,128)(2,1)S(1)}, bf16[64,2176]{1,0:T(8,128)(2,1)S(1)}, u32[]{:S(2)}, u32[]{:S(2)}) %collective-permute-start.9) | collective-permute-done | bytes 278560 | tf_op jit(solution)/shard_map/ppermute | solution.py:564
  46.7 1.5 collective-permute-start.10
  48.2 6.2 %copy.65 = bf16[384,4,2048]{2,0,1:T(8,128)(2,1)} copy(bf16[384,4,2048]{2,1,0:T(4,128)(2,1)S(1)} %bitcast.83) | data formatting | bytes 12582912 | tf_op args[4]
  54.3 3.4 %collective-permute-done.10.high = bf16[64,2176]{1,0:T(8,128)(2,1)S(1)} collective-permute-done((bf16[64,2176]{1,0:T(8,128)(2,1)S(1)}, bf16[64,2176]{1,0:T(8,128)(2,1)S(1)}, u32[]{:S(2)}, u32[]{:S(2)}) %collective-permute-start.10) | collective-permute-done | bytes 278560 | tf_op jit(solution)/shard_map/ppermute | solution.py:564
  59.0 1.5 collective-permute-start.19
  60.5 0.9 slice_bitcast_fusion.1
  61.3 2.1 %collective-permute-start.14 = (bf16[4,96,384]{2,1,0:T(8,128)(2,1)}, bf16[4,96,384]{2,1,0:T(8,128)(2,1)S(1)}, u32[]{:S(2)}, u32[]{:S(2)}) collective-permute-start(bf16[4,96,384]{2,1,0:T(8,128)(2,1)} %get-tuple-element.183), channel_id=1, source_target_pairs={{0,12},{1,13},{2,14},{3,15},{4,8},{5,9},{6,10},{7,11},{8,4},{9,5},... | collective-permute-start | bytes 884744 | tf_op jit(solution)/shard_map/ppermute | solution.py:564
  64.0 0.7 slice.47
  64.7 2.9 %collective-permute-done.16.low = bf16[64,2176]{1,0:T(8,128)(2,1)} collective-permute-done((bf16[64,2176]{1,0:T(8,128)(2,1)S(1)}, bf16[64,2176]{1,0:T(8,128)(2,1)}, u32[]{:S(2)}, u32[]{:S(2)}) %collective-permute-start.16) | collective-permute-done | bytes 278560 | tf_op jit(solution)/shard_map/ppermute | solution.py:564
  68.1 6.8 %shard_map.128 = (bf16[384,2048]{1,0:T(8,128)(2,1)}, bf16[4,96,384]{2,1,0:T(8,128)(2,1)}) custom-call(s32[1]{0:T(128)} %bitcast.5.first, bf16[128,2176]{1,0:T(8,128)(2,1)} %collective-permute-done.a, bf16[128,2176]{1,0:T(8,128)(2,1)} %copy-done.24, bf16[128,2176]{1,0:T(8,128)(2,1)} %copy-done.25, bf16[64,2176]{1,0:T(8,128)(2,1)} %copy-done.28, ...), custom_call_target="tpu_custom_call" | custom-call | flops 1409286144 | bytes 3670016 | tf_op jit(solution)/shard_map/pallas_call | solution.py:156
  74.9 1.2 collective-permute-done.17.high
  76.2 0.6 collective-permute-start.22
  77.3 1.0 slice_bitcast_fusion.refs_0_
  78.3 2.1 %shard_map.131 = (bf16[4,96,384]{2,1,0:T(8,128)(2,1)S(1)}, bf16[4,96,384]{2,1,0:T(8,128)(2,1)}, bf16[4,96,384]{2,1,0:T(8,128)(2,1)}) custom-call(bf16[4,96,384]{2,1,0:T(8,128)(2,1)S(1)} %slice_bitcast_fusion.refs_0_, bf16[4,96,384]{2,1,0:T(8,128)(2,1)S(1)} %collective-permute-done.8.refs_1_, bf16[4,96,384]{2,1,0:T(8,128)(2,1)S(1)} %collective-permute-done.14.refs_2_, ...), custom_call_target="tpu_custom_call" | custom-call | bytes 1769472 | tf_op jit(solution)/shard_map/pallas_call | solution.py:249
  80.4 1.8 %collective-permute-start.25 = (bf16[4,96,384]{2,1,0:T(8,128)(2,1)S(1)}, bf16[4,96,384]{2,1,0:T(8,128)(2,1)S(1)}, u32[]{:S(2)}, u32[]{:S(2)}) collective-permute-start(bf16[4,96,384]{2,1,0:T(8,128)(2,1)S(1)} %get-tuple-element.123), channel_id=1, source_target_pairs={{0,1},{1,0},{2,3},{3,2},{4,5},{5,4},{6,7},{7,6},{8,9},{9,8},{10,11... | collective-permute-start | bytes 884744 | tf_op jit(solution)/shard_map/ppermute | solution.py:564
  82.2 1.4 collective-permute-start.6
  83.9 6.8 %shard_map.129 = (bf16[384,2048]{1,0:T(8,128)(2,1)}, bf16[4,96,384]{2,1,0:T(8,128)(2,1)}) custom-call(s32[1]{0:T(128)} %bitcast.5.first, bf16[128,2176]{1,0:T(8,128)(2,1)} %copy-done.27, bf16[128,2176]{1,0:T(8,128)(2,1)} %copy-done.20, bf16[128,2176]{1,0:T(8,128)(2,1)} %copy-done.21, bf16[64,2176]{1,0:T(8,128)(2,1)} %collective-permute-done.16.low, ...), custom_call_target="tpu_custom_call" | custom-call | flops 1409286144 | bytes 3670016 | tf_op jit(solution)/shard_map/pallas_call | solution.py:156
  90.7 3.8 %collective-permute-start.20 = (bf16[4,96,384]{2,1,0:T(8,128)(2,1)}, bf16[4,96,384]{2,1,0:T(8,128)(2,1)}, u32[]{:S(2)}, u32[]{:S(2)}) collective-permute-start(bf16[4,96,384]{2,1,0:T(8,128)(2,1)} %get-tuple-element.118), channel_id=1, source_target_pairs={{0,8},{1,9},{2,10},{3,11},{4,0},{5,1},{6,2},{7,3},{8,12},{9,13},{1... | collective-permute-start | bytes 884744 | tf_op jit(solution)/shard_map/ppermute | solution.py:564
  94.4 0.8 collective-permute-start.26
  95.3 6.9 %shard_map.130 = (bf16[384,2048]{1,0:T(8,128)(2,1)}, bf16[4,96,384]{2,1,0:T(8,128)(2,1)}) custom-call(s32[1]{0:T(128)} %bitcast.5.first, bf16[128,2176]{1,0:T(8,128)(2,1)} %collective-permute-done.11.a, bf16[128,2176]{1,0:T(8,128)(2,1)} %copy-done.22, bf16[128,2176]{1,0:T(8,128)(2,1)} %copy-done.23, bf16[64,2176]{1,0:T(8,128)(2,1)} %copy-done.32, ...), custom_call_target="tpu_custom_call" | custom-call | flops 1409286144 | bytes 3670016 | tf_op jit(solution)/shard_map/pallas_call | solution.py:156
  102.2 2.3 %collective-permute-start.27 = (bf16[4,96,384]{2,1,0:T(8,128)(2,1)}, bf16[4,96,384]{2,1,0:T(8,128)(2,1)}, u32[]{:S(2)}, u32[]{:S(2)}) collective-permute-start(bf16[4,96,384]{2,1,0:T(8,128)(2,1)} %get-tuple-element.125), channel_id=1, source_target_pairs={{0,3},{1,2},{2,1},{3,0},{4,7},{5,6},{6,5},{7,4},{8,11},{9,10},{10,... | collective-permute-start | bytes 884744 | tf_op jit(solution)/shard_map/ppermute | solution.py:564
  104.5 2.6 %collective-permute-start.21 = (bf16[4,96,384]{2,1,0:T(8,128)(2,1)}, bf16[4,96,384]{2,1,0:T(8,128)(2,1)}, u32[]{:S(2)}, u32[]{:S(2)}) collective-permute-start(bf16[4,96,384]{2,1,0:T(8,128)(2,1)} %get-tuple-element.119), channel_id=1, source_target_pairs={{0,12},{1,13},{2,14},{3,15},{4,8},{5,9},{6,10},{7,11},{8,4},{9,5},... | collective-permute-start | bytes 884744 | tf_op jit(solution)/shard_map/ppermute | solution.py:564
  107.1 0.7 copy-done.1
  107.9 7.2 %shard_map.127 = (bf16[384,2048]{1,0:T(8,128)(2,1)}, bf16[4,96,384]{2,1,0:T(8,128)(2,1)}) custom-call(s32[1]{0:T(128)} %bitcast.5.first, bf16[128,2176]{1,0:T(8,128)(2,1)} %copy-done.17, bf16[128,2176]{1,0:T(8,128)(2,1)} %copy-done.18, bf16[128,2176]{1,0:T(8,128)(2,1)} %copy-done.19, bf16[64,2176]{1,0:T(8,128)(2,1)} %copy-done.29, ...), custom_call_target="tpu_custom_call" | custom-call | flops 1409286144 | bytes 3670016 | tf_op jit(solution)/shard_map/pallas_call | solution.py:156
  115.2 2.9 %shard_map.132.weighted = bf16[4,384,384]{2,1,0:T(8,128)(2,1)S(1)} custom-call(bf16[4,96,384]{2,1,0:T(8,128)(2,1)S(1)} %slice_bitcast_fusion.refs_0_, bf16[4,96,384]{2,1,0:T(8,128)(2,1)S(1)} %collective-permute-done.8.refs_1_, bf16[4,96,384]{2,1,0:T(8,128)(2,1)S(1)} %collective-permute-done.14.refs_2_, ...), custom_call_target="tpu_custom_call" | custom-call | bytes 4718592 | tf_op jit(solution)/shard_map/pallas_call | solution.py:207
  118.1 5.6 %collective-permute-done.24.refs_3_ = bf16[4,96,384]{2,1,0:T(8,128)(2,1)} collective-permute-done((bf16[4,96,384]{2,1,0:T(8,128)(2,1)}, bf16[4,96,384]{2,1,0:T(8,128)(2,1)}, u32[]{:S(2)}, u32[]{:S(2)}) %collective-permute-start.24) | collective-permute-done | bytes 294944 | tf_op jit(solution)/shard_map/ppermute | solution.py:564
  123.7 1.6 shard_map.133
  125.3 1.4 copy-done.7
  126.7 1.4 copy-done.8
  128.1 8.4 %shard_map.134 = (bf16[4,192,2048]{2,1,0:T(8,128)(2,1)S(1)}, bf16[4,192,2048]{2,1,0:T(8,128)(2,1)S(1)}) custom-call(s32[2]{0:T(128)S(1)} %and_select_fusion.owners, bf16[4,384,384]{2,1,0:T(8,128)(2,1)S(1)} %shard_map.132.weighted, bf16[384,2048]{1,0:T(8,128)(2,1)S(1)} %copy-done.8, bf16[384,2048]{1,0:T(8,128)(2,1)S(1)} %copy-done.5, ...), custom_call_target="tpu_custom_call" | custom-call | flops 2415919104 | bytes 12582912 | tf_op jit(solution)/shard_map/pallas_call | solution.py:313
  136.6 5.6 %collective-permute-done.28.refs_1_ = bf16[4,192,2048]{2,1,0:T(8,128)(2,1)S(1)} collective-permute-done((bf16[4,192,2048]{2,1,0:T(8,128)(2,1)S(1)}, bf16[4,192,2048]{2,1,0:T(8,128)(2,1)S(1)}, u32[]{:S(2)}, u32[]{:S(2)}) %collective-permute-start.28) | collective-permute-done | bytes 3145760 | tf_op jit(solution)/shard_map/ppermute | solution.py:651
  142.6 0.9 collective-permute-start.30
  143.5 2.2 %collective-permute-start.31 = (bf16[4,96,384]{2,1,0:T(8,128)(2,1)S(1)}, bf16[4,96,384]{2,1,0:T(8,128)(2,1)S(1)}, u32[]{:S(2)}, u32[]{:S(2)}) collective-permute-start(bf16[4,96,384]{2,1,0:T(8,128)(2,1)S(1)} %get-tuple-element.146), channel_id=1, source_target_pairs={{0,3},{1,2},{2,1},{3,0},{4,7},{5,6},{6,5},{7,4},{8,11},{9,10},{10,... | collective-permute-start | bytes 884744 | tf_op jit(solution)/shard_map/ppermute | solution.py:564
  145.7 2.8 %copy-done = f32[192,4,2048]{2,1,0:T(4,128)S(1)} copy-done((f32[192,4,2048]{2,1,0:T(4,128)S(1)}, f32[192,4,2048]{2,1,0:T(4,128)}, u32[]{:S(2)}) %copy-start) | copy-done | bytes 6291480
  148.5 7.4 %shard_map.136 = (f32[12288,128]{1,0:T(8,128)}, f32[12288,128]{1,0:T(8,128)}, f32[12288,128]{1,0:T(8,128)}, bf16[24576,128]{1,0:T(8,128)(2,1)}, bf16[6144,128]{1,0:T(8,128)(2,1)}) custom-call(s32[1]{0:T(128)} %bitcast.12.at, bf16[4,192,2048]{2,1,0:T(8,128)(2,1)S(1)} %get-tuple-element.152.refs_0_, bf16[4,192,2048]{2,1,0:T(8,128)(2,1)S(1)} %collective-permute-done.28.refs_1_, ...), custom_call_target="tpu_custom_call" | custom-call | flops 15728640 | bytes 15728640 | tf_op jit(solution)/shard_map/pallas_call | solution.py:386
  156.0 0.7 copy-done.11
  156.7 0.7 copy-done.13
  157.9 0.7 copy-done.15
  158.6 7.4 %shard_map.137 = (f32[12288,128]{1,0:T(8,128)}, f32[12288,128]{1,0:T(8,128)}, f32[12288,128]{1,0:T(8,128)}, bf16[24576,128]{1,0:T(8,128)(2,1)}, bf16[6144,128]{1,0:T(8,128)(2,1)}) custom-call(s32[1]{0:T(128)} %bitcast.12.at, ...), custom_call_target="tpu_custom_call", output_to_operand_aliasing={{0}: (6, {}), {1}: (7, {}), {2}: (8, {}), {3}: (9, {})} | custom-call | flops 15728640 | bytes 15728640 | tf_op jit(solution)/shard_map/pallas_call | solution.py:386
  166.1 1.0 copy-done.12
  167.1 1.0 copy-done.14
  168.0 1.0 copy-done.16
  169.0 5.3 %shard_map.135 = (bf16[1024,384]{1,0:T(8,128)(2,1)}, f32[8,1024]{1,0:T(8,128)S(1)}) custom-call(f32[8,128]{1,0:T(8,128)S(1)} %fusion.27.target, f32[8,128]{1,0:T(8,128)S(1)} %reshape.249.probs, bf16[1024,384]{1,0:T(8,128)(2,1)S(1)} %bitcast.73, bf16[4,96,384]{2,1,0:T(8,128)(2,1)S(1)} %copy-done.4, bf16[4,96,384]{2,1,0:T(8,128)(2,1)} %collective-permute-done.20.refs_1_, ...), custom_call_target="tpu_custom_call" | custom-call | flops 1207959552 | bytes 3145728 | tf_op jit(solution)/shard_map/pallas_call | solution.py:497
  174.4 0.7 copy.62
  175.1 3.2 %shard_map.138 = bf16[24576,128]{1,0:T(8,128)(2,1)} custom-call(s32[1]{0:T(128)} %bitcast.37.at, bf16[6144,128]{1,0:T(8,128)(2,1)} %collective-permute-done.32.low, bf16[6144,128]{1,0:T(8,128)(2,1)S(1)} %collective-permute-done.33.high, bf16[24576,128]{1,0:T(8,128)(2,1)} %get-tuple-element.163.full), custom_call_target="tpu_custom_call", output_to_operand_aliasing={{}: (3, {})} | custom-call | bytes 6291456 | tf_op jit(solution)/shard_map/pallas_call | solution.py:428
  (135 shorter events, 7.5 us)
Async XLA Ops:
  0.6 9.8 %copy-start.36 = (f32[128,8]{0,1:T(8,128)S(1)}, f32[128,8]{0,1:T(8,128)}, u32[]{:S(2)}) copy-start(f32[128,8]{0,1:T(8,128)} %param.10) | copy-start | bytes 12292
  0.6 10.0 %copy-start.9 = (bf16[128,8,384]{2,1,0:T(8,128)(2,1)S(1)}, bf16[128,8,384]{2,1,0:T(8,128)(2,1)}, u32[]{:S(2)}) copy-start(bf16[128,8,384]{2,1,0:T(8,128)(2,1)} %param.9) | copy-start | bytes 2359300
  2.6 9.9 %copy-start.17 = (bf16[128,2176]{1,0:T(8,128)(2,1)}, bf16[128,2176]{1,0:T(8,128)(2,1)S(1)}, u32[]{:S(2)}) copy-start(bf16[128,2176]{1,0:T(8,128)(2,1)S(1)} %fusion.9.a) | copy-start | bytes 1671172
  2.6 16.8 %collective-permute-start = (bf16[128,2176]{1,0:T(8,128)(2,1)S(1)}, bf16[128,2176]{1,0:T(8,128)(2,1)}, u32[]{:S(2)}, u32[]{:S(2)}) collective-permute-start(bf16[128,2176]{1,0:T(8,128)(2,1)S(1)} %fusion.9.a), channel_id=1, source_target_pairs={{0,4},{1,5},{2,6},{3,7},{4,12},{5,13},{6,14},{7,15},{8,0},{9,1},{1... | collective-permute-start | bytes 1671176 | tf_op jit(solution)/shard_map/ppermute | solution.py:564
  5.7 14.1 %collective-permute-start.1 = (bf16[128,2176]{1,0:T(8,128)(2,1)S(1)}, bf16[128,2176]{1,0:T(8,128)(2,1)S(1)}, u32[]{:S(2)}, u32[]{:S(2)}) collective-permute-start(bf16[128,2176]{1,0:T(8,128)(2,1)S(1)} %fusion.9.a), channel_id=1, source_target_pairs={{0,1},{1,0},{2,3},{3,2},{4,5},{5,4},{6,7},{7,6},{8,9},{9,8},{10,11... | collective-permute-start | bytes 1671176 | tf_op jit(solution)/shard_map/ppermute | solution.py:564
  7.2 13.8 %collective-permute-start.2 = (bf16[128,2176]{1,0:T(8,128)(2,1)S(1)}, bf16[128,2176]{1,0:T(8,128)(2,1)S(1)}, u32[]{:S(2)}, u32[]{:S(2)}) collective-permute-start(bf16[128,2176]{1,0:T(8,128)(2,1)S(1)} %fusion.9.a), channel_id=1, source_target_pairs={{0,2},{1,3},{2,0},{3,1},{4,6},{5,7},{6,4},{7,5},{8,10},{9,11},{10,... | collective-permute-start | bytes 1671176 | tf_op jit(solution)/shard_map/ppermute | solution.py:564
  10.6 37.6 %slice-start.4 = ((s8[6291456]{0:T(1024)(128)(4,1)}), s8[4194304]{0:T(1024)(128)(4,1)S(1)}, s32[]{:S(2)}) async-start(s8[6291456]{0:T(1024)(128)(4,1)} %bitcast.82), calls=%async_computation.4 | async-start | bytes 8388608
  10.7 37.5 %slice-start.5 = ((s8[6291456]{0:T(1024)(128)(4,1)}), s8[2097152]{0:T(1024)(128)(4,1)S(1)}, s32[]{:S(2)}) async-start(s8[6291456]{0:T(1024)(128)(4,1)} %bitcast.82), calls=%async_computation.5 | async-start | bytes 4194304
  12.6 47.9 %copy-start.26 = (bf16[1536,384]{1,0:T(8,128)(2,1)}, bf16[1536,384]{1,0:T(8,128)(2,1)S(1)}, u32[]{:S(2)}) copy-start(bf16[1536,384]{1,0:T(8,128)(2,1)S(1)} %fusion.2) | copy-start | bytes 3538948
  19.8 34.5 %copy-start.18 = (bf16[128,2176]{1,0:T(8,128)(2,1)}, bf16[128,2176]{1,0:T(8,128)(2,1)S(1)}, u32[]{:S(2)}) copy-start(bf16[128,2176]{1,0:T(8,128)(2,1)S(1)} %collective-permute-done.1.x) | copy-start | bytes 1671172
  21.0 20.0 %copy-start.19 = (bf16[128,2176]{1,0:T(8,128)(2,1)}, bf16[128,2176]{1,0:T(8,128)(2,1)S(1)}, u32[]{:S(2)}) copy-start(bf16[128,2176]{1,0:T(8,128)(2,1)S(1)} %collective-permute-done.2.y) | copy-start | bytes 1671172
  21.0 14.1 %collective-permute-start.3 = (bf16[128,2176]{1,0:T(8,128)(2,1)}, bf16[128,2176]{1,0:T(8,128)(2,1)S(1)}, u32[]{:S(2)}, u32[]{:S(2)}) collective-permute-start(bf16[128,2176]{1,0:T(8,128)(2,1)} %collective-permute-done.a), channel_id=1, source_target_pairs={{0,4},{1,5},{2,6},{3,7},{4,12},{5,13},{6,14},{7,15},{8,0},{9,1},{1... | collective-permute-start | bytes 1671176 | tf_op jit(solution)/shard_map/ppermute | solution.py:564
  23.6 12.8 %collective-permute-start.4 = (bf16[128,2176]{1,0:T(8,128)(2,1)}, bf16[128,2176]{1,0:T(8,128)(2,1)S(1)}, u32[]{:S(2)}, u32[]{:S(2)}) collective-permute-start(bf16[128,2176]{1,0:T(8,128)(2,1)} %collective-permute-done.a), channel_id=1, source_target_pairs={{0,1},{1,0},{2,3},{3,2},{4,5},{5,4},{6,7},{7,6},{8,9},{9,8},{10,11... | collective-permute-start | bytes 1671176 | tf_op jit(solution)/shard_map/ppermute | solution.py:564
  24.1 12.9 %collective-permute-start.5 = (bf16[128,2176]{1,0:T(8,128)(2,1)}, bf16[128,2176]{1,0:T(8,128)(2,1)S(1)}, u32[]{:S(2)}, u32[]{:S(2)}) collective-permute-start(bf16[128,2176]{1,0:T(8,128)(2,1)} %collective-permute-done.a), channel_id=1, source_target_pairs={{0,2},{1,3},{2,0},{3,1},{4,6},{5,7},{6,4},{7,5},{8,10},{9,11},{10,... | collective-permute-start | bytes 1671176 | tf_op jit(solution)/shard_map/ppermute | solution.py:564
  35.1 19.2 %copy-start.27 = (bf16[128,2176]{1,0:T(8,128)(2,1)}, bf16[128,2176]{1,0:T(8,128)(2,1)S(1)}, u32[]{:S(2)}) copy-start(bf16[128,2176]{1,0:T(8,128)(2,1)S(1)} %collective-permute-done.3.a) | copy-start | bytes 1671172
  36.4 4.6 %copy-start.24 = (bf16[128,2176]{1,0:T(8,128)(2,1)}, bf16[128,2176]{1,0:T(8,128)(2,1)S(1)}, u32[]{:S(2)}) copy-start(bf16[128,2176]{1,0:T(8,128)(2,1)S(1)} %collective-permute-done.4.x) | copy-start | bytes 1671172
  37.1 17.3 %copy-start.25 = (bf16[128,2176]{1,0:T(8,128)(2,1)}, bf16[128,2176]{1,0:T(8,128)(2,1)S(1)}, u32[]{:S(2)}) copy-start(bf16[128,2176]{1,0:T(8,128)(2,1)S(1)} %collective-permute-done.5.y) | copy-start | bytes 1671172
  37.1 9.6 %collective-permute-start.9 = (bf16[64,2176]{1,0:T(8,128)(2,1)S(1)}, bf16[64,2176]{1,0:T(8,128)(2,1)S(1)}, u32[]{:S(2)}, u32[]{:S(2)}) collective-permute-start(bf16[64,2176]{1,0:T(8,128)(2,1)S(1)} %slice.42), channel_id=1, source_target_pairs={{0,2},{1,3},{2,0},{3,1},{4,6},{5,7},{6,4},{7,5},{8,10},{9,11},{10,... | collective-permute-start | bytes 835592 | tf_op jit(solution)/shard_map/ppermute | solution.py:564
  38.7 19.1 %collective-permute-start.11 = (bf16[128,2176]{1,0:T(8,128)(2,1)S(1)}, bf16[128,2176]{1,0:T(8,128)(2,1)}, u32[]{:S(2)}, u32[]{:S(2)}) collective-permute-start(bf16[128,2176]{1,0:T(8,128)(2,1)S(1)} %collective-permute-done.3.a), channel_id=1, source_target_pairs={{0,4},{1,5},{2,6},{3,7},{4,12},{5,13},{6,14},{7,15},{8,0},{9,1},{1... | collective-permute-start | bytes 1671176 | tf_op jit(solution)/shard_map/ppermute | solution.py:564
  40.0 17.8 %collective-permute-start.12 = (bf16[128,2176]{1,0:T(8,128)(2,1)S(1)}, bf16[128,2176]{1,0:T(8,128)(2,1)S(1)}, u32[]{:S(2)}, u32[]{:S(2)}) collective-permute-start(bf16[128,2176]{1,0:T(8,128)(2,1)S(1)} %collective-permute-done.3.a), channel_id=1, source_target_pairs={{0,1},{1,0},{2,3},{3,2},{4,5},{5,4},{6,7},{7,6},{8,9},{9,8},{10,11... | collective-permute-start | bytes 1671176 | tf_op jit(solution)/shard_map/ppermute | solution.py:564
  40.5 17.2 %collective-permute-start.13 = (bf16[128,2176]{1,0:T(8,128)(2,1)S(1)}, bf16[128,2176]{1,0:T(8,128)(2,1)S(1)}, u32[]{:S(2)}, u32[]{:S(2)}) collective-permute-start(bf16[128,2176]{1,0:T(8,128)(2,1)S(1)} %collective-permute-done.3.a), channel_id=1, source_target_pairs={{0,2},{1,3},{2,0},{3,1},{4,6},{5,7},{6,4},{7,5},{8,10},{9,11},{10,... | collective-permute-start | bytes 1671176 | tf_op jit(solution)/shard_map/ppermute | solution.py:564
  41.1 16.7 %collective-permute-start.8 = (bf16[4,96,384]{2,1,0:T(8,128)(2,1)S(1)}, bf16[4,96,384]{2,1,0:T(8,128)(2,1)S(1)}, u32[]{:S(2)}, u32[]{:S(2)}) collective-permute-start(bf16[4,96,384]{2,1,0:T(8,128)(2,1)S(1)} %slice_bitcast_fusion.3), channel_id=1, source_target_pairs={{0,4},{1,5},{2,6},{3,7},{4,12},{5,13},{6,14},{7,15},{8,0},{9,1},{1... | collective-permute-start | bytes 884744 | tf_op jit(solution)/shard_map/ppermute | solution.py:564
  46.7 7.7 %copy-start.28 = (bf16[64,2176]{1,0:T(8,128)(2,1)}, bf16[64,2176]{1,0:T(8,128)(2,1)S(1)}, u32[]{:S(2)}) copy-start(bf16[64,2176]{1,0:T(8,128)(2,1)S(1)} %collective-permute-done.9.low) | copy-start | bytes 835588
  46.7 11.1 %collective-permute-start.10 = (bf16[64,2176]{1,0:T(8,128)(2,1)S(1)}, bf16[64,2176]{1,0:T(8,128)(2,1)S(1)}, u32[]{:S(2)}, u32[]{:S(2)}) collective-permute-start(bf16[64,2176]{1,0:T(8,128)(2,1)S(1)} %slice.43), channel_id=1, source_target_pairs={{0,1},{1,0},{2,3},{3,2},{4,5},{5,4},{6,7},{7,6},{8,9},{9,8},{10,11... | collective-permute-start | bytes 835592 | tf_op jit(solution)/shard_map/ppermute | solution.py:564
  57.8 17.1 %copy-start.20 = (bf16[128,2176]{1,0:T(8,128)(2,1)}, bf16[128,2176]{1,0:T(8,128)(2,1)S(1)}, u32[]{:S(2)}) copy-start(bf16[128,2176]{1,0:T(8,128)(2,1)S(1)} %collective-permute-done.12.x) | copy-start | bytes 1671172
  57.8 17.1 %copy-start.21 = (bf16[128,2176]{1,0:T(8,128)(2,1)}, bf16[128,2176]{1,0:T(8,128)(2,1)S(1)}, u32[]{:S(2)}) copy-start(bf16[128,2176]{1,0:T(8,128)(2,1)S(1)} %collective-permute-done.13.y) | copy-start | bytes 1671172
  57.8 9.8 %collective-permute-start.16 = (bf16[64,2176]{1,0:T(8,128)(2,1)S(1)}, bf16[64,2176]{1,0:T(8,128)(2,1)}, u32[]{:S(2)}, u32[]{:S(2)}) collective-permute-start(bf16[64,2176]{1,0:T(8,128)(2,1)S(1)} %slice.46), channel_id=1, source_target_pairs={{0,2},{1,3},{2,0},{3,1},{4,6},{5,7},{6,4},{7,5},{8,10},{9,11},{10,... | collective-permute-start | bytes 835592 | tf_op jit(solution)/shard_map/ppermute | solution.py:564
  58.5 17.7 %collective-permute-start.18 = (bf16[128,2176]{1,0:T(8,128)(2,1)}, bf16[128,2176]{1,0:T(8,128)(2,1)S(1)}, u32[]{:S(2)}, u32[]{:S(2)}) collective-permute-start(bf16[128,2176]{1,0:T(8,128)(2,1)} %collective-permute-done.11.a), channel_id=1, source_target_pairs={{0,1},{1,0},{2,3},{3,2},{4,5},{5,4},{6,7},{7,6},{8,9},{9,8},{10,11... | collective-permute-start | bytes 1671176 | tf_op jit(solution)/shard_map/ppermute | solution.py:564
  59.0 17.2 %collective-permute-start.19 = (bf16[128,2176]{1,0:T(8,128)(2,1)}, bf16[128,2176]{1,0:T(8,128)(2,1)S(1)}, u32[]{:S(2)}, u32[]{:S(2)}) collective-permute-start(bf16[128,2176]{1,0:T(8,128)(2,1)} %collective-permute-done.11.a), channel_id=1, source_target_pairs={{0,2},{1,3},{2,0},{3,1},{4,6},{5,7},{6,4},{7,5},{8,10},{9,11},{10,... | collective-permute-start | bytes 1671176 | tf_op jit(solution)/shard_map/ppermute | solution.py:564
  61.3 14.8 %collective-permute-start.14 = (bf16[4,96,384]{2,1,0:T(8,128)(2,1)}, bf16[4,96,384]{2,1,0:T(8,128)(2,1)S(1)}, u32[]{:S(2)}, u32[]{:S(2)}) collective-permute-start(bf16[4,96,384]{2,1,0:T(8,128)(2,1)} %get-tuple-element.183), channel_id=1, source_target_pairs={{0,12},{1,13},{2,14},{3,15},{4,8},{5,9},{6,10},{7,11},{8,4},{9,5},... | collective-permute-start | bytes 884744 | tf_op jit(solution)/shard_map/ppermute | solution.py:564
  63.5 12.7 %collective-permute-start.15 = (bf16[4,96,384]{2,1,0:T(8,128)(2,1)}, bf16[4,96,384]{2,1,0:T(8,128)(2,1)S(1)}, u32[]{:S(2)}, u32[]{:S(2)}) collective-permute-start(bf16[4,96,384]{2,1,0:T(8,128)(2,1)} %get-tuple-element.182), channel_id=1, source_target_pairs={{0,8},{1,9},{2,10},{3,11},{4,0},{5,1},{6,2},{7,3},{8,12},{9,13},{1... | collective-permute-start | bytes 884744 | tf_op jit(solution)/shard_map/ppermute | solution.py:564
  67.6 8.6 %collective-permute-start.17 = (bf16[64,2176]{1,0:T(8,128)(2,1)}, bf16[64,2176]{1,0:T(8,128)(2,1)}, u32[]{:S(2)}, u32[]{:S(2)}) collective-permute-start(bf16[64,2176]{1,0:T(8,128)(2,1)} %slice.47), channel_id=1, source_target_pairs={{0,1},{1,0},{2,3},{3,2},{4,5},{5,4},{6,7},{7,6},{8,9},{9,8},{10,11... | collective-permute-start | bytes 835592 | tf_op jit(solution)/shard_map/ppermute | solution.py:564
  74.9 7.3 %copy-start.35 = (bf16[64,2176]{1,0:T(8,128)(2,1)S(1)}, bf16[64,2176]{1,0:T(8,128)(2,1)}, u32[]{:S(2)}) copy-start(bf16[64,2176]{1,0:T(8,128)(2,1)} %slice.39) | copy-start | bytes 835588
  74.9 8.6 %copy-start.34 = (bf16[64,2176]{1,0:T(8,128)(2,1)S(1)}, bf16[64,2176]{1,0:T(8,128)(2,1)}, u32[]{:S(2)}) copy-start(bf16[64,2176]{1,0:T(8,128)(2,1)} %slice.40) | copy-start | bytes 835588
  76.2 14.5 %copy-start.22 = (bf16[128,2176]{1,0:T(8,128)(2,1)}, bf16[128,2176]{1,0:T(8,128)(2,1)S(1)}, u32[]{:S(2)}) copy-start(bf16[128,2176]{1,0:T(8,128)(2,1)S(1)} %collective-permute-done.18.x) | copy-start | bytes 1671172
  76.2 14.4 %collective-permute-start.22 = (bf16[64,2176]{1,0:T(8,128)(2,1)S(1)}, bf16[64,2176]{1,0:T(8,128)(2,1)S(1)}, u32[]{:S(2)}, u32[]{:S(2)}) collective-permute-start(bf16[64,2176]{1,0:T(8,128)(2,1)S(1)} %slice.49), channel_id=1, source_target_pairs={{0,2},{1,3},{2,0},{3,1},{4,6},{5,7},{6,4},{7,5},{8,10},{9,11},{10,... | collective-permute-start | bytes 835592 | tf_op jit(solution)/shard_map/ppermute | solution.py:564
  77.0 17.4 %collective-permute-start.23 = (bf16[64,2176]{1,0:T(8,128)(2,1)S(1)}, bf16[64,2176]{1,0:T(8,128)(2,1)S(1)}, u32[]{:S(2)}, u32[]{:S(2)}) collective-permute-start(bf16[64,2176]{1,0:T(8,128)(2,1)S(1)} %slice.50), channel_id=1, source_target_pairs={{0,1},{1,0},{2,3},{3,2},{4,5},{5,4},{6,7},{7,6},{8,9},{9,8},{10,11... | collective-permute-start | bytes 835592 | tf_op jit(solution)/shard_map/ppermute | solution.py:564
  80.4 26.8 %collective-permute-start.25 = (bf16[4,96,384]{2,1,0:T(8,128)(2,1)S(1)}, bf16[4,96,384]{2,1,0:T(8,128)(2,1)S(1)}, u32[]{:S(2)}, u32[]{:S(2)}) collective-permute-start(bf16[4,96,384]{2,1,0:T(8,128)(2,1)S(1)} %get-tuple-element.123), channel_id=1, source_target_pairs={{0,1},{1,0},{2,3},{3,2},{4,5},{5,4},{6,7},{7,6},{8,9},{9,8},{10,11... | collective-permute-start | bytes 884744 | tf_op jit(solution)/shard_map/ppermute | solution.py:564
  82.2 20.0 %collective-permute-start.6 = (bf16[64,2176]{1,0:T(8,128)(2,1)S(1)}, bf16[64,2176]{1,0:T(8,128)(2,1)S(1)}, u32[]{:S(2)}, u32[]{:S(2)}) collective-permute-start(bf16[64,2176]{1,0:T(8,128)(2,1)S(1)} %copy-done.35), channel_id=1, source_target_pairs={{0,2},{1,3},{2,0},{3,1},{4,6},{5,7},{6,4},{7,5},{8,10},{9,11},{10,... | collective-permute-start | bytes 835592 | tf_op jit(solution)/shard_map/ppermute | solution.py:564
  83.6 20.9 %collective-permute-start.7 = (bf16[64,2176]{1,0:T(8,128)(2,1)S(1)}, bf16[64,2176]{1,0:T(8,128)(2,1)S(1)}, u32[]{:S(2)}, u32[]{:S(2)}) collective-permute-start(bf16[64,2176]{1,0:T(8,128)(2,1)S(1)} %copy-done.34), channel_id=1, source_target_pairs={{0,1},{1,0},{2,3},{3,2},{4,5},{5,4},{6,7},{7,6},{8,9},{9,8},{10,11... | collective-permute-start | bytes 835592 | tf_op jit(solution)/shard_map/ppermute | solution.py:564
  90.7 4.6 %copy-start.32 = (bf16[64,2176]{1,0:T(8,128)(2,1)}, bf16[64,2176]{1,0:T(8,128)(2,1)S(1)}, u32[]{:S(2)}) copy-start(bf16[64,2176]{1,0:T(8,128)(2,1)S(1)} %collective-permute-done.22.low) | copy-start | bytes 835588
  90.7 27.4 %collective-permute-start.20 = (bf16[4,96,384]{2,1,0:T(8,128)(2,1)}, bf16[4,96,384]{2,1,0:T(8,128)(2,1)}, u32[]{:S(2)}, u32[]{:S(2)}) collective-permute-start(bf16[4,96,384]{2,1,0:T(8,128)(2,1)} %get-tuple-element.118), channel_id=1, source_target_pairs={{0,8},{1,9},{2,10},{3,11},{4,0},{5,1},{6,2},{7,3},{8,12},{9,13},{1... | collective-permute-start | bytes 884744 | tf_op jit(solution)/shard_map/ppermute | solution.py:564
  94.4 20.7 %collective-permute-start.26 = (bf16[4,96,384]{2,1,0:T(8,128)(2,1)}, bf16[4,96,384]{2,1,0:T(8,128)(2,1)}, u32[]{:S(2)}, u32[]{:S(2)}) collective-permute-start(bf16[4,96,384]{2,1,0:T(8,128)(2,1)} %get-tuple-element.124), channel_id=1, source_target_pairs={{0,2},{1,3},{2,0},{3,1},{4,6},{5,7},{6,4},{7,5},{8,10},{9,11},{10,... | collective-permute-start | bytes 884744 | tf_op jit(solution)/shard_map/ppermute | solution.py:564
  95.3 50.4 %slice-start.2 = ((s8[6291456]{0:T(1024)(128)(4,1)}), s8[2097152]{0:T(1024)(128)(4,1)S(1)}, s32[]{:S(2)}) async-start(s8[6291456]{0:T(1024)(128)(4,1)} %bitcast.67), calls=%async_computation.2 | async-start | bytes 4194304
  102.2 4.9 %copy-start.29 = (bf16[64,2176]{1,0:T(8,128)(2,1)}, bf16[64,2176]{1,0:T(8,128)(2,1)S(1)}, u32[]{:S(2)}) copy-start(bf16[64,2176]{1,0:T(8,128)(2,1)S(1)} %collective-permute-done.6.low) | copy-start | bytes 835588
  102.2 12.9 %collective-permute-start.27 = (bf16[4,96,384]{2,1,0:T(8,128)(2,1)}, bf16[4,96,384]{2,1,0:T(8,128)(2,1)}, u32[]{:S(2)}, u32[]{:S(2)}) collective-permute-start(bf16[4,96,384]{2,1,0:T(8,128)(2,1)} %get-tuple-element.125), channel_id=1, source_target_pairs={{0,3},{1,2},{2,1},{3,0},{4,7},{5,6},{6,5},{7,4},{8,11},{9,10},{10,... | collective-permute-start | bytes 884744 | tf_op jit(solution)/shard_map/ppermute | solution.py:564
  104.5 3.4 %copy-start.30 = (bf16[64,2176]{1,0:T(8,128)(2,1)}, bf16[64,2176]{1,0:T(8,128)(2,1)S(1)}, u32[]{:S(2)}) copy-start(bf16[64,2176]{1,0:T(8,128)(2,1)S(1)} %collective-permute-done.7.high) | copy-start | bytes 835588
  104.5 13.6 %collective-permute-start.21 = (bf16[4,96,384]{2,1,0:T(8,128)(2,1)}, bf16[4,96,384]{2,1,0:T(8,128)(2,1)}, u32[]{:S(2)}, u32[]{:S(2)}) collective-permute-start(bf16[4,96,384]{2,1,0:T(8,128)(2,1)} %get-tuple-element.119), channel_id=1, source_target_pairs={{0,12},{1,13},{2,14},{3,15},{4,8},{5,9},{6,10},{7,11},{8,4},{9,5},... | collective-permute-start | bytes 884744 | tf_op jit(solution)/shard_map/ppermute | solution.py:564
  107.9 15.8 %collective-permute-start.24 = (bf16[4,96,384]{2,1,0:T(8,128)(2,1)}, bf16[4,96,384]{2,1,0:T(8,128)(2,1)}, u32[]{:S(2)}, u32[]{:S(2)}) collective-permute-start(bf16[4,96,384]{2,1,0:T(8,128)(2,1)} %get-tuple-element.122), channel_id=1, source_target_pairs={{0,4},{1,5},{2,6},{3,7},{4,12},{5,13},{6,14},{7,15},{8,0},{9,1},{1... | collective-permute-start | bytes 884744 | tf_op jit(solution)/shard_map/ppermute | solution.py:564
  107.9 7.3 %copy-start.2 = (bf16[4,96,384]{2,1,0:T(8,128)(2,1)S(1)}, bf16[4,96,384]{2,1,0:T(8,128)(2,1)}, u32[]{:S(2)}) copy-start(bf16[4,96,384]{2,1,0:T(8,128)(2,1)} %copy-done.1) | copy-start | bytes 884740
  107.9 37.8 %slice-start.3 = ((s8[6291456]{0:T(1024)(128)(4,1)}), s8[4194304]{0:T(1024)(128)(4,1)S(1)}, s32[]{:S(2)}) async-start(s8[6291456]{0:T(1024)(128)(4,1)} %bitcast.67), calls=%async_computation.3 | async-start | bytes 8388608
  115.1 8.6 %copy-start.3 = (bf16[4,96,384]{2,1,0:T(8,128)(2,1)S(1)}, bf16[4,96,384]{2,1,0:T(8,128)(2,1)}, u32[]{:S(2)}) copy-start(bf16[4,96,384]{2,1,0:T(8,128)(2,1)} %get-tuple-element.98.refs_0_) | copy-start | bytes 884740
  115.1 10.1 %copy-start.5 = (bf16[384,2048]{1,0:T(8,128)(2,1)S(1)}, bf16[384,2048]{1,0:T(8,128)(2,1)}, u32[]{:S(2)}) copy-start(bf16[384,2048]{1,0:T(8,128)(2,1)} %get-tuple-element.134.refs_1_) | copy-start | bytes 4718596
  115.1 10.1 %copy-start.6 = (bf16[384,2048]{1,0:T(8,128)(2,1)S(1)}, bf16[384,2048]{1,0:T(8,128)(2,1)}, u32[]{:S(2)}) copy-start(bf16[384,2048]{1,0:T(8,128)(2,1)} %get-tuple-element.135.refs_2_) | copy-start | bytes 4718596
  115.2 30.5 %slice-start = ((s8[6291456]{0:T(1024)(128)(4,1)}), s8[4194304]{0:T(1024)(128)(4,1)S(1)}, s32[]{:S(2)}) async-start(s8[6291456]{0:T(1024)(128)(4,1)} %bitcast.63), calls=%async_computation | async-start | bytes 8388608
  128.1 17.6 %slice-start.1 = ((s8[6291456]{0:T(1024)(128)(4,1)}), s8[2097152]{0:T(1024)(128)(4,1)S(1)}, s32[]{:S(2)}) async-start(s8[6291456]{0:T(1024)(128)(4,1)} %bitcast.63), calls=%async_computation.1 | async-start | bytes 4194304
  136.5 5.7 %collective-permute-start.28 = (bf16[4,192,2048]{2,1,0:T(8,128)(2,1)S(1)}, bf16[4,192,2048]{2,1,0:T(8,128)(2,1)S(1)}, u32[]{:S(2)}, u32[]{:S(2)}) collective-permute-start(bf16[4,192,2048]{2,1,0:T(8,128)(2,1)S(1)} %get-tuple-element.138), channel_id=1, source_target_pairs={{0,16},{16,0},{1,17},{17,1},{2,18},{18,2},{3,19},{19,3},{4,20},{20... | collective-permute-start | bytes 9437192 | tf_op jit(solution)/shard_map/ppermute | solution.py:651
  142.2 13.7 %collective-permute-start.29 = (bf16[4,96,384]{2,1,0:T(8,128)(2,1)S(1)}, bf16[4,96,384]{2,1,0:T(8,128)(2,1)S(1)}, u32[]{:S(2)}, u32[]{:S(2)}) collective-permute-start(bf16[4,96,384]{2,1,0:T(8,128)(2,1)S(1)} %get-tuple-element.144), channel_id=1, source_target_pairs={{0,1},{1,0},{2,3},{3,2},{4,5},{5,4},{6,7},{7,6},{8,9},{9,8},{10,11... | collective-permute-start | bytes 884744 | tf_op jit(solution)/shard_map/ppermute | solution.py:564
  142.6 14.1 %collective-permute-start.30 = (bf16[4,96,384]{2,1,0:T(8,128)(2,1)S(1)}, bf16[4,96,384]{2,1,0:T(8,128)(2,1)S(1)}, u32[]{:S(2)}, u32[]{:S(2)}) collective-permute-start(bf16[4,96,384]{2,1,0:T(8,128)(2,1)S(1)} %get-tuple-element.145), channel_id=1, source_target_pairs={{0,2},{1,3},{2,0},{3,1},{4,6},{5,7},{6,4},{7,5},{8,10},{9,11},{10,... | collective-permute-start | bytes 884744 | tf_op jit(solution)/shard_map/ppermute | solution.py:564
  143.5 14.4 %collective-permute-start.31 = (bf16[4,96,384]{2,1,0:T(8,128)(2,1)S(1)}, bf16[4,96,384]{2,1,0:T(8,128)(2,1)S(1)}, u32[]{:S(2)}, u32[]{:S(2)}) collective-permute-start(bf16[4,96,384]{2,1,0:T(8,128)(2,1)S(1)} %get-tuple-element.146), channel_id=1, source_target_pairs={{0,3},{1,2},{2,1},{3,0},{4,7},{5,6},{6,5},{7,4},{8,11},{9,10},{10,... | collective-permute-start | bytes 884744 | tf_op jit(solution)/shard_map/ppermute | solution.py:564
  155.9 19.1 %collective-permute-start.32 = (bf16[6144,128]{1,0:T(8,128)(2,1)}, bf16[6144,128]{1,0:T(8,128)(2,1)}, u32[]{:S(2)}, u32[]{:S(2)}) collective-permute-start(bf16[6144,128]{1,0:T(8,128)(2,1)} %get-tuple-element.161), channel_id=1, source_target_pairs={{0,16},{16,0},{1,17},{17,1},{2,18},{18,2},{3,19},{19,3},{4,20},{20... | collective-permute-start | bytes 4718600 | tf_op jit(solution)/shard_map/ppermute | solution.py:669
  158.6 7.4 %copy-start.4 = (bf16[4,96,384]{2,1,0:T(8,128)(2,1)S(1)}, bf16[4,96,384]{2,1,0:T(8,128)(2,1)}, u32[]{:S(2)}) copy-start(bf16[4,96,384]{2,1,0:T(8,128)(2,1)} %get-tuple-element.98.refs_0_) | copy-start | bytes 884740
  158.6 7.4 %copy-start.10 = (bf16[128,8,384]{2,1,0:T(8,128)(2,1)S(1)}, bf16[128,8,384]{2,1,0:T(8,128)(2,1)}, u32[]{:S(2)}) copy-start(bf16[128,8,384]{2,1,0:T(8,128)(2,1)} %param.9) | copy-start | bytes 2359300
  166.1 9.0 %collective-permute-start.33 = (bf16[6144,128]{1,0:T(8,128)(2,1)}, bf16[6144,128]{1,0:T(8,128)(2,1)S(1)}, u32[]{:S(2)}, u32[]{:S(2)}) collective-permute-start(bf16[6144,128]{1,0:T(8,128)(2,1)} %get-tuple-element.162), channel_id=1, source_target_pairs={{0,16},{16,0},{1,17},{17,1},{2,18},{18,2},{3,19},{19,3},{4,20},{20... | collective-permute-start | bytes 4718600 | tf_op jit(solution)/shard_map/ppermute | solution.py:669
  (13 other events, 13.8 us)

commit v4 on v3

--- a/solution.py
+++ b/solution.py
@@ -74,109 +74,125 @@
     return (at[:, None] * 4 + (me % 4 ^ flips)[None, :]).reshape(size)
 
 
-def grads_kernel(first, a, x, y, low, high, by_expert, d_out, g_out, *scratch):
-    rows, match, d_rows, grads, weights, sems = scratch
+def grads_kernel(spans, first, *refs):
+    chunks = len(spans)
+    parts = [
+        [ref.at[pl.ds(*span)] for ref, span in zip(refs[5 * j :], spans[j])]
+        for j in range(chunks)
+    ]
+    by_expert, outs = refs[5 * chunks], refs[5 * chunks + 1 : 7 * chunks + 1]
+    all_rows, match, all_d_rows, all_grads, weights, sems, weight_sems = refs[-7:]
     experts, width, features = by_expert.shape
-    tokens = rows.shape[0] // 4
+    tokens = all_rows.shape[1] // 4
     slots = experts * CAP
-    pieces = (a, x, y, low, high)
-    loads, at = [], 0
-    for i, piece in enumerate(pieces):
-        place = rows.at[pl.ds(at, piece.shape[0])]
-        loads.append(pltpu.make_async_copy(piece, place, sems.at[i]))
-        loads[-1].start()
-        at += piece.shape[0]
-    for load in loads:
-        load.wait()
-    loads = [
-        pltpu.make_async_copy(by_expert.at[e], weights.at[e], sems.at[7 + e])
+    loads = []
+    for j, pieces in enumerate(parts):
+        at = 0
+        loads.append([])
+        for i, piece in enumerate(pieces):
+            place = all_rows.at[j, pl.ds(at, piece.shape[0])]
+            loads[j].append(pltpu.make_async_copy(piece, place, sems.at[j, i]))
+            loads[j][i].start()
+            at += piece.shape[0]
+    weight_loads = [
+        pltpu.make_async_copy(by_expert.at[e], weights.at[e], weight_sems.at[e])
         for e in range(experts)
     ]
-    for load in loads:
-        load.start()
 
     slot = lax.broadcasted_iota(jnp.int32, (slots, tokens), 0)
-    expert = first[0] + slot // CAP
+    expert = (first[0] + slot // CAP).astype(jnp.float32)
     place = (slot % CAP).astype(jnp.float32)
-    expert = expert.astype(jnp.float32)
     earlier = lax.broadcasted_iota(jnp.int32, (tokens, tokens), 0)
     earlier = earlier < lax.broadcasted_iota(jnp.int32, (tokens, tokens), 1)
     earlier = jnp.where(earlier, 1.0, 0.0).astype(jnp.bfloat16)
-    hits = []
-    for c in range(4):
-        ids = rows[c * tokens : (c + 1) * tokens, features:].astype(jnp.float32).T
-        named = jnp.zeros((slots, tokens), jnp.float32)
-        for k in range(TOP):
-            named = jnp.where(expert == ids[k : k + 1], 1.0, named)
-        rank = jnp.dot(
-            named.astype(jnp.bfloat16), earlier, preferred_element_type=jnp.float32
-        )
-        hits.append(jnp.where(rank == place, named, 0.0))
-    blank = jnp.zeros((CAP, tokens), jnp.float32)
-    lines = []
-    for e in range(experts):
+    stores = []
+    for j in range(chunks):
+        rows, d_rows, grads = all_rows.at[j], all_d_rows.at[j], all_grads.at[j]
+        for load in loads[j]:
+            load.wait()
+        if j == 0:
+            for load in weight_loads:
+                load.start()
+        hits = []
         for c in range(4):
-            line = [blank] * 4
-            line[c] = hits[c][e * CAP : (e + 1) * CAP]
-            lines.append(jnp.concatenate(line, axis=1))
-    match[...] = jnp.concatenate(lines, axis=0).astype(jnp.bfloat16)
-
-    step = min(512, features)
-    for at in range(0, features, step):
-        d_rows[:, at : at + step] = jnp.dot(
-            match[...], rows[:, at : at + step], preferred_element_type=jnp.float32
-        ).astype(jnp.bfloat16)
-    stores = [pltpu.make_async_copy(d_rows, d_out, sems.at[5])]
-    stores[0].start()
-    count = 4 * CAP
-    found = []
-    for e in range(experts):
-        loads[e].wait()
-        found.append(
-            lax.dot_general(
-                d_rows[e * count : (e + 1) * count],
-                weights[e],
-                (((1,), (1,)), ((), ())),
-                preferred_element_type=jnp.float32,
+            ids = rows[c * tokens : (c + 1) * tokens, features:].astype(jnp.float32).T
+            named = jnp.zeros((slots, tokens), jnp.float32)
+            for k in range(TOP):
+                named = jnp.where(expert == ids[k : k + 1], 1.0, named)
+            rank = jnp.dot(
+                named.astype(jnp.bfloat16), earlier, preferred_element_type=jnp.float32
             )
-        )
-    for c in range(4):
-        mine = [f[c * CAP : (c + 1) * CAP] for f in found]
-        grads[c] = jnp.concatenate(mine, axis=0).astype(jnp.bfloat16)
-    stores.append(pltpu.make_async_copy(grads, g_out, sems.at[6]))
-    stores[1].start()
+            hits.append(jnp.where(rank == place, named, 0.0))
+        blank = jnp.zeros((CAP, tokens), jnp.float32)
+        lines = []
+        for e in range(experts):
+            for c in range(4):
+                line = [blank] * 4
+                line[c] = hits[c][e * CAP : (e + 1) * CAP]
+                lines.append(jnp.concatenate(line, axis=1))
+        match[...] = jnp.concatenate(lines, axis=0).astype(jnp.bfloat16)
+
+        step = min(512, features)
+        for at in range(0, features, step):
+            d_rows[:, at : at + step] = jnp.dot(
+                match[...], rows[:, at : at + step], preferred_element_type=jnp.float32
+            ).astype(jnp.bfloat16)
+        stores.append(pltpu.make_async_copy(d_rows, outs[2 * j], sems.at[j, 5]))
+        stores[-1].start()
+        count = 4 * CAP
+        found = []
+        for e in range(experts):
+            if j == 0:
+                weight_loads[e].wait()
+            found.append(
+                lax.dot_general(
+                    d_rows[e * count : (e + 1) * count, :],
+                    weights[e],
+                    (((1,), (1,)), ((), ())),
+                    preferred_element_type=jnp.float32,
+                )
+            )
+        for c in range(4):
+            mine = [f[c * CAP : (c + 1) * CAP] for f in found]
+            grads[c] = jnp.concatenate(mine, axis=0).astype(jnp.bfloat16)
+        stores.append(pltpu.make_async_copy(grads, outs[2 * j + 1], sems.at[j, 6]))
+        stores[-1].start()
     for store in stores:
         store.wait()
 
 
-def chunk_grads(first, part, by_expert):
+def chunk_grads(first, parts, by_expert):
     experts, width, features = by_expert.shape
-    tokens, columns = part[0].shape
+    tokens, columns = parts[0][0][0].shape
+    spans = tuple(tuple(piece[1:] for piece in part) for part in parts)
     slots = experts * CAP
-    return pl.pallas_call(
-        grads_kernel,
-        out_shape=(
+    chunks = len(parts)
+    found = pl.pallas_call(
+        functools.partial(grads_kernel, spans),
+        out_shape=[
             jax.ShapeDtypeStruct((4 * slots, features), jnp.bfloat16),
             jax.ShapeDtypeStruct((4, slots, width), jnp.bfloat16),
-        ),
-        in_specs=[pl.BlockSpec(memory_space=pltpu.SMEM)]
-        + [HBM] * 6,
-        out_specs=(HBM, HBM),
+        ]
+        * chunks,
+        in_specs=[pl.BlockSpec(memory_space=pltpu.SMEM)] + [HBM] * (5 * chunks + 1),
+        out_specs=[HBM] * (2 * chunks),
         scratch_shapes=[
-            pltpu.VMEM((4 * tokens, columns), jnp.bfloat16),
+            pltpu.VMEM((chunks, 4 * tokens, columns), jnp.bfloat16),
             pltpu.VMEM((4 * slots, 4 * tokens), jnp.bfloat16),
-            pltpu.VMEM((4 * slots, features), jnp.bfloat16),
-            pltpu.VMEM((4, slots, width), jnp.bfloat16),
+            pltpu.VMEM((chunks, 4 * slots, features), jnp.bfloat16),
+            pltpu.VMEM((chunks, 4, slots, width), jnp.bfloat16),
             pltpu.VMEM(by_expert.shape, jnp.bfloat16),
-            pltpu.SemaphoreType.DMA((7 + experts,)),
+            pltpu.SemaphoreType.DMA((chunks, 7)),
+            pltpu.SemaphoreType.DMA((experts,)),
         ],
         compiler_params=pltpu.CompilerParams(vmem_limit_bytes=56 * MIB),
         cost_estimate=pl.CostEstimate(
-            flops=8 * slots * features * (4 * tokens + width),
-            bytes_accessed=8 * (slots + tokens) * features,
+            flops=8 * chunks * slots * features * (4 * tokens + width),
+            bytes_accessed=8 * chunks * (slots + tokens) * features,
             transcendentals=0,
         ),
-    )(first, *part, by_expert)
+    )(first, *(piece[0] for part in parts for piece in part), by_expert)
+    return found[::2], found[1::2]
 
 
 def order_kernel(pieces, *refs):
@@ -262,17 +278,17 @@
     )(*arrays)
 
 
-def partial_kernel(owners, weighted, *refs):
+def partial_kernel(start, total, owners, weighted, *refs):
     count = owners.shape[0]
     blocks, outs = refs[: -4 - count], refs[-4 - count : -4]
     w_in, rows, sums, sems = refs[-4:]
     experts, width, features = sums.shape
     share = width // count
-    slots = blocks[0].shape[0] // experts
+    slots = blocks[0].shape[0] // total
     loads = []
     for e in range(experts):
-        mine = [(weighted.at[e], w_in.at[e])] + [
-            (block.at[pl.ds(e * slots, slots)], rows.at[e, pl.ds(k * slots, slots)])
+        mine = [(weighted.at[start + e], w_in.at[e])] + [
+            (block.at[pl.ds((start + e) * slots, slots)], rows.at[e, pl.ds(k * slots, slots)])
             for k, block in enumerate(blocks)
         ]
         loads.append(
@@ -306,12 +322,13 @@
         store.wait()
 
 
-def partial_rows(owners, weighted, blocks):
-    experts, width, slots = weighted.shape
+def partial_rows(owners, weighted, blocks, start, stop):
+    total, width, slots = weighted.shape
+    experts = stop - start
     features = blocks[0].shape[1]
     count = owners.shape[0]
     return pl.pallas_call(
-        partial_kernel,
+        functools.partial(partial_kernel, start, total),
         out_shape=[jax.ShapeDtypeStruct((experts, width // count, features), jnp.bfloat16)]
         * count,
         in_specs=[pl.BlockSpec(memory_space=pltpu.SMEM)] + [HBM] * (1 + len(blocks)),
@@ -322,7 +339,7 @@
             pltpu.VMEM((experts, width, features), jnp.bfloat16),
             pltpu.SemaphoreType.DMA((experts, 1 + len(blocks) + count)),
         ],
-        compiler_params=pltpu.CompilerParams(vmem_limit_bytes=30 * MIB),
+        compiler_params=pltpu.CompilerParams(vmem_limit_bytes=16 * MIB),
         cost_estimate=pl.CostEstimate(
             flops=2 * experts * width * slots * features,
             bytes_accessed=2 * experts * (width + slots) * features,
@@ -342,16 +359,19 @@
     return estimate * (2.0 - x * estimate)
 
 
-def adam_kernel(count, kept, first, at, *refs):
+def adam_kernel(count, owners, kept, first, at, *refs):
     del at
     partials, (w, m1, m2) = refs[:count], refs[count : count + 3]
+    partials = [partials[i : i + owners] for i in range(0, count, owners)]
     new_w, new_m1, new_m2, full, copy, grad = refs[count + 3 + kept :]
-    experts, rows, features = partials[0].shape
+    _, rows, features = partials[0][0].shape
     tiles = features // LANES
-    for e in range(experts):
-        total = partials[0][e].astype(jnp.float32)
-        for part in partials[1:]:
-            total = total + part[e].astype(jnp.float32)
+    places = [(span, e) for span in partials for e in range(span[0].shape[0])]
+    experts = len(places)
+    for e, (span, at) in enumerate(places):
+        total = span[0][at].astype(jnp.float32)
+        for part in span[1:]:
+            total = total + part[at].astype(jnp.float32)
         for t in range(tiles):
             grad[pl.ds(t * experts + e, rows, stride=tiles * experts), :] = total[
                 :, t * LANES : (t + 1) * LANES
@@ -375,20 +395,26 @@
 
 
 def adam_rows(at, partials, w, m1, m2, total_rows, before, first, steps):
-    experts, rows, features = partials[0].shape
+    owners = len(partials[0])
+    partials = [part for span in partials for part in span]
+    _, rows, features = partials[0].shape
+    experts = sum(part.shape[0] for part in partials) // owners
     block = 16
     flat = block * experts * features // LANES
     count, kept = len(partials), len(before)
     whole = rows // block
-    part = pl.BlockSpec((experts, block, features), lambda i, at: (0, first + i, 0))
+    parts = [
+        pl.BlockSpec((part.shape[0], block, features), lambda i, at: (0, first + i, 0))
+        for part in partials
+    ]
     line = pl.BlockSpec((flat, LANES), lambda i, at: (first + i, 0))
     placed = pl.BlockSpec((flat, LANES), lambda i, at: (at[0] * whole + first + i, 0))
     return pl.pallas_call(
-        functools.partial(adam_kernel, count, kept, first),
+        functools.partial(adam_kernel, count, owners, kept, first),
         grid_spec=pltpu.PrefetchScalarGridSpec(
             num_scalar_prefetch=1,
             grid=(steps,),
-            in_specs=[part] * count + [INSIDE] * 3 + [HBM] * kept,
+            in_specs=parts + [INSIDE] * 3 + [HBM] * kept,
             out_specs=[line] * 3 + [placed, pl.BlockSpec((flat, LANES), lambda i, at: (i, 0))],
             scratch_shapes=[pltpu.VMEM((flat, LANES), jnp.float32)],
         ),
@@ -422,6 +448,7 @@
 
 def place_rows(owner, low, high, full):
     block = math.gcd(low.shape[0], high.shape[0])
+    block = block // 3 if block % 3 == 0 else block
     cut = low.shape[0] // block
     steps = cut + high.shape[0] // block
     shape = (block, LANES)
@@ -509,7 +536,7 @@
             pltpu.VMEM((8, choices), jnp.float32),
             pltpu.SemaphoreType.DMA((len(pieces) + 1 + steps,)),
         ],
-        compiler_params=pltpu.CompilerParams(vmem_limit_bytes=12 * MIB),
+        compiler_params=pltpu.CompilerParams(vmem_limit_bytes=56 * MIB),
         cost_estimate=pl.CostEstimate(
             flops=2 * choices * slots * width, bytes_accessed=8 * hidden.size, transcendentals=0
         ),
@@ -573,11 +600,16 @@
     near, parts, w_parts = {}, {}, {}
     d_rows, grads, back = {}, {}, {}
 
-    def add_chunk(j):
-        d_rows[j], grads[j] = chunk_grads(first, parts[j], by_expert)
+    def add_chunks(*chunks):
+        found = chunk_grads(first, [parts[j] for j in chunks], by_expert)
+        for j, d_chunk, g_chunk in zip(chunks, *found):
+            d_rows[j], grads[j] = d_chunk, g_chunk
 
     def flips(arrays):
         return [move(a, 0, c) for c, a in enumerate(arrays, 1)]
+
+    def whole(*arrays):
+        return tuple((a, 0, a.shape[0]) for a in arrays)
 
     def halves(j):
         _, by_x, by_y = near[j]
@@ -593,12 +625,16 @@
         if k < length:
             moving["x"] = move(own, 0, 1)
             moving["y"] = move(own, 0, 2)
-        if k > 1:
+        if 1 < k < length:
             moving["far"] = far(*halves(k - 1))
         if k == length:
-            moving["first"] = far(*first_cut)
+            both = zip(halves(last), first_cut)
+            moving["far"] = far(*(jnp.concatenate(pair) for pair in both))
+            for j in range(1, last - 1):
+                back[j] = move(grads[j], -j, 0)
+            moving["back"] = back
         if k > 2:
-            add_chunk(k - 2)
+            add_chunks(k - 2)
         if k == 0:
             moving["columns"] = columns
         if k == 1:
@@ -610,9 +646,6 @@
             for j in range(last, 1, -1):
                 w_parts[j] = move(w_send[j], j, 0)
         moving["done"] = (d_rows, grads, w_parts, w_send)
-        if k == length:
-            last_far = moving.pop("far")
-            first_far = moving.pop("first")
         moved = tie(moving)
         d_rows, grads, w_parts, w_send = moved["done"]
         if k == 0:
@@ -626,31 +659,36 @@
             w_arrays = [w_parts[j] for j in range(length)]
             w_flipped = flips(regroup(w_arrays))
         if 1 < k < length:
-            parts[k - 1] = near[k - 1] + moved["far"]
+            parts[k - 1] = whole(*near[k - 1]) + whole(*moved["far"])
         if k < length:
             near[k] = (own, moved["x"], moved["y"])
         own = moved.get("own")
-    parts[last] = near[last] + last_far
-    parts[0] = near[0] + first_far
-    for j in range(1, last):
-        back[j] = move(grads[j], -j, 0)
-    add_chunk(last)
+    back = moved["back"]
+    back[last - 1] = move(grads[last - 1], 1 - last, 0)
+    parts[last] = whole(*near[last]) + tuple((f, 0, half) for f in moved["far"])
+    parts[0] = whole(*near[0]) + tuple((f, half, half) for f in moved["far"])
+    add_chunks(last, 0)
     back[last] = move(grads[last], -last, 0)
-    add_chunk(0)
     back[0] = grads[0]
     back = [back[j] for j in range(length)]
     pieces = tuple((k, 0) if c == 0 else (length + c - 1, k) for k in range(length) for c in range(4))
     w_slots = order_slots(w_arrays + w_flipped, pieces)
-    d_rows, leaving = tie(([d_rows[j] for j in range(length)], regroup(back)))
+    d_rows = [d_rows[j] for j in range(length)]
+
     def outer_perm(steps):
         return [(i, (i + steps) % outer_size) for i in range(outer_size)]
 
     owners = (outer_at + jnp.arange(outer_size, dtype=jnp.int32)) % outer_size
-    mine, *sent = partial_rows(owners, w_slots, d_rows)
-    partials = [mine] + [
-        lax.ppermute(part, "outer", outer_perm(r)) for r, part in enumerate(sent, 1)
-    ]
-    partials, leaving = tie((partials, leaving))
+    partials = []
+    for start, stop in ((0, experts // 2), (experts // 2, experts)):
+        if start:
+            d_rows, back = tie((d_rows, back))
+        mine, *sent = partial_rows(owners, w_slots, d_rows, start, stop)
+        partials.append(
+            [mine]
+            + [lax.ppermute(part, "outer", outer_perm(r)) for r, part in enumerate(sent, 1)]
+        )
+    partials, leaving = tie((partials, regroup(back)))
     flipped = flips(leaving)
 
     at = outer_at.astype(jnp.int32)[None]

time: 179 us -> 160 us (0.89)
  local copies, waits for them, and re-layouts: 24.5 us -> 16.7 us
  waiting for transfers between devices: 42.2 us -> 36.7 us
  Pallas kernels: 65.8 us -> 62.1 us
  starting transfers between devices: 40.1 us -> 37.4 us
    unnamed x90 -> x80, local copies, waits for them, and re-layouts: 19.8 us -> 13.7 us
    ppermute x1 -> x2, waiting for transfers between devices: 5.65 us -> 1.71 us  [local(): lax.ppermute(part, 'outer', outer_perm(r))]
    pallas_call x7, Pallas kernels: 50.9 us -> 47.3 us  [the longest x3 23.3 us: chunk_grads(): pl.pallas_call(functools.partial(grads_kernel, spans), out_shape=[jax.Sha...]
    ppermute x31 -> x29, starting transfers between devices: 40 us -> 36.7 us  [move(): return lax.ppermute(block, 'inner', step_perm(size, steps, flip))]
    slice x8 -> x10, local copies, waits for them, and re-layouts: 2.3 us -> 0.13 us  [halves(): return (by_x[:half], by_y[half:])]
    ppermute x31 -> x29, waiting for transfers between devices: 36.6 us -> 35 us  [move(): return lax.ppermute(block, 'inner', step_perm(size, steps, flip))]
  transfers between devices with their start and end apart: 34 -> 33, of which waited for: 13 -> 12; matrix products, arithmetic and copies ran while one was open for 8% -> 9% of each run, Pallas kernels for 30% -> 37%
where the time goes in v4:
time: 160 us; the launch traced here: 159 us
  Pallas kernels  62.1 us (39%)
  starting transfers between devices  37.4 us (23%)
  waiting for transfers between devices  36.7 us (23%)
  local copies, waits for them, and re-layouts  16.7 us (10%)
  other arithmetic  2.77 us (2%)
  matrix products  2.23 us (1%)
    ppermute x29, starting transfers between devices, move(): return lax.ppermute(block, 'inner', step_perm(size, steps, flip))  36.7 us
    ppermute x29, waiting for transfers between devices, move(): return lax.ppermute(block, 'inner', step_perm(size, steps, flip))  35 us
    pallas_call x3, Pallas kernels, chunk_grads(): pl.pallas_call(functools.partial(grads_kernel, spans), out_shape=[jax.Sha...  23.3 us
    pallas_call x2, Pallas kernels, adam_rows(): pl.pallas_call(functools.partial(adam_kernel, count, owners, kept, first)...  15.1 us
    unnamed x80, local copies, waits for them, and re-layouts  13.7 us
    pallas_call x2, Pallas kernels, partial_rows(): pl.pallas_call(functools.partial(partial_kernel, start, total), out_shape...  8.96 us
    pallas_call x1, Pallas kernels, finish(): pl.pallas_call(functools.partial(finish_kernel, pieces), out_shape=(jax.S...  6.37 us
    pallas_call x2, Pallas kernels, regroup(): pl.pallas_call(regroup_kernel, out_shape=[jax.ShapeDtypeStruct((count, sl...  3.32 us
  transfers between devices with their start and end apart: 33, of which 12 were waited for; matrix products, arithmetic and copies ran while one was open for 9% of the time, Pallas kernels for 37%

profile of v4, /device:TPU:0, one launch (start us, length us, event | category | flops | bytes accessed | tf_op | source)
XLA Modules:
  0.0 159.4 jit_solution(7350727336533097689)
XLA Ops:
  0.7 0.8 convert_element_type.50
  1.5 1.1 fusion.9.refs_5_
  2.6 3.1 %collective-permute-start = (bf16[128,2176]{1,0:T(8,128)(2,1)S(1)}, bf16[128,2176]{1,0:T(8,128)(2,1)S(1)}, u32[]{:S(2)}, u32[]{:S(2)}) collective-permute-start(bf16[128,2176]{1,0:T(8,128)(2,1)S(1)} %fusion.9.refs_5_), channel_id=1, source_target_pairs={{0,4},{1,5},{2,6},{3,7},{4,12},{5,13},{6,14},{7,15},{8,0},{9,1},{1... | collective-permute-start | bytes 1671176 | tf_op jit(solution)/shard_map/ppermute | solution.py:591
  5.7 1.5 collective-permute-start.1
  7.2 1.5 collective-permute-start.2
  8.7 0.8 copy.48
  10.2 0.6 fusion.27.target
  11.1 0.7 reshape.249.probs
  11.8 1.9 %fusion.2 = bf16[1536,384]{1,0:T(8,128)(2,1)S(1)} fusion(s32[1024]{0:T(1024)S(1)} %fusion.41, bf16[128,8,384]{2,1,0:T(8,128)(2,1)S(1)} %copy-done.27, f32[128,8]{1,0:T(8,128)S(1)} %copy.50), kind=kOutput, calls=%fused_computation.4 | convolution fusion | flops 1211301888 | bytes 1974272 | tf_op jit(solution)/shard_map/dot_general | solution.py:583
  13.7 5.6 %collective-permute-done.refs_0_ = bf16[128,2176]{1,0:T(8,128)(2,1)S(1)} collective-permute-done((bf16[128,2176]{1,0:T(8,128)(2,1)S(1)}, bf16[128,2176]{1,0:T(8,128)(2,1)S(1)}, u32[]{:S(2)}, u32[]{:S(2)}) %collective-permute-start) | collective-permute-done | bytes 557088 | tf_op jit(solution)/shard_map/ppermute | solution.py:591
  19.8 1.2 collective-permute-done.2.refs_7_
  21.0 2.6 %collective-permute-start.3 = (bf16[128,2176]{1,0:T(8,128)(2,1)S(1)}, bf16[128,2176]{1,0:T(8,128)(2,1)S(1)}, u32[]{:S(2)}, u32[]{:S(2)}) collective-permute-start(bf16[128,2176]{1,0:T(8,128)(2,1)S(1)} %collective-permute-done.refs_0_), channel_id=1, source_target_pairs={{0,4},{1,5},{2,6},{3,7},{4,12},{5,13},{6,14},{7,15},{8,0},{9,1},{1... | collective-permute-start | bytes 1671176 | tf_op jit(solution)/shard_map/ppermute | solution.py:591
  23.6 0.5 collective-permute-start.4
  24.1 1.5 collective-permute-start.5
  25.7 9.1 %collective-permute-done.3.refs_0_ = bf16[128,2176]{1,0:T(8,128)(2,1)S(1)} collective-permute-done((bf16[128,2176]{1,0:T(8,128)(2,1)S(1)}, bf16[128,2176]{1,0:T(8,128)(2,1)S(1)}, u32[]{:S(2)}, u32[]{:S(2)}) %collective-permute-start.3) | collective-permute-done | bytes 557088 | tf_op jit(solution)/shard_map/ppermute | solution.py:591
  34.8 1.4 collective-permute-done.4.refs_1_
  36.2 0.6 collective-permute-done.5.refs_2_
  36.9 1.6 collective-permute-start.7
  38.5 1.2 collective-permute-start.9
  39.7 0.5 collective-permute-start.10
  40.2 0.5 collective-permute-start.11
  40.8 1.0 collective-permute-start.6
  41.8 4.7 %collective-permute-done.7.refs_3_ = bf16[64,2176]{1,0:T(8,128)(2,1)S(1)} collective-permute-done((bf16[64,2176]{1,0:T(8,128)(2,1)S(1)}, bf16[64,2176]{1,0:T(8,128)(2,1)S(1)}, u32[]{:S(2)}, u32[]{:S(2)}) %collective-permute-start.7) | collective-permute-done | bytes 278560 | tf_op jit(solution)/shard_map/ppermute | solution.py:591
  46.5 1.4 collective-permute-start.8
  48.0 6.2 %copy.65 = bf16[384,4,2048]{2,0,1:T(8,128)(2,1)} copy(bf16[384,4,2048]{2,1,0:T(4,128)(2,1)S(1)} %bitcast.81) | data formatting | bytes 12582912 | tf_op args[4]
  54.2 3.6 %collective-permute-done.8.refs_4_ = bf16[64,2176]{1,0:T(8,128)(2,1)S(1)} collective-permute-done((bf16[64,2176]{1,0:T(8,128)(2,1)S(1)}, bf16[64,2176]{1,0:T(8,128)(2,1)S(1)}, u32[]{:S(2)}, u32[]{:S(2)}) %collective-permute-start.8) | collective-permute-done | bytes 278560 | tf_op jit(solution)/shard_map/ppermute | solution.py:591
  57.9 0.6 collective-permute-start.16
  58.5 1.9 %collective-permute-start.17 = (bf16[128,2176]{1,0:T(8,128)(2,1)}, bf16[128,2176]{1,0:T(8,128)(2,1)S(1)}, u32[]{:S(2)}, u32[]{:S(2)}) collective-permute-start(bf16[128,2176]{1,0:T(8,128)(2,1)} %collective-permute-done.9.refs_0_), channel_id=1, source_target_pairs={{0,2},{1,3},{2,0},{3,1},{4,6},{5,7},{6,4},{7,5},{8,10},{9,11},{10,... | collective-permute-start | bytes 1671176 | tf_op jit(solution)/shard_map/ppermute | solution.py:591
  60.6 1.9 %collective-permute-start.12 = (bf16[4,96,384]{2,1,0:T(8,128)(2,1)S(1)}, bf16[4,96,384]{2,1,0:T(8,128)(2,1)S(1)}, u32[]{:S(2)}, u32[]{:S(2)}) collective-permute-start(bf16[4,96,384]{2,1,0:T(8,128)(2,1)S(1)} %get-tuple-element.201), channel_id=1, source_target_pairs={{0,12},{1,13},{2,14},{3,15},{4,8},{5,9},{6,10},{7,11},{8,4},{9,5},... | collective-permute-start | bytes 884744 | tf_op jit(solution)/shard_map/ppermute | solution.py:591
  62.4 0.9 collective-permute-start.13
  63.4 4.2 %collective-permute-done.14.refs_3_ = bf16[64,2176]{1,0:T(8,128)(2,1)} collective-permute-done((bf16[64,2176]{1,0:T(8,128)(2,1)S(1)}, bf16[64,2176]{1,0:T(8,128)(2,1)}, u32[]{:S(2)}, u32[]{:S(2)}) %collective-permute-start.14) | collective-permute-done | bytes 278560 | tf_op jit(solution)/shard_map/ppermute | solution.py:591
  67.6 0.5 collective-permute-start.15
  68.2 6.8 %shard_map.127 = (bf16[384,2048]{1,0:T(8,128)(2,1)}, bf16[4,96,384]{2,1,0:T(8,128)(2,1)}) custom-call(s32[1]{0:T(128)} %bitcast.5.first, bf16[128,2176]{1,0:T(8,128)(2,1)} %copy-done.21, bf16[128,2176]{1,0:T(8,128)(2,1)} %copy-done.18, bf16[128,2176]{1,0:T(8,128)(2,1)} %copy-done.19, bf16[64,2176]{1,0:T(8,128)(2,1)} %copy-done.23, ...), custom_call_target="tpu_custom_call" | custom-call | flops 1409286144 | bytes 3670016 | tf_op jit(solution)/shard_map/pallas_call | solution.py:170
  74.9 0.9 collective-permute-done.15.refs_4_
  76.0 0.6 collective-permute-start.19
  77.0 0.7 collective-permute-start.20
  77.6 2.3 %collective-permute-start.18 = (bf16[4,96,384]{2,1,0:T(8,128)(2,1)S(1)}, bf16[4,96,384]{2,1,0:T(8,128)(2,1)S(1)}, u32[]{:S(2)}, u32[]{:S(2)}) collective-permute-start(bf16[4,96,384]{2,1,0:T(8,128)(2,1)S(1)} %copy-done.31), channel_id=1, source_target_pairs={{0,8},{1,9},{2,10},{3,11},{4,0},{5,1},{6,2},{7,3},{8,12},{9,13},{1... | collective-permute-start | bytes 884744 | tf_op jit(solution)/shard_map/ppermute | solution.py:591
  79.9 1.0 slice_bitcast_fusion.refs_0_
  80.9 2.0 %shard_map.130 = (bf16[4,96,384]{2,1,0:T(8,128)(2,1)}, bf16[4,96,384]{2,1,0:T(8,128)(2,1)}, bf16[4,96,384]{2,1,0:T(8,128)(2,1)S(1)}) custom-call(bf16[4,96,384]{2,1,0:T(8,128)(2,1)S(1)} %slice_bitcast_fusion.refs_0_, bf16[4,96,384]{2,1,0:T(8,128)(2,1)S(1)} %collective-permute-done.6.refs_1_, bf16[4,96,384]{2,1,0:T(8,128)(2,1)S(1)} %collective-permute-done.12.refs_2_, ...), custom_call_target="tpu_custom_call" | custom-call | bytes 1769472 | tf_op jit(solution)/shard_map/pallas_call | solution.py:265
  83.0 1.6 %collective-permute-start.23 = (bf16[4,96,384]{2,1,0:T(8,128)(2,1)}, bf16[4,96,384]{2,1,0:T(8,128)(2,1)S(1)}, u32[]{:S(2)}, u32[]{:S(2)}) collective-permute-start(bf16[4,96,384]{2,1,0:T(8,128)(2,1)} %get-tuple-element.142), channel_id=1, source_target_pairs={{0,1},{1,0},{2,3},{3,2},{4,5},{5,4},{6,7},{7,6},{8,9},{9,8},{10,11... | collective-permute-start | bytes 884744 | tf_op jit(solution)/shard_map/ppermute | solution.py:591
  84.6 1.4 collective-permute-start.24
  86.0 6.7 %shard_map.128 = (bf16[384,2048]{1,0:T(8,128)(2,1)}, bf16[4,96,384]{2,1,0:T(8,128)(2,1)}) custom-call(s32[1]{0:T(128)} %bitcast.5.first, bf16[128,2176]{1,0:T(8,128)(2,1)} %copy-done.22, bf16[128,2176]{1,0:T(8,128)(2,1)} %copy-done.14, bf16[128,2176]{1,0:T(8,128)(2,1)} %copy-done.15, bf16[64,2176]{1,0:T(8,128)(2,1)} %collective-permute-done.14.refs_3_, ...), custom_call_target="tpu_custom_call" | custom-call | flops 1409286144 | bytes 3670016 | tf_op jit(solution)/shard_map/pallas_call | solution.py:170
  92.7 0.6 collective-permute-start.25
  93.3 2.7 %collective-permute-start.21 = (bf16[4,96,384]{2,1,0:T(8,128)(2,1)}, bf16[4,96,384]{2,1,0:T(8,128)(2,1)S(1)}, u32[]{:S(2)}, u32[]{:S(2)}) collective-permute-start(bf16[4,96,384]{2,1,0:T(8,128)(2,1)} %get-tuple-element.136), channel_id=1, source_target_pairs={{0,12},{1,13},{2,14},{3,15},{4,8},{5,9},{6,10},{7,11},{8,4},{9,5},... | collective-permute-start | bytes 884744 | tf_op jit(solution)/shard_map/ppermute | solution.py:591
  96.0 9.8 %shard_map.129 = (bf16[384,2048]{1,0:T(8,128)(2,1)}, bf16[4,96,384]{2,1,0:T(8,128)(2,1)}, bf16[384,2048]{1,0:T(8,128)(2,1)}, bf16[4,96,384]{2,1,0:T(8,128)(2,1)}) custom-call(s32[1]{0:T(128)} %bitcast.5.first, bf16[128,2176]{1,0:T(8,128)(2,1)} %collective-permute-done.9.refs_0_, bf16[128,2176]{1,0:T(8,128)(2,1)} %copy-done.16, bf16[128,2176]{1,0:T(8,128)(2,1)} %copy-done.17, ...), custom_call_target="tpu_custom_call" | custom-call | flops 2818572288 | bytes 7340032 | tf_op jit(solution)/shard_map/pallas_call | solution.py:170
  106.3 2.5 %shard_map.131.weighted = bf16[4,384,384]{2,1,0:T(8,128)(2,1)S(1)} custom-call(bf16[4,96,384]{2,1,0:T(8,128)(2,1)S(1)} %slice_bitcast_fusion.refs_0_, bf16[4,96,384]{2,1,0:T(8,128)(2,1)S(1)} %collective-permute-done.6.refs_1_, bf16[4,96,384]{2,1,0:T(8,128)(2,1)S(1)} %collective-permute-done.12.refs_2_, ...), custom_call_target="tpu_custom_call" | custom-call | bytes 4718592 | tf_op jit(solution)/shard_map/pallas_call | solution.py:223
  108.8 1.4 copy-done.3
  110.2 1.4 copy-done.4
  111.6 4.5 %shard_map.132 = (bf16[2,192,2048]{2,1,0:T(8,128)(2,1)S(1)}, bf16[2,192,2048]{2,1,0:T(8,128)(2,1)S(1)}) custom-call(s32[2]{0:T(128)S(1)} %and_select_fusion.owners, bf16[4,384,384]{2,1,0:T(8,128)(2,1)S(1)} %shard_map.131.weighted, bf16[384,2048]{1,0:T(8,128)(2,1)S(1)} %copy-done.4, bf16[384,2048]{1,0:T(8,128)(2,1)S(1)} %copy-done.1, ...), custom_call_target="tpu_custom_call" | custom-call | flops 1207959552 | bytes 6291456 | tf_op jit(solution)/shard_map/pallas_call | solution.py:330
  116.3 4.5 %shard_map.133 = (bf16[2,192,2048]{2,1,0:T(8,128)(2,1)S(1)}, bf16[2,192,2048]{2,1,0:T(8,128)(2,1)S(1)}) custom-call(s32[2]{0:T(128)S(1)} %and_select_fusion.owners, bf16[4,384,384]{2,1,0:T(8,128)(2,1)S(1)} %shard_map.131.weighted, bf16[384,2048]{1,0:T(8,128)(2,1)S(1)} %copy-done.4, bf16[384,2048]{1,0:T(8,128)(2,1)S(1)} %copy-done.1, ...), custom_call_target="tpu_custom_call" | custom-call | flops 1207959552 | bytes 6291456 | tf_op jit(solution)/shard_map/pallas_call | solution.py:330
  120.8 0.5 collective-permute-start.27
  121.3 1.3 shard_map.134
  122.6 1.7 %collective-permute-done.27.refs_3_ = bf16[2,192,2048]{2,1,0:T(8,128)(2,1)S(1)} collective-permute-done((bf16[2,192,2048]{2,1,0:T(8,128)(2,1)S(1)}, bf16[2,192,2048]{2,1,0:T(8,128)(2,1)S(1)}, u32[]{:S(2)}, u32[]{:S(2)}) %collective-permute-start.27) | collective-permute-done | bytes 1572896 | tf_op jit(solution)/shard_map/ppermute | solution.py:689
  124.3 1.5 collective-permute-start.28
  125.9 1.4 collective-permute-start.29
  127.3 0.6 collective-permute-start.30
  127.9 2.8 %copy-done = f32[192,4,2048]{2,1,0:T(4,128)S(1)} copy-done((f32[192,4,2048]{2,1,0:T(4,128)S(1)}, f32[192,4,2048]{2,1,0:T(4,128)}, u32[]{:S(2)}) %copy-start) | copy-done | bytes 6291480
  130.6 7.5 %shard_map.136 = (f32[12288,128]{1,0:T(8,128)}, f32[12288,128]{1,0:T(8,128)}, f32[12288,128]{1,0:T(8,128)}, bf16[24576,128]{1,0:T(8,128)(2,1)}, bf16[6144,128]{1,0:T(8,128)(2,1)}) custom-call(s32[1]{0:T(128)} %bitcast.12.at, bf16[2,192,2048]{2,1,0:T(8,128)(2,1)S(1)} %get-tuple-element.168.refs_0_, bf16[2,192,2048]{2,1,0:T(8,128)(2,1)S(1)} %collective-permute-done.26.refs_1_, ...), custom_call_target="tpu_custom_call" | custom-call | flops 15728640 | bytes 15728640 | tf_op jit(solution)/shard_map/pallas_call | solution.py:412
  138.2 3.0 %collective-permute-done.29.refs_5_ = bf16[4,96,384]{2,1,0:T(8,128)(2,1)S(1)} collective-permute-done((bf16[4,96,384]{2,1,0:T(8,128)(2,1)S(1)}, bf16[4,96,384]{2,1,0:T(8,128)(2,1)S(1)}, u32[]{:S(2)}, u32[]{:S(2)}) %collective-permute-start.29) | collective-permute-done | bytes 294944 | tf_op jit(solution)/shard_map/ppermute | solution.py:591
  141.2 7.6 %shard_map.137 = (f32[12288,128]{1,0:T(8,128)}, f32[12288,128]{1,0:T(8,128)}, f32[12288,128]{1,0:T(8,128)}, bf16[24576,128]{1,0:T(8,128)(2,1)}, bf16[6144,128]{1,0:T(8,128)(2,1)}) custom-call(s32[1]{0:T(128)} %bitcast.12.at, ...), custom_call_target="tpu_custom_call", output_to_operand_aliasing={{0}: (8, {}), {1}: (9, {}), {2}: (10, {}), {3}: (11, {})} | custom-call | flops 15728640 | bytes 15728640 | tf_op jit(solution)/shard_map/pallas_call | solution.py:412
  148.8 6.4 %shard_map.135 = (bf16[1024,384]{1,0:T(8,128)(2,1)}, f32[8,1024]{1,0:T(8,128)}) custom-call(f32[8,128]{1,0:T(8,128)} %fusion.27.target, f32[8,128]{1,0:T(8,128)} %reshape.249.probs, bf16[1024,384]{1,0:T(8,128)(2,1)} %bitcast.85, bf16[4,96,384]{2,1,0:T(8,128)(2,1)} %get-tuple-element.138.refs_0_, bf16[4,96,384]{2,1,0:T(8,128)(2,1)} %copy-done.5, ...), custom_call_target="tpu_custom_call" | custom-call | flops 1207959552 | bytes 3145728 | tf_op jit(solution)/shard_map/pallas_call | solution.py:524
  155.2 0.8 slice_reduce_fusion
  156.1 0.7 copy.62
  156.7 2.7 %shard_map.138 = bf16[24576,128]{1,0:T(8,128)(2,1)} custom-call(s32[1]{0:T(128)} %bitcast.37.at, bf16[6144,128]{1,0:T(8,128)(2,1)S(1)} %collective-permute-done.31.low, bf16[6144,128]{1,0:T(8,128)(2,1)S(1)} %collective-permute-done.32.high, bf16[24576,128]{1,0:T(8,128)(2,1)} %get-tuple-element.181.full), custom_call_target="tpu_custom_call", output_to_operand_aliasing={{}: (3, {})} | custom-call | bytes 6291456 | tf_op jit(solution)/shard_map/pallas_call | solution.py:455
  (127 shorter events, 2.8 us)
Async XLA Ops:
  0.6 10.3 %copy-start.26 = (f32[128,8]{0,1:T(8,128)S(1)}, f32[128,8]{0,1:T(8,128)}, u32[]{:S(2)}) copy-start(f32[128,8]{0,1:T(8,128)} %param.10) | copy-start | bytes 12292
  0.6 11.2 %copy-start.27 = (bf16[128,8,384]{2,1,0:T(8,128)(2,1)S(1)}, bf16[128,8,384]{2,1,0:T(8,128)(2,1)}, u32[]{:S(2)}) copy-start(bf16[128,8,384]{2,1,0:T(8,128)(2,1)} %param.9) | copy-start | bytes 2359300
  2.6 11.1 %copy-start.11 = (bf16[128,2176]{1,0:T(8,128)(2,1)}, bf16[128,2176]{1,0:T(8,128)(2,1)S(1)}, u32[]{:S(2)}) copy-start(bf16[128,2176]{1,0:T(8,128)(2,1)S(1)} %fusion.9.refs_5_) | copy-start | bytes 1671172
  2.6 16.7 %collective-permute-start = (bf16[128,2176]{1,0:T(8,128)(2,1)S(1)}, bf16[128,2176]{1,0:T(8,128)(2,1)S(1)}, u32[]{:S(2)}, u32[]{:S(2)}) collective-permute-start(bf16[128,2176]{1,0:T(8,128)(2,1)S(1)} %fusion.9.refs_5_), channel_id=1, source_target_pairs={{0,4},{1,5},{2,6},{3,7},{4,12},{5,13},{6,14},{7,15},{8,0},{9,1},{1... | collective-permute-start | bytes 1671176 | tf_op jit(solution)/shard_map/ppermute | solution.py:591
  5.7 14.1 %collective-permute-start.1 = (bf16[128,2176]{1,0:T(8,128)(2,1)S(1)}, bf16[128,2176]{1,0:T(8,128)(2,1)S(1)}, u32[]{:S(2)}, u32[]{:S(2)}) collective-permute-start(bf16[128,2176]{1,0:T(8,128)(2,1)S(1)} %fusion.9.refs_5_), channel_id=1, source_target_pairs={{0,1},{1,0},{2,3},{3,2},{4,5},{5,4},{6,7},{7,6},{8,9},{9,8},{10,11... | collective-permute-start | bytes 1671176 | tf_op jit(solution)/shard_map/ppermute | solution.py:591
  7.2 13.8 %collective-permute-start.2 = (bf16[128,2176]{1,0:T(8,128)(2,1)S(1)}, bf16[128,2176]{1,0:T(8,128)(2,1)S(1)}, u32[]{:S(2)}, u32[]{:S(2)}) collective-permute-start(bf16[128,2176]{1,0:T(8,128)(2,1)S(1)} %fusion.9.refs_5_), channel_id=1, source_target_pairs={{0,2},{1,3},{2,0},{3,1},{4,6},{5,7},{6,4},{7,5},{8,10},{9,11},{10,... | collective-permute-start | bytes 1671176 | tf_op jit(solution)/shard_map/ppermute | solution.py:591
  11.8 36.2 %slice-start.4 = ((s8[6291456]{0:T(1024)(128)(4,1)}), s8[4194304]{0:T(1024)(128)(4,1)S(1)}, s32[]{:S(2)}) async-start(s8[6291456]{0:T(1024)(128)(4,1)} %bitcast.80), calls=%async_computation.4 | async-start | bytes 8388608
  11.8 36.2 %slice-start.5 = ((s8[6291456]{0:T(1024)(128)(4,1)}), s8[2097152]{0:T(1024)(128)(4,1)S(1)}, s32[]{:S(2)}) async-start(s8[6291456]{0:T(1024)(128)(4,1)} %bitcast.80), calls=%async_computation.5 | async-start | bytes 4194304
  13.7 46.8 %copy-start.20 = (bf16[1536,384]{1,0:T(8,128)(2,1)}, bf16[1536,384]{1,0:T(8,128)(2,1)S(1)}, u32[]{:S(2)}) copy-start(bf16[1536,384]{1,0:T(8,128)(2,1)S(1)} %fusion.2) | copy-start | bytes 3538948
  19.4 19.1 %copy-start.21 = (bf16[128,2176]{1,0:T(8,128)(2,1)}, bf16[128,2176]{1,0:T(8,128)(2,1)S(1)}, u32[]{:S(2)}) copy-start(bf16[128,2176]{1,0:T(8,128)(2,1)S(1)} %collective-permute-done.refs_0_) | copy-start | bytes 1671172
  19.8 34.3 %copy-start.12 = (bf16[128,2176]{1,0:T(8,128)(2,1)}, bf16[128,2176]{1,0:T(8,128)(2,1)S(1)}, u32[]{:S(2)}) copy-start(bf16[128,2176]{1,0:T(8,128)(2,1)S(1)} %collective-permute-done.1.refs_6_) | copy-start | bytes 1671172
  21.0 33.1 %copy-start.13 = (bf16[128,2176]{1,0:T(8,128)(2,1)}, bf16[128,2176]{1,0:T(8,128)(2,1)S(1)}, u32[]{:S(2)}) copy-start(bf16[128,2176]{1,0:T(8,128)(2,1)S(1)} %collective-permute-done.2.refs_7_) | copy-start | bytes 1671172
  21.0 13.8 %collective-permute-start.3 = (bf16[128,2176]{1,0:T(8,128)(2,1)S(1)}, bf16[128,2176]{1,0:T(8,128)(2,1)S(1)}, u32[]{:S(2)}, u32[]{:S(2)}) collective-permute-start(bf16[128,2176]{1,0:T(8,128)(2,1)S(1)} %collective-permute-done.refs_0_), channel_id=1, source_target_pairs={{0,4},{1,5},{2,6},{3,7},{4,12},{5,13},{6,14},{7,15},{8,0},{9,1},{1... | collective-permute-start | bytes 1671176 | tf_op jit(solution)/shard_map/ppermute | solution.py:591
  23.6 12.6 %collective-permute-start.4 = (bf16[128,2176]{1,0:T(8,128)(2,1)S(1)}, bf16[128,2176]{1,0:T(8,128)(2,1)S(1)}, u32[]{:S(2)}, u32[]{:S(2)}) collective-permute-start(bf16[128,2176]{1,0:T(8,128)(2,1)S(1)} %collective-permute-done.refs_0_), channel_id=1, source_target_pairs={{0,1},{1,0},{2,3},{3,2},{4,5},{5,4},{6,7},{7,6},{8,9},{9,8},{10,11... | collective-permute-start | bytes 1671176 | tf_op jit(solution)/shard_map/ppermute | solution.py:591
  24.1 12.7 %collective-permute-start.5 = (bf16[128,2176]{1,0:T(8,128)(2,1)S(1)}, bf16[128,2176]{1,0:T(8,128)(2,1)S(1)}, u32[]{:S(2)}, u32[]{:S(2)}) collective-permute-start(bf16[128,2176]{1,0:T(8,128)(2,1)S(1)} %collective-permute-done.refs_0_), channel_id=1, source_target_pairs={{0,2},{1,3},{2,0},{3,1},{4,6},{5,7},{6,4},{7,5},{8,10},{9,11},{10,... | collective-permute-start | bytes 1671176 | tf_op jit(solution)/shard_map/ppermute | solution.py:591
  34.8 19.3 %copy-start.22 = (bf16[128,2176]{1,0:T(8,128)(2,1)}, bf16[128,2176]{1,0:T(8,128)(2,1)S(1)}, u32[]{:S(2)}) copy-start(bf16[128,2176]{1,0:T(8,128)(2,1)S(1)} %collective-permute-done.3.refs_0_) | copy-start | bytes 1671172
  36.2 17.9 %copy-start.18 = (bf16[128,2176]{1,0:T(8,128)(2,1)}, bf16[128,2176]{1,0:T(8,128)(2,1)S(1)}, u32[]{:S(2)}) copy-start(bf16[128,2176]{1,0:T(8,128)(2,1)S(1)} %collective-permute-done.4.refs_1_) | copy-start | bytes 1671172
  36.8 17.3 %copy-start.19 = (bf16[128,2176]{1,0:T(8,128)(2,1)}, bf16[128,2176]{1,0:T(8,128)(2,1)S(1)}, u32[]{:S(2)}) copy-start(bf16[128,2176]{1,0:T(8,128)(2,1)S(1)} %collective-permute-done.5.refs_2_) | copy-start | bytes 1671172
  36.9 9.7 %collective-permute-start.7 = (bf16[64,2176]{1,0:T(8,128)(2,1)S(1)}, bf16[64,2176]{1,0:T(8,128)(2,1)S(1)}, u32[]{:S(2)}, u32[]{:S(2)}) collective-permute-start(bf16[64,2176]{1,0:T(8,128)(2,1)S(1)} %slice.42), channel_id=1, source_target_pairs={{0,2},{1,3},{2,0},{3,1},{4,6},{5,7},{6,4},{7,5},{8,10},{9,11},{10,... | collective-permute-start | bytes 835592 | tf_op jit(solution)/shard_map/ppermute | solution.py:591
  38.5 19.3 %collective-permute-start.9 = (bf16[128,2176]{1,0:T(8,128)(2,1)S(1)}, bf16[128,2176]{1,0:T(8,128)(2,1)}, u32[]{:S(2)}, u32[]{:S(2)}) collective-permute-start(bf16[128,2176]{1,0:T(8,128)(2,1)S(1)} %collective-permute-done.3.refs_0_), channel_id=1, source_target_pairs={{0,4},{1,5},{2,6},{3,7},{4,12},{5,13},{6,14},{7,15},{8,0},{9,1},{1... | collective-permute-start | bytes 1671176 | tf_op jit(solution)/shard_map/ppermute | solution.py:591
  39.7 18.1 %collective-permute-start.10 = (bf16[128,2176]{1,0:T(8,128)(2,1)S(1)}, bf16[128,2176]{1,0:T(8,128)(2,1)S(1)}, u32[]{:S(2)}, u32[]{:S(2)}) collective-permute-start(bf16[128,2176]{1,0:T(8,128)(2,1)S(1)} %collective-permute-done.3.refs_0_), channel_id=1, source_target_pairs={{0,1},{1,0},{2,3},{3,2},{4,5},{5,4},{6,7},{7,6},{8,9},{9,8},{10,11... | collective-permute-start | bytes 1671176 | tf_op jit(solution)/shard_map/ppermute | solution.py:591
  40.2 17.6 %collective-permute-start.11 = (bf16[128,2176]{1,0:T(8,128)(2,1)S(1)}, bf16[128,2176]{1,0:T(8,128)(2,1)S(1)}, u32[]{:S(2)}, u32[]{:S(2)}) collective-permute-start(bf16[128,2176]{1,0:T(8,128)(2,1)S(1)} %collective-permute-done.3.refs_0_), channel_id=1, source_target_pairs={{0,2},{1,3},{2,0},{3,1},{4,6},{5,7},{6,4},{7,5},{8,10},{9,11},{10,... | collective-permute-start | bytes 1671176 | tf_op jit(solution)/shard_map/ppermute | solution.py:591
  40.8 17.0 %collective-permute-start.6 = (bf16[4,96,384]{2,1,0:T(8,128)(2,1)S(1)}, bf16[4,96,384]{2,1,0:T(8,128)(2,1)S(1)}, u32[]{:S(2)}, u32[]{:S(2)}) collective-permute-start(bf16[4,96,384]{2,1,0:T(8,128)(2,1)S(1)} %slice_bitcast_fusion.3), channel_id=1, source_target_pairs={{0,4},{1,5},{2,6},{3,7},{4,12},{5,13},{6,14},{7,15},{8,0},{9,1},{1... | collective-permute-start | bytes 884744 | tf_op jit(solution)/shard_map/ppermute | solution.py:591
  46.5 7.6 %copy-start.23 = (bf16[64,2176]{1,0:T(8,128)(2,1)}, bf16[64,2176]{1,0:T(8,128)(2,1)S(1)}, u32[]{:S(2)}) copy-start(bf16[64,2176]{1,0:T(8,128)(2,1)S(1)} %collective-permute-done.7.refs_3_) | copy-start | bytes 835588
  46.5 11.2 %collective-permute-start.8 = (bf16[64,2176]{1,0:T(8,128)(2,1)S(1)}, bf16[64,2176]{1,0:T(8,128)(2,1)S(1)}, u32[]{:S(2)}, u32[]{:S(2)}) collective-permute-start(bf16[64,2176]{1,0:T(8,128)(2,1)S(1)} %slice.43), channel_id=1, source_target_pairs={{0,1},{1,0},{2,3},{3,2},{4,5},{5,4},{6,7},{7,6},{8,9},{9,8},{10,11... | collective-permute-start | bytes 835592 | tf_op jit(solution)/shard_map/ppermute | solution.py:591
  57.8 5.6 %copy-start.25 = (bf16[64,2176]{1,0:T(8,128)(2,1)}, bf16[64,2176]{1,0:T(8,128)(2,1)S(1)}, u32[]{:S(2)}) copy-start(bf16[64,2176]{1,0:T(8,128)(2,1)S(1)} %collective-permute-done.8.refs_4_) | copy-start | bytes 835588
  57.8 2.8 %copy-start.14 = (bf16[128,2176]{1,0:T(8,128)(2,1)}, bf16[128,2176]{1,0:T(8,128)(2,1)S(1)}, u32[]{:S(2)}) copy-start(bf16[128,2176]{1,0:T(8,128)(2,1)S(1)} %collective-permute-done.10.refs_1_) | copy-start | bytes 1671172
  57.8 5.5 %copy-start.15 = (bf16[128,2176]{1,0:T(8,128)(2,1)}, bf16[128,2176]{1,0:T(8,128)(2,1)S(1)}, u32[]{:S(2)}) copy-start(bf16[128,2176]{1,0:T(8,128)(2,1)S(1)} %collective-permute-done.11.refs_2_) | copy-start | bytes 1671172
  57.8 9.8 %collective-permute-start.14 = (bf16[64,2176]{1,0:T(8,128)(2,1)S(1)}, bf16[64,2176]{1,0:T(8,128)(2,1)}, u32[]{:S(2)}, u32[]{:S(2)}) collective-permute-start(bf16[64,2176]{1,0:T(8,128)(2,1)S(1)} %slice.46), channel_id=1, source_target_pairs={{0,2},{1,3},{2,0},{3,1},{4,6},{5,7},{6,4},{7,5},{8,10},{9,11},{10,... | collective-permute-start | bytes 835592 | tf_op jit(solution)/shard_map/ppermute | solution.py:591
  57.9 18.0 %collective-permute-start.16 = (bf16[128,2176]{1,0:T(8,128)(2,1)}, bf16[128,2176]{1,0:T(8,128)(2,1)S(1)}, u32[]{:S(2)}, u32[]{:S(2)}) collective-permute-start(bf16[128,2176]{1,0:T(8,128)(2,1)} %collective-permute-done.9.refs_0_), channel_id=1, source_target_pairs={{0,1},{1,0},{2,3},{3,2},{4,5},{5,4},{6,7},{7,6},{8,9},{9,8},{10,11... | collective-permute-start | bytes 1671176 | tf_op jit(solution)/shard_map/ppermute | solution.py:591
  58.5 17.4 %collective-permute-start.17 = (bf16[128,2176]{1,0:T(8,128)(2,1)}, bf16[128,2176]{1,0:T(8,128)(2,1)S(1)}, u32[]{:S(2)}, u32[]{:S(2)}) collective-permute-start(bf16[128,2176]{1,0:T(8,128)(2,1)} %collective-permute-done.9.refs_0_), channel_id=1, source_target_pairs={{0,2},{1,3},{2,0},{3,1},{4,6},{5,7},{6,4},{7,5},{8,10},{9,11},{10,... | collective-permute-start | bytes 1671176 | tf_op jit(solution)/shard_map/ppermute | solution.py:591
  60.6 15.3 %collective-permute-start.12 = (bf16[4,96,384]{2,1,0:T(8,128)(2,1)S(1)}, bf16[4,96,384]{2,1,0:T(8,128)(2,1)S(1)}, u32[]{:S(2)}, u32[]{:S(2)}) collective-permute-start(bf16[4,96,384]{2,1,0:T(8,128)(2,1)S(1)} %get-tuple-element.201), channel_id=1, source_target_pairs={{0,12},{1,13},{2,14},{3,15},{4,8},{5,9},{6,10},{7,11},{8,4},{9,5},... | collective-permute-start | bytes 884744 | tf_op jit(solution)/shard_map/ppermute | solution.py:591
  62.4 13.5 %collective-permute-start.13 = (bf16[4,96,384]{2,1,0:T(8,128)(2,1)S(1)}, bf16[4,96,384]{2,1,0:T(8,128)(2,1)S(1)}, u32[]{:S(2)}, u32[]{:S(2)}) collective-permute-start(bf16[4,96,384]{2,1,0:T(8,128)(2,1)S(1)} %get-tuple-element.200), channel_id=1, source_target_pairs={{0,8},{1,9},{2,10},{3,11},{4,0},{5,1},{6,2},{7,3},{8,12},{9,13},{1... | collective-permute-start | bytes 884744 | tf_op jit(solution)/shard_map/ppermute | solution.py:591
  67.6 8.3 %collective-permute-start.15 = (bf16[64,2176]{1,0:T(8,128)(2,1)S(1)}, bf16[64,2176]{1,0:T(8,128)(2,1)S(1)}, u32[]{:S(2)}, u32[]{:S(2)}) collective-permute-start(bf16[64,2176]{1,0:T(8,128)(2,1)S(1)} %slice.47), channel_id=1, source_target_pairs={{0,1},{1,0},{2,3},{3,2},{4,5},{5,4},{6,7},{7,6},{8,9},{9,8},{10,11... | collective-permute-start | bytes 835592 | tf_op jit(solution)/shard_map/ppermute | solution.py:591
  68.1 7.8 %slice-start.6 = ((bf16[128,2176]{1,0:T(8,128)(2,1)}), bf16[64,2176]{1,0:T(8,128)(2,1)S(1)}, s32[]{:S(2)}) async-start(bf16[128,2176]{1,0:T(8,128)(2,1)} %copy-done.12), calls=%async_computation.6 | async-start | bytes 557056 | tf_op jit(solution)/shard_map/slice | solution.py:616
  76.0 17.3 %collective-permute-start.19 = (bf16[128,2176]{1,0:T(8,128)(2,1)S(1)}, bf16[128,2176]{1,0:T(8,128)(2,1)S(1)}, u32[]{:S(2)}, u32[]{:S(2)}) collective-permute-start(bf16[128,2176]{1,0:T(8,128)(2,1)S(1)} %pad_maximum_fusion), channel_id=1, source_target_pairs={{0,2},{1,3},{2,0},{3,1},{4,6},{5,7},{6,4},{7,5},{8,10},{9,11},{10,... | collective-permute-start | bytes 1671176 | tf_op jit(solution)/shard_map/ppermute | solution.py:591
  77.0 16.4 %collective-permute-start.20 = (bf16[128,2176]{1,0:T(8,128)(2,1)S(1)}, bf16[128,2176]{1,0:T(8,128)(2,1)S(1)}, u32[]{:S(2)}, u32[]{:S(2)}) collective-permute-start(bf16[128,2176]{1,0:T(8,128)(2,1)S(1)} %pad_maximum_fusion.1), channel_id=1, source_target_pairs={{0,1},{1,0},{2,3},{3,2},{4,5},{5,4},{6,7},{7,6},{8,9},{9,8},{10,11... | collective-permute-start | bytes 1671176 | tf_op jit(solution)/shard_map/ppermute | solution.py:591
  77.6 15.1 %collective-permute-start.18 = (bf16[4,96,384]{2,1,0:T(8,128)(2,1)S(1)}, bf16[4,96,384]{2,1,0:T(8,128)(2,1)S(1)}, u32[]{:S(2)}, u32[]{:S(2)}) collective-permute-start(bf16[4,96,384]{2,1,0:T(8,128)(2,1)S(1)} %copy-done.31), channel_id=1, source_target_pairs={{0,8},{1,9},{2,10},{3,11},{4,0},{5,1},{6,2},{7,3},{8,12},{9,13},{1... | collective-permute-start | bytes 884744 | tf_op jit(solution)/shard_map/ppermute | solution.py:591
  83.0 23.3 %collective-permute-start.23 = (bf16[4,96,384]{2,1,0:T(8,128)(2,1)}, bf16[4,96,384]{2,1,0:T(8,128)(2,1)S(1)}, u32[]{:S(2)}, u32[]{:S(2)}) collective-permute-start(bf16[4,96,384]{2,1,0:T(8,128)(2,1)} %get-tuple-element.142), channel_id=1, source_target_pairs={{0,1},{1,0},{2,3},{3,2},{4,5},{5,4},{6,7},{7,6},{8,9},{9,8},{10,11... | collective-permute-start | bytes 884744 | tf_op jit(solution)/shard_map/ppermute | solution.py:591
  84.6 21.7 %collective-permute-start.24 = (bf16[4,96,384]{2,1,0:T(8,128)(2,1)}, bf16[4,96,384]{2,1,0:T(8,128)(2,1)S(1)}, u32[]{:S(2)}, u32[]{:S(2)}) collective-permute-start(bf16[4,96,384]{2,1,0:T(8,128)(2,1)} %get-tuple-element.143), channel_id=1, source_target_pairs={{0,2},{1,3},{2,0},{3,1},{4,6},{5,7},{6,4},{7,5},{8,10},{9,11},{10,... | collective-permute-start | bytes 884744 | tf_op jit(solution)/shard_map/ppermute | solution.py:591
  92.7 28.6 %copy-start.5 = (bf16[4,96,384]{2,1,0:T(8,128)(2,1)}, bf16[4,96,384]{2,1,0:T(8,128)(2,1)S(1)}, u32[]{:S(2)}) copy-start(bf16[4,96,384]{2,1,0:T(8,128)(2,1)S(1)} %collective-permute-done.18.refs_1_) | copy-start | bytes 884740
  92.7 13.6 %collective-permute-start.25 = (bf16[4,96,384]{2,1,0:T(8,128)(2,1)S(1)}, bf16[4,96,384]{2,1,0:T(8,128)(2,1)S(1)}, u32[]{:S(2)}, u32[]{:S(2)}) collective-permute-start(bf16[4,96,384]{2,1,0:T(8,128)(2,1)S(1)} %get-tuple-element.144), channel_id=1, source_target_pairs={{0,3},{1,2},{2,1},{3,0},{4,7},{5,6},{6,5},{7,4},{8,11},{9,10},{10,... | collective-permute-start | bytes 884744 | tf_op jit(solution)/shard_map/ppermute | solution.py:591
  93.3 2.7 %copy-start.9 = (bf16[128,2176]{1,0:T(8,128)(2,1)}, bf16[128,2176]{1,0:T(8,128)(2,1)S(1)}, u32[]{:S(2)}) copy-start(bf16[128,2176]{1,0:T(8,128)(2,1)S(1)} %collective-permute-done.19.refs_3_.refs_8_) | copy-start | bytes 1671172
  93.3 2.7 %copy-start.10 = (bf16[128,2176]{1,0:T(8,128)(2,1)}, bf16[128,2176]{1,0:T(8,128)(2,1)S(1)}, u32[]{:S(2)}) copy-start(bf16[128,2176]{1,0:T(8,128)(2,1)S(1)} %collective-permute-done.20.refs_4_.refs_9_) | copy-start | bytes 1671172
  93.3 22.9 %collective-permute-start.21 = (bf16[4,96,384]{2,1,0:T(8,128)(2,1)}, bf16[4,96,384]{2,1,0:T(8,128)(2,1)S(1)}, u32[]{:S(2)}, u32[]{:S(2)}) collective-permute-start(bf16[4,96,384]{2,1,0:T(8,128)(2,1)} %get-tuple-element.136), channel_id=1, source_target_pairs={{0,12},{1,13},{2,14},{3,15},{4,8},{5,9},{6,10},{7,11},{8,4},{9,5},... | collective-permute-start | bytes 884744 | tf_op jit(solution)/shard_map/ppermute | solution.py:591
  105.9 10.3 %collective-permute-start.22 = (bf16[4,96,384]{2,1,0:T(8,128)(2,1)}, bf16[4,96,384]{2,1,0:T(8,128)(2,1)S(1)}, u32[]{:S(2)}, u32[]{:S(2)}) collective-permute-start(bf16[4,96,384]{2,1,0:T(8,128)(2,1)} %get-tuple-element.137), channel_id=1, source_target_pairs={{0,4},{1,5},{2,6},{3,7},{4,12},{5,13},{6,14},{7,15},{8,0},{9,1},{1... | collective-permute-start | bytes 884744 | tf_op jit(solution)/shard_map/ppermute | solution.py:591
  106.3 21.5 %slice-start.2 = ((s8[6291456]{0:T(1024)(128)(4,1)}), s8[4194304]{0:T(1024)(128)(4,1)S(1)}, s32[]{:S(2)}) async-start(s8[6291456]{0:T(1024)(128)(4,1)} %bitcast.67), calls=%async_computation.2 | async-start | bytes 8388608
  111.6 16.2 %slice-start = ((s8[6291456]{0:T(1024)(128)(4,1)}), s8[4194304]{0:T(1024)(128)(4,1)S(1)}, s32[]{:S(2)}) async-start(s8[6291456]{0:T(1024)(128)(4,1)} %bitcast.63), calls=%async_computation | async-start | bytes 8388608
  111.6 16.2 %slice-start.3 = ((s8[6291456]{0:T(1024)(128)(4,1)}), s8[2097152]{0:T(1024)(128)(4,1)S(1)}, s32[]{:S(2)}) async-start(s8[6291456]{0:T(1024)(128)(4,1)} %bitcast.67), calls=%async_computation.3 | async-start | bytes 4194304
  116.1 6.5 %collective-permute-start.26 = (bf16[2,192,2048]{2,1,0:T(8,128)(2,1)S(1)}, bf16[2,192,2048]{2,1,0:T(8,128)(2,1)S(1)}, u32[]{:S(2)}, u32[]{:S(2)}) collective-permute-start(bf16[2,192,2048]{2,1,0:T(8,128)(2,1)S(1)} %get-tuple-element.146), channel_id=1, source_target_pairs={{0,16},{16,0},{1,17},{17,1},{2,18},{18,2},{3,19},{19,3},{4,20},{20... | collective-permute-start | bytes 4718600 | tf_op jit(solution)/shard_map/ppermute | solution.py:689
  116.2 5.1 %copy-start.6 = (bf16[4,96,384]{2,1,0:T(8,128)(2,1)}, bf16[4,96,384]{2,1,0:T(8,128)(2,1)S(1)}, u32[]{:S(2)}) copy-start(bf16[4,96,384]{2,1,0:T(8,128)(2,1)S(1)} %collective-permute-done.21.refs_2_) | copy-start | bytes 884740
  116.2 5.1 %copy-start.8 = (bf16[4,96,384]{2,1,0:T(8,128)(2,1)}, bf16[4,96,384]{2,1,0:T(8,128)(2,1)S(1)}, u32[]{:S(2)}) copy-start(bf16[4,96,384]{2,1,0:T(8,128)(2,1)S(1)} %collective-permute-done.22.refs_3_) | copy-start | bytes 884740
  116.2 5.1 %copy-start.7 = (bf16[4,96,384]{2,1,0:T(8,128)(2,1)S(1)}, bf16[4,96,384]{2,1,0:T(8,128)(2,1)}, u32[]{:S(2)}) copy-start(bf16[4,96,384]{2,1,0:T(8,128)(2,1)} %get-tuple-element.138.refs_0_) | copy-start | bytes 884740
  116.2 11.6 %slice-start.1 = ((s8[6291456]{0:T(1024)(128)(4,1)}), s8[2097152]{0:T(1024)(128)(4,1)S(1)}, s32[]{:S(2)}) async-start(s8[6291456]{0:T(1024)(128)(4,1)} %bitcast.63), calls=%async_computation.1 | async-start | bytes 4194304
  120.8 3.6 %collective-permute-start.27 = (bf16[2,192,2048]{2,1,0:T(8,128)(2,1)S(1)}, bf16[2,192,2048]{2,1,0:T(8,128)(2,1)S(1)}, u32[]{:S(2)}, u32[]{:S(2)}) collective-permute-start(bf16[2,192,2048]{2,1,0:T(8,128)(2,1)S(1)} %get-tuple-element.152), channel_id=1, source_target_pairs={{0,16},{16,0},{1,17},{17,1},{2,18},{18,2},{3,19},{19,3},{4,20},{20... | collective-permute-start | bytes 4718600 | tf_op jit(solution)/shard_map/ppermute | solution.py:689
  124.3 13.8 %collective-permute-start.28 = (bf16[4,96,384]{2,1,0:T(8,128)(2,1)S(1)}, bf16[4,96,384]{2,1,0:T(8,128)(2,1)S(1)}, u32[]{:S(2)}, u32[]{:S(2)}) collective-permute-start(bf16[4,96,384]{2,1,0:T(8,128)(2,1)S(1)} %get-tuple-element.160), channel_id=1, source_target_pairs={{0,1},{1,0},{2,3},{3,2},{4,5},{5,4},{6,7},{7,6},{8,9},{9,8},{10,11... | collective-permute-start | bytes 884744 | tf_op jit(solution)/shard_map/ppermute | solution.py:591
  125.9 15.3 %collective-permute-start.29 = (bf16[4,96,384]{2,1,0:T(8,128)(2,1)S(1)}, bf16[4,96,384]{2,1,0:T(8,128)(2,1)S(1)}, u32[]{:S(2)}, u32[]{:S(2)}) collective-permute-start(bf16[4,96,384]{2,1,0:T(8,128)(2,1)S(1)} %get-tuple-element.161), channel_id=1, source_target_pairs={{0,2},{1,3},{2,0},{3,1},{4,6},{5,7},{6,4},{7,5},{8,10},{9,11},{10,... | collective-permute-start | bytes 884744 | tf_op jit(solution)/shard_map/ppermute | solution.py:591
  127.3 13.9 %collective-permute-start.30 = (bf16[4,96,384]{2,1,0:T(8,128)(2,1)S(1)}, bf16[4,96,384]{2,1,0:T(8,128)(2,1)S(1)}, u32[]{:S(2)}, u32[]{:S(2)}) collective-permute-start(bf16[4,96,384]{2,1,0:T(8,128)(2,1)S(1)} %get-tuple-element.162), channel_id=1, source_target_pairs={{0,3},{1,2},{2,1},{3,0},{4,7},{5,6},{6,5},{7,4},{8,11},{9,10},{10,... | collective-permute-start | bytes 884744 | tf_op jit(solution)/shard_map/ppermute | solution.py:591
  127.8 2.8 %copy-start = (f32[192,4,2048]{2,1,0:T(4,128)S(1)}, f32[192,4,2048]{2,1,0:T(4,128)}, u32[]{:S(2)}) copy-start(f32[192,4,2048]{2,1,0:T(4,128)} %param.15) | copy-start | bytes 18874372
  138.1 18.6 %collective-permute-start.31 = (bf16[6144,128]{1,0:T(8,128)(2,1)}, bf16[6144,128]{1,0:T(8,128)(2,1)S(1)}, u32[]{:S(2)}, u32[]{:S(2)}) collective-permute-start(bf16[6144,128]{1,0:T(8,128)(2,1)} %get-tuple-element.179), channel_id=1, source_target_pairs={{0,16},{16,0},{1,17},{17,1},{2,18},{18,2},{3,19},{19,3},{4,20},{20... | collective-permute-start | bytes 4718600 | tf_op jit(solution)/shard_map/ppermute | solution.py:707
  138.2 10.6 %copy-start.28 = (bf16[4,96,384]{2,1,0:T(8,128)(2,1)}, bf16[4,96,384]{2,1,0:T(8,128)(2,1)S(1)}, u32[]{:S(2)}) copy-start(bf16[4,96,384]{2,1,0:T(8,128)(2,1)S(1)} %collective-permute-done.28.refs_4_) | copy-start | bytes 884740
  141.2 7.6 %copy-start.29 = (bf16[4,96,384]{2,1,0:T(8,128)(2,1)}, bf16[4,96,384]{2,1,0:T(8,128)(2,1)S(1)}, u32[]{:S(2)}) copy-start(bf16[4,96,384]{2,1,0:T(8,128)(2,1)S(1)} %collective-permute-done.29.refs_5_) | copy-start | bytes 884740
  141.2 7.6 %copy-start.30 = (bf16[4,96,384]{2,1,0:T(8,128)(2,1)}, bf16[4,96,384]{2,1,0:T(8,128)(2,1)S(1)}, u32[]{:S(2)}) copy-start(bf16[4,96,384]{2,1,0:T(8,128)(2,1)S(1)} %collective-permute-done.30.refs_6_) | copy-start | bytes 884740
  148.8 8.0 %collective-permute-start.32 = (bf16[6144,128]{1,0:T(8,128)(2,1)}, bf16[6144,128]{1,0:T(8,128)(2,1)S(1)}, u32[]{:S(2)}, u32[]{:S(2)}) collective-permute-start(bf16[6144,128]{1,0:T(8,128)(2,1)} %get-tuple-element.180), channel_id=1, source_target_pairs={{0,16},{16,0},{1,17},{17,1},{2,18},{18,2},{3,19},{19,3},{4,20},{20... | collective-permute-start | bytes 4718600 | tf_op jit(solution)/shard_map/ppermute | solution.py:707
  (9 other events, 14.1 us)

commit v5 on v4

--- a/solution.py
+++ b/solution.py
@@ -161,7 +161,7 @@
         store.wait()
 
 
-def chunk_grads(first, parts, by_expert):
+def chunk_grads(first, parts, by_expert, vmem):
     experts, width, features = by_expert.shape
     tokens, columns = parts[0][0][0].shape
     spans = tuple(tuple(piece[1:] for piece in part) for part in parts)
@@ -185,7 +185,7 @@
             pltpu.SemaphoreType.DMA((chunks, 7)),
             pltpu.SemaphoreType.DMA((experts,)),
         ],
-        compiler_params=pltpu.CompilerParams(vmem_limit_bytes=56 * MIB),
+        compiler_params=pltpu.CompilerParams(vmem_limit_bytes=vmem * MIB),
         cost_estimate=pl.CostEstimate(
             flops=8 * chunks * slots * features * (4 * tokens + width),
             bytes_accessed=8 * chunks * (slots + tokens) * features,
@@ -231,7 +231,7 @@
             pltpu.VMEM(shape, jnp.bfloat16),
             pltpu.SemaphoreType.DMA((size + 1,)),
         ],
-        compiler_params=pltpu.CompilerParams(vmem_limit_bytes=10 * MIB),
+        compiler_params=pltpu.CompilerParams(vmem_limit_bytes=8 * MIB),
         cost_estimate=pl.CostEstimate(
             flops=0, bytes_accessed=8 * size * slots * width, transcendentals=0
         ),
@@ -271,7 +271,7 @@
             pltpu.VMEM((count, 3, slots, width), jnp.bfloat16),
             pltpu.SemaphoreType.DMA((count + 3,)),
         ],
-        compiler_params=pltpu.CompilerParams(vmem_limit_bytes=10 * MIB),
+        compiler_params=pltpu.CompilerParams(vmem_limit_bytes=3 * MIB),
         cost_estimate=pl.CostEstimate(
             flops=0, bytes_accessed=12 * count * slots * width, transcendentals=0
         ),
@@ -339,7 +339,7 @@
             pltpu.VMEM((experts, width, features), jnp.bfloat16),
             pltpu.SemaphoreType.DMA((experts, 1 + len(blocks) + count)),
         ],
-        compiler_params=pltpu.CompilerParams(vmem_limit_bytes=16 * MIB),
+        compiler_params=pltpu.CompilerParams(vmem_limit_bytes=9 * MIB),
         cost_estimate=pl.CostEstimate(
             flops=2 * experts * width * slots * features,
             bytes_accessed=2 * experts * (width + slots) * features,
@@ -368,20 +368,22 @@
     tiles = features // LANES
     places = [(span, e) for span in partials for e in range(span[0].shape[0])]
     experts = len(places)
+    unit = tiles * experts
+    stride = unit + 1
     for e, (span, at) in enumerate(places):
         total = span[0][at].astype(jnp.float32)
         for part in span[1:]:
             total = total + part[at].astype(jnp.float32)
         for t in range(tiles):
-            grad[pl.ds(t * experts + e, rows, stride=tiles * experts), :] = total[
+            grad[pl.ds(t * experts + e, rows, stride=stride), :] = total[
                 :, t * LANES : (t + 1) * LANES
             ]
-    block = grad.shape[0]
+    block = rows * unit
     base = pl.multiple_of((first + pl.program_id(0)) * block, block)
-    for start in range(0, block, 128):
-        here = slice(start, start + 128)
-        there = pl.ds(base + start, 128)
-        g = grad[here]
+    for h in range(rows):
+        here = slice(h * unit, (h + 1) * unit)
+        there = pl.ds(base + h * unit, unit)
+        g = grad[h * stride : h * stride + unit]
         one = beta_one * m1[there] + (1.0 - beta_one) * g
         two = beta_two * m2[there] + (1.0 - beta_two) * g * g
         new_m1[here] = one
@@ -416,7 +418,7 @@
             grid=(steps,),
             in_specs=parts + [INSIDE] * 3 + [HBM] * kept,
             out_specs=[line] * 3 + [placed, pl.BlockSpec((flat, LANES), lambda i, at: (i, 0))],
-            scratch_shapes=[pltpu.VMEM((flat, LANES), jnp.float32)],
+            scratch_shapes=[pltpu.VMEM((flat + block, LANES), jnp.float32)],
         ),
         out_shape=[jax.ShapeDtypeStruct(w.shape, jnp.float32)] * 3
         + [
@@ -600,8 +602,8 @@
     near, parts, w_parts = {}, {}, {}
     d_rows, grads, back = {}, {}, {}
 
-    def add_chunks(*chunks):
-        found = chunk_grads(first, [parts[j] for j in chunks], by_expert)
+    def add_chunks(*chunks, vmem=56):
+        found = chunk_grads(first, [parts[j] for j in chunks], by_expert, vmem)
         for j, d_chunk, g_chunk in zip(chunks, *found):
             d_rows[j], grads[j] = d_chunk, g_chunk
 
@@ -639,15 +641,19 @@
             moving["columns"] = columns
         if k == 1:
             moving["cut"] = halves(0)
+            moving["send"] = [w_send[j] for j in range(length)]
         if k == last - 1:
             moving["weights"] = by_expert
             w_parts[1] = move(w_send[1], 1, 0)
         if k == last:
             for j in range(last, 1, -1):
                 w_parts[j] = move(w_send[j], j, 0)
-        moving["done"] = (d_rows, grads, w_parts, w_send)
+        if k != 1:
+            moving["send"] = w_send
+        moving["done"] = (d_rows, grads, w_parts)
         moved = tie(moving)
-        d_rows, grads, w_parts, w_send = moved["done"]
+        d_rows, grads, w_parts = moved["done"]
+        w_send = moved["send"]
         if k == 0:
             columns = moved["columns"]
         if k == 1:
@@ -667,7 +673,7 @@
     back[last - 1] = move(grads[last - 1], 1 - last, 0)
     parts[last] = whole(*near[last]) + tuple((f, 0, half) for f in moved["far"])
     parts[0] = whole(*near[0]) + tuple((f, half, half) for f in moved["far"])
-    add_chunks(last, 0)
+    add_chunks(last, 0, vmem=24)
     back[last] = move(grads[last], -last, 0)
     back[0] = grads[0]
     back = [back[j] for j in range(length)]

time: 160 us -> 175 us (1.094)
  local copies, waits for them, and re-layouts: 16.7 us -> 33.7 us
  Pallas kernels: 62.1 us -> 58.6 us
  waiting for transfers between devices: 36.7 us -> 33.2 us
  starting transfers between devices: 37.4 us -> 40.7 us
    unnamed x80 -> x112, local copies, waits for them, and re-layouts: 13.7 us -> 30 us
    ppermute x29, starting transfers between devices: 36.7 us -> 40.1 us  [move(): return lax.ppermute(block, 'inner', step_perm(size, steps, flip))]
    ppermute x29, waiting for transfers between devices: 35 us -> 31.8 us  [move(): return lax.ppermute(block, 'inner', step_perm(size, steps, flip))]
    pallas_call x2, Pallas kernels: 15.1 us -> 12.4 us  [adam_rows(): pl.pallas_call(functools.partial(adam_kernel, count, owners, kept, first)...]
  transfers between devices with their start and end apart: 33 -> 33, of which waited for: 12 -> 11; matrix products, arithmetic and copies ran while one was open for 9% -> 9% of each run, Pallas kernels for 37% -> 32%
where the time goes in v5:
time: 175 us; the launch traced here: 174 us
  Pallas kernels  58.6 us (33%)
  starting transfers between devices  40.7 us (23%)
  local copies, waits for them, and re-layouts  33.7 us (19%)
  waiting for transfers between devices  33.2 us (19%)
  other arithmetic  4.43 us (3%)
  matrix products  2.23 us (1%)
    ppermute x29, starting transfers between devices, move(): return lax.ppermute(block, 'inner', step_perm(size, steps, flip))  40.1 us
    ppermute x29, waiting for transfers between devices, move(): return lax.ppermute(block, 'inner', step_perm(size, steps, flip))  31.8 us
    unnamed x112, local copies, waits for them, and re-layouts  30 us
    pallas_call x3, Pallas kernels, chunk_grads(): pl.pallas_call(functools.partial(grads_kernel, spans), out_shape=[jax.Sha...  22.3 us
    pallas_call x2, Pallas kernels, adam_rows(): pl.pallas_call(functools.partial(adam_kernel, count, owners, kept, first)...  12.4 us
    pallas_call x2, Pallas kernels, partial_rows(): pl.pallas_call(functools.partial(partial_kernel, start, total), out_shape...  8.96 us
    pallas_call x1, Pallas kernels, finish(): pl.pallas_call(functools.partial(finish_kernel, pieces), out_shape=(jax.S...  6.37 us
    pallas_call x2, Pallas kernels, regroup(): pl.pallas_call(regroup_kernel, out_shape=[jax.ShapeDtypeStruct((count, sl...  3.73 us
  transfers between devices with their start and end apart: 33, of which 11 were waited for; matrix products, arithmetic and copies ran while one was open for 9% of the time, Pallas kernels for 32%

profile of v5, /device:TPU:0, one launch (start us, length us, event | category | flops | bytes accessed | tf_op | source)
XLA Modules:
  0.0 174.2 jit_solution(11481294935261792714)
XLA Ops:
  1.5 1.1 fusion.9.refs_5_
  2.6 3.1 %collective-permute-start = (bf16[128,2176]{1,0:T(8,128)(2,1)S(1)}, bf16[128,2176]{1,0:T(8,128)(2,1)}, u32[]{:S(2)}, u32[]{:S(2)}) collective-permute-start(bf16[128,2176]{1,0:T(8,128)(2,1)S(1)} %fusion.9.refs_5_), channel_id=1, source_target_pairs={{0,4},{1,5},{2,6},{3,7},{4,12},{5,13},{6,14},{7,15},{8,0},{9,1},{1... | collective-permute-start | bytes 1671176 | tf_op jit(solution)/shard_map/ppermute | solution.py:593
  5.7 1.5 collective-permute-start.1
  7.2 1.5 collective-permute-start.2
  11.8 1.9 %fusion.2 = bf16[1536,384]{1,0:T(8,128)(2,1)S(1)} fusion(s32[1024]{0:T(1024)S(1)} %fusion.41, bf16[128,8,384]{2,1,0:T(8,128)(2,1)S(1)} %copy-done.42, f32[128,8]{1,0:T(8,128)S(1)} %copy.50), kind=kOutput, calls=%fused_computation.4 | convolution fusion | flops 1211301888 | bytes 1974272 | tf_op jit(solution)/shard_map/dot_general | solution.py:585
  13.7 5.7 %collective-permute-done.refs_0_ = bf16[128,2176]{1,0:T(8,128)(2,1)} collective-permute-done((bf16[128,2176]{1,0:T(8,128)(2,1)S(1)}, bf16[128,2176]{1,0:T(8,128)(2,1)}, u32[]{:S(2)}, u32[]{:S(2)}) %collective-permute-start) | collective-permute-done | bytes 557088 | tf_op jit(solution)/shard_map/ppermute | solution.py:593
  19.8 1.2 collective-permute-done.2.refs_7_
  21.0 2.6 %collective-permute-start.3 = (bf16[128,2176]{1,0:T(8,128)(2,1)}, bf16[128,2176]{1,0:T(8,128)(2,1)S(1)}, u32[]{:S(2)}, u32[]{:S(2)}) collective-permute-start(bf16[128,2176]{1,0:T(8,128)(2,1)} %collective-permute-done.refs_0_), channel_id=1, source_target_pairs={{0,4},{1,5},{2,6},{3,7},{4,12},{5,13},{6,14},{7,15},{8,0},{9,1},{1... | collective-permute-start | bytes 1671176 | tf_op jit(solution)/shard_map/ppermute | solution.py:593
  24.1 1.5 collective-permute-start.5
  25.7 1.0 slice_bitcast_fusion
  26.6 8.5 %collective-permute-done.3.refs_0_ = bf16[128,2176]{1,0:T(8,128)(2,1)S(1)} collective-permute-done((bf16[128,2176]{1,0:T(8,128)(2,1)}, bf16[128,2176]{1,0:T(8,128)(2,1)S(1)}, u32[]{:S(2)}, u32[]{:S(2)}) %collective-permute-start.3) | collective-permute-done | bytes 557088 | tf_op jit(solution)/shard_map/ppermute | solution.py:593
  35.1 1.3 collective-permute-done.4.refs_1_
  37.2 1.5 collective-permute-start.7
  38.7 1.3 collective-permute-start.9
  40.0 1.0 collective-permute-start.10
  41.5 1.2 collective-permute-start.6
  42.7 4.0 %collective-permute-done.7.refs_3_ = bf16[64,2176]{1,0:T(8,128)(2,1)S(1)} collective-permute-done((bf16[64,2176]{1,0:T(8,128)(2,1)S(1)}, bf16[64,2176]{1,0:T(8,128)(2,1)S(1)}, u32[]{:S(2)}, u32[]{:S(2)}) %collective-permute-start.7) | collective-permute-done | bytes 278560 | tf_op jit(solution)/shard_map/ppermute | solution.py:593
  46.8 1.4 collective-permute-start.8
  48.2 6.2 %copy.65 = bf16[384,4,2048]{2,0,1:T(8,128)(2,1)} copy(bf16[384,4,2048]{2,1,0:T(4,128)(2,1)S(1)} %bitcast.83) | data formatting | bytes 12582912 | tf_op args[4]
  54.3 3.1 %collective-permute-done.8.refs_4_ = bf16[64,2176]{1,0:T(8,128)(2,1)S(1)} collective-permute-done((bf16[64,2176]{1,0:T(8,128)(2,1)S(1)}, bf16[64,2176]{1,0:T(8,128)(2,1)S(1)}, u32[]{:S(2)}, u32[]{:S(2)}) %collective-permute-start.8) | collective-permute-done | bytes 278560 | tf_op jit(solution)/shard_map/ppermute | solution.py:593
  57.5 1.2 copy-done.40
  59.2 1.3 collective-permute-start.16
  60.5 1.5 collective-permute-start.17
  62.0 1.3 collective-permute-start.12
  63.3 1.6 collective-permute-start.13
  65.7 2.6 %collective-permute-done.14.refs_3_ = bf16[64,2176]{1,0:T(8,128)(2,1)S(1)} collective-permute-done((bf16[64,2176]{1,0:T(8,128)(2,1)S(1)}, bf16[64,2176]{1,0:T(8,128)(2,1)S(1)}, u32[]{:S(2)}, u32[]{:S(2)}) %collective-permute-start.14) | collective-permute-done | bytes 278560 | tf_op jit(solution)/shard_map/ppermute | solution.py:593
  68.3 1.3 collective-permute-start.15
  69.6 6.8 %shard_map.127 = (bf16[384,2048]{1,0:T(8,128)(2,1)}, bf16[4,96,384]{2,1,0:T(8,128)(2,1)}) custom-call(s32[1]{0:T(128)} %bitcast.5.first, bf16[128,2176]{1,0:T(8,128)(2,1)} %collective-permute-done.refs_0_, bf16[128,2176]{1,0:T(8,128)(2,1)} %copy-done.35, bf16[128,2176]{1,0:T(8,128)(2,1)} %copy-done.36, bf16[64,2176]{1,0:T(8,128)(2,1)} %copy-done.39, ...), custom_call_target="tpu_custom_call" | custom-call | flops 1409286144 | bytes 3670016 | tf_op jit(solution)/shard_map/pallas_call | solution.py:170
  76.5 0.9 pad_maximum_fusion
  78.2 0.9 pad_maximum_fusion.1
  79.1 1.5 collective-permute-start.20
  80.7 2.8 %collective-permute-start.18 = (bf16[4,96,384]{2,1,0:T(8,128)(2,1)}, bf16[4,96,384]{2,1,0:T(8,128)(2,1)S(1)}, u32[]{:S(2)}, u32[]{:S(2)}) collective-permute-start(bf16[4,96,384]{2,1,0:T(8,128)(2,1)} %get-tuple-element.126), channel_id=1, source_target_pairs={{0,8},{1,9},{2,10},{3,11},{4,0},{5,1},{6,2},{7,3},{8,12},{9,13},{1... | collective-permute-start | bytes 884744 | tf_op jit(solution)/shard_map/ppermute | solution.py:593
  83.5 2.1 %shard_map.130 = (bf16[4,96,384]{2,1,0:T(8,128)(2,1)}, bf16[4,96,384]{2,1,0:T(8,128)(2,1)}, bf16[4,96,384]{2,1,0:T(8,128)(2,1)S(1)}) custom-call(bf16[4,96,384]{2,1,0:T(8,128)(2,1)S(1)} %get-tuple-element.132.refs_0_, bf16[4,96,384]{2,1,0:T(8,128)(2,1)S(1)} %collective-permute-done.6.refs_1_, bf16[4,96,384]{2,1,0:T(8,128)(2,1)S(1)} %collective-permute-done.12.refs_2_, ...), custom_call_target="tpu_custom_call" | custom-call | bytes 1769472 | tf_op jit(solution)/shard_map/pallas_call | solution.py:265
  86.3 1.7 %collective-permute-start.23 = (bf16[4,96,384]{2,1,0:T(8,128)(2,1)}, bf16[4,96,384]{2,1,0:T(8,128)(2,1)}, u32[]{:S(2)}, u32[]{:S(2)}) collective-permute-start(bf16[4,96,384]{2,1,0:T(8,128)(2,1)} %get-tuple-element.152), channel_id=1, source_target_pairs={{0,1},{1,0},{2,3},{3,2},{4,5},{5,4},{6,7},{7,6},{8,9},{9,8},{10,11... | collective-permute-start | bytes 884744 | tf_op jit(solution)/shard_map/ppermute | solution.py:593
  88.1 1.5 collective-permute-start.24
  89.6 6.7 %shard_map.128 = (bf16[384,2048]{1,0:T(8,128)(2,1)}, bf16[4,96,384]{2,1,0:T(8,128)(2,1)}) custom-call(s32[1]{0:T(128)} %bitcast.5.first, bf16[128,2176]{1,0:T(8,128)(2,1)} %copy-done.37, bf16[128,2176]{1,0:T(8,128)(2,1)} %copy-done.33, bf16[128,2176]{1,0:T(8,128)(2,1)} %copy-done.34, bf16[64,2176]{1,0:T(8,128)(2,1)} %copy-done.38, ...), custom_call_target="tpu_custom_call" | custom-call | flops 1409286144 | bytes 3670016 | tf_op jit(solution)/shard_map/pallas_call | solution.py:170
  99.0 2.6 %collective-permute-start.21 = (bf16[4,96,384]{2,1,0:T(8,128)(2,1)}, bf16[4,96,384]{2,1,0:T(8,128)(2,1)}, u32[]{:S(2)}, u32[]{:S(2)}) collective-permute-start(bf16[4,96,384]{2,1,0:T(8,128)(2,1)} %get-tuple-element.146), channel_id=1, source_target_pairs={{0,12},{1,13},{2,14},{3,15},{4,8},{5,9},{6,10},{7,11},{8,4},{9,5},... | collective-permute-start | bytes 884744 | tf_op jit(solution)/shard_map/ppermute | solution.py:593
  101.7 1.1 copy-done.6
  102.7 1.1 copy-done.8
  103.8 1.1 copy-done.10
  104.8 1.1 copy-done.12
  105.9 1.1 copy-done.14
  107.0 1.1 copy-done.16
  108.0 1.1 copy-done.18
  109.1 1.1 copy-done.26
  110.1 8.8 %shard_map.129 = (bf16[384,2048]{1,0:T(8,128)(2,1)S(1)}, bf16[4,96,384]{2,1,0:T(8,128)(2,1)}, bf16[384,2048]{1,0:T(8,128)(2,1)S(1)}, bf16[4,96,384]{2,1,0:T(8,128)(2,1)S(1)}) custom-call(s32[1]{0:T(128)} %bitcast.5.first, bf16[128,2176]{1,0:T(8,128)(2,1)S(1)} %copy-done.26, bf16[128,2176]{1,0:T(8,128)(2,1)S(1)} %copy-done.16, ...), custom_call_target="tpu_custom_call" | custom-call | flops 2818572288 | bytes 7340032 | tf_op jit(solution)/shard_map/pallas_call | solution.py:170
  118.9 1.1 copy-done.3
  120.8 1.1 copy-done.20
  122.0 1.0 copy-done.22
  122.9 1.0 copy-done.24
  123.9 2.3 %shard_map.131.weighted = bf16[4,384,384]{2,1,0:T(8,128)(2,1)S(1)} custom-call(bf16[4,96,384]{2,1,0:T(8,128)(2,1)S(1)} %get-tuple-element.132.refs_0_, bf16[4,96,384]{2,1,0:T(8,128)(2,1)S(1)} %copy-done.20, bf16[4,96,384]{2,1,0:T(8,128)(2,1)S(1)} %copy-done.22, bf16[4,96,384]{2,1,0:T(8,128)(2,1)S(1)} %copy-done.24, ...), custom_call_target="tpu_custom_call" | custom-call | bytes 4718592 | tf_op jit(solution)/shard_map/pallas_call | solution.py:223
  126.2 1.4 copy-done.4
  127.6 4.5 %shard_map.132 = (bf16[2,192,2048]{2,1,0:T(8,128)(2,1)S(1)}, bf16[2,192,2048]{2,1,0:T(8,128)(2,1)S(1)}) custom-call(s32[2]{0:T(128)S(1)} %and_select_fusion.owners, bf16[4,384,384]{2,1,0:T(8,128)(2,1)S(1)} %shard_map.131.weighted, bf16[384,2048]{1,0:T(8,128)(2,1)S(1)} %copy-done.4, bf16[384,2048]{1,0:T(8,128)(2,1)S(1)} %copy-done.1, ...), custom_call_target="tpu_custom_call" | custom-call | flops 1207959552 | bytes 6291456 | tf_op jit(solution)/shard_map/pallas_call | solution.py:330
  132.2 4.5 %shard_map.133 = (bf16[2,192,2048]{2,1,0:T(8,128)(2,1)S(1)}, bf16[2,192,2048]{2,1,0:T(8,128)(2,1)S(1)}) custom-call(s32[2]{0:T(128)S(1)} %and_select_fusion.owners, bf16[4,384,384]{2,1,0:T(8,128)(2,1)S(1)} %shard_map.131.weighted, bf16[384,2048]{1,0:T(8,128)(2,1)S(1)} %copy-done.4, bf16[384,2048]{1,0:T(8,128)(2,1)S(1)} %copy-done.1, ...), custom_call_target="tpu_custom_call" | custom-call | flops 1207959552 | bytes 6291456 | tf_op jit(solution)/shard_map/pallas_call | solution.py:330
  137.2 1.7 shard_map.134
  138.9 1.4 collective-permute-done.27.refs_3_
  140.3 1.8 %collective-permute-start.28 = (bf16[4,96,384]{2,1,0:T(8,128)(2,1)S(1)}, bf16[4,96,384]{2,1,0:T(8,128)(2,1)S(1)}, u32[]{:S(2)}, u32[]{:S(2)}) collective-permute-start(bf16[4,96,384]{2,1,0:T(8,128)(2,1)S(1)} %get-tuple-element.170), channel_id=1, source_target_pairs={{0,1},{1,0},{2,3},{3,2},{4,5},{5,4},{6,7},{7,6},{8,9},{9,8},{10,11... | collective-permute-start | bytes 884744 | tf_op jit(solution)/shard_map/ppermute | solution.py:593
  142.0 1.4 collective-permute-start.29
  143.8 2.8 %copy-done = f32[192,4,2048]{2,1,0:T(4,128)S(1)} copy-done((f32[192,4,2048]{2,1,0:T(4,128)S(1)}, f32[192,4,2048]{2,1,0:T(4,128)}, u32[]{:S(2)}) %copy-start) | copy-done | bytes 6291480
  146.6 6.2 %shard_map.136 = (f32[12288,128]{1,0:T(8,128)}, f32[12288,128]{1,0:T(8,128)}, f32[12288,128]{1,0:T(8,128)}, bf16[24576,128]{1,0:T(8,128)(2,1)}, bf16[6144,128]{1,0:T(8,128)(2,1)}) custom-call(s32[1]{0:T(128)} %bitcast.12.at, bf16[2,192,2048]{2,1,0:T(8,128)(2,1)S(1)} %get-tuple-element.178.refs_0_, bf16[2,192,2048]{2,1,0:T(8,128)(2,1)S(1)} %collective-permute-done.26.refs_1_, ...), custom_call_target="tpu_custom_call" | custom-call | flops 15728640 | bytes 15728640 | tf_op jit(solution)/shard_map/pallas_call | solution.py:414
  152.8 4.6 %collective-permute-done.29.refs_5_ = bf16[4,96,384]{2,1,0:T(8,128)(2,1)S(1)} collective-permute-done((bf16[4,96,384]{2,1,0:T(8,128)(2,1)S(1)}, bf16[4,96,384]{2,1,0:T(8,128)(2,1)S(1)}, u32[]{:S(2)}, u32[]{:S(2)}) %collective-permute-start.29) | collective-permute-done | bytes 294944 | tf_op jit(solution)/shard_map/ppermute | solution.py:593
  157.4 6.2 %shard_map.137 = (f32[12288,128]{1,0:T(8,128)}, f32[12288,128]{1,0:T(8,128)}, f32[12288,128]{1,0:T(8,128)}, bf16[24576,128]{1,0:T(8,128)(2,1)}, bf16[6144,128]{1,0:T(8,128)(2,1)}) custom-call(s32[1]{0:T(128)} %bitcast.12.at, ...), custom_call_target="tpu_custom_call", output_to_operand_aliasing={{0}: (8, {}), {1}: (9, {}), {2}: (10, {}), {3}: (11, {})} | custom-call | flops 15728640 | bytes 15728640 | tf_op jit(solution)/shard_map/pallas_call | solution.py:414
  163.7 6.4 %shard_map.135 = (bf16[1024,384]{1,0:T(8,128)(2,1)}, f32[8,1024]{1,0:T(8,128)}) custom-call(f32[8,128]{1,0:T(8,128)} %fusion.27.target, f32[8,128]{1,0:T(8,128)} %reshape.249.probs, bf16[1024,384]{1,0:T(8,128)(2,1)} %bitcast.85, bf16[4,96,384]{2,1,0:T(8,128)(2,1)} %copy-done.29, bf16[4,96,384]{2,1,0:T(8,128)(2,1)} %copy-done.27, ...), custom_call_target="tpu_custom_call" | custom-call | flops 1207959552 | bytes 3145728 | tf_op jit(solution)/shard_map/pallas_call | solution.py:526
  171.6 2.7 %shard_map.138 = bf16[24576,128]{1,0:T(8,128)(2,1)} custom-call(s32[1]{0:T(128)} %bitcast.37.at, bf16[6144,128]{1,0:T(8,128)(2,1)S(1)} %collective-permute-done.31.low, bf16[6144,128]{1,0:T(8,128)(2,1)S(1)} %collective-permute-done.32.high, bf16[24576,128]{1,0:T(8,128)(2,1)} %get-tuple-element.191.full), custom_call_target="tpu_custom_call", output_to_operand_aliasing={{}: (3, {})} | custom-call | bytes 6291456 | tf_op jit(solution)/shard_map/pallas_call | solution.py:457
  (158 shorter events, 15.1 us)
Async XLA Ops:
  0.6 10.3 %copy-start.41 = (f32[128,8]{0,1:T(8,128)S(1)}, f32[128,8]{0,1:T(8,128)}, u32[]{:S(2)}) copy-start(f32[128,8]{0,1:T(8,128)} %param.10) | copy-start | bytes 12292
  0.6 11.2 %copy-start.42 = (bf16[128,8,384]{2,1,0:T(8,128)(2,1)S(1)}, bf16[128,8,384]{2,1,0:T(8,128)(2,1)}, u32[]{:S(2)}) copy-start(bf16[128,8,384]{2,1,0:T(8,128)(2,1)} %param.9) | copy-start | bytes 2359300
  2.6 11.1 %copy-start.9 = (bf16[128,2176]{1,0:T(8,128)(2,1)}, bf16[128,2176]{1,0:T(8,128)(2,1)S(1)}, u32[]{:S(2)}) copy-start(bf16[128,2176]{1,0:T(8,128)(2,1)S(1)} %fusion.9.refs_5_) | copy-start | bytes 1671172
  2.6 16.8 %collective-permute-start = (bf16[128,2176]{1,0:T(8,128)(2,1)S(1)}, bf16[128,2176]{1,0:T(8,128)(2,1)}, u32[]{:S(2)}, u32[]{:S(2)}) collective-permute-start(bf16[128,2176]{1,0:T(8,128)(2,1)S(1)} %fusion.9.refs_5_), channel_id=1, source_target_pairs={{0,4},{1,5},{2,6},{3,7},{4,12},{5,13},{6,14},{7,15},{8,0},{9,1},{1... | collective-permute-start | bytes 1671176 | tf_op jit(solution)/shard_map/ppermute | solution.py:593
  5.7 14.1 %collective-permute-start.1 = (bf16[128,2176]{1,0:T(8,128)(2,1)S(1)}, bf16[128,2176]{1,0:T(8,128)(2,1)S(1)}, u32[]{:S(2)}, u32[]{:S(2)}) collective-permute-start(bf16[128,2176]{1,0:T(8,128)(2,1)S(1)} %fusion.9.refs_5_), channel_id=1, source_target_pairs={{0,1},{1,0},{2,3},{3,2},{4,5},{5,4},{6,7},{7,6},{8,9},{9,8},{10,11... | collective-permute-start | bytes 1671176 | tf_op jit(solution)/shard_map/ppermute | solution.py:593
  7.2 13.8 %collective-permute-start.2 = (bf16[128,2176]{1,0:T(8,128)(2,1)S(1)}, bf16[128,2176]{1,0:T(8,128)(2,1)S(1)}, u32[]{:S(2)}, u32[]{:S(2)}) collective-permute-start(bf16[128,2176]{1,0:T(8,128)(2,1)S(1)} %fusion.9.refs_5_), channel_id=1, source_target_pairs={{0,2},{1,3},{2,0},{3,1},{4,6},{5,7},{6,4},{7,5},{8,10},{9,11},{10,... | collective-permute-start | bytes 1671176 | tf_op jit(solution)/shard_map/ppermute | solution.py:593
  11.8 36.4 %slice-start.8 = ((s8[6291456]{0:T(1024)(128)(4,1)}), s8[4194304]{0:T(1024)(128)(4,1)S(1)}, s32[]{:S(2)}) async-start(s8[6291456]{0:T(1024)(128)(4,1)} %bitcast.82), calls=%async_computation.8 | async-start | bytes 8388608
  11.8 36.4 %slice-start.9 = ((s8[6291456]{0:T(1024)(128)(4,1)}), s8[2097152]{0:T(1024)(128)(4,1)S(1)}, s32[]{:S(2)}) async-start(s8[6291456]{0:T(1024)(128)(4,1)} %bitcast.82), calls=%async_computation.9 | async-start | bytes 4194304
  19.8 6.8 %copy-start.11 = (bf16[128,2176]{1,0:T(8,128)(2,1)}, bf16[128,2176]{1,0:T(8,128)(2,1)S(1)}, u32[]{:S(2)}) copy-start(bf16[128,2176]{1,0:T(8,128)(2,1)S(1)} %collective-permute-done.1.refs_6_) | copy-start | bytes 1671172
  21.0 5.6 %copy-start.13 = (bf16[128,2176]{1,0:T(8,128)(2,1)}, bf16[128,2176]{1,0:T(8,128)(2,1)S(1)}, u32[]{:S(2)}) copy-start(bf16[128,2176]{1,0:T(8,128)(2,1)S(1)} %collective-permute-done.2.refs_7_) | copy-start | bytes 1671172
  21.0 14.1 %collective-permute-start.3 = (bf16[128,2176]{1,0:T(8,128)(2,1)}, bf16[128,2176]{1,0:T(8,128)(2,1)S(1)}, u32[]{:S(2)}, u32[]{:S(2)}) collective-permute-start(bf16[128,2176]{1,0:T(8,128)(2,1)} %collective-permute-done.refs_0_), channel_id=1, source_target_pairs={{0,4},{1,5},{2,6},{3,7},{4,12},{5,13},{6,14},{7,15},{8,0},{9,1},{1... | collective-permute-start | bytes 1671176 | tf_op jit(solution)/shard_map/ppermute | solution.py:593
  23.6 12.8 %collective-permute-start.4 = (bf16[128,2176]{1,0:T(8,128)(2,1)}, bf16[128,2176]{1,0:T(8,128)(2,1)S(1)}, u32[]{:S(2)}, u32[]{:S(2)}) collective-permute-start(bf16[128,2176]{1,0:T(8,128)(2,1)} %collective-permute-done.refs_0_), channel_id=1, source_target_pairs={{0,1},{1,0},{2,3},{3,2},{4,5},{5,4},{6,7},{7,6},{8,9},{9,8},{10,11... | collective-permute-start | bytes 1671176 | tf_op jit(solution)/shard_map/ppermute | solution.py:593
  24.1 12.6 %collective-permute-start.5 = (bf16[128,2176]{1,0:T(8,128)(2,1)}, bf16[128,2176]{1,0:T(8,128)(2,1)S(1)}, u32[]{:S(2)}, u32[]{:S(2)}) collective-permute-start(bf16[128,2176]{1,0:T(8,128)(2,1)} %collective-permute-done.refs_0_), channel_id=1, source_target_pairs={{0,2},{1,3},{2,0},{3,1},{4,6},{5,7},{6,4},{7,5},{8,10},{9,11},{10,... | collective-permute-start | bytes 1671176 | tf_op jit(solution)/shard_map/ppermute | solution.py:593
  35.1 19.2 %copy-start.37 = (bf16[128,2176]{1,0:T(8,128)(2,1)}, bf16[128,2176]{1,0:T(8,128)(2,1)S(1)}, u32[]{:S(2)}) copy-start(bf16[128,2176]{1,0:T(8,128)(2,1)S(1)} %collective-permute-done.3.refs_0_) | copy-start | bytes 1671172
  36.8 17.6 %copy-start.36 = (bf16[128,2176]{1,0:T(8,128)(2,1)}, bf16[128,2176]{1,0:T(8,128)(2,1)S(1)}, u32[]{:S(2)}) copy-start(bf16[128,2176]{1,0:T(8,128)(2,1)S(1)} %collective-permute-done.5.refs_2_) | copy-start | bytes 1671172
  37.2 9.5 %collective-permute-start.7 = (bf16[64,2176]{1,0:T(8,128)(2,1)S(1)}, bf16[64,2176]{1,0:T(8,128)(2,1)S(1)}, u32[]{:S(2)}, u32[]{:S(2)}) collective-permute-start(bf16[64,2176]{1,0:T(8,128)(2,1)S(1)} %slice.45), channel_id=1, source_target_pairs={{0,2},{1,3},{2,0},{3,1},{4,6},{5,7},{6,4},{7,5},{8,10},{9,11},{10,... | collective-permute-start | bytes 835592 | tf_op jit(solution)/shard_map/ppermute | solution.py:593
  38.7 18.7 %collective-permute-start.9 = (bf16[128,2176]{1,0:T(8,128)(2,1)S(1)}, bf16[128,2176]{1,0:T(8,128)(2,1)S(1)}, u32[]{:S(2)}, u32[]{:S(2)}) collective-permute-start(bf16[128,2176]{1,0:T(8,128)(2,1)S(1)} %collective-permute-done.3.refs_0_), channel_id=1, source_target_pairs={{0,4},{1,5},{2,6},{3,7},{4,12},{5,13},{6,14},{7,15},{8,0},{9,1},{1... | collective-permute-start | bytes 1671176 | tf_op jit(solution)/shard_map/ppermute | solution.py:593
  40.0 17.5 %collective-permute-start.10 = (bf16[128,2176]{1,0:T(8,128)(2,1)S(1)}, bf16[128,2176]{1,0:T(8,128)(2,1)S(1)}, u32[]{:S(2)}, u32[]{:S(2)}) collective-permute-start(bf16[128,2176]{1,0:T(8,128)(2,1)S(1)} %collective-permute-done.3.refs_0_), channel_id=1, source_target_pairs={{0,1},{1,0},{2,3},{3,2},{4,5},{5,4},{6,7},{7,6},{8,9},{9,8},{10,11... | collective-permute-start | bytes 1671176 | tf_op jit(solution)/shard_map/ppermute | solution.py:593
  41.0 16.5 %collective-permute-start.11 = (bf16[128,2176]{1,0:T(8,128)(2,1)S(1)}, bf16[128,2176]{1,0:T(8,128)(2,1)S(1)}, u32[]{:S(2)}, u32[]{:S(2)}) collective-permute-start(bf16[128,2176]{1,0:T(8,128)(2,1)S(1)} %collective-permute-done.3.refs_0_), channel_id=1, source_target_pairs={{0,2},{1,3},{2,0},{3,1},{4,6},{5,7},{6,4},{7,5},{8,10},{9,11},{10,... | collective-permute-start | bytes 1671176 | tf_op jit(solution)/shard_map/ppermute | solution.py:593
  41.5 15.9 %collective-permute-start.6 = (bf16[4,96,384]{2,1,0:T(8,128)(2,1)S(1)}, bf16[4,96,384]{2,1,0:T(8,128)(2,1)S(1)}, u32[]{:S(2)}, u32[]{:S(2)}) collective-permute-start(bf16[4,96,384]{2,1,0:T(8,128)(2,1)S(1)} %get-tuple-element.105), channel_id=1, source_target_pairs={{0,4},{1,5},{2,6},{3,7},{4,12},{5,13},{6,14},{7,15},{8,0},{9,1},{1... | collective-permute-start | bytes 884744 | tf_op jit(solution)/shard_map/ppermute | solution.py:593
  46.8 7.6 %copy-start.39 = (bf16[64,2176]{1,0:T(8,128)(2,1)}, bf16[64,2176]{1,0:T(8,128)(2,1)S(1)}, u32[]{:S(2)}) copy-start(bf16[64,2176]{1,0:T(8,128)(2,1)S(1)} %collective-permute-done.7.refs_3_) | copy-start | bytes 835588
  46.8 10.7 %collective-permute-start.8 = (bf16[64,2176]{1,0:T(8,128)(2,1)S(1)}, bf16[64,2176]{1,0:T(8,128)(2,1)S(1)}, u32[]{:S(2)}, u32[]{:S(2)}) collective-permute-start(bf16[64,2176]{1,0:T(8,128)(2,1)S(1)} %slice.46), channel_id=1, source_target_pairs={{0,1},{1,0},{2,3},{3,2},{4,5},{5,4},{6,7},{7,6},{8,9},{9,8},{10,11... | collective-permute-start | bytes 835592 | tf_op jit(solution)/shard_map/ppermute | solution.py:593
  57.4 26.1 %copy-start.19 = (bf16[4,96,384]{2,1,0:T(8,128)(2,1)}, bf16[4,96,384]{2,1,0:T(8,128)(2,1)S(1)}, u32[]{:S(2)}) copy-start(bf16[4,96,384]{2,1,0:T(8,128)(2,1)S(1)} %collective-permute-done.6.refs_1_) | copy-start | bytes 884740
  57.5 18.9 %copy-start.25 = (bf16[128,2176]{1,0:T(8,128)(2,1)}, bf16[128,2176]{1,0:T(8,128)(2,1)S(1)}, u32[]{:S(2)}) copy-start(bf16[128,2176]{1,0:T(8,128)(2,1)S(1)} %collective-permute-done.9.refs_0_) | copy-start | bytes 1671172
  57.5 3.0 %copy-start.33 = (bf16[128,2176]{1,0:T(8,128)(2,1)}, bf16[128,2176]{1,0:T(8,128)(2,1)S(1)}, u32[]{:S(2)}) copy-start(bf16[128,2176]{1,0:T(8,128)(2,1)S(1)} %collective-permute-done.10.refs_1_) | copy-start | bytes 1671172
  57.5 7.5 %copy-start.34 = (bf16[128,2176]{1,0:T(8,128)(2,1)}, bf16[128,2176]{1,0:T(8,128)(2,1)S(1)}, u32[]{:S(2)}) copy-start(bf16[128,2176]{1,0:T(8,128)(2,1)S(1)} %collective-permute-done.11.refs_2_) | copy-start | bytes 1671172
  58.7 9.6 %collective-permute-start.14 = (bf16[64,2176]{1,0:T(8,128)(2,1)S(1)}, bf16[64,2176]{1,0:T(8,128)(2,1)S(1)}, u32[]{:S(2)}, u32[]{:S(2)}) collective-permute-start(bf16[64,2176]{1,0:T(8,128)(2,1)S(1)} %slice.47), channel_id=1, source_target_pairs={{0,2},{1,3},{2,0},{3,1},{4,6},{5,7},{6,4},{7,5},{8,10},{9,11},{10,... | collective-permute-start | bytes 835592 | tf_op jit(solution)/shard_map/ppermute | solution.py:593
  59.2 17.2 %collective-permute-start.16 = (bf16[128,2176]{1,0:T(8,128)(2,1)S(1)}, bf16[128,2176]{1,0:T(8,128)(2,1)S(1)}, u32[]{:S(2)}, u32[]{:S(2)}) collective-permute-start(bf16[128,2176]{1,0:T(8,128)(2,1)S(1)} %collective-permute-done.9.refs_0_), channel_id=1, source_target_pairs={{0,1},{1,0},{2,3},{3,2},{4,5},{5,4},{6,7},{7,6},{8,9},{9,8},{10,11... | collective-permute-start | bytes 1671176 | tf_op jit(solution)/shard_map/ppermute | solution.py:593
  60.5 16.0 %collective-permute-start.17 = (bf16[128,2176]{1,0:T(8,128)(2,1)S(1)}, bf16[128,2176]{1,0:T(8,128)(2,1)S(1)}, u32[]{:S(2)}, u32[]{:S(2)}) collective-permute-start(bf16[128,2176]{1,0:T(8,128)(2,1)S(1)} %collective-permute-done.9.refs_0_), channel_id=1, source_target_pairs={{0,2},{1,3},{2,0},{3,1},{4,6},{5,7},{6,4},{7,5},{8,10},{9,11},{10,... | collective-permute-start | bytes 1671176 | tf_op jit(solution)/shard_map/ppermute | solution.py:593
  62.0 14.4 %collective-permute-start.12 = (bf16[4,96,384]{2,1,0:T(8,128)(2,1)}, bf16[4,96,384]{2,1,0:T(8,128)(2,1)S(1)}, u32[]{:S(2)}, u32[]{:S(2)}) collective-permute-start(bf16[4,96,384]{2,1,0:T(8,128)(2,1)} %get-tuple-element.119), channel_id=1, source_target_pairs={{0,12},{1,13},{2,14},{3,15},{4,8},{5,9},{6,10},{7,11},{8,4},{9,5},... | collective-permute-start | bytes 884744 | tf_op jit(solution)/shard_map/ppermute | solution.py:593
  63.3 13.1 %collective-permute-start.13 = (bf16[4,96,384]{2,1,0:T(8,128)(2,1)}, bf16[4,96,384]{2,1,0:T(8,128)(2,1)S(1)}, u32[]{:S(2)}, u32[]{:S(2)}) collective-permute-start(bf16[4,96,384]{2,1,0:T(8,128)(2,1)} %get-tuple-element.120), channel_id=1, source_target_pairs={{0,8},{1,9},{2,10},{3,11},{4,0},{5,1},{6,2},{7,3},{8,12},{9,13},{1... | collective-permute-start | bytes 884744 | tf_op jit(solution)/shard_map/ppermute | solution.py:593
  68.3 8.1 %collective-permute-start.15 = (bf16[64,2176]{1,0:T(8,128)(2,1)}, bf16[64,2176]{1,0:T(8,128)(2,1)}, u32[]{:S(2)}, u32[]{:S(2)}) collective-permute-start(bf16[64,2176]{1,0:T(8,128)(2,1)} %slice.48), channel_id=1, source_target_pairs={{0,1},{1,0},{2,3},{3,2},{4,5},{5,4},{6,7},{7,6},{8,9},{9,8},{10,11... | collective-permute-start | bytes 835592 | tf_op jit(solution)/shard_map/ppermute | solution.py:593
  69.6 6.9 %slice-start.6 = ((bf16[128,2176]{1,0:T(8,128)(2,1)}), bf16[64,2176]{1,0:T(8,128)(2,1)S(1)}, s32[]{:S(2)}) async-start(bf16[128,2176]{1,0:T(8,128)(2,1)} %copy-done.11), calls=%async_computation.6 | async-start | bytes 557056 | tf_op jit(solution)/shard_map/slice | solution.py:618
  76.4 7.1 %copy-start.21 = (bf16[4,96,384]{2,1,0:T(8,128)(2,1)}, bf16[4,96,384]{2,1,0:T(8,128)(2,1)S(1)}, u32[]{:S(2)}) copy-start(bf16[4,96,384]{2,1,0:T(8,128)(2,1)S(1)} %collective-permute-done.12.refs_2_) | copy-start | bytes 884740
  76.4 7.1 %copy-start.23 = (bf16[4,96,384]{2,1,0:T(8,128)(2,1)}, bf16[4,96,384]{2,1,0:T(8,128)(2,1)S(1)}, u32[]{:S(2)}) copy-start(bf16[4,96,384]{2,1,0:T(8,128)(2,1)S(1)} %collective-permute-done.13.refs_3_) | copy-start | bytes 884740
  77.4 20.0 %collective-permute-start.19 = (bf16[128,2176]{1,0:T(8,128)(2,1)}, bf16[128,2176]{1,0:T(8,128)(2,1)S(1)}, u32[]{:S(2)}, u32[]{:S(2)}) collective-permute-start(bf16[128,2176]{1,0:T(8,128)(2,1)} %pad_maximum_fusion), channel_id=1, source_target_pairs={{0,2},{1,3},{2,0},{3,1},{4,6},{5,7},{6,4},{7,5},{8,10},{9,11},{10,... | collective-permute-start | bytes 1671176 | tf_op jit(solution)/shard_map/ppermute | solution.py:593
  78.2 23.5 %slice-start = ((s8[6291456]{0:T(1024)(128)(4,1)}), s8[4194304]{0:T(1024)(128)(4,1)S(1)}, s32[]{:S(2)}) async-start(s8[6291456]{0:T(1024)(128)(4,1)} %bitcast.65), calls=%async_computation | async-start | bytes 8388608
  79.1 19.1 %collective-permute-start.20 = (bf16[128,2176]{1,0:T(8,128)(2,1)}, bf16[128,2176]{1,0:T(8,128)(2,1)S(1)}, u32[]{:S(2)}, u32[]{:S(2)}) collective-permute-start(bf16[128,2176]{1,0:T(8,128)(2,1)} %pad_maximum_fusion.1), channel_id=1, source_target_pairs={{0,1},{1,0},{2,3},{3,2},{4,5},{5,4},{6,7},{7,6},{8,9},{9,8},{10,11... | collective-permute-start | bytes 1671176 | tf_op jit(solution)/shard_map/ppermute | solution.py:593
  80.7 15.7 %collective-permute-start.18 = (bf16[4,96,384]{2,1,0:T(8,128)(2,1)}, bf16[4,96,384]{2,1,0:T(8,128)(2,1)S(1)}, u32[]{:S(2)}, u32[]{:S(2)}) collective-permute-start(bf16[4,96,384]{2,1,0:T(8,128)(2,1)} %get-tuple-element.126), channel_id=1, source_target_pairs={{0,8},{1,9},{2,10},{3,11},{4,0},{5,1},{6,2},{7,3},{8,12},{9,13},{1... | collective-permute-start | bytes 884744 | tf_op jit(solution)/shard_map/ppermute | solution.py:593
  86.3 34.5 %collective-permute-start.23 = (bf16[4,96,384]{2,1,0:T(8,128)(2,1)}, bf16[4,96,384]{2,1,0:T(8,128)(2,1)}, u32[]{:S(2)}, u32[]{:S(2)}) collective-permute-start(bf16[4,96,384]{2,1,0:T(8,128)(2,1)} %get-tuple-element.152), channel_id=1, source_target_pairs={{0,1},{1,0},{2,3},{3,2},{4,5},{5,4},{6,7},{7,6},{8,9},{9,8},{10,11... | collective-permute-start | bytes 884744 | tf_op jit(solution)/shard_map/ppermute | solution.py:593
  88.1 13.6 %slice-start.1 = ((s8[6291456]{0:T(1024)(128)(4,1)}), s8[2097152]{0:T(1024)(128)(4,1)S(1)}, s32[]{:S(2)}) async-start(s8[6291456]{0:T(1024)(128)(4,1)} %bitcast.65), calls=%async_computation.1 | async-start | bytes 4194304
  88.1 32.7 %collective-permute-start.24 = (bf16[4,96,384]{2,1,0:T(8,128)(2,1)}, bf16[4,96,384]{2,1,0:T(8,128)(2,1)}, u32[]{:S(2)}, u32[]{:S(2)}) collective-permute-start(bf16[4,96,384]{2,1,0:T(8,128)(2,1)} %get-tuple-element.153), channel_id=1, source_target_pairs={{0,2},{1,3},{2,0},{3,1},{4,6},{5,7},{6,4},{7,5},{8,10},{9,11},{10,... | collective-permute-start | bytes 884744 | tf_op jit(solution)/shard_map/ppermute | solution.py:593
  97.1 23.8 %collective-permute-start.25 = (bf16[4,96,384]{2,1,0:T(8,128)(2,1)}, bf16[4,96,384]{2,1,0:T(8,128)(2,1)}, u32[]{:S(2)}, u32[]{:S(2)}) collective-permute-start(bf16[4,96,384]{2,1,0:T(8,128)(2,1)} %copy-done.32), channel_id=1, source_target_pairs={{0,3},{1,2},{2,1},{3,0},{4,7},{5,6},{6,5},{7,4},{8,11},{9,10},{10,... | collective-permute-start | bytes 884744 | tf_op jit(solution)/shard_map/ppermute | solution.py:593
  99.0 33.1 %collective-permute-start.21 = (bf16[4,96,384]{2,1,0:T(8,128)(2,1)}, bf16[4,96,384]{2,1,0:T(8,128)(2,1)}, u32[]{:S(2)}, u32[]{:S(2)}) collective-permute-start(bf16[4,96,384]{2,1,0:T(8,128)(2,1)} %get-tuple-element.146), channel_id=1, source_target_pairs={{0,12},{1,13},{2,14},{3,15},{4,8},{5,9},{6,10},{7,11},{8,4},{9,5},... | collective-permute-start | bytes 884744 | tf_op jit(solution)/shard_map/ppermute | solution.py:593
  120.8 11.4 %collective-permute-start.22 = (bf16[4,96,384]{2,1,0:T(8,128)(2,1)}, bf16[4,96,384]{2,1,0:T(8,128)(2,1)S(1)}, u32[]{:S(2)}, u32[]{:S(2)}) collective-permute-start(bf16[4,96,384]{2,1,0:T(8,128)(2,1)} %get-tuple-element.147), channel_id=1, source_target_pairs={{0,4},{1,5},{2,6},{3,7},{4,12},{5,13},{6,14},{7,15},{8,0},{9,1},{1... | collective-permute-start | bytes 884744 | tf_op jit(solution)/shard_map/ppermute | solution.py:593
  120.8 5.4 %copy-start.1 = (bf16[384,2048]{1,0:T(8,128)(2,1)S(1)}, bf16[384,2048]{1,0:T(8,128)(2,1)}, u32[]{:S(2)}) copy-start(bf16[384,2048]{1,0:T(8,128)(2,1)} %get-tuple-element.158.refs_1_) | copy-start | bytes 4718596
  120.8 5.4 %copy-start.2 = (bf16[384,2048]{1,0:T(8,128)(2,1)S(1)}, bf16[384,2048]{1,0:T(8,128)(2,1)}, u32[]{:S(2)}) copy-start(bf16[384,2048]{1,0:T(8,128)(2,1)} %get-tuple-element.159.refs_2_) | copy-start | bytes 4718596
  123.9 19.9 %slice-start.4 = ((s8[6291456]{0:T(1024)(128)(4,1)}), s8[4194304]{0:T(1024)(128)(4,1)S(1)}, s32[]{:S(2)}) async-start(s8[6291456]{0:T(1024)(128)(4,1)} %bitcast.72), calls=%async_computation.4 | async-start | bytes 8388608
  127.6 16.2 %slice-start.2 = ((s8[6291456]{0:T(1024)(128)(4,1)}), s8[4194304]{0:T(1024)(128)(4,1)S(1)}, s32[]{:S(2)}) async-start(s8[6291456]{0:T(1024)(128)(4,1)} %bitcast.68), calls=%async_computation.2 | async-start | bytes 8388608
  127.6 16.2 %slice-start.5 = ((s8[6291456]{0:T(1024)(128)(4,1)}), s8[2097152]{0:T(1024)(128)(4,1)S(1)}, s32[]{:S(2)}) async-start(s8[6291456]{0:T(1024)(128)(4,1)} %bitcast.72), calls=%async_computation.5 | async-start | bytes 4194304
  132.1 6.8 %collective-permute-start.26 = (bf16[2,192,2048]{2,1,0:T(8,128)(2,1)S(1)}, bf16[2,192,2048]{2,1,0:T(8,128)(2,1)S(1)}, u32[]{:S(2)}, u32[]{:S(2)}) collective-permute-start(bf16[2,192,2048]{2,1,0:T(8,128)(2,1)S(1)} %get-tuple-element.156), channel_id=1, source_target_pairs={{0,16},{16,0},{1,17},{17,1},{2,18},{18,2},{3,19},{19,3},{4,20},{20... | collective-permute-start | bytes 4718600 | tf_op jit(solution)/shard_map/ppermute | solution.py:695
  132.2 5.1 %copy-start.31 = (bf16[4,96,384]{2,1,0:T(8,128)(2,1)}, bf16[4,96,384]{2,1,0:T(8,128)(2,1)S(1)}, u32[]{:S(2)}) copy-start(bf16[4,96,384]{2,1,0:T(8,128)(2,1)S(1)} %collective-permute-done.22.refs_3_) | copy-start | bytes 884740
  132.2 5.1 %copy-start.28 = (bf16[4,96,384]{2,1,0:T(8,128)(2,1)S(1)}, bf16[4,96,384]{2,1,0:T(8,128)(2,1)}, u32[]{:S(2)}) copy-start(bf16[4,96,384]{2,1,0:T(8,128)(2,1)} %copy-done.27) | copy-start | bytes 884740
  132.2 5.1 %copy-start.30 = (bf16[4,96,384]{2,1,0:T(8,128)(2,1)S(1)}, bf16[4,96,384]{2,1,0:T(8,128)(2,1)}, u32[]{:S(2)}) copy-start(bf16[4,96,384]{2,1,0:T(8,128)(2,1)} %copy-done.29) | copy-start | bytes 884740
  132.2 11.6 %slice-start.3 = ((s8[6291456]{0:T(1024)(128)(4,1)}), s8[2097152]{0:T(1024)(128)(4,1)S(1)}, s32[]{:S(2)}) async-start(s8[6291456]{0:T(1024)(128)(4,1)} %bitcast.68), calls=%async_computation.3 | async-start | bytes 4194304
  136.7 3.6 %collective-permute-start.27 = (bf16[2,192,2048]{2,1,0:T(8,128)(2,1)S(1)}, bf16[2,192,2048]{2,1,0:T(8,128)(2,1)S(1)}, u32[]{:S(2)}, u32[]{:S(2)}) collective-permute-start(bf16[2,192,2048]{2,1,0:T(8,128)(2,1)S(1)} %get-tuple-element.162), channel_id=1, source_target_pairs={{0,16},{16,0},{1,17},{17,1},{2,18},{18,2},{3,19},{19,3},{4,20},{20... | collective-permute-start | bytes 4718600 | tf_op jit(solution)/shard_map/ppermute | solution.py:695
  140.3 12.5 %collective-permute-start.28 = (bf16[4,96,384]{2,1,0:T(8,128)(2,1)S(1)}, bf16[4,96,384]{2,1,0:T(8,128)(2,1)S(1)}, u32[]{:S(2)}, u32[]{:S(2)}) collective-permute-start(bf16[4,96,384]{2,1,0:T(8,128)(2,1)S(1)} %get-tuple-element.170), channel_id=1, source_target_pairs={{0,1},{1,0},{2,3},{3,2},{4,5},{5,4},{6,7},{7,6},{8,9},{9,8},{10,11... | collective-permute-start | bytes 884744 | tf_op jit(solution)/shard_map/ppermute | solution.py:593
  142.0 15.3 %collective-permute-start.29 = (bf16[4,96,384]{2,1,0:T(8,128)(2,1)S(1)}, bf16[4,96,384]{2,1,0:T(8,128)(2,1)S(1)}, u32[]{:S(2)}, u32[]{:S(2)}) collective-permute-start(bf16[4,96,384]{2,1,0:T(8,128)(2,1)S(1)} %get-tuple-element.171), channel_id=1, source_target_pairs={{0,2},{1,3},{2,0},{3,1},{4,6},{5,7},{6,4},{7,5},{8,10},{9,11},{10,... | collective-permute-start | bytes 884744 | tf_op jit(solution)/shard_map/ppermute | solution.py:593
  143.4 13.9 %collective-permute-start.30 = (bf16[4,96,384]{2,1,0:T(8,128)(2,1)S(1)}, bf16[4,96,384]{2,1,0:T(8,128)(2,1)S(1)}, u32[]{:S(2)}, u32[]{:S(2)}) collective-permute-start(bf16[4,96,384]{2,1,0:T(8,128)(2,1)S(1)} %get-tuple-element.172), channel_id=1, source_target_pairs={{0,3},{1,2},{2,1},{3,0},{4,7},{5,6},{6,5},{7,4},{8,11},{9,10},{10,... | collective-permute-start | bytes 884744 | tf_op jit(solution)/shard_map/ppermute | solution.py:593
  152.7 18.8 %collective-permute-start.31 = (bf16[6144,128]{1,0:T(8,128)(2,1)}, bf16[6144,128]{1,0:T(8,128)(2,1)S(1)}, u32[]{:S(2)}, u32[]{:S(2)}) collective-permute-start(bf16[6144,128]{1,0:T(8,128)(2,1)} %get-tuple-element.189), channel_id=1, source_target_pairs={{0,16},{16,0},{1,17},{17,1},{2,18},{18,2},{3,19},{19,3},{4,20},{20... | collective-permute-start | bytes 4718600 | tf_op jit(solution)/shard_map/ppermute | solution.py:713
  152.8 10.8 %copy-start.43 = (bf16[4,96,384]{2,1,0:T(8,128)(2,1)}, bf16[4,96,384]{2,1,0:T(8,128)(2,1)S(1)}, u32[]{:S(2)}) copy-start(bf16[4,96,384]{2,1,0:T(8,128)(2,1)S(1)} %collective-permute-done.28.refs_4_) | copy-start | bytes 884740
  157.3 6.2 %copy-start.44 = (bf16[4,96,384]{2,1,0:T(8,128)(2,1)}, bf16[4,96,384]{2,1,0:T(8,128)(2,1)S(1)}, u32[]{:S(2)}) copy-start(bf16[4,96,384]{2,1,0:T(8,128)(2,1)S(1)} %collective-permute-done.29.refs_5_) | copy-start | bytes 884740
  157.4 6.2 %copy-start.45 = (bf16[4,96,384]{2,1,0:T(8,128)(2,1)}, bf16[4,96,384]{2,1,0:T(8,128)(2,1)S(1)}, u32[]{:S(2)}) copy-start(bf16[4,96,384]{2,1,0:T(8,128)(2,1)S(1)} %collective-permute-done.30.refs_6_) | copy-start | bytes 884740
  163.6 8.0 %collective-permute-start.32 = (bf16[6144,128]{1,0:T(8,128)(2,1)}, bf16[6144,128]{1,0:T(8,128)(2,1)S(1)}, u32[]{:S(2)}, u32[]{:S(2)}) collective-permute-start(bf16[6144,128]{1,0:T(8,128)(2,1)} %get-tuple-element.190), channel_id=1, source_target_pairs={{0,16},{16,0},{1,17},{17,1},{2,18},{18,2},{3,19},{19,3},{4,20},{20... | collective-permute-start | bytes 4718600 | tf_op jit(solution)/shard_map/ppermute | solution.py:713
  (25 other events, 30.2 us)

commit v6 on v5

--- a/solution.py
+++ b/solution.py
@@ -1,5 +1,4 @@
 import functools
-import math
 
 import jax
 import jax.numpy as jnp
@@ -13,6 +12,7 @@
 TOP = 8
 LANES = 128
 MIB = 1 << 20
+SMALL = pl.CostEstimate(flops=0, bytes_accessed=1 << 16, transcendentals=0)
 
 
 beta_one = 0.9
@@ -231,7 +231,7 @@
             pltpu.VMEM(shape, jnp.bfloat16),
             pltpu.SemaphoreType.DMA((size + 1,)),
         ],
-        compiler_params=pltpu.CompilerParams(vmem_limit_bytes=8 * MIB),
+        compiler_params=pltpu.CompilerParams(vmem_limit_bytes=10 * MIB),
         cost_estimate=pl.CostEstimate(
             flops=0, bytes_accessed=8 * size * slots * width, transcendentals=0
         ),
@@ -271,7 +271,7 @@
             pltpu.VMEM((count, 3, slots, width), jnp.bfloat16),
             pltpu.SemaphoreType.DMA((count + 3,)),
         ],
-        compiler_params=pltpu.CompilerParams(vmem_limit_bytes=3 * MIB),
+        compiler_params=pltpu.CompilerParams(vmem_limit_bytes=10 * MIB),
         cost_estimate=pl.CostEstimate(
             flops=0, bytes_accessed=12 * count * slots * width, transcendentals=0
         ),
@@ -339,7 +339,7 @@
             pltpu.VMEM((experts, width, features), jnp.bfloat16),
             pltpu.SemaphoreType.DMA((experts, 1 + len(blocks) + count)),
         ],
-        compiler_params=pltpu.CompilerParams(vmem_limit_bytes=9 * MIB),
+        compiler_params=pltpu.CompilerParams(vmem_limit_bytes=16 * MIB),
         cost_estimate=pl.CostEstimate(
             flops=2 * experts * width * slots * features,
             bytes_accessed=2 * experts * (width + slots) * features,
@@ -417,62 +417,41 @@
             num_scalar_prefetch=1,
             grid=(steps,),
             in_specs=parts + [INSIDE] * 3 + [HBM] * kept,
-            out_specs=[line] * 3 + [placed, pl.BlockSpec((flat, LANES), lambda i, at: (i, 0))],
+            out_specs=[line] * 3 + [placed, line],
             scratch_shapes=[pltpu.VMEM((flat + block, LANES), jnp.float32)],
         ),
         out_shape=[jax.ShapeDtypeStruct(w.shape, jnp.float32)] * 3
         + [
             jax.ShapeDtypeStruct((total_rows, LANES), jnp.bfloat16),
-            jax.ShapeDtypeStruct((steps * flat, LANES), jnp.bfloat16),
+            jax.ShapeDtypeStruct(w.shape, jnp.bfloat16),
         ],
         input_output_aliases={4 + count + i: i for i in range(kept)},
         compiler_params=pltpu.CompilerParams(vmem_limit_bytes=10 * MIB),
-        cost_estimate=pl.CostEstimate(
-            flops=20 * steps * flat * LANES,
-            bytes_accessed=20 * steps * flat * LANES,
-            transcendentals=0,
-        ),
+        cost_estimate=SMALL,
     )(at, *partials, w, m1, m2, *before)
 
 
-def place_kernel(cut, at, low, high, full, out):
+def place_kernel(at, got, full, out):
     del at, full
-    here = pl.program_id(0)
-
-    @pl.when(here < cut)
-    def _():
-        out[...] = low[...]
-
-    @pl.when(here >= cut)
-    def _():
-        out[...] = high[...]
-
-
-def place_rows(owner, low, high, full):
-    block = math.gcd(low.shape[0], high.shape[0])
-    block = block // 3 if block % 3 == 0 else block
-    cut = low.shape[0] // block
-    steps = cut + high.shape[0] // block
-    shape = (block, LANES)
+    out[...] = got[...]
+
+
+def place_rows(owner, got, full):
+    steps = 6
+    block = got.shape[0] // steps
     return pl.pallas_call(
-        functools.partial(place_kernel, cut),
+        place_kernel,
         grid_spec=pltpu.PrefetchScalarGridSpec(
             num_scalar_prefetch=1,
             grid=(steps,),
-            in_specs=[
-                pl.BlockSpec(shape, lambda i, at: (jnp.minimum(i, cut - 1), 0)),
-                pl.BlockSpec(shape, lambda i, at: (jnp.maximum(i - cut, 0), 0)),
-                HBM,
-            ],
-            out_specs=pl.BlockSpec(shape, lambda i, at: (at[0] * steps + i, 0)),
+            in_specs=[pl.BlockSpec((block, LANES), lambda i, at: (i, 0)), HBM],
+            out_specs=pl.BlockSpec((block, LANES), lambda i, at: (at[0] * steps + i, 0)),
         ),
         out_shape=jax.ShapeDtypeStruct(full.shape, full.dtype),
-        input_output_aliases={3: 0},
-        compiler_params=pltpu.CompilerParams(vmem_limit_bytes=12 * MIB),
-        cost_estimate=pl.CostEstimate(
-            flops=0, bytes_accessed=4 * (low.size + high.size), transcendentals=0
-        ),
-    )(owner, low, high, full)
+        input_output_aliases={2: 0},
+        compiler_params=pltpu.CompilerParams(vmem_limit_bytes=14 * MIB),
+        cost_estimate=pl.CostEstimate(flops=0, bytes_accessed=4 * got.size, transcendentals=0),
+    )(owner, got, full)
 
 
 def finish_kernel(pieces, target, probs, hidden, *refs):
@@ -673,7 +652,7 @@
     back[last - 1] = move(grads[last - 1], 1 - last, 0)
     parts[last] = whole(*near[last]) + tuple((f, 0, half) for f in moved["far"])
     parts[0] = whole(*near[0]) + tuple((f, half, half) for f in moved["far"])
-    add_chunks(last, 0, vmem=24)
+    add_chunks(last, 0, vmem=56)
     back[last] = move(grads[last], -last, 0)
     back[0] = grads[0]
     back = [back[j] for j in range(length)]
@@ -700,25 +679,19 @@
     at = outer_at.astype(jnp.int32)[None]
     total_rows = secondary.size // LANES
     blocks = rows // 16
-    cuts = [0, blocks // 2, blocks]
-    outs, copies = [], []
+    cuts = [0, blocks - blocks // 3, blocks]
+    outs = []
     for start, stop in zip(cuts[:-1], cuts[1:]):
-        if start:
+        if stop == blocks:
             partials, flipped = tie((partials, flipped))
-        *outs, copy = adam_rows(
+        outs = adam_rows(
             at, partials, *state, total_rows, outs, start, stop - start
         )
-        copies.append(copy)
-    sent = [
-        [lax.ppermute(copy, "outer", outer_perm(r)) for r in range(1, outer_size)]
-        for copy in copies
-    ]
-    new_weight, new_moment1, new_moment2, full = outs
+    new_weight, new_moment1, new_moment2, full, copy = outs
     for r in range(1, outer_size):
+        got = lax.ppermute(copy, "outer", outer_perm(r))
         owner = (outer_at + outer_size - r) % outer_size
-        full = place_rows(
-            owner.astype(jnp.int32)[None], sent[0][r - 1], sent[1][r - 1], full
-        )
+        full = place_rows(owner.astype(jnp.int32)[None], got, full)
 
     d_hidden, d_probs = finish(
         *columns, hidden.reshape(choices, hidden_width), back + flipped, pieces

time: 175 us -> 157 us (0.90)
  local copies, waits for them, and re-layouts: 33.7 us -> 18 us
  starting transfers between devices: 40.7 us -> 38.8 us
    unnamed x112 -> x74, local copies, waits for them, and re-layouts: 30 us -> 13.4 us
    ppermute x29, starting transfers between devices: 40.1 us -> 38.1 us  [move(): return lax.ppermute(block, 'inner', step_perm(size, steps, flip))]
  transfers between devices with their start and end apart: 33 -> 32, of which waited for: 11 -> 12; matrix products, arithmetic and copies ran while one was open for 9% -> 11% of each run, Pallas kernels for 32% -> 33%
where the time goes in v6:
time: 157 us
  Pallas kernels  59.4 us (38%)
  starting transfers between devices  38.8 us (25%)
  waiting for transfers between devices  33 us (21%)
  local copies, waits for them, and re-layouts  18 us (11%)
  matrix products  3.51 us (2%)
  other arithmetic  2.7 us (2%)
    ppermute x29, starting transfers between devices, move(): return lax.ppermute(block, 'inner', step_perm(size, steps, flip))  38.1 us
    ppermute x29, waiting for transfers between devices, move(): return lax.ppermute(block, 'inner', step_perm(size, steps, flip))  31.3 us
    pallas_call x3, Pallas kernels, chunk_grads(): pl.pallas_call(functools.partial(grads_kernel, spans), out_shape=[jax.Sha...  23.3 us
    unnamed x74, local copies, waits for them, and re-layouts  13.4 us
    pallas_call x2, Pallas kernels, adam_rows(): pl.pallas_call(functools.partial(adam_kernel, count, owners, kept, first)...  12.4 us
    pallas_call x2, Pallas kernels, partial_rows(): pl.pallas_call(functools.partial(partial_kernel, start, total), out_shape...  8.97 us
    pallas_call x1, Pallas kernels, finish(): pl.pallas_call(functools.partial(finish_kernel, pieces), out_shape=(jax.S...  6.38 us
    pallas_call x2, Pallas kernels, regroup(): pl.pallas_call(regroup_kernel, out_shape=[jax.ShapeDtypeStruct((count, sl...  3.29 us
  transfers between devices with their start and end apart: 32, of which 12 were waited for; matrix products, arithmetic and copies ran while one was open for 11% of the time, Pallas kernels for 33%

profile of v6, /device:TPU:0, one launch (start us, length us, event | category | flops | bytes accessed | tf_op | source)
XLA Modules:
  0.0 156.7 jit_solution(772166888709846457)
XLA Ops:
  0.6 0.7 convert_element_type.46
  1.5 1.1 fusion.9.refs_5_
  2.6 3.1 %collective-permute-start = (bf16[128,2176]{1,0:T(8,128)(2,1)S(1)}, bf16[128,2176]{1,0:T(8,128)(2,1)S(1)}, u32[]{:S(2)}, u32[]{:S(2)}) collective-permute-start(bf16[128,2176]{1,0:T(8,128)(2,1)S(1)} %fusion.9.refs_5_), channel_id=1, source_target_pairs={{0,4},{1,5},{2,6},{3,7},{4,12},{5,13},{6,14},{7,15},{8,0},{9,1},{1... | collective-permute-start | bytes 1671176 | tf_op jit(solution)/shard_map/ppermute | solution.py:572
  5.6 1.5 collective-permute-start.1
  7.1 1.5 collective-permute-start.2
  8.7 0.8 copy.49
  10.2 0.6 fusion.27.target
  11.0 0.7 reshape.249.probs
  11.7 3.2 %fusion.2 = bf16[1536,384]{1,0:T(8,128)(2,1)S(1)} fusion(s32[1024]{0:T(1024)S(1)} %fusion.41, bf16[128,8,384]{2,1,0:T(8,128)(2,1)} %param.9, f32[128,8]{1,0:T(8,128)S(1)} %copy.51), kind=kOutput, calls=%fused_computation.4 | convolution fusion | flops 1211301888 | bytes 1974272 | tf_op jit(solution)/shard_map/dot_general | solution.py:564
  14.9 4.4 %collective-permute-done.refs_0_ = bf16[128,2176]{1,0:T(8,128)(2,1)S(1)} collective-permute-done((bf16[128,2176]{1,0:T(8,128)(2,1)S(1)}, bf16[128,2176]{1,0:T(8,128)(2,1)S(1)}, u32[]{:S(2)}, u32[]{:S(2)}) %collective-permute-start) | collective-permute-done | bytes 557088 | tf_op jit(solution)/shard_map/ppermute | solution.py:572
  19.7 1.2 collective-permute-done.2.refs_7_
  20.9 2.6 %collective-permute-start.3 = (bf16[128,2176]{1,0:T(8,128)(2,1)S(1)}, bf16[128,2176]{1,0:T(8,128)(2,1)S(1)}, u32[]{:S(2)}, u32[]{:S(2)}) collective-permute-start(bf16[128,2176]{1,0:T(8,128)(2,1)S(1)} %collective-permute-done.refs_0_), channel_id=1, source_target_pairs={{0,4},{1,5},{2,6},{3,7},{4,12},{5,13},{6,14},{7,15},{8,0},{9,1},{1... | collective-permute-start | bytes 1671176 | tf_op jit(solution)/shard_map/ppermute | solution.py:572
  23.5 0.5 collective-permute-start.4
  24.1 1.5 collective-permute-start.5
  25.6 1.0 slice_bitcast_fusion
  26.6 8.2 %collective-permute-done.3.refs_0_ = bf16[128,2176]{1,0:T(8,128)(2,1)S(1)} collective-permute-done((bf16[128,2176]{1,0:T(8,128)(2,1)S(1)}, bf16[128,2176]{1,0:T(8,128)(2,1)S(1)}, u32[]{:S(2)}, u32[]{:S(2)}) %collective-permute-start.3) | collective-permute-done | bytes 557088 | tf_op jit(solution)/shard_map/ppermute | solution.py:572
  34.7 1.4 collective-permute-done.4.refs_1_
  36.1 0.6 collective-permute-done.5.refs_2_
  36.8 1.6 %collective-permute-start.7 = (bf16[64,2176]{1,0:T(8,128)(2,1)S(1)}, bf16[64,2176]{1,0:T(8,128)(2,1)S(1)}, u32[]{:S(2)}, u32[]{:S(2)}) collective-permute-start(bf16[64,2176]{1,0:T(8,128)(2,1)S(1)} %slice.45), channel_id=1, source_target_pairs={{0,2},{1,3},{2,0},{3,1},{4,6},{5,7},{6,4},{7,5},{8,10},{9,11},{10,... | collective-permute-start | bytes 835592 | tf_op jit(solution)/shard_map/ppermute | solution.py:572
  38.4 1.2 collective-permute-start.9
  39.6 0.5 collective-permute-start.10
  40.7 1.0 collective-permute-start.6
  41.6 4.8 %collective-permute-done.7.refs_3_ = bf16[64,2176]{1,0:T(8,128)(2,1)S(1)} collective-permute-done((bf16[64,2176]{1,0:T(8,128)(2,1)S(1)}, bf16[64,2176]{1,0:T(8,128)(2,1)S(1)}, u32[]{:S(2)}, u32[]{:S(2)}) %collective-permute-start.7) | collective-permute-done | bytes 278560 | tf_op jit(solution)/shard_map/ppermute | solution.py:572
  46.5 1.4 collective-permute-start.8
  47.9 6.2 %copy.66 = bf16[384,4,2048]{2,0,1:T(8,128)(2,1)} copy(bf16[384,4,2048]{2,1,0:T(4,128)(2,1)S(1)} %bitcast.78) | data formatting | bytes 12582912 | tf_op args[4]
  54.1 3.6 %collective-permute-done.8.refs_4_ = bf16[64,2176]{1,0:T(8,128)(2,1)S(1)} collective-permute-done((bf16[64,2176]{1,0:T(8,128)(2,1)S(1)}, bf16[64,2176]{1,0:T(8,128)(2,1)S(1)}, u32[]{:S(2)}, u32[]{:S(2)}) %collective-permute-start.8) | collective-permute-done | bytes 278560 | tf_op jit(solution)/shard_map/ppermute | solution.py:572
  57.8 0.6 collective-permute-start.16
  58.5 1.9 %collective-permute-start.17 = (bf16[128,2176]{1,0:T(8,128)(2,1)}, bf16[128,2176]{1,0:T(8,128)(2,1)}, u32[]{:S(2)}, u32[]{:S(2)}) collective-permute-start(bf16[128,2176]{1,0:T(8,128)(2,1)} %collective-permute-done.9.refs_0_), channel_id=1, source_target_pairs={{0,2},{1,3},{2,0},{3,1},{4,6},{5,7},{6,4},{7,5},{8,10},{9,11},{10,... | collective-permute-start | bytes 1671176 | tf_op jit(solution)/shard_map/ppermute | solution.py:572
  60.4 1.8 %collective-permute-start.12 = (bf16[4,96,384]{2,1,0:T(8,128)(2,1)}, bf16[4,96,384]{2,1,0:T(8,128)(2,1)S(1)}, u32[]{:S(2)}, u32[]{:S(2)}) collective-permute-start(bf16[4,96,384]{2,1,0:T(8,128)(2,1)} %get-tuple-element.119), channel_id=1, source_target_pairs={{0,12},{1,13},{2,14},{3,15},{4,8},{5,9},{6,10},{7,11},{8,4},{9,5},... | collective-permute-start | bytes 884744 | tf_op jit(solution)/shard_map/ppermute | solution.py:572
  62.2 0.8 collective-permute-start.13
  63.0 0.7 slice.48
  63.8 3.7 %collective-permute-done.14.refs_3_ = bf16[64,2176]{1,0:T(8,128)(2,1)S(1)} collective-permute-done((bf16[64,2176]{1,0:T(8,128)(2,1)S(1)}, bf16[64,2176]{1,0:T(8,128)(2,1)S(1)}, u32[]{:S(2)}, u32[]{:S(2)}) %collective-permute-start.14) | collective-permute-done | bytes 278560 | tf_op jit(solution)/shard_map/ppermute | solution.py:572
  67.4 0.5 collective-permute-start.15
  68.0 6.8 %shard_map.127 = (bf16[384,2048]{1,0:T(8,128)(2,1)}, bf16[4,96,384]{2,1,0:T(8,128)(2,1)}) custom-call(s32[1]{0:T(128)} %bitcast.5.first, bf16[128,2176]{1,0:T(8,128)(2,1)} %copy-done.19, bf16[128,2176]{1,0:T(8,128)(2,1)} %copy-done.17, bf16[128,2176]{1,0:T(8,128)(2,1)} %copy-done.18, bf16[64,2176]{1,0:T(8,128)(2,1)} %copy-done.22, ...), custom_call_target="tpu_custom_call" | custom-call | flops 1409286144 | bytes 3670016 | tf_op jit(solution)/shard_map/pallas_call | solution.py:170
  74.8 0.7 collective-permute-done.15.refs_4_
  76.0 1.0 slice.50
  77.1 0.7 collective-permute-start.20
  77.8 3.0 %collective-permute-start.18 = (bf16[4,96,384]{2,1,0:T(8,128)(2,1)S(1)}, bf16[4,96,384]{2,1,0:T(8,128)(2,1)S(1)}, u32[]{:S(2)}, u32[]{:S(2)}) collective-permute-start(bf16[4,96,384]{2,1,0:T(8,128)(2,1)S(1)} %copy-done.28), channel_id=1, source_target_pairs={{0,8},{1,9},{2,10},{3,11},{4,0},{5,1},{6,2},{7,3},{8,12},{9,13},{1... | collective-permute-start | bytes 884744 | tf_op jit(solution)/shard_map/ppermute | solution.py:572
  80.7 2.0 %shard_map.130 = (bf16[4,96,384]{2,1,0:T(8,128)(2,1)}, bf16[4,96,384]{2,1,0:T(8,128)(2,1)}, bf16[4,96,384]{2,1,0:T(8,128)(2,1)S(1)}) custom-call(bf16[4,96,384]{2,1,0:T(8,128)(2,1)S(1)} %get-tuple-element.132.refs_0_, bf16[4,96,384]{2,1,0:T(8,128)(2,1)S(1)} %collective-permute-done.6.refs_1_, bf16[4,96,384]{2,1,0:T(8,128)(2,1)S(1)} %collective-permute-done.12.refs_2_, ...), custom_call_target="tpu_custom_call" | custom-call | bytes 1769472 | tf_op jit(solution)/shard_map/pallas_call | solution.py:265
  82.7 1.6 %collective-permute-start.23 = (bf16[4,96,384]{2,1,0:T(8,128)(2,1)}, bf16[4,96,384]{2,1,0:T(8,128)(2,1)S(1)}, u32[]{:S(2)}, u32[]{:S(2)}) collective-permute-start(bf16[4,96,384]{2,1,0:T(8,128)(2,1)} %get-tuple-element.152), channel_id=1, source_target_pairs={{0,1},{1,0},{2,3},{3,2},{4,5},{5,4},{6,7},{7,6},{8,9},{9,8},{10,11... | collective-permute-start | bytes 884744 | tf_op jit(solution)/shard_map/ppermute | solution.py:572
  84.4 1.5 collective-permute-start.24
  85.9 6.7 %shard_map.128 = (bf16[384,2048]{1,0:T(8,128)(2,1)}, bf16[4,96,384]{2,1,0:T(8,128)(2,1)}) custom-call(s32[1]{0:T(128)} %bitcast.5.first, bf16[128,2176]{1,0:T(8,128)(2,1)} %copy-done.20, bf16[128,2176]{1,0:T(8,128)(2,1)} %copy-done.14, bf16[128,2176]{1,0:T(8,128)(2,1)} %copy-done.15, bf16[64,2176]{1,0:T(8,128)(2,1)} %copy-done.21, ...), custom_call_target="tpu_custom_call" | custom-call | flops 1409286144 | bytes 3670016 | tf_op jit(solution)/shard_map/pallas_call | solution.py:170
  93.1 2.7 %collective-permute-start.21 = (bf16[4,96,384]{2,1,0:T(8,128)(2,1)}, bf16[4,96,384]{2,1,0:T(8,128)(2,1)S(1)}, u32[]{:S(2)}, u32[]{:S(2)}) collective-permute-start(bf16[4,96,384]{2,1,0:T(8,128)(2,1)} %get-tuple-element.146), channel_id=1, source_target_pairs={{0,12},{1,13},{2,14},{3,15},{4,8},{5,9},{6,10},{7,11},{8,4},{9,5},... | collective-permute-start | bytes 884744 | tf_op jit(solution)/shard_map/ppermute | solution.py:572
  95.8 9.8 %shard_map.129 = (bf16[384,2048]{1,0:T(8,128)(2,1)}, bf16[4,96,384]{2,1,0:T(8,128)(2,1)}, bf16[384,2048]{1,0:T(8,128)(2,1)}, bf16[4,96,384]{2,1,0:T(8,128)(2,1)}) custom-call(s32[1]{0:T(128)} %bitcast.5.first, bf16[128,2176]{1,0:T(8,128)(2,1)} %collective-permute-done.9.refs_0_, bf16[128,2176]{1,0:T(8,128)(2,1)} %copy-done.16, ...), custom_call_target="tpu_custom_call" | custom-call | flops 2818572288 | bytes 7340032 | tf_op jit(solution)/shard_map/pallas_call | solution.py:170
  105.6 1.4 collective-permute-start.22
  107.1 2.5 %shard_map.131.weighted = bf16[4,384,384]{2,1,0:T(8,128)(2,1)S(1)} custom-call(bf16[4,96,384]{2,1,0:T(8,128)(2,1)S(1)} %get-tuple-element.132.refs_0_, bf16[4,96,384]{2,1,0:T(8,128)(2,1)S(1)} %collective-permute-done.6.refs_1_, bf16[4,96,384]{2,1,0:T(8,128)(2,1)S(1)} %collective-permute-done.12.refs_2_, ...), custom_call_target="tpu_custom_call" | custom-call | bytes 4718592 | tf_op jit(solution)/shard_map/pallas_call | solution.py:223
  109.6 1.4 copy-done.3
  111.0 1.4 copy-done.4
  112.4 4.5 %shard_map.132 = (bf16[2,192,2048]{2,1,0:T(8,128)(2,1)S(1)}, bf16[2,192,2048]{2,1,0:T(8,128)(2,1)S(1)}) custom-call(s32[2]{0:T(128)S(1)} %and_select_fusion.owners, bf16[4,384,384]{2,1,0:T(8,128)(2,1)S(1)} %shard_map.131.weighted, bf16[384,2048]{1,0:T(8,128)(2,1)S(1)} %copy-done.4, bf16[384,2048]{1,0:T(8,128)(2,1)S(1)} %copy-done.1, ...), custom_call_target="tpu_custom_call" | custom-call | flops 1207959552 | bytes 6291456 | tf_op jit(solution)/shard_map/pallas_call | solution.py:330
  117.1 4.5 %shard_map.133 = (bf16[2,192,2048]{2,1,0:T(8,128)(2,1)S(1)}, bf16[2,192,2048]{2,1,0:T(8,128)(2,1)S(1)}) custom-call(s32[2]{0:T(128)S(1)} %and_select_fusion.owners, bf16[4,384,384]{2,1,0:T(8,128)(2,1)S(1)} %shard_map.131.weighted, bf16[384,2048]{1,0:T(8,128)(2,1)S(1)} %copy-done.4, bf16[384,2048]{1,0:T(8,128)(2,1)S(1)} %copy-done.1, ...), custom_call_target="tpu_custom_call" | custom-call | flops 1207959552 | bytes 6291456 | tf_op jit(solution)/shard_map/pallas_call | solution.py:330
  121.6 0.5 collective-permute-start.27
  122.1 1.3 shard_map.134
  123.4 1.7 %collective-permute-done.27.refs_3_ = bf16[2,192,2048]{2,1,0:T(8,128)(2,1)S(1)} collective-permute-done((bf16[2,192,2048]{2,1,0:T(8,128)(2,1)S(1)}, bf16[2,192,2048]{2,1,0:T(8,128)(2,1)S(1)}, u32[]{:S(2)}, u32[]{:S(2)}) %collective-permute-start.27) | collective-permute-done | bytes 1572896 | tf_op jit(solution)/shard_map/ppermute | solution.py:674
  125.1 0.5 collective-permute-start.28
  125.6 1.5 collective-permute-start.29
  127.2 1.5 collective-permute-start.30
  128.7 2.8 %copy-done = f32[192,4,2048]{2,1,0:T(4,128)S(1)} copy-done((f32[192,4,2048]{2,1,0:T(4,128)S(1)}, f32[192,4,2048]{2,1,0:T(4,128)}, u32[]{:S(2)}) %copy-start) | copy-done | bytes 6291480
  131.4 8.0 %shard_map.136 = (f32[12288,128]{1,0:T(8,128)}, f32[12288,128]{1,0:T(8,128)}, f32[12288,128]{1,0:T(8,128)}, bf16[24576,128]{1,0:T(8,128)(2,1)}, bf16[12288,128]{1,0:T(8,128)(2,1)}) custom-call(s32[1]{0:T(128)} %bitcast.12.at, bf16[2,192,2048]{2,1,0:T(8,128)(2,1)S(1)} %get-tuple-element.178.refs_0_, ...), custom_call_target="tpu_custom_call" | custom-call | bytes 65536 | tf_op jit(solution)/shard_map/pallas_call | solution.py:414
  139.5 2.2 %collective-permute-done.30.refs_6_ = bf16[4,96,384]{2,1,0:T(8,128)(2,1)S(1)} collective-permute-done((bf16[4,96,384]{2,1,0:T(8,128)(2,1)S(1)}, bf16[4,96,384]{2,1,0:T(8,128)(2,1)S(1)}, u32[]{:S(2)}, u32[]{:S(2)}) %collective-permute-start.30) | collective-permute-done | bytes 294944 | tf_op jit(solution)/shard_map/ppermute | solution.py:572
  141.7 4.4 %shard_map.137 = (f32[12288,128]{1,0:T(8,128)}, f32[12288,128]{1,0:T(8,128)}, f32[12288,128]{1,0:T(8,128)}, bf16[24576,128]{1,0:T(8,128)(2,1)}, bf16[12288,128]{1,0:T(8,128)(2,1)}) custom-call(s32[1]{0:T(128)} %bitcast.12.at, ...), custom_call_target="tpu_custom_call", output_to_operand_aliasing={{0}: (8, {}), {1}: (9, {}), {2}: (10, {}), {3}: (11, {}), {... | custom-call | bytes 65536 | tf_op jit(solution)/shard_map/pallas_call | solution.py:414
  146.2 6.4 %shard_map.135 = (bf16[1024,384]{1,0:T(8,128)(2,1)}, f32[8,1024]{1,0:T(8,128)}) custom-call(f32[8,128]{1,0:T(8,128)} %fusion.27.target, f32[8,128]{1,0:T(8,128)} %reshape.249.probs, bf16[1024,384]{1,0:T(8,128)(2,1)} %bitcast.83, bf16[4,96,384]{2,1,0:T(8,128)(2,1)} %get-tuple-element.148.refs_0_, bf16[4,96,384]{2,1,0:T(8,128)(2,1)} %copy-done.5, ...), custom_call_target="tpu_custom_call" | custom-call | flops 1207959552 | bytes 3145728 | tf_op jit(solution)/shard_map/pallas_call | solution.py:505
  152.6 0.8 slice_reduce_fusion
  153.4 0.7 copy.63
  154.1 2.7 %shard_map.138 = bf16[24576,128]{1,0:T(8,128)(2,1)} custom-call(s32[1]{0:T(128)} %bitcast.37.at, bf16[12288,128]{1,0:T(8,128)(2,1)S(1)} %collective-permute-done.31.got, bf16[24576,128]{1,0:T(8,128)(2,1)} %get-tuple-element.191.full), custom_call_target="tpu_custom_call", output_to_operand_aliasing={{}: (2, {})} | custom-call | bytes 6291456 | tf_op jit(solution)/shard_map/pallas_call | solution.py:442
  (117 shorter events, 3.5 us)
Async XLA Ops:
  0.6 10.3 %copy-start.24 = (f32[128,8]{0,1:T(8,128)S(1)}, f32[128,8]{0,1:T(8,128)}, u32[]{:S(2)}) copy-start(f32[128,8]{0,1:T(8,128)} %param.10) | copy-start | bytes 12292
  2.6 12.4 %copy-start.11 = (bf16[128,2176]{1,0:T(8,128)(2,1)}, bf16[128,2176]{1,0:T(8,128)(2,1)S(1)}, u32[]{:S(2)}) copy-start(bf16[128,2176]{1,0:T(8,128)(2,1)S(1)} %fusion.9.refs_5_) | copy-start | bytes 1671172
  2.6 16.7 %collective-permute-start = (bf16[128,2176]{1,0:T(8,128)(2,1)S(1)}, bf16[128,2176]{1,0:T(8,128)(2,1)S(1)}, u32[]{:S(2)}, u32[]{:S(2)}) collective-permute-start(bf16[128,2176]{1,0:T(8,128)(2,1)S(1)} %fusion.9.refs_5_), channel_id=1, source_target_pairs={{0,4},{1,5},{2,6},{3,7},{4,12},{5,13},{6,14},{7,15},{8,0},{9,1},{1... | collective-permute-start | bytes 1671176 | tf_op jit(solution)/shard_map/ppermute | solution.py:572
  5.6 14.1 %collective-permute-start.1 = (bf16[128,2176]{1,0:T(8,128)(2,1)S(1)}, bf16[128,2176]{1,0:T(8,128)(2,1)S(1)}, u32[]{:S(2)}, u32[]{:S(2)}) collective-permute-start(bf16[128,2176]{1,0:T(8,128)(2,1)S(1)} %fusion.9.refs_5_), channel_id=1, source_target_pairs={{0,1},{1,0},{2,3},{3,2},{4,5},{5,4},{6,7},{7,6},{8,9},{9,8},{10,11... | collective-permute-start | bytes 1671176 | tf_op jit(solution)/shard_map/ppermute | solution.py:572
  7.1 13.8 %collective-permute-start.2 = (bf16[128,2176]{1,0:T(8,128)(2,1)S(1)}, bf16[128,2176]{1,0:T(8,128)(2,1)S(1)}, u32[]{:S(2)}, u32[]{:S(2)}) collective-permute-start(bf16[128,2176]{1,0:T(8,128)(2,1)S(1)} %fusion.9.refs_5_), channel_id=1, source_target_pairs={{0,2},{1,3},{2,0},{3,1},{4,6},{5,7},{6,4},{7,5},{8,10},{9,11},{10,... | collective-permute-start | bytes 1671176 | tf_op jit(solution)/shard_map/ppermute | solution.py:572
  11.7 36.2 %slice-start.4 = ((s8[6291456]{0:T(1024)(128)(4,1)}), s8[4194304]{0:T(1024)(128)(4,1)S(1)}, s32[]{:S(2)}) async-start(s8[6291456]{0:T(1024)(128)(4,1)} %bitcast.77), calls=%async_computation.4 | async-start | bytes 8388608
  11.7 36.2 %slice-start.5 = ((s8[6291456]{0:T(1024)(128)(4,1)}), s8[2097152]{0:T(1024)(128)(4,1)S(1)}, s32[]{:S(2)}) async-start(s8[6291456]{0:T(1024)(128)(4,1)} %bitcast.77), calls=%async_computation.5 | async-start | bytes 4194304
  19.3 7.3 %copy-start.19 = (bf16[128,2176]{1,0:T(8,128)(2,1)}, bf16[128,2176]{1,0:T(8,128)(2,1)S(1)}, u32[]{:S(2)}) copy-start(bf16[128,2176]{1,0:T(8,128)(2,1)S(1)} %collective-permute-done.refs_0_) | copy-start | bytes 1671172
  19.7 6.8 %copy-start.12 = (bf16[128,2176]{1,0:T(8,128)(2,1)}, bf16[128,2176]{1,0:T(8,128)(2,1)S(1)}, u32[]{:S(2)}) copy-start(bf16[128,2176]{1,0:T(8,128)(2,1)S(1)} %collective-permute-done.1.refs_6_) | copy-start | bytes 1671172
  20.9 5.6 %copy-start.13 = (bf16[128,2176]{1,0:T(8,128)(2,1)}, bf16[128,2176]{1,0:T(8,128)(2,1)S(1)}, u32[]{:S(2)}) copy-start(bf16[128,2176]{1,0:T(8,128)(2,1)S(1)} %collective-permute-done.2.refs_7_) | copy-start | bytes 1671172
  20.9 13.8 %collective-permute-start.3 = (bf16[128,2176]{1,0:T(8,128)(2,1)S(1)}, bf16[128,2176]{1,0:T(8,128)(2,1)S(1)}, u32[]{:S(2)}, u32[]{:S(2)}) collective-permute-start(bf16[128,2176]{1,0:T(8,128)(2,1)S(1)} %collective-permute-done.refs_0_), channel_id=1, source_target_pairs={{0,4},{1,5},{2,6},{3,7},{4,12},{5,13},{6,14},{7,15},{8,0},{9,1},{1... | collective-permute-start | bytes 1671176 | tf_op jit(solution)/shard_map/ppermute | solution.py:572
  23.5 12.6 %collective-permute-start.4 = (bf16[128,2176]{1,0:T(8,128)(2,1)S(1)}, bf16[128,2176]{1,0:T(8,128)(2,1)S(1)}, u32[]{:S(2)}, u32[]{:S(2)}) collective-permute-start(bf16[128,2176]{1,0:T(8,128)(2,1)S(1)} %collective-permute-done.refs_0_), channel_id=1, source_target_pairs={{0,1},{1,0},{2,3},{3,2},{4,5},{5,4},{6,7},{7,6},{8,9},{9,8},{10,11... | collective-permute-start | bytes 1671176 | tf_op jit(solution)/shard_map/ppermute | solution.py:572
  24.1 12.7 %collective-permute-start.5 = (bf16[128,2176]{1,0:T(8,128)(2,1)S(1)}, bf16[128,2176]{1,0:T(8,128)(2,1)S(1)}, u32[]{:S(2)}, u32[]{:S(2)}) collective-permute-start(bf16[128,2176]{1,0:T(8,128)(2,1)S(1)} %collective-permute-done.refs_0_), channel_id=1, source_target_pairs={{0,2},{1,3},{2,0},{3,1},{4,6},{5,7},{6,4},{7,5},{8,10},{9,11},{10,... | collective-permute-start | bytes 1671176 | tf_op jit(solution)/shard_map/ppermute | solution.py:572
  34.7 19.3 %copy-start.20 = (bf16[128,2176]{1,0:T(8,128)(2,1)}, bf16[128,2176]{1,0:T(8,128)(2,1)S(1)}, u32[]{:S(2)}) copy-start(bf16[128,2176]{1,0:T(8,128)(2,1)S(1)} %collective-permute-done.3.refs_0_) | copy-start | bytes 1671172
  36.1 4.0 %copy-start.17 = (bf16[128,2176]{1,0:T(8,128)(2,1)}, bf16[128,2176]{1,0:T(8,128)(2,1)S(1)}, u32[]{:S(2)}) copy-start(bf16[128,2176]{1,0:T(8,128)(2,1)S(1)} %collective-permute-done.4.refs_1_) | copy-start | bytes 1671172
  36.8 17.3 %copy-start.18 = (bf16[128,2176]{1,0:T(8,128)(2,1)}, bf16[128,2176]{1,0:T(8,128)(2,1)S(1)}, u32[]{:S(2)}) copy-start(bf16[128,2176]{1,0:T(8,128)(2,1)S(1)} %collective-permute-done.5.refs_2_) | copy-start | bytes 1671172
  36.8 9.7 %collective-permute-start.7 = (bf16[64,2176]{1,0:T(8,128)(2,1)S(1)}, bf16[64,2176]{1,0:T(8,128)(2,1)S(1)}, u32[]{:S(2)}, u32[]{:S(2)}) collective-permute-start(bf16[64,2176]{1,0:T(8,128)(2,1)S(1)} %slice.45), channel_id=1, source_target_pairs={{0,2},{1,3},{2,0},{3,1},{4,6},{5,7},{6,4},{7,5},{8,10},{9,11},{10,... | collective-permute-start | bytes 835592 | tf_op jit(solution)/shard_map/ppermute | solution.py:572
  38.4 19.3 %collective-permute-start.9 = (bf16[128,2176]{1,0:T(8,128)(2,1)S(1)}, bf16[128,2176]{1,0:T(8,128)(2,1)}, u32[]{:S(2)}, u32[]{:S(2)}) collective-permute-start(bf16[128,2176]{1,0:T(8,128)(2,1)S(1)} %collective-permute-done.3.refs_0_), channel_id=1, source_target_pairs={{0,4},{1,5},{2,6},{3,7},{4,12},{5,13},{6,14},{7,15},{8,0},{9,1},{1... | collective-permute-start | bytes 1671176 | tf_op jit(solution)/shard_map/ppermute | solution.py:572
  39.6 18.1 %collective-permute-start.10 = (bf16[128,2176]{1,0:T(8,128)(2,1)S(1)}, bf16[128,2176]{1,0:T(8,128)(2,1)S(1)}, u32[]{:S(2)}, u32[]{:S(2)}) collective-permute-start(bf16[128,2176]{1,0:T(8,128)(2,1)S(1)} %collective-permute-done.3.refs_0_), channel_id=1, source_target_pairs={{0,1},{1,0},{2,3},{3,2},{4,5},{5,4},{6,7},{7,6},{8,9},{9,8},{10,11... | collective-permute-start | bytes 1671176 | tf_op jit(solution)/shard_map/ppermute | solution.py:572
  40.1 17.6 %collective-permute-start.11 = (bf16[128,2176]{1,0:T(8,128)(2,1)S(1)}, bf16[128,2176]{1,0:T(8,128)(2,1)S(1)}, u32[]{:S(2)}, u32[]{:S(2)}) collective-permute-start(bf16[128,2176]{1,0:T(8,128)(2,1)S(1)} %collective-permute-done.3.refs_0_), channel_id=1, source_target_pairs={{0,2},{1,3},{2,0},{3,1},{4,6},{5,7},{6,4},{7,5},{8,10},{9,11},{10,... | collective-permute-start | bytes 1671176 | tf_op jit(solution)/shard_map/ppermute | solution.py:572
  40.7 17.0 %collective-permute-start.6 = (bf16[4,96,384]{2,1,0:T(8,128)(2,1)S(1)}, bf16[4,96,384]{2,1,0:T(8,128)(2,1)S(1)}, u32[]{:S(2)}, u32[]{:S(2)}) collective-permute-start(bf16[4,96,384]{2,1,0:T(8,128)(2,1)S(1)} %get-tuple-element.105), channel_id=1, source_target_pairs={{0,4},{1,5},{2,6},{3,7},{4,12},{5,13},{6,14},{7,15},{8,0},{9,1},{1... | collective-permute-start | bytes 884744 | tf_op jit(solution)/shard_map/ppermute | solution.py:572
  46.5 7.6 %copy-start.22 = (bf16[64,2176]{1,0:T(8,128)(2,1)}, bf16[64,2176]{1,0:T(8,128)(2,1)S(1)}, u32[]{:S(2)}) copy-start(bf16[64,2176]{1,0:T(8,128)(2,1)S(1)} %collective-permute-done.7.refs_3_) | copy-start | bytes 835588
  46.5 11.2 %collective-permute-start.8 = (bf16[64,2176]{1,0:T(8,128)(2,1)S(1)}, bf16[64,2176]{1,0:T(8,128)(2,1)S(1)}, u32[]{:S(2)}, u32[]{:S(2)}) collective-permute-start(bf16[64,2176]{1,0:T(8,128)(2,1)S(1)} %slice.46), channel_id=1, source_target_pairs={{0,1},{1,0},{2,3},{3,2},{4,5},{5,4},{6,7},{7,6},{8,9},{9,8},{10,11... | collective-permute-start | bytes 835592 | tf_op jit(solution)/shard_map/ppermute | solution.py:572
  57.7 9.7 %copy-start.23 = (bf16[64,2176]{1,0:T(8,128)(2,1)}, bf16[64,2176]{1,0:T(8,128)(2,1)S(1)}, u32[]{:S(2)}) copy-start(bf16[64,2176]{1,0:T(8,128)(2,1)S(1)} %collective-permute-done.8.refs_4_) | copy-start | bytes 835588
  57.7 17.0 %copy-start.14 = (bf16[128,2176]{1,0:T(8,128)(2,1)}, bf16[128,2176]{1,0:T(8,128)(2,1)S(1)}, u32[]{:S(2)}) copy-start(bf16[128,2176]{1,0:T(8,128)(2,1)S(1)} %collective-permute-done.10.refs_1_) | copy-start | bytes 1671172
  57.7 17.0 %copy-start.15 = (bf16[128,2176]{1,0:T(8,128)(2,1)}, bf16[128,2176]{1,0:T(8,128)(2,1)S(1)}, u32[]{:S(2)}) copy-start(bf16[128,2176]{1,0:T(8,128)(2,1)S(1)} %collective-permute-done.11.refs_2_) | copy-start | bytes 1671172
  57.8 9.7 %collective-permute-start.14 = (bf16[64,2176]{1,0:T(8,128)(2,1)S(1)}, bf16[64,2176]{1,0:T(8,128)(2,1)S(1)}, u32[]{:S(2)}, u32[]{:S(2)}) collective-permute-start(bf16[64,2176]{1,0:T(8,128)(2,1)S(1)} %slice.47), channel_id=1, source_target_pairs={{0,2},{1,3},{2,0},{3,1},{4,6},{5,7},{6,4},{7,5},{8,10},{9,11},{10,... | collective-permute-start | bytes 835592 | tf_op jit(solution)/shard_map/ppermute | solution.py:572
  57.8 17.6 %collective-permute-start.16 = (bf16[128,2176]{1,0:T(8,128)(2,1)}, bf16[128,2176]{1,0:T(8,128)(2,1)S(1)}, u32[]{:S(2)}, u32[]{:S(2)}) collective-permute-start(bf16[128,2176]{1,0:T(8,128)(2,1)} %collective-permute-done.9.refs_0_), channel_id=1, source_target_pairs={{0,1},{1,0},{2,3},{3,2},{4,5},{5,4},{6,7},{7,6},{8,9},{9,8},{10,11... | collective-permute-start | bytes 1671176 | tf_op jit(solution)/shard_map/ppermute | solution.py:572
  58.5 17.0 %collective-permute-start.17 = (bf16[128,2176]{1,0:T(8,128)(2,1)}, bf16[128,2176]{1,0:T(8,128)(2,1)}, u32[]{:S(2)}, u32[]{:S(2)}) collective-permute-start(bf16[128,2176]{1,0:T(8,128)(2,1)} %collective-permute-done.9.refs_0_), channel_id=1, source_target_pairs={{0,2},{1,3},{2,0},{3,1},{4,6},{5,7},{6,4},{7,5},{8,10},{9,11},{10,... | collective-permute-start | bytes 1671176 | tf_op jit(solution)/shard_map/ppermute | solution.py:572
  60.4 15.0 %collective-permute-start.12 = (bf16[4,96,384]{2,1,0:T(8,128)(2,1)}, bf16[4,96,384]{2,1,0:T(8,128)(2,1)S(1)}, u32[]{:S(2)}, u32[]{:S(2)}) collective-permute-start(bf16[4,96,384]{2,1,0:T(8,128)(2,1)} %get-tuple-element.119), channel_id=1, source_target_pairs={{0,12},{1,13},{2,14},{3,15},{4,8},{5,9},{6,10},{7,11},{8,4},{9,5},... | collective-permute-start | bytes 884744 | tf_op jit(solution)/shard_map/ppermute | solution.py:572
  62.2 13.2 %collective-permute-start.13 = (bf16[4,96,384]{2,1,0:T(8,128)(2,1)}, bf16[4,96,384]{2,1,0:T(8,128)(2,1)S(1)}, u32[]{:S(2)}, u32[]{:S(2)}) collective-permute-start(bf16[4,96,384]{2,1,0:T(8,128)(2,1)} %get-tuple-element.120), channel_id=1, source_target_pairs={{0,8},{1,9},{2,10},{3,11},{4,0},{5,1},{6,2},{7,3},{8,12},{9,13},{1... | collective-permute-start | bytes 884744 | tf_op jit(solution)/shard_map/ppermute | solution.py:572
  67.4 7.3 %copy-start.21 = (bf16[64,2176]{1,0:T(8,128)(2,1)}, bf16[64,2176]{1,0:T(8,128)(2,1)S(1)}, u32[]{:S(2)}) copy-start(bf16[64,2176]{1,0:T(8,128)(2,1)S(1)} %collective-permute-done.14.refs_3_) | copy-start | bytes 835588
  67.4 8.0 %collective-permute-start.15 = (bf16[64,2176]{1,0:T(8,128)(2,1)}, bf16[64,2176]{1,0:T(8,128)(2,1)}, u32[]{:S(2)}, u32[]{:S(2)}) collective-permute-start(bf16[64,2176]{1,0:T(8,128)(2,1)} %slice.48), channel_id=1, source_target_pairs={{0,1},{1,0},{2,3},{3,2},{4,5},{5,4},{6,7},{7,6},{8,9},{9,8},{10,11... | collective-permute-start | bytes 835592 | tf_op jit(solution)/shard_map/ppermute | solution.py:572
  68.0 7.6 %slice-start.6 = ((bf16[128,2176]{1,0:T(8,128)(2,1)}), bf16[64,2176]{1,0:T(8,128)(2,1)S(1)}, s32[]{:S(2)}) async-start(bf16[128,2176]{1,0:T(8,128)(2,1)} %copy-done.12), calls=%async_computation.6 | async-start | bytes 557056 | tf_op jit(solution)/shard_map/slice | solution.py:597
  75.6 17.5 %collective-permute-start.19 = (bf16[128,2176]{1,0:T(8,128)(2,1)S(1)}, bf16[128,2176]{1,0:T(8,128)(2,1)S(1)}, u32[]{:S(2)}, u32[]{:S(2)}) collective-permute-start(bf16[128,2176]{1,0:T(8,128)(2,1)S(1)} %pad_maximum_fusion), channel_id=1, source_target_pairs={{0,2},{1,3},{2,0},{3,1},{4,6},{5,7},{6,4},{7,5},{8,10},{9,11},{10,... | collective-permute-start | bytes 1671176 | tf_op jit(solution)/shard_map/ppermute | solution.py:572
  77.1 16.0 %collective-permute-start.20 = (bf16[128,2176]{1,0:T(8,128)(2,1)S(1)}, bf16[128,2176]{1,0:T(8,128)(2,1)S(1)}, u32[]{:S(2)}, u32[]{:S(2)}) collective-permute-start(bf16[128,2176]{1,0:T(8,128)(2,1)S(1)} %pad_maximum_fusion.1), channel_id=1, source_target_pairs={{0,1},{1,0},{2,3},{3,2},{4,5},{5,4},{6,7},{7,6},{8,9},{9,8},{10,11... | collective-permute-start | bytes 1671176 | tf_op jit(solution)/shard_map/ppermute | solution.py:572
  77.8 14.8 %collective-permute-start.18 = (bf16[4,96,384]{2,1,0:T(8,128)(2,1)S(1)}, bf16[4,96,384]{2,1,0:T(8,128)(2,1)S(1)}, u32[]{:S(2)}, u32[]{:S(2)}) collective-permute-start(bf16[4,96,384]{2,1,0:T(8,128)(2,1)S(1)} %copy-done.28), channel_id=1, source_target_pairs={{0,8},{1,9},{2,10},{3,11},{4,0},{5,1},{6,2},{7,3},{8,12},{9,13},{1... | collective-permute-start | bytes 884744 | tf_op jit(solution)/shard_map/ppermute | solution.py:572
  82.7 24.4 %collective-permute-start.23 = (bf16[4,96,384]{2,1,0:T(8,128)(2,1)}, bf16[4,96,384]{2,1,0:T(8,128)(2,1)S(1)}, u32[]{:S(2)}, u32[]{:S(2)}) collective-permute-start(bf16[4,96,384]{2,1,0:T(8,128)(2,1)} %get-tuple-element.152), channel_id=1, source_target_pairs={{0,1},{1,0},{2,3},{3,2},{4,5},{5,4},{6,7},{7,6},{8,9},{9,8},{10,11... | collective-permute-start | bytes 884744 | tf_op jit(solution)/shard_map/ppermute | solution.py:572
  84.4 22.7 %collective-permute-start.24 = (bf16[4,96,384]{2,1,0:T(8,128)(2,1)}, bf16[4,96,384]{2,1,0:T(8,128)(2,1)S(1)}, u32[]{:S(2)}, u32[]{:S(2)}) collective-permute-start(bf16[4,96,384]{2,1,0:T(8,128)(2,1)} %get-tuple-element.153), channel_id=1, source_target_pairs={{0,2},{1,3},{2,0},{3,1},{4,6},{5,7},{6,4},{7,5},{8,10},{9,11},{10,... | collective-permute-start | bytes 884744 | tf_op jit(solution)/shard_map/ppermute | solution.py:572
  92.6 29.5 %copy-start.5 = (bf16[4,96,384]{2,1,0:T(8,128)(2,1)}, bf16[4,96,384]{2,1,0:T(8,128)(2,1)S(1)}, u32[]{:S(2)}) copy-start(bf16[4,96,384]{2,1,0:T(8,128)(2,1)S(1)} %collective-permute-done.18.refs_1_) | copy-start | bytes 884740
  92.6 14.5 %collective-permute-start.25 = (bf16[4,96,384]{2,1,0:T(8,128)(2,1)S(1)}, bf16[4,96,384]{2,1,0:T(8,128)(2,1)S(1)}, u32[]{:S(2)}, u32[]{:S(2)}) collective-permute-start(bf16[4,96,384]{2,1,0:T(8,128)(2,1)S(1)} %get-tuple-element.154), channel_id=1, source_target_pairs={{0,3},{1,2},{2,1},{3,0},{4,7},{5,6},{6,5},{7,4},{8,11},{9,10},{10,... | collective-permute-start | bytes 884744 | tf_op jit(solution)/shard_map/ppermute | solution.py:572
  93.1 2.7 %copy-start.9 = (bf16[128,2176]{1,0:T(8,128)(2,1)}, bf16[128,2176]{1,0:T(8,128)(2,1)S(1)}, u32[]{:S(2)}) copy-start(bf16[128,2176]{1,0:T(8,128)(2,1)S(1)} %collective-permute-done.19.refs_3_.refs_8_) | copy-start | bytes 1671172
  93.1 2.7 %copy-start.10 = (bf16[128,2176]{1,0:T(8,128)(2,1)}, bf16[128,2176]{1,0:T(8,128)(2,1)S(1)}, u32[]{:S(2)}) copy-start(bf16[128,2176]{1,0:T(8,128)(2,1)S(1)} %collective-permute-done.20.refs_4_.refs_9_) | copy-start | bytes 1671172
  93.1 23.9 %collective-permute-start.21 = (bf16[4,96,384]{2,1,0:T(8,128)(2,1)}, bf16[4,96,384]{2,1,0:T(8,128)(2,1)S(1)}, u32[]{:S(2)}, u32[]{:S(2)}) collective-permute-start(bf16[4,96,384]{2,1,0:T(8,128)(2,1)} %get-tuple-element.146), channel_id=1, source_target_pairs={{0,12},{1,13},{2,14},{3,15},{4,8},{5,9},{6,10},{7,11},{8,4},{9,5},... | collective-permute-start | bytes 884744 | tf_op jit(solution)/shard_map/ppermute | solution.py:572
  105.6 11.4 %collective-permute-start.22 = (bf16[4,96,384]{2,1,0:T(8,128)(2,1)}, bf16[4,96,384]{2,1,0:T(8,128)(2,1)S(1)}, u32[]{:S(2)}, u32[]{:S(2)}) collective-permute-start(bf16[4,96,384]{2,1,0:T(8,128)(2,1)} %get-tuple-element.147), channel_id=1, source_target_pairs={{0,4},{1,5},{2,6},{3,7},{4,12},{5,13},{6,14},{7,15},{8,0},{9,1},{1... | collective-permute-start | bytes 884744 | tf_op jit(solution)/shard_map/ppermute | solution.py:572
  107.1 2.5 %copy-start.1 = (bf16[384,2048]{1,0:T(8,128)(2,1)S(1)}, bf16[384,2048]{1,0:T(8,128)(2,1)}, u32[]{:S(2)}) copy-start(bf16[384,2048]{1,0:T(8,128)(2,1)} %get-tuple-element.158.refs_1_) | copy-start | bytes 4718596
  107.1 2.5 %copy-start.2 = (bf16[384,2048]{1,0:T(8,128)(2,1)S(1)}, bf16[384,2048]{1,0:T(8,128)(2,1)}, u32[]{:S(2)}) copy-start(bf16[384,2048]{1,0:T(8,128)(2,1)} %get-tuple-element.159.refs_2_) | copy-start | bytes 4718596
  107.1 21.5 %slice-start.2 = ((s8[6291456]{0:T(1024)(128)(4,1)}), s8[4194304]{0:T(1024)(128)(4,1)S(1)}, s32[]{:S(2)}) async-start(s8[6291456]{0:T(1024)(128)(4,1)} %bitcast.67), calls=%async_computation.2 | async-start | bytes 8388608
  112.4 16.2 %slice-start = ((s8[6291456]{0:T(1024)(128)(4,1)}), s8[4194304]{0:T(1024)(128)(4,1)S(1)}, s32[]{:S(2)}) async-start(s8[6291456]{0:T(1024)(128)(4,1)} %bitcast.63), calls=%async_computation | async-start | bytes 8388608
  112.4 16.2 %slice-start.3 = ((s8[6291456]{0:T(1024)(128)(4,1)}), s8[2097152]{0:T(1024)(128)(4,1)S(1)}, s32[]{:S(2)}) async-start(s8[6291456]{0:T(1024)(128)(4,1)} %bitcast.67), calls=%async_computation.3 | async-start | bytes 4194304
  116.9 6.5 %collective-permute-start.26 = (bf16[2,192,2048]{2,1,0:T(8,128)(2,1)S(1)}, bf16[2,192,2048]{2,1,0:T(8,128)(2,1)S(1)}, u32[]{:S(2)}, u32[]{:S(2)}) collective-permute-start(bf16[2,192,2048]{2,1,0:T(8,128)(2,1)S(1)} %get-tuple-element.156), channel_id=1, source_target_pairs={{0,16},{16,0},{1,17},{17,1},{2,18},{18,2},{3,19},{19,3},{4,20},{20... | collective-permute-start | bytes 4718600 | tf_op jit(solution)/shard_map/ppermute | solution.py:674
  117.0 5.1 %copy-start.6 = (bf16[4,96,384]{2,1,0:T(8,128)(2,1)}, bf16[4,96,384]{2,1,0:T(8,128)(2,1)S(1)}, u32[]{:S(2)}) copy-start(bf16[4,96,384]{2,1,0:T(8,128)(2,1)S(1)} %collective-permute-done.21.refs_2_) | copy-start | bytes 884740
  117.0 5.1 %copy-start.8 = (bf16[4,96,384]{2,1,0:T(8,128)(2,1)}, bf16[4,96,384]{2,1,0:T(8,128)(2,1)S(1)}, u32[]{:S(2)}) copy-start(bf16[4,96,384]{2,1,0:T(8,128)(2,1)S(1)} %collective-permute-done.22.refs_3_) | copy-start | bytes 884740
  117.0 5.1 %copy-start.7 = (bf16[4,96,384]{2,1,0:T(8,128)(2,1)S(1)}, bf16[4,96,384]{2,1,0:T(8,128)(2,1)}, u32[]{:S(2)}) copy-start(bf16[4,96,384]{2,1,0:T(8,128)(2,1)} %get-tuple-element.148.refs_0_) | copy-start | bytes 884740
  117.1 11.6 %slice-start.1 = ((s8[6291456]{0:T(1024)(128)(4,1)}), s8[2097152]{0:T(1024)(128)(4,1)S(1)}, s32[]{:S(2)}) async-start(s8[6291456]{0:T(1024)(128)(4,1)} %bitcast.63), calls=%async_computation.1 | async-start | bytes 4194304
  121.6 3.6 %collective-permute-start.27 = (bf16[2,192,2048]{2,1,0:T(8,128)(2,1)S(1)}, bf16[2,192,2048]{2,1,0:T(8,128)(2,1)S(1)}, u32[]{:S(2)}, u32[]{:S(2)}) collective-permute-start(bf16[2,192,2048]{2,1,0:T(8,128)(2,1)S(1)} %get-tuple-element.162), channel_id=1, source_target_pairs={{0,16},{16,0},{1,17},{17,1},{2,18},{18,2},{3,19},{19,3},{4,20},{20... | collective-permute-start | bytes 4718600 | tf_op jit(solution)/shard_map/ppermute | solution.py:674
  125.1 14.3 %collective-permute-start.28 = (bf16[4,96,384]{2,1,0:T(8,128)(2,1)S(1)}, bf16[4,96,384]{2,1,0:T(8,128)(2,1)S(1)}, u32[]{:S(2)}, u32[]{:S(2)}) collective-permute-start(bf16[4,96,384]{2,1,0:T(8,128)(2,1)S(1)} %get-tuple-element.170), channel_id=1, source_target_pairs={{0,1},{1,0},{2,3},{3,2},{4,5},{5,4},{6,7},{7,6},{8,9},{9,8},{10,11... | collective-permute-start | bytes 884744 | tf_op jit(solution)/shard_map/ppermute | solution.py:572
  125.6 13.8 %collective-permute-start.29 = (bf16[4,96,384]{2,1,0:T(8,128)(2,1)S(1)}, bf16[4,96,384]{2,1,0:T(8,128)(2,1)S(1)}, u32[]{:S(2)}, u32[]{:S(2)}) collective-permute-start(bf16[4,96,384]{2,1,0:T(8,128)(2,1)S(1)} %get-tuple-element.171), channel_id=1, source_target_pairs={{0,2},{1,3},{2,0},{3,1},{4,6},{5,7},{6,4},{7,5},{8,10},{9,11},{10,... | collective-permute-start | bytes 884744 | tf_op jit(solution)/shard_map/ppermute | solution.py:572
  127.2 14.5 %collective-permute-start.30 = (bf16[4,96,384]{2,1,0:T(8,128)(2,1)S(1)}, bf16[4,96,384]{2,1,0:T(8,128)(2,1)S(1)}, u32[]{:S(2)}, u32[]{:S(2)}) collective-permute-start(bf16[4,96,384]{2,1,0:T(8,128)(2,1)S(1)} %get-tuple-element.172), channel_id=1, source_target_pairs={{0,3},{1,2},{2,1},{3,0},{4,7},{5,6},{6,5},{7,4},{8,11},{9,10},{10,... | collective-permute-start | bytes 884744 | tf_op jit(solution)/shard_map/ppermute | solution.py:572
  128.7 2.8 %copy-start = (f32[192,4,2048]{2,1,0:T(4,128)S(1)}, f32[192,4,2048]{2,1,0:T(4,128)}, u32[]{:S(2)}) copy-start(f32[192,4,2048]{2,1,0:T(4,128)} %param.15) | copy-start | bytes 18874372
  139.4 6.6 %copy-start.25 = (bf16[4,96,384]{2,1,0:T(8,128)(2,1)}, bf16[4,96,384]{2,1,0:T(8,128)(2,1)S(1)}, u32[]{:S(2)}) copy-start(bf16[4,96,384]{2,1,0:T(8,128)(2,1)S(1)} %collective-permute-done.28.refs_4_) | copy-start | bytes 884740
  139.4 6.6 %copy-start.26 = (bf16[4,96,384]{2,1,0:T(8,128)(2,1)}, bf16[4,96,384]{2,1,0:T(8,128)(2,1)S(1)}, u32[]{:S(2)}) copy-start(bf16[4,96,384]{2,1,0:T(8,128)(2,1)S(1)} %collective-permute-done.29.refs_5_) | copy-start | bytes 884740
  141.7 4.4 %copy-start.27 = (bf16[4,96,384]{2,1,0:T(8,128)(2,1)}, bf16[4,96,384]{2,1,0:T(8,128)(2,1)S(1)}, u32[]{:S(2)}) copy-start(bf16[4,96,384]{2,1,0:T(8,128)(2,1)S(1)} %collective-permute-done.30.refs_6_) | copy-start | bytes 884740
  146.1 8.0 %collective-permute-start.31 = (bf16[12288,128]{1,0:T(8,128)(2,1)}, bf16[12288,128]{1,0:T(8,128)(2,1)S(1)}, u32[]{:S(2)}, u32[]{:S(2)}) collective-permute-start(bf16[12288,128]{1,0:T(8,128)(2,1)} %get-tuple-element.190), channel_id=1, source_target_pairs={{0,16},{16,0},{1,17},{17,1},{2,18},{18,2},{3,19},{19,3},{4,20},{20... | collective-permute-start | bytes 9437192 | tf_op jit(solution)/shard_map/ppermute | solution.py:692
  (5 other events, 9.0 us)

commit v7 on v6

--- a/solution.py
+++ b/solution.py
@@ -74,14 +74,14 @@
     return (at[:, None] * 4 + (me % 4 ^ flips)[None, :]).reshape(size)
 
 
-def grads_kernel(spans, first, *refs):
+def grads_kernel(spans, keep, first, *refs):
     chunks = len(spans)
     parts = [
         [ref.at[pl.ds(*span)] for ref, span in zip(refs[5 * j :], spans[j])]
         for j in range(chunks)
     ]
     by_expert, outs = refs[5 * chunks], refs[5 * chunks + 1 : 7 * chunks + 1]
-    all_rows, match, all_d_rows, all_grads, weights, sems, weight_sems = refs[-7:]
+    all_rows, match, all_grads, weights, sems, weight_sems, *all_d_rows = refs[7 * chunks + 1 :]
     experts, width, features = by_expert.shape
     tokens = all_rows.shape[1] // 4
     slots = experts * CAP
@@ -107,7 +107,8 @@
     earlier = jnp.where(earlier, 1.0, 0.0).astype(jnp.bfloat16)
     stores = []
     for j in range(chunks):
-        rows, d_rows, grads = all_rows.at[j], all_d_rows.at[j], all_grads.at[j]
+        rows, grads = all_rows.at[j], all_grads.at[j]
+        d_rows = outs[2 * j] if keep else all_d_rows[0].at[j]
         for load in loads[j]:
             load.wait()
         if j == 0:
@@ -137,8 +138,9 @@
             d_rows[:, at : at + step] = jnp.dot(
                 match[...], rows[:, at : at + step], preferred_element_type=jnp.float32
             ).astype(jnp.bfloat16)
-        stores.append(pltpu.make_async_copy(d_rows, outs[2 * j], sems.at[j, 5]))
-        stores[-1].start()
+        if not keep:
+            stores.append(pltpu.make_async_copy(d_rows, outs[2 * j], sems.at[j, 5]))
+            stores[-1].start()
         count = 4 * CAP
         found = []
         for e in range(experts):
@@ -161,31 +163,31 @@
         store.wait()
 
 
-def chunk_grads(first, parts, by_expert, vmem):
+def chunk_grads(first, parts, by_expert, keep):
     experts, width, features = by_expert.shape
     tokens, columns = parts[0][0][0].shape
     spans = tuple(tuple(piece[1:] for piece in part) for part in parts)
     slots = experts * CAP
     chunks = len(parts)
     found = pl.pallas_call(
-        functools.partial(grads_kernel, spans),
+        functools.partial(grads_kernel, spans, keep),
         out_shape=[
             jax.ShapeDtypeStruct((4 * slots, features), jnp.bfloat16),
             jax.ShapeDtypeStruct((4, slots, width), jnp.bfloat16),
         ]
         * chunks,
         in_specs=[pl.BlockSpec(memory_space=pltpu.SMEM)] + [HBM] * (5 * chunks + 1),
-        out_specs=[HBM] * (2 * chunks),
+        out_specs=[INSIDE if keep else HBM, HBM] * chunks,
         scratch_shapes=[
             pltpu.VMEM((chunks, 4 * tokens, columns), jnp.bfloat16),
             pltpu.VMEM((4 * slots, 4 * tokens), jnp.bfloat16),
-            pltpu.VMEM((chunks, 4 * slots, features), jnp.bfloat16),
             pltpu.VMEM((chunks, 4, slots, width), jnp.bfloat16),
             pltpu.VMEM(by_expert.shape, jnp.bfloat16),
             pltpu.SemaphoreType.DMA((chunks, 7)),
             pltpu.SemaphoreType.DMA((experts,)),
-        ],
-        compiler_params=pltpu.CompilerParams(vmem_limit_bytes=vmem * MIB),
+        ]
+        + ([] if keep else [pltpu.VMEM((chunks, 4 * slots, features), jnp.bfloat16)]),
+        compiler_params=pltpu.CompilerParams(vmem_limit_bytes=(52 if keep else 56) * MIB),
         cost_estimate=pl.CostEstimate(
             flops=8 * chunks * slots * features * (4 * tokens + width),
             bytes_accessed=8 * chunks * (slots + tokens) * features,
@@ -467,7 +469,7 @@
     for load in loads:
         load.start()
     targets, scales = target[...].T, probs[...].T
-    for load in loads:
+    for load in loads[:-1]:
         load.wait()
     ones = jnp.ones((8, width), jnp.bfloat16)
     across = (((1,), (1,)), ((), ()))
@@ -487,6 +489,8 @@
             pltpu.make_async_copy(outs.at[here], d_hidden.at[here], sems.at[len(loads) + n])
         )
         stores[n].start()
+        if n == 0:
+            loads[-1].wait()
         product = states[here].astype(jnp.float32) * g
         high = product.astype(jnp.bfloat16)
         low = (product - high.astype(jnp.float32)).astype(jnp.bfloat16)
@@ -581,8 +585,8 @@
     near, parts, w_parts = {}, {}, {}
     d_rows, grads, back = {}, {}, {}
 
-    def add_chunks(*chunks, vmem=56):
-        found = chunk_grads(first, [parts[j] for j in chunks], by_expert, vmem)
+    def add_chunks(*chunks, keep=False):
+        found = chunk_grads(first, [parts[j] for j in chunks], by_expert, keep)
         for j, d_chunk, g_chunk in zip(chunks, *found):
             d_rows[j], grads[j] = d_chunk, g_chunk
 
@@ -652,7 +656,7 @@
     back[last - 1] = move(grads[last - 1], 1 - last, 0)
     parts[last] = whole(*near[last]) + tuple((f, 0, half) for f in moved["far"])
     parts[0] = whole(*near[0]) + tuple((f, half, half) for f in moved["far"])
-    add_chunks(last, 0, vmem=56)
+    add_chunks(last, 0)
     back[last] = move(grads[last], -last, 0)
     back[0] = grads[0]
     back = [back[j] for j in range(length)]
@@ -679,7 +683,7 @@
     at = outer_at.astype(jnp.int32)[None]
     total_rows = secondary.size // LANES
     blocks = rows // 16
-    cuts = [0, blocks - blocks // 3, blocks]
+    cuts = [0, blocks - max(1, blocks // 6), blocks]
     outs = []
     for start, stop in zip(cuts[:-1], cuts[1:]):
         if stop == blocks:

time: 157 us -> 155 us (0.987)
  waiting for transfers between devices: 33 us -> 31.2 us
    ppermute x29, waiting for transfers between devices: 31.3 us -> 29.5 us  [move(): return lax.ppermute(block, 'inner', step_perm(size, steps, flip))]
  transfers between devices with their start and end apart: 32 -> 32, of which waited for: 12 -> 12; matrix products, arithmetic and copies ran while one was open for 11% -> 11% of each run, Pallas kernels for 33% -> 35%
where the time goes in v7:
time: 155 us
  Pallas kernels  59.2 us (38%)
  starting transfers between devices  38.8 us (25%)
  waiting for transfers between devices  31.2 us (20%)
  local copies, waits for them, and re-layouts  18 us (12%)
  matrix products  3.51 us (2%)
  other arithmetic  2.7 us (2%)
    ppermute x29, starting transfers between devices, move(): return lax.ppermute(block, 'inner', step_perm(size, steps, flip))  38.1 us
    ppermute x29, waiting for transfers between devices, move(): return lax.ppermute(block, 'inner', step_perm(size, steps, flip))  29.5 us
    pallas_call x3, Pallas kernels, chunk_grads(): pl.pallas_call(functools.partial(grads_kernel, spans, keep), out_shape=[j...  23.3 us
    unnamed x74, local copies, waits for them, and re-layouts  13.4 us
    pallas_call x2, Pallas kernels, adam_rows(): pl.pallas_call(functools.partial(adam_kernel, count, owners, kept, first)...  12.3 us
    pallas_call x2, Pallas kernels, partial_rows(): pl.pallas_call(functools.partial(partial_kernel, start, total), out_shape...  8.97 us
    pallas_call x1, Pallas kernels, finish(): pl.pallas_call(functools.partial(finish_kernel, pieces), out_shape=(jax.S...  6.16 us
    pallas_call x2, Pallas kernels, regroup(): pl.pallas_call(regroup_kernel, out_shape=[jax.ShapeDtypeStruct((count, sl...  3.29 us
  transfers between devices with their start and end apart: 32, of which 12 were waited for; matrix products, arithmetic and copies ran while one was open for 11% of the time, Pallas kernels for 35%

profile of v7, /device:TPU:0, one launch (start us, length us, event | category | flops | bytes accessed | tf_op | source)
XLA Modules:
  0.0 154.7 jit_solution(5376901265870701258)
XLA Ops:
  0.6 0.7 convert_element_type.46
  1.5 1.1 fusion.9.refs_5_
  2.6 3.1 %collective-permute-start = (bf16[128,2176]{1,0:T(8,128)(2,1)S(1)}, bf16[128,2176]{1,0:T(8,128)(2,1)S(1)}, u32[]{:S(2)}, u32[]{:S(2)}) collective-permute-start(bf16[128,2176]{1,0:T(8,128)(2,1)S(1)} %fusion.9.refs_5_), channel_id=1, source_target_pairs={{0,4},{1,5},{2,6},{3,7},{4,12},{5,13},{6,14},{7,15},{8,0},{9,1},{1... | collective-permute-start | bytes 1671176 | tf_op jit(solution)/shard_map/ppermute | solution.py:576
  5.6 1.5 collective-permute-start.1
  7.1 1.5 collective-permute-start.2
  8.7 0.8 copy.49
  10.2 0.6 fusion.27.target
  11.0 0.7 reshape.249.probs
  11.7 3.2 %fusion.2 = bf16[1536,384]{1,0:T(8,128)(2,1)S(1)} fusion(s32[1024]{0:T(1024)S(1)} %fusion.41, bf16[128,8,384]{2,1,0:T(8,128)(2,1)} %param.9, f32[128,8]{1,0:T(8,128)S(1)} %copy.51), kind=kOutput, calls=%fused_computation.4 | convolution fusion | flops 1211301888 | bytes 1974272 | tf_op jit(solution)/shard_map/dot_general | solution.py:568
  14.9 4.4 %collective-permute-done.refs_0_ = bf16[128,2176]{1,0:T(8,128)(2,1)S(1)} collective-permute-done((bf16[128,2176]{1,0:T(8,128)(2,1)S(1)}, bf16[128,2176]{1,0:T(8,128)(2,1)S(1)}, u32[]{:S(2)}, u32[]{:S(2)}) %collective-permute-start) | collective-permute-done | bytes 557088 | tf_op jit(solution)/shard_map/ppermute | solution.py:576
  19.7 1.2 collective-permute-done.2.refs_7_
  20.9 2.6 %collective-permute-start.3 = (bf16[128,2176]{1,0:T(8,128)(2,1)S(1)}, bf16[128,2176]{1,0:T(8,128)(2,1)S(1)}, u32[]{:S(2)}, u32[]{:S(2)}) collective-permute-start(bf16[128,2176]{1,0:T(8,128)(2,1)S(1)} %collective-permute-done.refs_0_), channel_id=1, source_target_pairs={{0,4},{1,5},{2,6},{3,7},{4,12},{5,13},{6,14},{7,15},{8,0},{9,1},{1... | collective-permute-start | bytes 1671176 | tf_op jit(solution)/shard_map/ppermute | solution.py:576
  23.5 0.5 collective-permute-start.4
  24.1 1.5 collective-permute-start.5
  25.6 1.0 slice_bitcast_fusion
  26.6 8.2 %collective-permute-done.3.refs_0_ = bf16[128,2176]{1,0:T(8,128)(2,1)S(1)} collective-permute-done((bf16[128,2176]{1,0:T(8,128)(2,1)S(1)}, bf16[128,2176]{1,0:T(8,128)(2,1)S(1)}, u32[]{:S(2)}, u32[]{:S(2)}) %collective-permute-start.3) | collective-permute-done | bytes 557088 | tf_op jit(solution)/shard_map/ppermute | solution.py:576
  34.7 1.4 collective-permute-done.4.refs_1_
  36.1 0.6 collective-permute-done.5.refs_2_
  36.8 1.6 %collective-permute-start.7 = (bf16[64,2176]{1,0:T(8,128)(2,1)S(1)}, bf16[64,2176]{1,0:T(8,128)(2,1)S(1)}, u32[]{:S(2)}, u32[]{:S(2)}) collective-permute-start(bf16[64,2176]{1,0:T(8,128)(2,1)S(1)} %slice.45), channel_id=1, source_target_pairs={{0,2},{1,3},{2,0},{3,1},{4,6},{5,7},{6,4},{7,5},{8,10},{9,11},{10,... | collective-permute-start | bytes 835592 | tf_op jit(solution)/shard_map/ppermute | solution.py:576
  38.4 1.2 collective-permute-start.9
  39.6 0.5 collective-permute-start.10
  40.1 0.5 collective-permute-start.11
  40.7 1.0 collective-permute-start.6
  41.6 4.8 %collective-permute-done.7.refs_3_ = bf16[64,2176]{1,0:T(8,128)(2,1)S(1)} collective-permute-done((bf16[64,2176]{1,0:T(8,128)(2,1)S(1)}, bf16[64,2176]{1,0:T(8,128)(2,1)S(1)}, u32[]{:S(2)}, u32[]{:S(2)}) %collective-permute-start.7) | collective-permute-done | bytes 278560 | tf_op jit(solution)/shard_map/ppermute | solution.py:576
  46.5 1.4 collective-permute-start.8
  47.9 6.2 %copy.66 = bf16[384,4,2048]{2,0,1:T(8,128)(2,1)} copy(bf16[384,4,2048]{2,1,0:T(4,128)(2,1)S(1)} %bitcast.78) | data formatting | bytes 12582912 | tf_op args[4]
  54.1 3.6 %collective-permute-done.8.refs_4_ = bf16[64,2176]{1,0:T(8,128)(2,1)S(1)} collective-permute-done((bf16[64,2176]{1,0:T(8,128)(2,1)S(1)}, bf16[64,2176]{1,0:T(8,128)(2,1)S(1)}, u32[]{:S(2)}, u32[]{:S(2)}) %collective-permute-start.8) | collective-permute-done | bytes 278560 | tf_op jit(solution)/shard_map/ppermute | solution.py:576
  57.8 0.6 collective-permute-start.16
  58.5 1.9 %collective-permute-start.17 = (bf16[128,2176]{1,0:T(8,128)(2,1)}, bf16[128,2176]{1,0:T(8,128)(2,1)}, u32[]{:S(2)}, u32[]{:S(2)}) collective-permute-start(bf16[128,2176]{1,0:T(8,128)(2,1)} %collective-permute-done.9.refs_0_), channel_id=1, source_target_pairs={{0,2},{1,3},{2,0},{3,1},{4,6},{5,7},{6,4},{7,5},{8,10},{9,11},{10,... | collective-permute-start | bytes 1671176 | tf_op jit(solution)/shard_map/ppermute | solution.py:576
  60.4 1.8 %collective-permute-start.12 = (bf16[4,96,384]{2,1,0:T(8,128)(2,1)}, bf16[4,96,384]{2,1,0:T(8,128)(2,1)S(1)}, u32[]{:S(2)}, u32[]{:S(2)}) collective-permute-start(bf16[4,96,384]{2,1,0:T(8,128)(2,1)} %get-tuple-element.119), channel_id=1, source_target_pairs={{0,12},{1,13},{2,14},{3,15},{4,8},{5,9},{6,10},{7,11},{8,4},{9,5},... | collective-permute-start | bytes 884744 | tf_op jit(solution)/shard_map/ppermute | solution.py:576
  62.2 0.8 collective-permute-start.13
  63.0 0.7 slice.48
  63.8 3.7 %collective-permute-done.14.refs_3_ = bf16[64,2176]{1,0:T(8,128)(2,1)S(1)} collective-permute-done((bf16[64,2176]{1,0:T(8,128)(2,1)S(1)}, bf16[64,2176]{1,0:T(8,128)(2,1)S(1)}, u32[]{:S(2)}, u32[]{:S(2)}) %collective-permute-start.14) | collective-permute-done | bytes 278560 | tf_op jit(solution)/shard_map/ppermute | solution.py:576
  67.4 0.5 collective-permute-start.15
  68.0 6.8 %shard_map.127 = (bf16[384,2048]{1,0:T(8,128)(2,1)}, bf16[4,96,384]{2,1,0:T(8,128)(2,1)}) custom-call(s32[1]{0:T(128)} %bitcast.5.first, bf16[128,2176]{1,0:T(8,128)(2,1)} %copy-done.19, bf16[128,2176]{1,0:T(8,128)(2,1)} %copy-done.17, bf16[128,2176]{1,0:T(8,128)(2,1)} %copy-done.18, bf16[64,2176]{1,0:T(8,128)(2,1)} %copy-done.22, ...), custom_call_target="tpu_custom_call" | custom-call | flops 1409286144 | bytes 3670016 | tf_op jit(solution)/shard_map/pallas_call | solution.py:172
  74.8 0.7 collective-permute-done.15.refs_4_
  76.0 1.0 slice.50
  77.1 0.7 collective-permute-start.20
  77.8 3.0 %collective-permute-start.18 = (bf16[4,96,384]{2,1,0:T(8,128)(2,1)S(1)}, bf16[4,96,384]{2,1,0:T(8,128)(2,1)S(1)}, u32[]{:S(2)}, u32[]{:S(2)}) collective-permute-start(bf16[4,96,384]{2,1,0:T(8,128)(2,1)S(1)} %copy-done.28), channel_id=1, source_target_pairs={{0,8},{1,9},{2,10},{3,11},{4,0},{5,1},{6,2},{7,3},{8,12},{9,13},{1... | collective-permute-start | bytes 884744 | tf_op jit(solution)/shard_map/ppermute | solution.py:576
  80.7 2.0 %shard_map.130 = (bf16[4,96,384]{2,1,0:T(8,128)(2,1)}, bf16[4,96,384]{2,1,0:T(8,128)(2,1)}, bf16[4,96,384]{2,1,0:T(8,128)(2,1)S(1)}) custom-call(bf16[4,96,384]{2,1,0:T(8,128)(2,1)S(1)} %get-tuple-element.132.refs_0_, bf16[4,96,384]{2,1,0:T(8,128)(2,1)S(1)} %collective-permute-done.6.refs_1_, bf16[4,96,384]{2,1,0:T(8,128)(2,1)S(1)} %collective-permute-done.12.refs_2_, ...), custom_call_target="tpu_custom_call" | custom-call | bytes 1769472 | tf_op jit(solution)/shard_map/pallas_call | solution.py:267
  82.7 1.6 %collective-permute-start.23 = (bf16[4,96,384]{2,1,0:T(8,128)(2,1)}, bf16[4,96,384]{2,1,0:T(8,128)(2,1)S(1)}, u32[]{:S(2)}, u32[]{:S(2)}) collective-permute-start(bf16[4,96,384]{2,1,0:T(8,128)(2,1)} %get-tuple-element.152), channel_id=1, source_target_pairs={{0,1},{1,0},{2,3},{3,2},{4,5},{5,4},{6,7},{7,6},{8,9},{9,8},{10,11... | collective-permute-start | bytes 884744 | tf_op jit(solution)/shard_map/ppermute | solution.py:576
  84.4 1.5 collective-permute-start.24
  85.9 6.7 %shard_map.128 = (bf16[384,2048]{1,0:T(8,128)(2,1)}, bf16[4,96,384]{2,1,0:T(8,128)(2,1)}) custom-call(s32[1]{0:T(128)} %bitcast.5.first, bf16[128,2176]{1,0:T(8,128)(2,1)} %copy-done.20, bf16[128,2176]{1,0:T(8,128)(2,1)} %copy-done.14, bf16[128,2176]{1,0:T(8,128)(2,1)} %copy-done.15, bf16[64,2176]{1,0:T(8,128)(2,1)} %copy-done.21, ...), custom_call_target="tpu_custom_call" | custom-call | flops 1409286144 | bytes 3670016 | tf_op jit(solution)/shard_map/pallas_call | solution.py:172
  93.1 2.7 %collective-permute-start.21 = (bf16[4,96,384]{2,1,0:T(8,128)(2,1)}, bf16[4,96,384]{2,1,0:T(8,128)(2,1)S(1)}, u32[]{:S(2)}, u32[]{:S(2)}) collective-permute-start(bf16[4,96,384]{2,1,0:T(8,128)(2,1)} %get-tuple-element.146), channel_id=1, source_target_pairs={{0,12},{1,13},{2,14},{3,15},{4,8},{5,9},{6,10},{7,11},{8,4},{9,5},... | collective-permute-start | bytes 884744 | tf_op jit(solution)/shard_map/ppermute | solution.py:576
  95.8 9.8 %shard_map.129 = (bf16[384,2048]{1,0:T(8,128)(2,1)}, bf16[4,96,384]{2,1,0:T(8,128)(2,1)}, bf16[384,2048]{1,0:T(8,128)(2,1)}, bf16[4,96,384]{2,1,0:T(8,128)(2,1)}) custom-call(s32[1]{0:T(128)} %bitcast.5.first, bf16[128,2176]{1,0:T(8,128)(2,1)} %collective-permute-done.9.refs_0_, bf16[128,2176]{1,0:T(8,128)(2,1)} %copy-done.16, ...), custom_call_target="tpu_custom_call" | custom-call | flops 2818572288 | bytes 7340032 | tf_op jit(solution)/shard_map/pallas_call | solution.py:172
  105.6 1.4 collective-permute-start.22
  107.1 2.5 %shard_map.131.weighted = bf16[4,384,384]{2,1,0:T(8,128)(2,1)S(1)} custom-call(bf16[4,96,384]{2,1,0:T(8,128)(2,1)S(1)} %get-tuple-element.132.refs_0_, bf16[4,96,384]{2,1,0:T(8,128)(2,1)S(1)} %collective-permute-done.6.refs_1_, bf16[4,96,384]{2,1,0:T(8,128)(2,1)S(1)} %collective-permute-done.12.refs_2_, ...), custom_call_target="tpu_custom_call" | custom-call | bytes 4718592 | tf_op jit(solution)/shard_map/pallas_call | solution.py:225
  109.6 1.4 copy-done.3
  111.0 1.4 copy-done.4
  112.4 4.5 %shard_map.132 = (bf16[2,192,2048]{2,1,0:T(8,128)(2,1)S(1)}, bf16[2,192,2048]{2,1,0:T(8,128)(2,1)S(1)}) custom-call(s32[2]{0:T(128)S(1)} %and_select_fusion.owners, bf16[4,384,384]{2,1,0:T(8,128)(2,1)S(1)} %shard_map.131.weighted, bf16[384,2048]{1,0:T(8,128)(2,1)S(1)} %copy-done.4, bf16[384,2048]{1,0:T(8,128)(2,1)S(1)} %copy-done.1, ...), custom_call_target="tpu_custom_call" | custom-call | flops 1207959552 | bytes 6291456 | tf_op jit(solution)/shard_map/pallas_call | solution.py:332
  117.1 4.5 %shard_map.133 = (bf16[2,192,2048]{2,1,0:T(8,128)(2,1)S(1)}, bf16[2,192,2048]{2,1,0:T(8,128)(2,1)S(1)}) custom-call(s32[2]{0:T(128)S(1)} %and_select_fusion.owners, bf16[4,384,384]{2,1,0:T(8,128)(2,1)S(1)} %shard_map.131.weighted, bf16[384,2048]{1,0:T(8,128)(2,1)S(1)} %copy-done.4, bf16[384,2048]{1,0:T(8,128)(2,1)S(1)} %copy-done.1, ...), custom_call_target="tpu_custom_call" | custom-call | flops 1207959552 | bytes 6291456 | tf_op jit(solution)/shard_map/pallas_call | solution.py:332
  121.6 0.5 collective-permute-start.27
  122.1 1.3 shard_map.134
  123.4 1.7 %collective-permute-done.27.refs_3_ = bf16[2,192,2048]{2,1,0:T(8,128)(2,1)S(1)} collective-permute-done((bf16[2,192,2048]{2,1,0:T(8,128)(2,1)S(1)}, bf16[2,192,2048]{2,1,0:T(8,128)(2,1)S(1)}, u32[]{:S(2)}, u32[]{:S(2)}) %collective-permute-start.27) | collective-permute-done | bytes 1572896 | tf_op jit(solution)/shard_map/ppermute | solution.py:678
  125.1 0.5 collective-permute-start.28
  125.6 1.5 collective-permute-start.29
  127.2 1.5 collective-permute-start.30
  128.7 2.8 %copy-done = f32[192,4,2048]{2,1,0:T(4,128)S(1)} copy-done((f32[192,4,2048]{2,1,0:T(4,128)S(1)}, f32[192,4,2048]{2,1,0:T(4,128)}, u32[]{:S(2)}) %copy-start) | copy-done | bytes 6291480
  131.4 9.8 %shard_map.136 = (f32[12288,128]{1,0:T(8,128)}, f32[12288,128]{1,0:T(8,128)}, f32[12288,128]{1,0:T(8,128)}, bf16[24576,128]{1,0:T(8,128)(2,1)}, bf16[12288,128]{1,0:T(8,128)(2,1)}) custom-call(s32[1]{0:T(128)} %bitcast.12.at, bf16[2,192,2048]{2,1,0:T(8,128)(2,1)S(1)} %get-tuple-element.178.refs_0_, ...), custom_call_target="tpu_custom_call" | custom-call | bytes 65536 | tf_op jit(solution)/shard_map/pallas_call | solution.py:416
  141.7 2.6 %shard_map.137 = (f32[12288,128]{1,0:T(8,128)}, f32[12288,128]{1,0:T(8,128)}, f32[12288,128]{1,0:T(8,128)}, bf16[24576,128]{1,0:T(8,128)(2,1)}, bf16[12288,128]{1,0:T(8,128)(2,1)}) custom-call(s32[1]{0:T(128)} %bitcast.12.at, ...), custom_call_target="tpu_custom_call", output_to_operand_aliasing={{0}: (8, {}), {1}: (9, {}), {2}: (10, {}), {3}: (11, {}), {... | custom-call | bytes 65536 | tf_op jit(solution)/shard_map/pallas_call | solution.py:416
  144.4 6.2 %shard_map.135 = (bf16[1024,384]{1,0:T(8,128)(2,1)}, f32[8,1024]{1,0:T(8,128)}) custom-call(f32[8,128]{1,0:T(8,128)} %fusion.27.target, f32[8,128]{1,0:T(8,128)} %reshape.249.probs, bf16[1024,384]{1,0:T(8,128)(2,1)} %bitcast.83, bf16[4,96,384]{2,1,0:T(8,128)(2,1)} %get-tuple-element.148.refs_0_, bf16[4,96,384]{2,1,0:T(8,128)(2,1)} %copy-done.5, ...), custom_call_target="tpu_custom_call" | custom-call | flops 1207959552 | bytes 3145728 | tf_op jit(solution)/shard_map/pallas_call | solution.py:509
  150.6 0.8 slice_reduce_fusion
  151.4 0.7 copy.63
  152.1 2.7 %shard_map.138 = bf16[24576,128]{1,0:T(8,128)(2,1)} custom-call(s32[1]{0:T(128)} %bitcast.37.at, bf16[12288,128]{1,0:T(8,128)(2,1)S(1)} %collective-permute-done.31.got, bf16[24576,128]{1,0:T(8,128)(2,1)} %get-tuple-element.191.full), custom_call_target="tpu_custom_call", output_to_operand_aliasing={{}: (2, {})} | custom-call | bytes 6291456 | tf_op jit(solution)/shard_map/pallas_call | solution.py:444
  (117 shorter events, 3.5 us)
Async XLA Ops:
  0.6 10.3 %copy-start.24 = (f32[128,8]{0,1:T(8,128)S(1)}, f32[128,8]{0,1:T(8,128)}, u32[]{:S(2)}) copy-start(f32[128,8]{0,1:T(8,128)} %param.10) | copy-start | bytes 12292
  2.6 12.4 %copy-start.11 = (bf16[128,2176]{1,0:T(8,128)(2,1)}, bf16[128,2176]{1,0:T(8,128)(2,1)S(1)}, u32[]{:S(2)}) copy-start(bf16[128,2176]{1,0:T(8,128)(2,1)S(1)} %fusion.9.refs_5_) | copy-start | bytes 1671172
  2.6 16.7 %collective-permute-start = (bf16[128,2176]{1,0:T(8,128)(2,1)S(1)}, bf16[128,2176]{1,0:T(8,128)(2,1)S(1)}, u32[]{:S(2)}, u32[]{:S(2)}) collective-permute-start(bf16[128,2176]{1,0:T(8,128)(2,1)S(1)} %fusion.9.refs_5_), channel_id=1, source_target_pairs={{0,4},{1,5},{2,6},{3,7},{4,12},{5,13},{6,14},{7,15},{8,0},{9,1},{1... | collective-permute-start | bytes 1671176 | tf_op jit(solution)/shard_map/ppermute | solution.py:576
  5.6 14.1 %collective-permute-start.1 = (bf16[128,2176]{1,0:T(8,128)(2,1)S(1)}, bf16[128,2176]{1,0:T(8,128)(2,1)S(1)}, u32[]{:S(2)}, u32[]{:S(2)}) collective-permute-start(bf16[128,2176]{1,0:T(8,128)(2,1)S(1)} %fusion.9.refs_5_), channel_id=1, source_target_pairs={{0,1},{1,0},{2,3},{3,2},{4,5},{5,4},{6,7},{7,6},{8,9},{9,8},{10,11... | collective-permute-start | bytes 1671176 | tf_op jit(solution)/shard_map/ppermute | solution.py:576
  7.1 13.8 %collective-permute-start.2 = (bf16[128,2176]{1,0:T(8,128)(2,1)S(1)}, bf16[128,2176]{1,0:T(8,128)(2,1)S(1)}, u32[]{:S(2)}, u32[]{:S(2)}) collective-permute-start(bf16[128,2176]{1,0:T(8,128)(2,1)S(1)} %fusion.9.refs_5_), channel_id=1, source_target_pairs={{0,2},{1,3},{2,0},{3,1},{4,6},{5,7},{6,4},{7,5},{8,10},{9,11},{10,... | collective-permute-start | bytes 1671176 | tf_op jit(solution)/shard_map/ppermute | solution.py:576
  11.7 36.2 %slice-start.4 = ((s8[6291456]{0:T(1024)(128)(4,1)}), s8[4194304]{0:T(1024)(128)(4,1)S(1)}, s32[]{:S(2)}) async-start(s8[6291456]{0:T(1024)(128)(4,1)} %bitcast.77), calls=%async_computation.4 | async-start | bytes 8388608
  11.7 36.2 %slice-start.5 = ((s8[6291456]{0:T(1024)(128)(4,1)}), s8[2097152]{0:T(1024)(128)(4,1)S(1)}, s32[]{:S(2)}) async-start(s8[6291456]{0:T(1024)(128)(4,1)} %bitcast.77), calls=%async_computation.5 | async-start | bytes 4194304
  19.3 7.3 %copy-start.19 = (bf16[128,2176]{1,0:T(8,128)(2,1)}, bf16[128,2176]{1,0:T(8,128)(2,1)S(1)}, u32[]{:S(2)}) copy-start(bf16[128,2176]{1,0:T(8,128)(2,1)S(1)} %collective-permute-done.refs_0_) | copy-start | bytes 1671172
  19.7 6.8 %copy-start.12 = (bf16[128,2176]{1,0:T(8,128)(2,1)}, bf16[128,2176]{1,0:T(8,128)(2,1)S(1)}, u32[]{:S(2)}) copy-start(bf16[128,2176]{1,0:T(8,128)(2,1)S(1)} %collective-permute-done.1.refs_6_) | copy-start | bytes 1671172
  20.9 5.6 %copy-start.13 = (bf16[128,2176]{1,0:T(8,128)(2,1)}, bf16[128,2176]{1,0:T(8,128)(2,1)S(1)}, u32[]{:S(2)}) copy-start(bf16[128,2176]{1,0:T(8,128)(2,1)S(1)} %collective-permute-done.2.refs_7_) | copy-start | bytes 1671172
  20.9 13.8 %collective-permute-start.3 = (bf16[128,2176]{1,0:T(8,128)(2,1)S(1)}, bf16[128,2176]{1,0:T(8,128)(2,1)S(1)}, u32[]{:S(2)}, u32[]{:S(2)}) collective-permute-start(bf16[128,2176]{1,0:T(8,128)(2,1)S(1)} %collective-permute-done.refs_0_), channel_id=1, source_target_pairs={{0,4},{1,5},{2,6},{3,7},{4,12},{5,13},{6,14},{7,15},{8,0},{9,1},{1... | collective-permute-start | bytes 1671176 | tf_op jit(solution)/shard_map/ppermute | solution.py:576
  23.5 12.6 %collective-permute-start.4 = (bf16[128,2176]{1,0:T(8,128)(2,1)S(1)}, bf16[128,2176]{1,0:T(8,128)(2,1)S(1)}, u32[]{:S(2)}, u32[]{:S(2)}) collective-permute-start(bf16[128,2176]{1,0:T(8,128)(2,1)S(1)} %collective-permute-done.refs_0_), channel_id=1, source_target_pairs={{0,1},{1,0},{2,3},{3,2},{4,5},{5,4},{6,7},{7,6},{8,9},{9,8},{10,11... | collective-permute-start | bytes 1671176 | tf_op jit(solution)/shard_map/ppermute | solution.py:576
  24.1 12.7 %collective-permute-start.5 = (bf16[128,2176]{1,0:T(8,128)(2,1)S(1)}, bf16[128,2176]{1,0:T(8,128)(2,1)S(1)}, u32[]{:S(2)}, u32[]{:S(2)}) collective-permute-start(bf16[128,2176]{1,0:T(8,128)(2,1)S(1)} %collective-permute-done.refs_0_), channel_id=1, source_target_pairs={{0,2},{1,3},{2,0},{3,1},{4,6},{5,7},{6,4},{7,5},{8,10},{9,11},{10,... | collective-permute-start | bytes 1671176 | tf_op jit(solution)/shard_map/ppermute | solution.py:576
  34.7 19.3 %copy-start.20 = (bf16[128,2176]{1,0:T(8,128)(2,1)}, bf16[128,2176]{1,0:T(8,128)(2,1)S(1)}, u32[]{:S(2)}) copy-start(bf16[128,2176]{1,0:T(8,128)(2,1)S(1)} %collective-permute-done.3.refs_0_) | copy-start | bytes 1671172
  36.1 4.0 %copy-start.17 = (bf16[128,2176]{1,0:T(8,128)(2,1)}, bf16[128,2176]{1,0:T(8,128)(2,1)S(1)}, u32[]{:S(2)}) copy-start(bf16[128,2176]{1,0:T(8,128)(2,1)S(1)} %collective-permute-done.4.refs_1_) | copy-start | bytes 1671172
  36.8 17.3 %copy-start.18 = (bf16[128,2176]{1,0:T(8,128)(2,1)}, bf16[128,2176]{1,0:T(8,128)(2,1)S(1)}, u32[]{:S(2)}) copy-start(bf16[128,2176]{1,0:T(8,128)(2,1)S(1)} %collective-permute-done.5.refs_2_) | copy-start | bytes 1671172
  36.8 9.7 %collective-permute-start.7 = (bf16[64,2176]{1,0:T(8,128)(2,1)S(1)}, bf16[64,2176]{1,0:T(8,128)(2,1)S(1)}, u32[]{:S(2)}, u32[]{:S(2)}) collective-permute-start(bf16[64,2176]{1,0:T(8,128)(2,1)S(1)} %slice.45), channel_id=1, source_target_pairs={{0,2},{1,3},{2,0},{3,1},{4,6},{5,7},{6,4},{7,5},{8,10},{9,11},{10,... | collective-permute-start | bytes 835592 | tf_op jit(solution)/shard_map/ppermute | solution.py:576
  38.4 19.3 %collective-permute-start.9 = (bf16[128,2176]{1,0:T(8,128)(2,1)S(1)}, bf16[128,2176]{1,0:T(8,128)(2,1)}, u32[]{:S(2)}, u32[]{:S(2)}) collective-permute-start(bf16[128,2176]{1,0:T(8,128)(2,1)S(1)} %collective-permute-done.3.refs_0_), channel_id=1, source_target_pairs={{0,4},{1,5},{2,6},{3,7},{4,12},{5,13},{6,14},{7,15},{8,0},{9,1},{1... | collective-permute-start | bytes 1671176 | tf_op jit(solution)/shard_map/ppermute | solution.py:576
  39.6 18.1 %collective-permute-start.10 = (bf16[128,2176]{1,0:T(8,128)(2,1)S(1)}, bf16[128,2176]{1,0:T(8,128)(2,1)S(1)}, u32[]{:S(2)}, u32[]{:S(2)}) collective-permute-start(bf16[128,2176]{1,0:T(8,128)(2,1)S(1)} %collective-permute-done.3.refs_0_), channel_id=1, source_target_pairs={{0,1},{1,0},{2,3},{3,2},{4,5},{5,4},{6,7},{7,6},{8,9},{9,8},{10,11... | collective-permute-start | bytes 1671176 | tf_op jit(solution)/shard_map/ppermute | solution.py:576
  40.1 17.6 %collective-permute-start.11 = (bf16[128,2176]{1,0:T(8,128)(2,1)S(1)}, bf16[128,2176]{1,0:T(8,128)(2,1)S(1)}, u32[]{:S(2)}, u32[]{:S(2)}) collective-permute-start(bf16[128,2176]{1,0:T(8,128)(2,1)S(1)} %collective-permute-done.3.refs_0_), channel_id=1, source_target_pairs={{0,2},{1,3},{2,0},{3,1},{4,6},{5,7},{6,4},{7,5},{8,10},{9,11},{10,... | collective-permute-start | bytes 1671176 | tf_op jit(solution)/shard_map/ppermute | solution.py:576
  40.7 17.0 %collective-permute-start.6 = (bf16[4,96,384]{2,1,0:T(8,128)(2,1)S(1)}, bf16[4,96,384]{2,1,0:T(8,128)(2,1)S(1)}, u32[]{:S(2)}, u32[]{:S(2)}) collective-permute-start(bf16[4,96,384]{2,1,0:T(8,128)(2,1)S(1)} %get-tuple-element.105), channel_id=1, source_target_pairs={{0,4},{1,5},{2,6},{3,7},{4,12},{5,13},{6,14},{7,15},{8,0},{9,1},{1... | collective-permute-start | bytes 884744 | tf_op jit(solution)/shard_map/ppermute | solution.py:576
  46.5 7.6 %copy-start.22 = (bf16[64,2176]{1,0:T(8,128)(2,1)}, bf16[64,2176]{1,0:T(8,128)(2,1)S(1)}, u32[]{:S(2)}) copy-start(bf16[64,2176]{1,0:T(8,128)(2,1)S(1)} %collective-permute-done.7.refs_3_) | copy-start | bytes 835588
  46.5 11.2 %collective-permute-start.8 = (bf16[64,2176]{1,0:T(8,128)(2,1)S(1)}, bf16[64,2176]{1,0:T(8,128)(2,1)S(1)}, u32[]{:S(2)}, u32[]{:S(2)}) collective-permute-start(bf16[64,2176]{1,0:T(8,128)(2,1)S(1)} %slice.46), channel_id=1, source_target_pairs={{0,1},{1,0},{2,3},{3,2},{4,5},{5,4},{6,7},{7,6},{8,9},{9,8},{10,11... | collective-permute-start | bytes 835592 | tf_op jit(solution)/shard_map/ppermute | solution.py:576
  57.7 9.7 %copy-start.23 = (bf16[64,2176]{1,0:T(8,128)(2,1)}, bf16[64,2176]{1,0:T(8,128)(2,1)S(1)}, u32[]{:S(2)}) copy-start(bf16[64,2176]{1,0:T(8,128)(2,1)S(1)} %collective-permute-done.8.refs_4_) | copy-start | bytes 835588
  57.7 17.0 %copy-start.14 = (bf16[128,2176]{1,0:T(8,128)(2,1)}, bf16[128,2176]{1,0:T(8,128)(2,1)S(1)}, u32[]{:S(2)}) copy-start(bf16[128,2176]{1,0:T(8,128)(2,1)S(1)} %collective-permute-done.10.refs_1_) | copy-start | bytes 1671172
  57.7 17.0 %copy-start.15 = (bf16[128,2176]{1,0:T(8,128)(2,1)}, bf16[128,2176]{1,0:T(8,128)(2,1)S(1)}, u32[]{:S(2)}) copy-start(bf16[128,2176]{1,0:T(8,128)(2,1)S(1)} %collective-permute-done.11.refs_2_) | copy-start | bytes 1671172
  57.8 9.7 %collective-permute-start.14 = (bf16[64,2176]{1,0:T(8,128)(2,1)S(1)}, bf16[64,2176]{1,0:T(8,128)(2,1)S(1)}, u32[]{:S(2)}, u32[]{:S(2)}) collective-permute-start(bf16[64,2176]{1,0:T(8,128)(2,1)S(1)} %slice.47), channel_id=1, source_target_pairs={{0,2},{1,3},{2,0},{3,1},{4,6},{5,7},{6,4},{7,5},{8,10},{9,11},{10,... | collective-permute-start | bytes 835592 | tf_op jit(solution)/shard_map/ppermute | solution.py:576
  57.8 17.6 %collective-permute-start.16 = (bf16[128,2176]{1,0:T(8,128)(2,1)}, bf16[128,2176]{1,0:T(8,128)(2,1)S(1)}, u32[]{:S(2)}, u32[]{:S(2)}) collective-permute-start(bf16[128,2176]{1,0:T(8,128)(2,1)} %collective-permute-done.9.refs_0_), channel_id=1, source_target_pairs={{0,1},{1,0},{2,3},{3,2},{4,5},{5,4},{6,7},{7,6},{8,9},{9,8},{10,11... | collective-permute-start | bytes 1671176 | tf_op jit(solution)/shard_map/ppermute | solution.py:576
  58.5 17.0 %collective-permute-start.17 = (bf16[128,2176]{1,0:T(8,128)(2,1)}, bf16[128,2176]{1,0:T(8,128)(2,1)}, u32[]{:S(2)}, u32[]{:S(2)}) collective-permute-start(bf16[128,2176]{1,0:T(8,128)(2,1)} %collective-permute-done.9.refs_0_), channel_id=1, source_target_pairs={{0,2},{1,3},{2,0},{3,1},{4,6},{5,7},{6,4},{7,5},{8,10},{9,11},{10,... | collective-permute-start | bytes 1671176 | tf_op jit(solution)/shard_map/ppermute | solution.py:576
  60.4 15.0 %collective-permute-start.12 = (bf16[4,96,384]{2,1,0:T(8,128)(2,1)}, bf16[4,96,384]{2,1,0:T(8,128)(2,1)S(1)}, u32[]{:S(2)}, u32[]{:S(2)}) collective-permute-start(bf16[4,96,384]{2,1,0:T(8,128)(2,1)} %get-tuple-element.119), channel_id=1, source_target_pairs={{0,12},{1,13},{2,14},{3,15},{4,8},{5,9},{6,10},{7,11},{8,4},{9,5},... | collective-permute-start | bytes 884744 | tf_op jit(solution)/shard_map/ppermute | solution.py:576
  62.2 13.2 %collective-permute-start.13 = (bf16[4,96,384]{2,1,0:T(8,128)(2,1)}, bf16[4,96,384]{2,1,0:T(8,128)(2,1)S(1)}, u32[]{:S(2)}, u32[]{:S(2)}) collective-permute-start(bf16[4,96,384]{2,1,0:T(8,128)(2,1)} %get-tuple-element.120), channel_id=1, source_target_pairs={{0,8},{1,9},{2,10},{3,11},{4,0},{5,1},{6,2},{7,3},{8,12},{9,13},{1... | collective-permute-start | bytes 884744 | tf_op jit(solution)/shard_map/ppermute | solution.py:576
  67.4 7.3 %copy-start.21 = (bf16[64,2176]{1,0:T(8,128)(2,1)}, bf16[64,2176]{1,0:T(8,128)(2,1)S(1)}, u32[]{:S(2)}) copy-start(bf16[64,2176]{1,0:T(8,128)(2,1)S(1)} %collective-permute-done.14.refs_3_) | copy-start | bytes 835588
  67.4 8.0 %collective-permute-start.15 = (bf16[64,2176]{1,0:T(8,128)(2,1)}, bf16[64,2176]{1,0:T(8,128)(2,1)}, u32[]{:S(2)}, u32[]{:S(2)}) collective-permute-start(bf16[64,2176]{1,0:T(8,128)(2,1)} %slice.48), channel_id=1, source_target_pairs={{0,1},{1,0},{2,3},{3,2},{4,5},{5,4},{6,7},{7,6},{8,9},{9,8},{10,11... | collective-permute-start | bytes 835592 | tf_op jit(solution)/shard_map/ppermute | solution.py:576
  68.0 7.6 %slice-start.6 = ((bf16[128,2176]{1,0:T(8,128)(2,1)}), bf16[64,2176]{1,0:T(8,128)(2,1)S(1)}, s32[]{:S(2)}) async-start(bf16[128,2176]{1,0:T(8,128)(2,1)} %copy-done.12), calls=%async_computation.6 | async-start | bytes 557056 | tf_op jit(solution)/shard_map/slice | solution.py:601
  75.6 17.5 %collective-permute-start.19 = (bf16[128,2176]{1,0:T(8,128)(2,1)S(1)}, bf16[128,2176]{1,0:T(8,128)(2,1)S(1)}, u32[]{:S(2)}, u32[]{:S(2)}) collective-permute-start(bf16[128,2176]{1,0:T(8,128)(2,1)S(1)} %pad_maximum_fusion), channel_id=1, source_target_pairs={{0,2},{1,3},{2,0},{3,1},{4,6},{5,7},{6,4},{7,5},{8,10},{9,11},{10,... | collective-permute-start | bytes 1671176 | tf_op jit(solution)/shard_map/ppermute | solution.py:576
  77.1 16.0 %collective-permute-start.20 = (bf16[128,2176]{1,0:T(8,128)(2,1)S(1)}, bf16[128,2176]{1,0:T(8,128)(2,1)S(1)}, u32[]{:S(2)}, u32[]{:S(2)}) collective-permute-start(bf16[128,2176]{1,0:T(8,128)(2,1)S(1)} %pad_maximum_fusion.1), channel_id=1, source_target_pairs={{0,1},{1,0},{2,3},{3,2},{4,5},{5,4},{6,7},{7,6},{8,9},{9,8},{10,11... | collective-permute-start | bytes 1671176 | tf_op jit(solution)/shard_map/ppermute | solution.py:576
  77.8 14.8 %collective-permute-start.18 = (bf16[4,96,384]{2,1,0:T(8,128)(2,1)S(1)}, bf16[4,96,384]{2,1,0:T(8,128)(2,1)S(1)}, u32[]{:S(2)}, u32[]{:S(2)}) collective-permute-start(bf16[4,96,384]{2,1,0:T(8,128)(2,1)S(1)} %copy-done.28), channel_id=1, source_target_pairs={{0,8},{1,9},{2,10},{3,11},{4,0},{5,1},{6,2},{7,3},{8,12},{9,13},{1... | collective-permute-start | bytes 884744 | tf_op jit(solution)/shard_map/ppermute | solution.py:576
  82.7 24.4 %collective-permute-start.23 = (bf16[4,96,384]{2,1,0:T(8,128)(2,1)}, bf16[4,96,384]{2,1,0:T(8,128)(2,1)S(1)}, u32[]{:S(2)}, u32[]{:S(2)}) collective-permute-start(bf16[4,96,384]{2,1,0:T(8,128)(2,1)} %get-tuple-element.152), channel_id=1, source_target_pairs={{0,1},{1,0},{2,3},{3,2},{4,5},{5,4},{6,7},{7,6},{8,9},{9,8},{10,11... | collective-permute-start | bytes 884744 | tf_op jit(solution)/shard_map/ppermute | solution.py:576
  84.4 22.7 %collective-permute-start.24 = (bf16[4,96,384]{2,1,0:T(8,128)(2,1)}, bf16[4,96,384]{2,1,0:T(8,128)(2,1)S(1)}, u32[]{:S(2)}, u32[]{:S(2)}) collective-permute-start(bf16[4,96,384]{2,1,0:T(8,128)(2,1)} %get-tuple-element.153), channel_id=1, source_target_pairs={{0,2},{1,3},{2,0},{3,1},{4,6},{5,7},{6,4},{7,5},{8,10},{9,11},{10,... | collective-permute-start | bytes 884744 | tf_op jit(solution)/shard_map/ppermute | solution.py:576
  92.6 29.5 %copy-start.5 = (bf16[4,96,384]{2,1,0:T(8,128)(2,1)}, bf16[4,96,384]{2,1,0:T(8,128)(2,1)S(1)}, u32[]{:S(2)}) copy-start(bf16[4,96,384]{2,1,0:T(8,128)(2,1)S(1)} %collective-permute-done.18.refs_1_) | copy-start | bytes 884740
  92.6 14.5 %collective-permute-start.25 = (bf16[4,96,384]{2,1,0:T(8,128)(2,1)S(1)}, bf16[4,96,384]{2,1,0:T(8,128)(2,1)S(1)}, u32[]{:S(2)}, u32[]{:S(2)}) collective-permute-start(bf16[4,96,384]{2,1,0:T(8,128)(2,1)S(1)} %get-tuple-element.154), channel_id=1, source_target_pairs={{0,3},{1,2},{2,1},{3,0},{4,7},{5,6},{6,5},{7,4},{8,11},{9,10},{10,... | collective-permute-start | bytes 884744 | tf_op jit(solution)/shard_map/ppermute | solution.py:576
  93.1 2.7 %copy-start.9 = (bf16[128,2176]{1,0:T(8,128)(2,1)}, bf16[128,2176]{1,0:T(8,128)(2,1)S(1)}, u32[]{:S(2)}) copy-start(bf16[128,2176]{1,0:T(8,128)(2,1)S(1)} %collective-permute-done.19.refs_3_.refs_8_) | copy-start | bytes 1671172
  93.1 2.7 %copy-start.10 = (bf16[128,2176]{1,0:T(8,128)(2,1)}, bf16[128,2176]{1,0:T(8,128)(2,1)S(1)}, u32[]{:S(2)}) copy-start(bf16[128,2176]{1,0:T(8,128)(2,1)S(1)} %collective-permute-done.20.refs_4_.refs_9_) | copy-start | bytes 1671172
  93.1 23.9 %collective-permute-start.21 = (bf16[4,96,384]{2,1,0:T(8,128)(2,1)}, bf16[4,96,384]{2,1,0:T(8,128)(2,1)S(1)}, u32[]{:S(2)}, u32[]{:S(2)}) collective-permute-start(bf16[4,96,384]{2,1,0:T(8,128)(2,1)} %get-tuple-element.146), channel_id=1, source_target_pairs={{0,12},{1,13},{2,14},{3,15},{4,8},{5,9},{6,10},{7,11},{8,4},{9,5},... | collective-permute-start | bytes 884744 | tf_op jit(solution)/shard_map/ppermute | solution.py:576
  105.6 11.4 %collective-permute-start.22 = (bf16[4,96,384]{2,1,0:T(8,128)(2,1)}, bf16[4,96,384]{2,1,0:T(8,128)(2,1)S(1)}, u32[]{:S(2)}, u32[]{:S(2)}) collective-permute-start(bf16[4,96,384]{2,1,0:T(8,128)(2,1)} %get-tuple-element.147), channel_id=1, source_target_pairs={{0,4},{1,5},{2,6},{3,7},{4,12},{5,13},{6,14},{7,15},{8,0},{9,1},{1... | collective-permute-start | bytes 884744 | tf_op jit(solution)/shard_map/ppermute | solution.py:576
  107.1 2.5 %copy-start.1 = (bf16[384,2048]{1,0:T(8,128)(2,1)S(1)}, bf16[384,2048]{1,0:T(8,128)(2,1)}, u32[]{:S(2)}) copy-start(bf16[384,2048]{1,0:T(8,128)(2,1)} %get-tuple-element.158.refs_1_) | copy-start | bytes 4718596
  107.1 2.5 %copy-start.2 = (bf16[384,2048]{1,0:T(8,128)(2,1)S(1)}, bf16[384,2048]{1,0:T(8,128)(2,1)}, u32[]{:S(2)}) copy-start(bf16[384,2048]{1,0:T(8,128)(2,1)} %get-tuple-element.159.refs_2_) | copy-start | bytes 4718596
  107.1 21.5 %slice-start.2 = ((s8[6291456]{0:T(1024)(128)(4,1)}), s8[4194304]{0:T(1024)(128)(4,1)S(1)}, s32[]{:S(2)}) async-start(s8[6291456]{0:T(1024)(128)(4,1)} %bitcast.67), calls=%async_computation.2 | async-start | bytes 8388608
  112.4 16.2 %slice-start = ((s8[6291456]{0:T(1024)(128)(4,1)}), s8[4194304]{0:T(1024)(128)(4,1)S(1)}, s32[]{:S(2)}) async-start(s8[6291456]{0:T(1024)(128)(4,1)} %bitcast.63), calls=%async_computation | async-start | bytes 8388608
  112.4 16.2 %slice-start.3 = ((s8[6291456]{0:T(1024)(128)(4,1)}), s8[2097152]{0:T(1024)(128)(4,1)S(1)}, s32[]{:S(2)}) async-start(s8[6291456]{0:T(1024)(128)(4,1)} %bitcast.67), calls=%async_computation.3 | async-start | bytes 4194304
  116.9 6.5 %collective-permute-start.26 = (bf16[2,192,2048]{2,1,0:T(8,128)(2,1)S(1)}, bf16[2,192,2048]{2,1,0:T(8,128)(2,1)S(1)}, u32[]{:S(2)}, u32[]{:S(2)}) collective-permute-start(bf16[2,192,2048]{2,1,0:T(8,128)(2,1)S(1)} %get-tuple-element.156), channel_id=1, source_target_pairs={{0,16},{16,0},{1,17},{17,1},{2,18},{18,2},{3,19},{19,3},{4,20},{20... | collective-permute-start | bytes 4718600 | tf_op jit(solution)/shard_map/ppermute | solution.py:678
  117.0 5.1 %copy-start.6 = (bf16[4,96,384]{2,1,0:T(8,128)(2,1)}, bf16[4,96,384]{2,1,0:T(8,128)(2,1)S(1)}, u32[]{:S(2)}) copy-start(bf16[4,96,384]{2,1,0:T(8,128)(2,1)S(1)} %collective-permute-done.21.refs_2_) | copy-start | bytes 884740
  117.0 5.1 %copy-start.8 = (bf16[4,96,384]{2,1,0:T(8,128)(2,1)}, bf16[4,96,384]{2,1,0:T(8,128)(2,1)S(1)}, u32[]{:S(2)}) copy-start(bf16[4,96,384]{2,1,0:T(8,128)(2,1)S(1)} %collective-permute-done.22.refs_3_) | copy-start | bytes 884740
  117.0 5.1 %copy-start.7 = (bf16[4,96,384]{2,1,0:T(8,128)(2,1)S(1)}, bf16[4,96,384]{2,1,0:T(8,128)(2,1)}, u32[]{:S(2)}) copy-start(bf16[4,96,384]{2,1,0:T(8,128)(2,1)} %get-tuple-element.148.refs_0_) | copy-start | bytes 884740
  117.1 11.6 %slice-start.1 = ((s8[6291456]{0:T(1024)(128)(4,1)}), s8[2097152]{0:T(1024)(128)(4,1)S(1)}, s32[]{:S(2)}) async-start(s8[6291456]{0:T(1024)(128)(4,1)} %bitcast.63), calls=%async_computation.1 | async-start | bytes 4194304
  121.6 3.6 %collective-permute-start.27 = (bf16[2,192,2048]{2,1,0:T(8,128)(2,1)S(1)}, bf16[2,192,2048]{2,1,0:T(8,128)(2,1)S(1)}, u32[]{:S(2)}, u32[]{:S(2)}) collective-permute-start(bf16[2,192,2048]{2,1,0:T(8,128)(2,1)S(1)} %get-tuple-element.162), channel_id=1, source_target_pairs={{0,16},{16,0},{1,17},{17,1},{2,18},{18,2},{3,19},{19,3},{4,20},{20... | collective-permute-start | bytes 4718600 | tf_op jit(solution)/shard_map/ppermute | solution.py:678
  125.1 16.1 %collective-permute-start.28 = (bf16[4,96,384]{2,1,0:T(8,128)(2,1)S(1)}, bf16[4,96,384]{2,1,0:T(8,128)(2,1)S(1)}, u32[]{:S(2)}, u32[]{:S(2)}) collective-permute-start(bf16[4,96,384]{2,1,0:T(8,128)(2,1)S(1)} %get-tuple-element.170), channel_id=1, source_target_pairs={{0,1},{1,0},{2,3},{3,2},{4,5},{5,4},{6,7},{7,6},{8,9},{9,8},{10,11... | collective-permute-start | bytes 884744 | tf_op jit(solution)/shard_map/ppermute | solution.py:576
  125.6 15.6 %collective-permute-start.29 = (bf16[4,96,384]{2,1,0:T(8,128)(2,1)S(1)}, bf16[4,96,384]{2,1,0:T(8,128)(2,1)S(1)}, u32[]{:S(2)}, u32[]{:S(2)}) collective-permute-start(bf16[4,96,384]{2,1,0:T(8,128)(2,1)S(1)} %get-tuple-element.171), channel_id=1, source_target_pairs={{0,2},{1,3},{2,0},{3,1},{4,6},{5,7},{6,4},{7,5},{8,10},{9,11},{10,... | collective-permute-start | bytes 884744 | tf_op jit(solution)/shard_map/ppermute | solution.py:576
  127.2 14.5 %collective-permute-start.30 = (bf16[4,96,384]{2,1,0:T(8,128)(2,1)S(1)}, bf16[4,96,384]{2,1,0:T(8,128)(2,1)S(1)}, u32[]{:S(2)}, u32[]{:S(2)}) collective-permute-start(bf16[4,96,384]{2,1,0:T(8,128)(2,1)S(1)} %get-tuple-element.172), channel_id=1, source_target_pairs={{0,3},{1,2},{2,1},{3,0},{4,7},{5,6},{6,5},{7,4},{8,11},{9,10},{10,... | collective-permute-start | bytes 884744 | tf_op jit(solution)/shard_map/ppermute | solution.py:576
  128.7 2.8 %copy-start = (f32[192,4,2048]{2,1,0:T(4,128)S(1)}, f32[192,4,2048]{2,1,0:T(4,128)}, u32[]{:S(2)}) copy-start(f32[192,4,2048]{2,1,0:T(4,128)} %param.15) | copy-start | bytes 18874372
  141.2 3.1 %copy-start.25 = (bf16[4,96,384]{2,1,0:T(8,128)(2,1)}, bf16[4,96,384]{2,1,0:T(8,128)(2,1)S(1)}, u32[]{:S(2)}) copy-start(bf16[4,96,384]{2,1,0:T(8,128)(2,1)S(1)} %collective-permute-done.28.refs_4_) | copy-start | bytes 884740
  141.2 3.1 %copy-start.26 = (bf16[4,96,384]{2,1,0:T(8,128)(2,1)}, bf16[4,96,384]{2,1,0:T(8,128)(2,1)S(1)}, u32[]{:S(2)}) copy-start(bf16[4,96,384]{2,1,0:T(8,128)(2,1)S(1)} %collective-permute-done.29.refs_5_) | copy-start | bytes 884740
  141.7 2.6 %copy-start.27 = (bf16[4,96,384]{2,1,0:T(8,128)(2,1)}, bf16[4,96,384]{2,1,0:T(8,128)(2,1)S(1)}, u32[]{:S(2)}) copy-start(bf16[4,96,384]{2,1,0:T(8,128)(2,1)S(1)} %collective-permute-done.30.refs_6_) | copy-start | bytes 884740
  144.3 7.8 %collective-permute-start.31 = (bf16[12288,128]{1,0:T(8,128)(2,1)}, bf16[12288,128]{1,0:T(8,128)(2,1)S(1)}, u32[]{:S(2)}, u32[]{:S(2)}) collective-permute-start(bf16[12288,128]{1,0:T(8,128)(2,1)} %get-tuple-element.190), channel_id=1, source_target_pairs={{0,16},{16,0},{1,17},{17,1},{2,18},{18,2},{3,19},{19,3},{4,20},{20... | collective-permute-start | bytes 9437192 | tf_op jit(solution)/shard_map/ppermute | solution.py:696
  (5 other events, 9.0 us)

commit v8 on v7

--- a/solution.py
+++ b/solution.py
@@ -457,7 +457,7 @@
 
 
 def finish_kernel(pieces, target, probs, hidden, *refs):
-    back, (d_hidden, d_probs, rows, states, outs, sums, sems) = refs[:-7], refs[-7:]
+    back, (d_hidden, d_probs, rows, states, outs, sems) = refs[:-6], refs[-6:]
     count = back[0].shape[1]
     choices, width = hidden.shape
     slots = rows.shape[0]
@@ -471,9 +471,14 @@
     targets, scales = target[...].T, probs[...].T
     for load in loads[:-1]:
         load.wait()
-    ones = jnp.ones((8, width), jnp.bfloat16)
+    ones = jnp.ones((TOP, width), jnp.bfloat16)
     across = (((1,), (1,)), ((), ()))
     step = 2 * LANES
+    row = lax.broadcasted_iota(jnp.int32, (TOP, step), 0)
+    choice = lax.broadcasted_iota(jnp.int32, (TOP, step), 1) % TOP
+    token = lax.broadcasted_iota(jnp.int32, (step, choices // TOP), 0) // TOP
+    lane = lax.broadcasted_iota(jnp.int32, (step, choices // TOP), 1)
+    total = jnp.zeros((TOP, choices // TOP), jnp.float32)
     stores = []
     for n, at in enumerate(range(0, choices, step)):
         here = slice(at, at + step)
@@ -494,10 +499,19 @@
         product = states[here].astype(jnp.float32) * g
         high = product.astype(jnp.bfloat16)
         low = (product - high.astype(jnp.float32)).astype(jnp.bfloat16)
-        sums[:, here] = lax.dot_general(
+        sums = lax.dot_general(
             ones, high, across, preferred_element_type=jnp.float32
         ) + lax.dot_general(ones, low, across, preferred_element_type=jnp.float32)
-    d_probs[...] = sums[...]
+        sums = jnp.where(choice == row, sums, 0.0)
+        high = sums.astype(jnp.bfloat16)
+        low = (sums - high.astype(jnp.float32)).astype(jnp.bfloat16)
+        chosen = jnp.where(token + at // TOP == lane, 1.0, 0.0).astype(jnp.bfloat16)
+        total = (
+            total
+            + jnp.dot(high, chosen, preferred_element_type=jnp.float32)
+            + jnp.dot(low, chosen, preferred_element_type=jnp.float32)
+        )
+    d_probs[...] = total
     for store in stores:
         store.wait()
 
@@ -510,7 +524,7 @@
         functools.partial(finish_kernel, pieces),
         out_shape=(
             jax.ShapeDtypeStruct((choices, width), jnp.bfloat16),
-            jax.ShapeDtypeStruct((8, choices), jnp.float32),
+            jax.ShapeDtypeStruct((TOP, choices // TOP), jnp.float32),
         ),
         in_specs=[INSIDE, INSIDE] + [HBM] * (1 + len(back)),
         out_specs=(HBM, INSIDE),
@@ -518,7 +532,6 @@
             pltpu.VMEM((slots, width), jnp.bfloat16),
             pltpu.VMEM((choices, width), jnp.bfloat16),
             pltpu.VMEM((choices, width), jnp.bfloat16),
-            pltpu.VMEM((8, choices), jnp.float32),
             pltpu.SemaphoreType.DMA((len(pieces) + 1 + steps,)),
         ],
         compiler_params=pltpu.CompilerParams(vmem_limit_bytes=56 * MIB),
@@ -702,7 +715,7 @@
     )
     return (
         d_hidden.reshape(hidden.shape),
-        d_probs[0].reshape(probs.shape),
+        d_probs.T,
         lane_unview(new_weight, weight.shape),
         lane_unview(new_moment1, weight.shape),
         lane_unview(new_moment2, weight.shape),

time: 155 us -> 154 us (level)
    unnamed x74 -> x73, local copies, waits for them, and re-layouts: 13.4 us -> 12.8 us
  transfers between devices with their start and end apart: 32 -> 32, of which waited for: 12 -> 12; matrix products, arithmetic and copies ran while one was open for 11% -> 10% of each run, Pallas kernels for 35% -> 35%
where the time goes in v8:
time: 154 us
  Pallas kernels  59.8 us (39%)
  starting transfers between devices  38.7 us (25%)
  waiting for transfers between devices  31.2 us (20%)
  local copies, waits for them, and re-layouts  16.5 us (11%)
  matrix products  3.51 us (2%)
  other arithmetic  2.7 us (2%)
    ppermute x29, starting transfers between devices, move(): return lax.ppermute(block, 'inner', step_perm(size, steps, flip))  38.1 us
    ppermute x29, waiting for transfers between devices, move(): return lax.ppermute(block, 'inner', step_perm(size, steps, flip))  29.5 us
    pallas_call x3, Pallas kernels, chunk_grads(): pl.pallas_call(functools.partial(grads_kernel, spans, keep), out_shape=[j...  23.3 us
    unnamed x73, local copies, waits for them, and re-layouts  12.8 us
    pallas_call x2, Pallas kernels, adam_rows(): pl.pallas_call(functools.partial(adam_kernel, count, owners, kept, first)...  12.3 us
    pallas_call x2, Pallas kernels, partial_rows(): pl.pallas_call(functools.partial(partial_kernel, start, total), out_shape...  8.96 us
    pallas_call x1, Pallas kernels, finish(): pl.pallas_call(functools.partial(finish_kernel, pieces), out_shape=(jax.S...  6.75 us
    pallas_call x2, Pallas kernels, regroup(): pl.pallas_call(regroup_kernel, out_shape=[jax.ShapeDtypeStruct((count, sl...  3.29 us
  transfers between devices with their start and end apart: 32, of which 12 were waited for; matrix products, arithmetic and copies ran while one was open for 10% of the time, Pallas kernels for 35%

profile of v8, /device:TPU:0, one launch (start us, length us, event | category | flops | bytes accessed | tf_op | source)
XLA Modules:
  0.0 153.8 jit_solution(7964383677942541221)
XLA Ops:
  0.6 0.7 convert_element_type.46
  1.5 1.1 fusion.9.refs_5_
  2.6 3.1 %collective-permute-start = (bf16[128,2176]{1,0:T(8,128)(2,1)S(1)}, bf16[128,2176]{1,0:T(8,128)(2,1)S(1)}, u32[]{:S(2)}, u32[]{:S(2)}) collective-permute-start(bf16[128,2176]{1,0:T(8,128)(2,1)S(1)} %fusion.9.refs_5_), channel_id=1, source_target_pairs={{0,4},{1,5},{2,6},{3,7},{4,12},{5,13},{6,14},{7,15},{8,0},{9,1},{1... | collective-permute-start | bytes 1671176 | tf_op jit(solution)/shard_map/ppermute | solution.py:589
  5.6 1.5 collective-permute-start.1
  7.1 1.5 collective-permute-start.2
  8.7 0.8 copy.47
  10.2 0.6 fusion.27.target
  11.0 0.7 reshape.249.probs
  11.7 3.2 %fusion.2 = bf16[1536,384]{1,0:T(8,128)(2,1)S(1)} fusion(s32[1024]{0:T(1024)S(1)} %fusion.41, bf16[128,8,384]{2,1,0:T(8,128)(2,1)} %param.9, f32[128,8]{1,0:T(8,128)S(1)} %copy.49), kind=kOutput, calls=%fused_computation.4 | convolution fusion | flops 1211301888 | bytes 1974272 | tf_op jit(solution)/shard_map/dot_general | solution.py:581
  14.9 4.4 %collective-permute-done.refs_0_ = bf16[128,2176]{1,0:T(8,128)(2,1)S(1)} collective-permute-done((bf16[128,2176]{1,0:T(8,128)(2,1)S(1)}, bf16[128,2176]{1,0:T(8,128)(2,1)S(1)}, u32[]{:S(2)}, u32[]{:S(2)}) %collective-permute-start) | collective-permute-done | bytes 557088 | tf_op jit(solution)/shard_map/ppermute | solution.py:589
  19.7 1.2 collective-permute-done.2.refs_7_
  20.9 2.6 %collective-permute-start.3 = (bf16[128,2176]{1,0:T(8,128)(2,1)S(1)}, bf16[128,2176]{1,0:T(8,128)(2,1)S(1)}, u32[]{:S(2)}, u32[]{:S(2)}) collective-permute-start(bf16[128,2176]{1,0:T(8,128)(2,1)S(1)} %collective-permute-done.refs_0_), channel_id=1, source_target_pairs={{0,4},{1,5},{2,6},{3,7},{4,12},{5,13},{6,14},{7,15},{8,0},{9,1},{1... | collective-permute-start | bytes 1671176 | tf_op jit(solution)/shard_map/ppermute | solution.py:589
  23.5 0.5 collective-permute-start.4
  24.1 1.5 collective-permute-start.5
  25.6 1.0 slice_bitcast_fusion
  26.6 8.2 %collective-permute-done.3.refs_0_ = bf16[128,2176]{1,0:T(8,128)(2,1)S(1)} collective-permute-done((bf16[128,2176]{1,0:T(8,128)(2,1)S(1)}, bf16[128,2176]{1,0:T(8,128)(2,1)S(1)}, u32[]{:S(2)}, u32[]{:S(2)}) %collective-permute-start.3) | collective-permute-done | bytes 557088 | tf_op jit(solution)/shard_map/ppermute | solution.py:589
  34.7 1.4 collective-permute-done.4.refs_1_
  36.1 0.6 collective-permute-done.5.refs_2_
  36.8 1.6 %collective-permute-start.7 = (bf16[64,2176]{1,0:T(8,128)(2,1)S(1)}, bf16[64,2176]{1,0:T(8,128)(2,1)S(1)}, u32[]{:S(2)}, u32[]{:S(2)}) collective-permute-start(bf16[64,2176]{1,0:T(8,128)(2,1)S(1)} %slice.42), channel_id=1, source_target_pairs={{0,2},{1,3},{2,0},{3,1},{4,6},{5,7},{6,4},{7,5},{8,10},{9,11},{10,... | collective-permute-start | bytes 835592 | tf_op jit(solution)/shard_map/ppermute | solution.py:589
  38.4 1.2 collective-permute-start.9
  39.6 0.5 collective-permute-start.10
  40.1 0.5 collective-permute-start.11
  40.7 1.0 collective-permute-start.6
  41.6 4.8 %collective-permute-done.7.refs_3_ = bf16[64,2176]{1,0:T(8,128)(2,1)S(1)} collective-permute-done((bf16[64,2176]{1,0:T(8,128)(2,1)S(1)}, bf16[64,2176]{1,0:T(8,128)(2,1)S(1)}, u32[]{:S(2)}, u32[]{:S(2)}) %collective-permute-start.7) | collective-permute-done | bytes 278560 | tf_op jit(solution)/shard_map/ppermute | solution.py:589
  46.5 1.4 collective-permute-start.8
  47.9 6.2 %copy.63 = bf16[384,4,2048]{2,0,1:T(8,128)(2,1)} copy(bf16[384,4,2048]{2,1,0:T(4,128)(2,1)S(1)} %bitcast.79) | data formatting | bytes 12582912 | tf_op args[4]
  54.1 3.6 %collective-permute-done.8.refs_4_ = bf16[64,2176]{1,0:T(8,128)(2,1)S(1)} collective-permute-done((bf16[64,2176]{1,0:T(8,128)(2,1)S(1)}, bf16[64,2176]{1,0:T(8,128)(2,1)S(1)}, u32[]{:S(2)}, u32[]{:S(2)}) %collective-permute-start.8) | collective-permute-done | bytes 278560 | tf_op jit(solution)/shard_map/ppermute | solution.py:589
  57.8 0.6 collective-permute-start.16
  58.5 1.9 %collective-permute-start.17 = (bf16[128,2176]{1,0:T(8,128)(2,1)}, bf16[128,2176]{1,0:T(8,128)(2,1)}, u32[]{:S(2)}, u32[]{:S(2)}) collective-permute-start(bf16[128,2176]{1,0:T(8,128)(2,1)} %collective-permute-done.9.refs_0_), channel_id=1, source_target_pairs={{0,2},{1,3},{2,0},{3,1},{4,6},{5,7},{6,4},{7,5},{8,10},{9,11},{10,... | collective-permute-start | bytes 1671176 | tf_op jit(solution)/shard_map/ppermute | solution.py:589
  60.4 1.8 %collective-permute-start.12 = (bf16[4,96,384]{2,1,0:T(8,128)(2,1)}, bf16[4,96,384]{2,1,0:T(8,128)(2,1)S(1)}, u32[]{:S(2)}, u32[]{:S(2)}) collective-permute-start(bf16[4,96,384]{2,1,0:T(8,128)(2,1)} %get-tuple-element.119), channel_id=1, source_target_pairs={{0,12},{1,13},{2,14},{3,15},{4,8},{5,9},{6,10},{7,11},{8,4},{9,5},... | collective-permute-start | bytes 884744 | tf_op jit(solution)/shard_map/ppermute | solution.py:589
  62.2 0.8 collective-permute-start.13
  63.0 0.7 slice.45
  63.8 3.7 %collective-permute-done.14.refs_3_ = bf16[64,2176]{1,0:T(8,128)(2,1)S(1)} collective-permute-done((bf16[64,2176]{1,0:T(8,128)(2,1)S(1)}, bf16[64,2176]{1,0:T(8,128)(2,1)S(1)}, u32[]{:S(2)}, u32[]{:S(2)}) %collective-permute-start.14) | collective-permute-done | bytes 278560 | tf_op jit(solution)/shard_map/ppermute | solution.py:589
  67.4 0.5 collective-permute-start.15
  68.0 6.8 %shard_map.127 = (bf16[384,2048]{1,0:T(8,128)(2,1)}, bf16[4,96,384]{2,1,0:T(8,128)(2,1)}) custom-call(s32[1]{0:T(128)} %bitcast.5.first, bf16[128,2176]{1,0:T(8,128)(2,1)} %copy-done.19, bf16[128,2176]{1,0:T(8,128)(2,1)} %copy-done.17, bf16[128,2176]{1,0:T(8,128)(2,1)} %copy-done.18, bf16[64,2176]{1,0:T(8,128)(2,1)} %copy-done.22, ...), custom_call_target="tpu_custom_call" | custom-call | flops 1409286144 | bytes 3670016 | tf_op jit(solution)/shard_map/pallas_call | solution.py:172
  74.8 0.6 collective-permute-done.15.refs_4_
  75.6 0.5 collective-permute-start.19
  76.0 1.0 slice.47
  77.1 0.7 collective-permute-start.20
  77.8 3.0 %collective-permute-start.18 = (bf16[4,96,384]{2,1,0:T(8,128)(2,1)S(1)}, bf16[4,96,384]{2,1,0:T(8,128)(2,1)S(1)}, u32[]{:S(2)}, u32[]{:S(2)}) collective-permute-start(bf16[4,96,384]{2,1,0:T(8,128)(2,1)S(1)} %copy-done.28), channel_id=1, source_target_pairs={{0,8},{1,9},{2,10},{3,11},{4,0},{5,1},{6,2},{7,3},{8,12},{9,13},{1... | collective-permute-start | bytes 884744 | tf_op jit(solution)/shard_map/ppermute | solution.py:589
  80.7 2.0 %shard_map.130 = (bf16[4,96,384]{2,1,0:T(8,128)(2,1)}, bf16[4,96,384]{2,1,0:T(8,128)(2,1)}, bf16[4,96,384]{2,1,0:T(8,128)(2,1)S(1)}) custom-call(bf16[4,96,384]{2,1,0:T(8,128)(2,1)S(1)} %get-tuple-element.132.refs_0_, bf16[4,96,384]{2,1,0:T(8,128)(2,1)S(1)} %collective-permute-done.6.refs_1_, bf16[4,96,384]{2,1,0:T(8,128)(2,1)S(1)} %collective-permute-done.12.refs_2_, ...), custom_call_target="tpu_custom_call" | custom-call | bytes 1769472 | tf_op jit(solution)/shard_map/pallas_call | solution.py:267
  82.7 1.6 %collective-permute-start.23 = (bf16[4,96,384]{2,1,0:T(8,128)(2,1)}, bf16[4,96,384]{2,1,0:T(8,128)(2,1)S(1)}, u32[]{:S(2)}, u32[]{:S(2)}) collective-permute-start(bf16[4,96,384]{2,1,0:T(8,128)(2,1)} %get-tuple-element.152), channel_id=1, source_target_pairs={{0,1},{1,0},{2,3},{3,2},{4,5},{5,4},{6,7},{7,6},{8,9},{9,8},{10,11... | collective-permute-start | bytes 884744 | tf_op jit(solution)/shard_map/ppermute | solution.py:589
  84.4 1.5 collective-permute-start.24
  85.9 6.7 %shard_map.128 = (bf16[384,2048]{1,0:T(8,128)(2,1)}, bf16[4,96,384]{2,1,0:T(8,128)(2,1)}) custom-call(s32[1]{0:T(128)} %bitcast.5.first, bf16[128,2176]{1,0:T(8,128)(2,1)} %copy-done.20, bf16[128,2176]{1,0:T(8,128)(2,1)} %copy-done.14, bf16[128,2176]{1,0:T(8,128)(2,1)} %copy-done.15, bf16[64,2176]{1,0:T(8,128)(2,1)} %copy-done.21, ...), custom_call_target="tpu_custom_call" | custom-call | flops 1409286144 | bytes 3670016 | tf_op jit(solution)/shard_map/pallas_call | solution.py:172
  93.1 2.7 %collective-permute-start.21 = (bf16[4,96,384]{2,1,0:T(8,128)(2,1)}, bf16[4,96,384]{2,1,0:T(8,128)(2,1)S(1)}, u32[]{:S(2)}, u32[]{:S(2)}) collective-permute-start(bf16[4,96,384]{2,1,0:T(8,128)(2,1)} %get-tuple-element.146), channel_id=1, source_target_pairs={{0,12},{1,13},{2,14},{3,15},{4,8},{5,9},{6,10},{7,11},{8,4},{9,5},... | collective-permute-start | bytes 884744 | tf_op jit(solution)/shard_map/ppermute | solution.py:589
  95.8 9.9 %shard_map.129 = (bf16[384,2048]{1,0:T(8,128)(2,1)}, bf16[4,96,384]{2,1,0:T(8,128)(2,1)}, bf16[384,2048]{1,0:T(8,128)(2,1)}, bf16[4,96,384]{2,1,0:T(8,128)(2,1)}) custom-call(s32[1]{0:T(128)} %bitcast.5.first, bf16[128,2176]{1,0:T(8,128)(2,1)} %collective-permute-done.9.refs_0_, bf16[128,2176]{1,0:T(8,128)(2,1)} %copy-done.16, ...), custom_call_target="tpu_custom_call" | custom-call | flops 2818572288 | bytes 7340032 | tf_op jit(solution)/shard_map/pallas_call | solution.py:172
  105.7 1.4 collective-permute-start.22
  107.1 2.5 %shard_map.131.weighted = bf16[4,384,384]{2,1,0:T(8,128)(2,1)S(1)} custom-call(bf16[4,96,384]{2,1,0:T(8,128)(2,1)S(1)} %get-tuple-element.132.refs_0_, bf16[4,96,384]{2,1,0:T(8,128)(2,1)S(1)} %collective-permute-done.6.refs_1_, bf16[4,96,384]{2,1,0:T(8,128)(2,1)S(1)} %collective-permute-done.12.refs_2_, ...), custom_call_target="tpu_custom_call" | custom-call | bytes 4718592 | tf_op jit(solution)/shard_map/pallas_call | solution.py:225
  109.6 1.4 copy-done.3
  111.0 1.4 copy-done.4
  112.4 4.5 %shard_map.132 = (bf16[2,192,2048]{2,1,0:T(8,128)(2,1)S(1)}, bf16[2,192,2048]{2,1,0:T(8,128)(2,1)S(1)}) custom-call(s32[2]{0:T(128)S(1)} %and_select_fusion.owners, bf16[4,384,384]{2,1,0:T(8,128)(2,1)S(1)} %shard_map.131.weighted, bf16[384,2048]{1,0:T(8,128)(2,1)S(1)} %copy-done.4, bf16[384,2048]{1,0:T(8,128)(2,1)S(1)} %copy-done.1, ...), custom_call_target="tpu_custom_call" | custom-call | flops 1207959552 | bytes 6291456 | tf_op jit(solution)/shard_map/pallas_call | solution.py:332
  117.1 4.5 %shard_map.133 = (bf16[2,192,2048]{2,1,0:T(8,128)(2,1)S(1)}, bf16[2,192,2048]{2,1,0:T(8,128)(2,1)S(1)}) custom-call(s32[2]{0:T(128)S(1)} %and_select_fusion.owners, bf16[4,384,384]{2,1,0:T(8,128)(2,1)S(1)} %shard_map.131.weighted, bf16[384,2048]{1,0:T(8,128)(2,1)S(1)} %copy-done.4, bf16[384,2048]{1,0:T(8,128)(2,1)S(1)} %copy-done.1, ...), custom_call_target="tpu_custom_call" | custom-call | flops 1207959552 | bytes 6291456 | tf_op jit(solution)/shard_map/pallas_call | solution.py:332
  121.5 0.5 collective-permute-start.27
  122.1 1.3 shard_map.134
  123.4 1.7 %collective-permute-done.27.refs_3_ = bf16[2,192,2048]{2,1,0:T(8,128)(2,1)S(1)} collective-permute-done((bf16[2,192,2048]{2,1,0:T(8,128)(2,1)S(1)}, bf16[2,192,2048]{2,1,0:T(8,128)(2,1)S(1)}, u32[]{:S(2)}, u32[]{:S(2)}) %collective-permute-start.27) | collective-permute-done | bytes 1572896 | tf_op jit(solution)/shard_map/ppermute | solution.py:691
  125.1 0.5 collective-permute-start.28
  125.6 1.5 collective-permute-start.29
  127.2 1.4 collective-permute-start.30
  128.7 2.8 %copy-done = f32[192,4,2048]{2,1,0:T(4,128)S(1)} copy-done((f32[192,4,2048]{2,1,0:T(4,128)S(1)}, f32[192,4,2048]{2,1,0:T(4,128)}, u32[]{:S(2)}) %copy-start) | copy-done | bytes 6291480
  131.4 9.7 %shard_map.136 = (f32[12288,128]{1,0:T(8,128)}, f32[12288,128]{1,0:T(8,128)}, f32[12288,128]{1,0:T(8,128)}, bf16[24576,128]{1,0:T(8,128)(2,1)}, bf16[12288,128]{1,0:T(8,128)(2,1)}) custom-call(s32[1]{0:T(128)} %bitcast.13.at, bf16[2,192,2048]{2,1,0:T(8,128)(2,1)S(1)} %get-tuple-element.178.refs_0_, ...), custom_call_target="tpu_custom_call" | custom-call | bytes 65536 | tf_op jit(solution)/shard_map/pallas_call | solution.py:416
  141.2 0.5 collective-permute-done.30.refs_6_
  141.7 2.6 %shard_map.137 = (f32[12288,128]{1,0:T(8,128)}, f32[12288,128]{1,0:T(8,128)}, f32[12288,128]{1,0:T(8,128)}, bf16[24576,128]{1,0:T(8,128)(2,1)}, bf16[12288,128]{1,0:T(8,128)(2,1)}) custom-call(s32[1]{0:T(128)} %bitcast.13.at, ...), custom_call_target="tpu_custom_call", output_to_operand_aliasing={{0}: (8, {}), {1}: (9, {}), {2}: (10, {}), {3}: (11, {}), {... | custom-call | bytes 65536 | tf_op jit(solution)/shard_map/pallas_call | solution.py:416
  144.4 6.7 %shard_map.135 = (bf16[1024,384]{1,0:T(8,128)(2,1)}, f32[8,128]{1,0:T(8,128)}) custom-call(f32[8,128]{1,0:T(8,128)} %fusion.27.target, f32[8,128]{1,0:T(8,128)} %reshape.249.probs, bf16[1024,384]{1,0:T(8,128)(2,1)} %bitcast.84, bf16[4,96,384]{2,1,0:T(8,128)(2,1)} %get-tuple-element.148.refs_0_, bf16[4,96,384]{2,1,0:T(8,128)(2,1)} %copy-done.5, ...), custom_call_target="tpu_custom_call" | custom-call | flops 1207959552 | bytes 3145728 | tf_op jit(solution)/shard_map/pallas_call | solution.py:523
  151.1 2.7 %shard_map.138 = bf16[24576,128]{1,0:T(8,128)(2,1)} custom-call(s32[1]{0:T(128)} %bitcast.38.at, bf16[12288,128]{1,0:T(8,128)(2,1)S(1)} %collective-permute-done.31.got, bf16[24576,128]{1,0:T(8,128)(2,1)} %get-tuple-element.191.full), custom_call_target="tpu_custom_call", output_to_operand_aliasing={{}: (2, {})} | custom-call | bytes 6291456 | tf_op jit(solution)/shard_map/pallas_call | solution.py:444
  (114 shorter events, 2.4 us)
Async XLA Ops:
  0.6 10.3 %copy-start.24 = (f32[128,8]{0,1:T(8,128)S(1)}, f32[128,8]{0,1:T(8,128)}, u32[]{:S(2)}) copy-start(f32[128,8]{0,1:T(8,128)} %param.10) | copy-start | bytes 12292
  2.6 12.4 %copy-start.11 = (bf16[128,2176]{1,0:T(8,128)(2,1)}, bf16[128,2176]{1,0:T(8,128)(2,1)S(1)}, u32[]{:S(2)}) copy-start(bf16[128,2176]{1,0:T(8,128)(2,1)S(1)} %fusion.9.refs_5_) | copy-start | bytes 1671172
  2.6 16.7 %collective-permute-start = (bf16[128,2176]{1,0:T(8,128)(2,1)S(1)}, bf16[128,2176]{1,0:T(8,128)(2,1)S(1)}, u32[]{:S(2)}, u32[]{:S(2)}) collective-permute-start(bf16[128,2176]{1,0:T(8,128)(2,1)S(1)} %fusion.9.refs_5_), channel_id=1, source_target_pairs={{0,4},{1,5},{2,6},{3,7},{4,12},{5,13},{6,14},{7,15},{8,0},{9,1},{1... | collective-permute-start | bytes 1671176 | tf_op jit(solution)/shard_map/ppermute | solution.py:589
  5.6 14.1 %collective-permute-start.1 = (bf16[128,2176]{1,0:T(8,128)(2,1)S(1)}, bf16[128,2176]{1,0:T(8,128)(2,1)S(1)}, u32[]{:S(2)}, u32[]{:S(2)}) collective-permute-start(bf16[128,2176]{1,0:T(8,128)(2,1)S(1)} %fusion.9.refs_5_), channel_id=1, source_target_pairs={{0,1},{1,0},{2,3},{3,2},{4,5},{5,4},{6,7},{7,6},{8,9},{9,8},{10,11... | collective-permute-start | bytes 1671176 | tf_op jit(solution)/shard_map/ppermute | solution.py:589
  7.1 13.8 %collective-permute-start.2 = (bf16[128,2176]{1,0:T(8,128)(2,1)S(1)}, bf16[128,2176]{1,0:T(8,128)(2,1)S(1)}, u32[]{:S(2)}, u32[]{:S(2)}) collective-permute-start(bf16[128,2176]{1,0:T(8,128)(2,1)S(1)} %fusion.9.refs_5_), channel_id=1, source_target_pairs={{0,2},{1,3},{2,0},{3,1},{4,6},{5,7},{6,4},{7,5},{8,10},{9,11},{10,... | collective-permute-start | bytes 1671176 | tf_op jit(solution)/shard_map/ppermute | solution.py:589
  11.7 36.2 %slice-start.4 = ((s8[6291456]{0:T(1024)(128)(4,1)}), s8[4194304]{0:T(1024)(128)(4,1)S(1)}, s32[]{:S(2)}) async-start(s8[6291456]{0:T(1024)(128)(4,1)} %bitcast.78), calls=%async_computation.4 | async-start | bytes 8388608
  11.7 36.2 %slice-start.5 = ((s8[6291456]{0:T(1024)(128)(4,1)}), s8[2097152]{0:T(1024)(128)(4,1)S(1)}, s32[]{:S(2)}) async-start(s8[6291456]{0:T(1024)(128)(4,1)} %bitcast.78), calls=%async_computation.5 | async-start | bytes 4194304
  19.3 7.3 %copy-start.19 = (bf16[128,2176]{1,0:T(8,128)(2,1)}, bf16[128,2176]{1,0:T(8,128)(2,1)S(1)}, u32[]{:S(2)}) copy-start(bf16[128,2176]{1,0:T(8,128)(2,1)S(1)} %collective-permute-done.refs_0_) | copy-start | bytes 1671172
  19.7 6.8 %copy-start.12 = (bf16[128,2176]{1,0:T(8,128)(2,1)}, bf16[128,2176]{1,0:T(8,128)(2,1)S(1)}, u32[]{:S(2)}) copy-start(bf16[128,2176]{1,0:T(8,128)(2,1)S(1)} %collective-permute-done.1.refs_6_) | copy-start | bytes 1671172
  20.9 5.6 %copy-start.13 = (bf16[128,2176]{1,0:T(8,128)(2,1)}, bf16[128,2176]{1,0:T(8,128)(2,1)S(1)}, u32[]{:S(2)}) copy-start(bf16[128,2176]{1,0:T(8,128)(2,1)S(1)} %collective-permute-done.2.refs_7_) | copy-start | bytes 1671172
  20.9 13.8 %collective-permute-start.3 = (bf16[128,2176]{1,0:T(8,128)(2,1)S(1)}, bf16[128,2176]{1,0:T(8,128)(2,1)S(1)}, u32[]{:S(2)}, u32[]{:S(2)}) collective-permute-start(bf16[128,2176]{1,0:T(8,128)(2,1)S(1)} %collective-permute-done.refs_0_), channel_id=1, source_target_pairs={{0,4},{1,5},{2,6},{3,7},{4,12},{5,13},{6,14},{7,15},{8,0},{9,1},{1... | collective-permute-start | bytes 1671176 | tf_op jit(solution)/shard_map/ppermute | solution.py:589
  23.5 12.6 %collective-permute-start.4 = (bf16[128,2176]{1,0:T(8,128)(2,1)S(1)}, bf16[128,2176]{1,0:T(8,128)(2,1)S(1)}, u32[]{:S(2)}, u32[]{:S(2)}) collective-permute-start(bf16[128,2176]{1,0:T(8,128)(2,1)S(1)} %collective-permute-done.refs_0_), channel_id=1, source_target_pairs={{0,1},{1,0},{2,3},{3,2},{4,5},{5,4},{6,7},{7,6},{8,9},{9,8},{10,11... | collective-permute-start | bytes 1671176 | tf_op jit(solution)/shard_map/ppermute | solution.py:589
  24.1 12.7 %collective-permute-start.5 = (bf16[128,2176]{1,0:T(8,128)(2,1)S(1)}, bf16[128,2176]{1,0:T(8,128)(2,1)S(1)}, u32[]{:S(2)}, u32[]{:S(2)}) collective-permute-start(bf16[128,2176]{1,0:T(8,128)(2,1)S(1)} %collective-permute-done.refs_0_), channel_id=1, source_target_pairs={{0,2},{1,3},{2,0},{3,1},{4,6},{5,7},{6,4},{7,5},{8,10},{9,11},{10,... | collective-permute-start | bytes 1671176 | tf_op jit(solution)/shard_map/ppermute | solution.py:589
  34.7 19.3 %copy-start.20 = (bf16[128,2176]{1,0:T(8,128)(2,1)}, bf16[128,2176]{1,0:T(8,128)(2,1)S(1)}, u32[]{:S(2)}) copy-start(bf16[128,2176]{1,0:T(8,128)(2,1)S(1)} %collective-permute-done.3.refs_0_) | copy-start | bytes 1671172
  36.1 4.0 %copy-start.17 = (bf16[128,2176]{1,0:T(8,128)(2,1)}, bf16[128,2176]{1,0:T(8,128)(2,1)S(1)}, u32[]{:S(2)}) copy-start(bf16[128,2176]{1,0:T(8,128)(2,1)S(1)} %collective-permute-done.4.refs_1_) | copy-start | bytes 1671172
  36.8 17.3 %copy-start.18 = (bf16[128,2176]{1,0:T(8,128)(2,1)}, bf16[128,2176]{1,0:T(8,128)(2,1)S(1)}, u32[]{:S(2)}) copy-start(bf16[128,2176]{1,0:T(8,128)(2,1)S(1)} %collective-permute-done.5.refs_2_) | copy-start | bytes 1671172
  36.8 9.7 %collective-permute-start.7 = (bf16[64,2176]{1,0:T(8,128)(2,1)S(1)}, bf16[64,2176]{1,0:T(8,128)(2,1)S(1)}, u32[]{:S(2)}, u32[]{:S(2)}) collective-permute-start(bf16[64,2176]{1,0:T(8,128)(2,1)S(1)} %slice.42), channel_id=1, source_target_pairs={{0,2},{1,3},{2,0},{3,1},{4,6},{5,7},{6,4},{7,5},{8,10},{9,11},{10,... | collective-permute-start | bytes 835592 | tf_op jit(solution)/shard_map/ppermute | solution.py:589
  38.4 19.3 %collective-permute-start.9 = (bf16[128,2176]{1,0:T(8,128)(2,1)S(1)}, bf16[128,2176]{1,0:T(8,128)(2,1)}, u32[]{:S(2)}, u32[]{:S(2)}) collective-permute-start(bf16[128,2176]{1,0:T(8,128)(2,1)S(1)} %collective-permute-done.3.refs_0_), channel_id=1, source_target_pairs={{0,4},{1,5},{2,6},{3,7},{4,12},{5,13},{6,14},{7,15},{8,0},{9,1},{1... | collective-permute-start | bytes 1671176 | tf_op jit(solution)/shard_map/ppermute | solution.py:589
  39.6 18.1 %collective-permute-start.10 = (bf16[128,2176]{1,0:T(8,128)(2,1)S(1)}, bf16[128,2176]{1,0:T(8,128)(2,1)S(1)}, u32[]{:S(2)}, u32[]{:S(2)}) collective-permute-start(bf16[128,2176]{1,0:T(8,128)(2,1)S(1)} %collective-permute-done.3.refs_0_), channel_id=1, source_target_pairs={{0,1},{1,0},{2,3},{3,2},{4,5},{5,4},{6,7},{7,6},{8,9},{9,8},{10,11... | collective-permute-start | bytes 1671176 | tf_op jit(solution)/shard_map/ppermute | solution.py:589
  40.1 17.6 %collective-permute-start.11 = (bf16[128,2176]{1,0:T(8,128)(2,1)S(1)}, bf16[128,2176]{1,0:T(8,128)(2,1)S(1)}, u32[]{:S(2)}, u32[]{:S(2)}) collective-permute-start(bf16[128,2176]{1,0:T(8,128)(2,1)S(1)} %collective-permute-done.3.refs_0_), channel_id=1, source_target_pairs={{0,2},{1,3},{2,0},{3,1},{4,6},{5,7},{6,4},{7,5},{8,10},{9,11},{10,... | collective-permute-start | bytes 1671176 | tf_op jit(solution)/shard_map/ppermute | solution.py:589
  40.7 17.0 %collective-permute-start.6 = (bf16[4,96,384]{2,1,0:T(8,128)(2,1)S(1)}, bf16[4,96,384]{2,1,0:T(8,128)(2,1)S(1)}, u32[]{:S(2)}, u32[]{:S(2)}) collective-permute-start(bf16[4,96,384]{2,1,0:T(8,128)(2,1)S(1)} %get-tuple-element.105), channel_id=1, source_target_pairs={{0,4},{1,5},{2,6},{3,7},{4,12},{5,13},{6,14},{7,15},{8,0},{9,1},{1... | collective-permute-start | bytes 884744 | tf_op jit(solution)/shard_map/ppermute | solution.py:589
  46.5 7.6 %copy-start.22 = (bf16[64,2176]{1,0:T(8,128)(2,1)}, bf16[64,2176]{1,0:T(8,128)(2,1)S(1)}, u32[]{:S(2)}) copy-start(bf16[64,2176]{1,0:T(8,128)(2,1)S(1)} %collective-permute-done.7.refs_3_) | copy-start | bytes 835588
  46.5 11.2 %collective-permute-start.8 = (bf16[64,2176]{1,0:T(8,128)(2,1)S(1)}, bf16[64,2176]{1,0:T(8,128)(2,1)S(1)}, u32[]{:S(2)}, u32[]{:S(2)}) collective-permute-start(bf16[64,2176]{1,0:T(8,128)(2,1)S(1)} %slice.43), channel_id=1, source_target_pairs={{0,1},{1,0},{2,3},{3,2},{4,5},{5,4},{6,7},{7,6},{8,9},{9,8},{10,11... | collective-permute-start | bytes 835592 | tf_op jit(solution)/shard_map/ppermute | solution.py:589
  57.7 9.7 %copy-start.23 = (bf16[64,2176]{1,0:T(8,128)(2,1)}, bf16[64,2176]{1,0:T(8,128)(2,1)S(1)}, u32[]{:S(2)}) copy-start(bf16[64,2176]{1,0:T(8,128)(2,1)S(1)} %collective-permute-done.8.refs_4_) | copy-start | bytes 835588
  57.7 17.1 %copy-start.14 = (bf16[128,2176]{1,0:T(8,128)(2,1)}, bf16[128,2176]{1,0:T(8,128)(2,1)S(1)}, u32[]{:S(2)}) copy-start(bf16[128,2176]{1,0:T(8,128)(2,1)S(1)} %collective-permute-done.10.refs_1_) | copy-start | bytes 1671172
  57.7 17.0 %copy-start.15 = (bf16[128,2176]{1,0:T(8,128)(2,1)}, bf16[128,2176]{1,0:T(8,128)(2,1)S(1)}, u32[]{:S(2)}) copy-start(bf16[128,2176]{1,0:T(8,128)(2,1)S(1)} %collective-permute-done.11.refs_2_) | copy-start | bytes 1671172
  57.8 9.7 %collective-permute-start.14 = (bf16[64,2176]{1,0:T(8,128)(2,1)S(1)}, bf16[64,2176]{1,0:T(8,128)(2,1)S(1)}, u32[]{:S(2)}, u32[]{:S(2)}) collective-permute-start(bf16[64,2176]{1,0:T(8,128)(2,1)S(1)} %slice.44), channel_id=1, source_target_pairs={{0,2},{1,3},{2,0},{3,1},{4,6},{5,7},{6,4},{7,5},{8,10},{9,11},{10,... | collective-permute-start | bytes 835592 | tf_op jit(solution)/shard_map/ppermute | solution.py:589
  57.8 17.6 %collective-permute-start.16 = (bf16[128,2176]{1,0:T(8,128)(2,1)}, bf16[128,2176]{1,0:T(8,128)(2,1)S(1)}, u32[]{:S(2)}, u32[]{:S(2)}) collective-permute-start(bf16[128,2176]{1,0:T(8,128)(2,1)} %collective-permute-done.9.refs_0_), channel_id=1, source_target_pairs={{0,1},{1,0},{2,3},{3,2},{4,5},{5,4},{6,7},{7,6},{8,9},{9,8},{10,11... | collective-permute-start | bytes 1671176 | tf_op jit(solution)/shard_map/ppermute | solution.py:589
  58.5 17.0 %collective-permute-start.17 = (bf16[128,2176]{1,0:T(8,128)(2,1)}, bf16[128,2176]{1,0:T(8,128)(2,1)}, u32[]{:S(2)}, u32[]{:S(2)}) collective-permute-start(bf16[128,2176]{1,0:T(8,128)(2,1)} %collective-permute-done.9.refs_0_), channel_id=1, source_target_pairs={{0,2},{1,3},{2,0},{3,1},{4,6},{5,7},{6,4},{7,5},{8,10},{9,11},{10,... | collective-permute-start | bytes 1671176 | tf_op jit(solution)/shard_map/ppermute | solution.py:589
  60.4 15.0 %collective-permute-start.12 = (bf16[4,96,384]{2,1,0:T(8,128)(2,1)}, bf16[4,96,384]{2,1,0:T(8,128)(2,1)S(1)}, u32[]{:S(2)}, u32[]{:S(2)}) collective-permute-start(bf16[4,96,384]{2,1,0:T(8,128)(2,1)} %get-tuple-element.119), channel_id=1, source_target_pairs={{0,12},{1,13},{2,14},{3,15},{4,8},{5,9},{6,10},{7,11},{8,4},{9,5},... | collective-permute-start | bytes 884744 | tf_op jit(solution)/shard_map/ppermute | solution.py:589
  62.2 13.2 %collective-permute-start.13 = (bf16[4,96,384]{2,1,0:T(8,128)(2,1)}, bf16[4,96,384]{2,1,0:T(8,128)(2,1)S(1)}, u32[]{:S(2)}, u32[]{:S(2)}) collective-permute-start(bf16[4,96,384]{2,1,0:T(8,128)(2,1)} %get-tuple-element.120), channel_id=1, source_target_pairs={{0,8},{1,9},{2,10},{3,11},{4,0},{5,1},{6,2},{7,3},{8,12},{9,13},{1... | collective-permute-start | bytes 884744 | tf_op jit(solution)/shard_map/ppermute | solution.py:589
  67.4 7.3 %copy-start.21 = (bf16[64,2176]{1,0:T(8,128)(2,1)}, bf16[64,2176]{1,0:T(8,128)(2,1)S(1)}, u32[]{:S(2)}) copy-start(bf16[64,2176]{1,0:T(8,128)(2,1)S(1)} %collective-permute-done.14.refs_3_) | copy-start | bytes 835588
  67.4 8.0 %collective-permute-start.15 = (bf16[64,2176]{1,0:T(8,128)(2,1)}, bf16[64,2176]{1,0:T(8,128)(2,1)}, u32[]{:S(2)}, u32[]{:S(2)}) collective-permute-start(bf16[64,2176]{1,0:T(8,128)(2,1)} %slice.45), channel_id=1, source_target_pairs={{0,1},{1,0},{2,3},{3,2},{4,5},{5,4},{6,7},{7,6},{8,9},{9,8},{10,11... | collective-permute-start | bytes 835592 | tf_op jit(solution)/shard_map/ppermute | solution.py:589
  68.0 7.6 %slice-start.6 = ((bf16[128,2176]{1,0:T(8,128)(2,1)}), bf16[64,2176]{1,0:T(8,128)(2,1)S(1)}, s32[]{:S(2)}) async-start(bf16[128,2176]{1,0:T(8,128)(2,1)} %copy-done.12), calls=%async_computation.6 | async-start | bytes 557056 | tf_op jit(solution)/shard_map/slice | solution.py:614
  75.6 17.5 %collective-permute-start.19 = (bf16[128,2176]{1,0:T(8,128)(2,1)S(1)}, bf16[128,2176]{1,0:T(8,128)(2,1)S(1)}, u32[]{:S(2)}, u32[]{:S(2)}) collective-permute-start(bf16[128,2176]{1,0:T(8,128)(2,1)S(1)} %pad_maximum_fusion), channel_id=1, source_target_pairs={{0,2},{1,3},{2,0},{3,1},{4,6},{5,7},{6,4},{7,5},{8,10},{9,11},{10,... | collective-permute-start | bytes 1671176 | tf_op jit(solution)/shard_map/ppermute | solution.py:589
  77.1 16.0 %collective-permute-start.20 = (bf16[128,2176]{1,0:T(8,128)(2,1)S(1)}, bf16[128,2176]{1,0:T(8,128)(2,1)S(1)}, u32[]{:S(2)}, u32[]{:S(2)}) collective-permute-start(bf16[128,2176]{1,0:T(8,128)(2,1)S(1)} %pad_maximum_fusion.1), channel_id=1, source_target_pairs={{0,1},{1,0},{2,3},{3,2},{4,5},{5,4},{6,7},{7,6},{8,9},{9,8},{10,11... | collective-permute-start | bytes 1671176 | tf_op jit(solution)/shard_map/ppermute | solution.py:589
  77.8 14.8 %collective-permute-start.18 = (bf16[4,96,384]{2,1,0:T(8,128)(2,1)S(1)}, bf16[4,96,384]{2,1,0:T(8,128)(2,1)S(1)}, u32[]{:S(2)}, u32[]{:S(2)}) collective-permute-start(bf16[4,96,384]{2,1,0:T(8,128)(2,1)S(1)} %copy-done.28), channel_id=1, source_target_pairs={{0,8},{1,9},{2,10},{3,11},{4,0},{5,1},{6,2},{7,3},{8,12},{9,13},{1... | collective-permute-start | bytes 884744 | tf_op jit(solution)/shard_map/ppermute | solution.py:589
  82.7 24.4 %collective-permute-start.23 = (bf16[4,96,384]{2,1,0:T(8,128)(2,1)}, bf16[4,96,384]{2,1,0:T(8,128)(2,1)S(1)}, u32[]{:S(2)}, u32[]{:S(2)}) collective-permute-start(bf16[4,96,384]{2,1,0:T(8,128)(2,1)} %get-tuple-element.152), channel_id=1, source_target_pairs={{0,1},{1,0},{2,3},{3,2},{4,5},{5,4},{6,7},{7,6},{8,9},{9,8},{10,11... | collective-permute-start | bytes 884744 | tf_op jit(solution)/shard_map/ppermute | solution.py:589
  84.4 22.7 %collective-permute-start.24 = (bf16[4,96,384]{2,1,0:T(8,128)(2,1)}, bf16[4,96,384]{2,1,0:T(8,128)(2,1)S(1)}, u32[]{:S(2)}, u32[]{:S(2)}) collective-permute-start(bf16[4,96,384]{2,1,0:T(8,128)(2,1)} %get-tuple-element.153), channel_id=1, source_target_pairs={{0,2},{1,3},{2,0},{3,1},{4,6},{5,7},{6,4},{7,5},{8,10},{9,11},{10,... | collective-permute-start | bytes 884744 | tf_op jit(solution)/shard_map/ppermute | solution.py:589
  92.6 29.5 %copy-start.5 = (bf16[4,96,384]{2,1,0:T(8,128)(2,1)}, bf16[4,96,384]{2,1,0:T(8,128)(2,1)S(1)}, u32[]{:S(2)}) copy-start(bf16[4,96,384]{2,1,0:T(8,128)(2,1)S(1)} %collective-permute-done.18.refs_1_) | copy-start | bytes 884740
  92.6 14.5 %collective-permute-start.25 = (bf16[4,96,384]{2,1,0:T(8,128)(2,1)S(1)}, bf16[4,96,384]{2,1,0:T(8,128)(2,1)S(1)}, u32[]{:S(2)}, u32[]{:S(2)}) collective-permute-start(bf16[4,96,384]{2,1,0:T(8,128)(2,1)S(1)} %get-tuple-element.154), channel_id=1, source_target_pairs={{0,3},{1,2},{2,1},{3,0},{4,7},{5,6},{6,5},{7,4},{8,11},{9,10},{10,... | collective-permute-start | bytes 884744 | tf_op jit(solution)/shard_map/ppermute | solution.py:589
  93.1 2.7 %copy-start.9 = (bf16[128,2176]{1,0:T(8,128)(2,1)}, bf16[128,2176]{1,0:T(8,128)(2,1)S(1)}, u32[]{:S(2)}) copy-start(bf16[128,2176]{1,0:T(8,128)(2,1)S(1)} %collective-permute-done.19.refs_3_.refs_8_) | copy-start | bytes 1671172
  93.1 2.7 %copy-start.10 = (bf16[128,2176]{1,0:T(8,128)(2,1)}, bf16[128,2176]{1,0:T(8,128)(2,1)S(1)}, u32[]{:S(2)}) copy-start(bf16[128,2176]{1,0:T(8,128)(2,1)S(1)} %collective-permute-done.20.refs_4_.refs_9_) | copy-start | bytes 1671172
  93.1 23.9 %collective-permute-start.21 = (bf16[4,96,384]{2,1,0:T(8,128)(2,1)}, bf16[4,96,384]{2,1,0:T(8,128)(2,1)S(1)}, u32[]{:S(2)}, u32[]{:S(2)}) collective-permute-start(bf16[4,96,384]{2,1,0:T(8,128)(2,1)} %get-tuple-element.146), channel_id=1, source_target_pairs={{0,12},{1,13},{2,14},{3,15},{4,8},{5,9},{6,10},{7,11},{8,4},{9,5},... | collective-permute-start | bytes 884744 | tf_op jit(solution)/shard_map/ppermute | solution.py:589
  105.7 11.4 %collective-permute-start.22 = (bf16[4,96,384]{2,1,0:T(8,128)(2,1)}, bf16[4,96,384]{2,1,0:T(8,128)(2,1)S(1)}, u32[]{:S(2)}, u32[]{:S(2)}) collective-permute-start(bf16[4,96,384]{2,1,0:T(8,128)(2,1)} %get-tuple-element.147), channel_id=1, source_target_pairs={{0,4},{1,5},{2,6},{3,7},{4,12},{5,13},{6,14},{7,15},{8,0},{9,1},{1... | collective-permute-start | bytes 884744 | tf_op jit(solution)/shard_map/ppermute | solution.py:589
  107.1 2.5 %copy-start.1 = (bf16[384,2048]{1,0:T(8,128)(2,1)S(1)}, bf16[384,2048]{1,0:T(8,128)(2,1)}, u32[]{:S(2)}) copy-start(bf16[384,2048]{1,0:T(8,128)(2,1)} %get-tuple-element.158.refs_1_) | copy-start | bytes 4718596
  107.1 2.5 %copy-start.2 = (bf16[384,2048]{1,0:T(8,128)(2,1)S(1)}, bf16[384,2048]{1,0:T(8,128)(2,1)}, u32[]{:S(2)}) copy-start(bf16[384,2048]{1,0:T(8,128)(2,1)} %get-tuple-element.159.refs_2_) | copy-start | bytes 4718596
  107.1 21.5 %slice-start.2 = ((s8[6291456]{0:T(1024)(128)(4,1)}), s8[4194304]{0:T(1024)(128)(4,1)S(1)}, s32[]{:S(2)}) async-start(s8[6291456]{0:T(1024)(128)(4,1)} %bitcast.68), calls=%async_computation.2 | async-start | bytes 8388608
  112.4 16.2 %slice-start = ((s8[6291456]{0:T(1024)(128)(4,1)}), s8[4194304]{0:T(1024)(128)(4,1)S(1)}, s32[]{:S(2)}) async-start(s8[6291456]{0:T(1024)(128)(4,1)} %bitcast.64), calls=%async_computation | async-start | bytes 8388608
  112.4 16.2 %slice-start.3 = ((s8[6291456]{0:T(1024)(128)(4,1)}), s8[2097152]{0:T(1024)(128)(4,1)S(1)}, s32[]{:S(2)}) async-start(s8[6291456]{0:T(1024)(128)(4,1)} %bitcast.68), calls=%async_computation.3 | async-start | bytes 4194304
  116.9 6.5 %collective-permute-start.26 = (bf16[2,192,2048]{2,1,0:T(8,128)(2,1)S(1)}, bf16[2,192,2048]{2,1,0:T(8,128)(2,1)S(1)}, u32[]{:S(2)}, u32[]{:S(2)}) collective-permute-start(bf16[2,192,2048]{2,1,0:T(8,128)(2,1)S(1)} %get-tuple-element.156), channel_id=1, source_target_pairs={{0,16},{16,0},{1,17},{17,1},{2,18},{18,2},{3,19},{19,3},{4,20},{20... | collective-permute-start | bytes 4718600 | tf_op jit(solution)/shard_map/ppermute | solution.py:691
  117.0 5.1 %copy-start.6 = (bf16[4,96,384]{2,1,0:T(8,128)(2,1)}, bf16[4,96,384]{2,1,0:T(8,128)(2,1)S(1)}, u32[]{:S(2)}) copy-start(bf16[4,96,384]{2,1,0:T(8,128)(2,1)S(1)} %collective-permute-done.21.refs_2_) | copy-start | bytes 884740
  117.0 5.1 %copy-start.8 = (bf16[4,96,384]{2,1,0:T(8,128)(2,1)}, bf16[4,96,384]{2,1,0:T(8,128)(2,1)S(1)}, u32[]{:S(2)}) copy-start(bf16[4,96,384]{2,1,0:T(8,128)(2,1)S(1)} %collective-permute-done.22.refs_3_) | copy-start | bytes 884740
  117.0 5.1 %copy-start.7 = (bf16[4,96,384]{2,1,0:T(8,128)(2,1)S(1)}, bf16[4,96,384]{2,1,0:T(8,128)(2,1)}, u32[]{:S(2)}) copy-start(bf16[4,96,384]{2,1,0:T(8,128)(2,1)} %get-tuple-element.148.refs_0_) | copy-start | bytes 884740
  117.0 11.6 %slice-start.1 = ((s8[6291456]{0:T(1024)(128)(4,1)}), s8[2097152]{0:T(1024)(128)(4,1)S(1)}, s32[]{:S(2)}) async-start(s8[6291456]{0:T(1024)(128)(4,1)} %bitcast.64), calls=%async_computation.1 | async-start | bytes 4194304
  121.5 3.6 %collective-permute-start.27 = (bf16[2,192,2048]{2,1,0:T(8,128)(2,1)S(1)}, bf16[2,192,2048]{2,1,0:T(8,128)(2,1)S(1)}, u32[]{:S(2)}, u32[]{:S(2)}) collective-permute-start(bf16[2,192,2048]{2,1,0:T(8,128)(2,1)S(1)} %get-tuple-element.162), channel_id=1, source_target_pairs={{0,16},{16,0},{1,17},{17,1},{2,18},{18,2},{3,19},{19,3},{4,20},{20... | collective-permute-start | bytes 4718600 | tf_op jit(solution)/shard_map/ppermute | solution.py:691
  125.1 16.0 %collective-permute-start.28 = (bf16[4,96,384]{2,1,0:T(8,128)(2,1)S(1)}, bf16[4,96,384]{2,1,0:T(8,128)(2,1)S(1)}, u32[]{:S(2)}, u32[]{:S(2)}) collective-permute-start(bf16[4,96,384]{2,1,0:T(8,128)(2,1)S(1)} %get-tuple-element.170), channel_id=1, source_target_pairs={{0,1},{1,0},{2,3},{3,2},{4,5},{5,4},{6,7},{7,6},{8,9},{9,8},{10,11... | collective-permute-start | bytes 884744 | tf_op jit(solution)/shard_map/ppermute | solution.py:589
  125.6 15.5 %collective-permute-start.29 = (bf16[4,96,384]{2,1,0:T(8,128)(2,1)S(1)}, bf16[4,96,384]{2,1,0:T(8,128)(2,1)S(1)}, u32[]{:S(2)}, u32[]{:S(2)}) collective-permute-start(bf16[4,96,384]{2,1,0:T(8,128)(2,1)S(1)} %get-tuple-element.171), channel_id=1, source_target_pairs={{0,2},{1,3},{2,0},{3,1},{4,6},{5,7},{6,4},{7,5},{8,10},{9,11},{10,... | collective-permute-start | bytes 884744 | tf_op jit(solution)/shard_map/ppermute | solution.py:589
  127.2 14.5 %collective-permute-start.30 = (bf16[4,96,384]{2,1,0:T(8,128)(2,1)S(1)}, bf16[4,96,384]{2,1,0:T(8,128)(2,1)S(1)}, u32[]{:S(2)}, u32[]{:S(2)}) collective-permute-start(bf16[4,96,384]{2,1,0:T(8,128)(2,1)S(1)} %get-tuple-element.172), channel_id=1, source_target_pairs={{0,3},{1,2},{2,1},{3,0},{4,7},{5,6},{6,5},{7,4},{8,11},{9,10},{10,... | collective-permute-start | bytes 884744 | tf_op jit(solution)/shard_map/ppermute | solution.py:589
  128.6 2.8 %copy-start = (f32[192,4,2048]{2,1,0:T(4,128)S(1)}, f32[192,4,2048]{2,1,0:T(4,128)}, u32[]{:S(2)}) copy-start(f32[192,4,2048]{2,1,0:T(4,128)} %param.15) | copy-start | bytes 18874372
  141.2 3.1 %copy-start.25 = (bf16[4,96,384]{2,1,0:T(8,128)(2,1)}, bf16[4,96,384]{2,1,0:T(8,128)(2,1)S(1)}, u32[]{:S(2)}) copy-start(bf16[4,96,384]{2,1,0:T(8,128)(2,1)S(1)} %collective-permute-done.28.refs_4_) | copy-start | bytes 884740
  141.2 3.1 %copy-start.26 = (bf16[4,96,384]{2,1,0:T(8,128)(2,1)}, bf16[4,96,384]{2,1,0:T(8,128)(2,1)S(1)}, u32[]{:S(2)}) copy-start(bf16[4,96,384]{2,1,0:T(8,128)(2,1)S(1)} %collective-permute-done.29.refs_5_) | copy-start | bytes 884740
  141.7 2.6 %copy-start.27 = (bf16[4,96,384]{2,1,0:T(8,128)(2,1)}, bf16[4,96,384]{2,1,0:T(8,128)(2,1)S(1)}, u32[]{:S(2)}) copy-start(bf16[4,96,384]{2,1,0:T(8,128)(2,1)S(1)} %collective-permute-done.30.refs_6_) | copy-start | bytes 884740
  144.3 6.8 %collective-permute-start.31 = (bf16[12288,128]{1,0:T(8,128)(2,1)}, bf16[12288,128]{1,0:T(8,128)(2,1)S(1)}, u32[]{:S(2)}, u32[]{:S(2)}) collective-permute-start(bf16[12288,128]{1,0:T(8,128)(2,1)} %get-tuple-element.190), channel_id=1, source_target_pairs={{0,16},{16,0},{1,17},{17,1},{2,18},{18,2},{3,19},{19,3},{4,20},{20... | collective-permute-start | bytes 9437192 | tf_op jit(solution)/shard_map/ppermute | solution.py:709
  (5 other events, 9.0 us)

commit v9 on v8

--- a/solution.py
+++ b/solution.py
@@ -92,8 +92,9 @@
         for i, piece in enumerate(pieces):
             place = all_rows.at[j, pl.ds(at, piece.shape[0])]
             loads[j].append(pltpu.make_async_copy(piece, place, sems.at[j, i]))
-            loads[j][i].start()
             at += piece.shape[0]
+    for load in loads[0]:
+        load.start()
     weight_loads = [
         pltpu.make_async_copy(by_expert.at[e], weights.at[e], weight_sems.at[e])
         for e in range(experts)
@@ -113,6 +114,9 @@
             load.wait()
         if j == 0:
             for load in weight_loads:
+                load.start()
+        if j + 1 < chunks:
+            for load in loads[j + 1]:
                 load.start()
         hits = []
         for c in range(4):
@@ -233,7 +237,7 @@
             pltpu.VMEM(shape, jnp.bfloat16),
             pltpu.SemaphoreType.DMA((size + 1,)),
         ],
-        compiler_params=pltpu.CompilerParams(vmem_limit_bytes=10 * MIB),
+        compiler_params=pltpu.CompilerParams(vmem_limit_bytes=8 * MIB),
         cost_estimate=pl.CostEstimate(
             flops=0, bytes_accessed=8 * size * slots * width, transcendentals=0
         ),
@@ -273,7 +277,7 @@
             pltpu.VMEM((count, 3, slots, width), jnp.bfloat16),
             pltpu.SemaphoreType.DMA((count + 3,)),
         ],
-        compiler_params=pltpu.CompilerParams(vmem_limit_bytes=10 * MIB),
+        compiler_params=pltpu.CompilerParams(vmem_limit_bytes=3 * MIB),
         cost_estimate=pl.CostEstimate(
             flops=0, bytes_accessed=12 * count * slots * width, transcendentals=0
         ),
@@ -341,7 +345,7 @@
             pltpu.VMEM((experts, width, features), jnp.bfloat16),
             pltpu.SemaphoreType.DMA((experts, 1 + len(blocks) + count)),
         ],
-        compiler_params=pltpu.CompilerParams(vmem_limit_bytes=16 * MIB),
+        compiler_params=pltpu.CompilerParams(vmem_limit_bytes=9 * MIB),
         cost_estimate=pl.CostEstimate(
             flops=2 * experts * width * slots * features,
             bytes_accessed=2 * experts * (width + slots) * features,

time: 154 us -> 155 us (level)
  transfers between devices with their start and end apart: 32 -> 32, of which waited for: 12 -> 12; matrix products, arithmetic and copies ran while one was open for 10% -> 10% of each run, Pallas kernels for 35% -> 36%
where the time goes in v9:
time: 155 us
  Pallas kernels  60.6 us (39%)
  starting transfers between devices  38.8 us (25%)
  waiting for transfers between devices  31.2 us (20%)
  local copies, waits for them, and re-layouts  16.5 us (11%)
  matrix products  3.51 us (2%)
  other arithmetic  2.7 us (2%)
    ppermute x29, starting transfers between devices, move(): return lax.ppermute(block, 'inner', step_perm(size, steps, flip))  38.1 us
    ppermute x29, waiting for transfers between devices, move(): return lax.ppermute(block, 'inner', step_perm(size, steps, flip))  29.5 us
    pallas_call x3, Pallas kernels, chunk_grads(): pl.pallas_call(functools.partial(grads_kernel, spans, keep), out_shape=[j...  24.2 us
    unnamed x73, local copies, waits for them, and re-layouts  12.8 us
    pallas_call x2, Pallas kernels, adam_rows(): pl.pallas_call(functools.partial(adam_kernel, count, owners, kept, first)...  12.3 us
    pallas_call x2, Pallas kernels, partial_rows(): pl.pallas_call(functools.partial(partial_kernel, start, total), out_shape...  8.96 us
    pallas_call x1, Pallas kernels, finish(): pl.pallas_call(functools.partial(finish_kernel, pieces), out_shape=(jax.S...  6.75 us
    pallas_call x2, Pallas kernels, regroup(): pl.pallas_call(regroup_kernel, out_shape=[jax.ShapeDtypeStruct((count, sl...  3.29 us
  transfers between devices with their start and end apart: 32, of which 12 were waited for; matrix products, arithmetic and copies ran while one was open for 10% of the time, Pallas kernels for 36%

profile of v9, /device:TPU:0, one launch (start us, length us, event | category | flops | bytes accessed | tf_op | source)
XLA Modules:
  0.0 154.7 jit_solution(9021781495563744882)
XLA Ops:
  0.6 0.7 convert_element_type.46
  1.5 1.1 fusion.9.refs_5_
  2.6 3.1 %collective-permute-start = (bf16[128,2176]{1,0:T(8,128)(2,1)S(1)}, bf16[128,2176]{1,0:T(8,128)(2,1)S(1)}, u32[]{:S(2)}, u32[]{:S(2)}) collective-permute-start(bf16[128,2176]{1,0:T(8,128)(2,1)S(1)} %fusion.9.refs_5_), channel_id=1, source_target_pairs={{0,4},{1,5},{2,6},{3,7},{4,12},{5,13},{6,14},{7,15},{8,0},{9,1},{1... | collective-permute-start | bytes 1671176 | tf_op jit(solution)/shard_map/ppermute | solution.py:593
  5.6 1.5 collective-permute-start.1
  7.1 1.5 collective-permute-start.2
  8.7 0.8 copy.47
  10.2 0.6 fusion.27.target
  11.0 0.7 reshape.249.probs
  11.7 3.2 %fusion.2 = bf16[1536,384]{1,0:T(8,128)(2,1)S(1)} fusion(s32[1024]{0:T(1024)S(1)} %fusion.41, bf16[128,8,384]{2,1,0:T(8,128)(2,1)} %param.9, f32[128,8]{1,0:T(8,128)S(1)} %copy.49), kind=kOutput, calls=%fused_computation.4 | convolution fusion | flops 1211301888 | bytes 1974272 | tf_op jit(solution)/shard_map/dot_general | solution.py:585
  14.9 4.4 %collective-permute-done.refs_0_ = bf16[128,2176]{1,0:T(8,128)(2,1)S(1)} collective-permute-done((bf16[128,2176]{1,0:T(8,128)(2,1)S(1)}, bf16[128,2176]{1,0:T(8,128)(2,1)S(1)}, u32[]{:S(2)}, u32[]{:S(2)}) %collective-permute-start) | collective-permute-done | bytes 557088 | tf_op jit(solution)/shard_map/ppermute | solution.py:593
  19.7 1.2 collective-permute-done.2.refs_7_
  20.9 2.6 %collective-permute-start.3 = (bf16[128,2176]{1,0:T(8,128)(2,1)S(1)}, bf16[128,2176]{1,0:T(8,128)(2,1)S(1)}, u32[]{:S(2)}, u32[]{:S(2)}) collective-permute-start(bf16[128,2176]{1,0:T(8,128)(2,1)S(1)} %collective-permute-done.refs_0_), channel_id=1, source_target_pairs={{0,4},{1,5},{2,6},{3,7},{4,12},{5,13},{6,14},{7,15},{8,0},{9,1},{1... | collective-permute-start | bytes 1671176 | tf_op jit(solution)/shard_map/ppermute | solution.py:593
  23.5 0.5 collective-permute-start.4
  24.1 1.5 collective-permute-start.5
  25.6 1.0 slice_bitcast_fusion
  26.6 8.2 %collective-permute-done.3.refs_0_ = bf16[128,2176]{1,0:T(8,128)(2,1)S(1)} collective-permute-done((bf16[128,2176]{1,0:T(8,128)(2,1)S(1)}, bf16[128,2176]{1,0:T(8,128)(2,1)S(1)}, u32[]{:S(2)}, u32[]{:S(2)}) %collective-permute-start.3) | collective-permute-done | bytes 557088 | tf_op jit(solution)/shard_map/ppermute | solution.py:593
  34.7 1.4 collective-permute-done.4.refs_1_
  36.1 0.6 collective-permute-done.5.refs_2_
  36.8 1.6 %collective-permute-start.7 = (bf16[64,2176]{1,0:T(8,128)(2,1)S(1)}, bf16[64,2176]{1,0:T(8,128)(2,1)S(1)}, u32[]{:S(2)}, u32[]{:S(2)}) collective-permute-start(bf16[64,2176]{1,0:T(8,128)(2,1)S(1)} %slice.42), channel_id=1, source_target_pairs={{0,2},{1,3},{2,0},{3,1},{4,6},{5,7},{6,4},{7,5},{8,10},{9,11},{10,... | collective-permute-start | bytes 835592 | tf_op jit(solution)/shard_map/ppermute | solution.py:593
  38.4 1.2 collective-permute-start.9
  39.6 0.5 collective-permute-start.10
  40.1 0.5 collective-permute-start.11
  40.7 1.0 collective-permute-start.6
  41.6 4.8 %collective-permute-done.7.refs_3_ = bf16[64,2176]{1,0:T(8,128)(2,1)S(1)} collective-permute-done((bf16[64,2176]{1,0:T(8,128)(2,1)S(1)}, bf16[64,2176]{1,0:T(8,128)(2,1)S(1)}, u32[]{:S(2)}, u32[]{:S(2)}) %collective-permute-start.7) | collective-permute-done | bytes 278560 | tf_op jit(solution)/shard_map/ppermute | solution.py:593
  46.5 1.4 collective-permute-start.8
  47.9 6.2 %copy.63 = bf16[384,4,2048]{2,0,1:T(8,128)(2,1)} copy(bf16[384,4,2048]{2,1,0:T(4,128)(2,1)S(1)} %bitcast.79) | data formatting | bytes 12582912 | tf_op args[4]
  54.1 3.6 %collective-permute-done.8.refs_4_ = bf16[64,2176]{1,0:T(8,128)(2,1)S(1)} collective-permute-done((bf16[64,2176]{1,0:T(8,128)(2,1)S(1)}, bf16[64,2176]{1,0:T(8,128)(2,1)S(1)}, u32[]{:S(2)}, u32[]{:S(2)}) %collective-permute-start.8) | collective-permute-done | bytes 278560 | tf_op jit(solution)/shard_map/ppermute | solution.py:593
  57.8 0.6 collective-permute-start.16
  58.5 1.9 %collective-permute-start.17 = (bf16[128,2176]{1,0:T(8,128)(2,1)}, bf16[128,2176]{1,0:T(8,128)(2,1)}, u32[]{:S(2)}, u32[]{:S(2)}) collective-permute-start(bf16[128,2176]{1,0:T(8,128)(2,1)} %collective-permute-done.9.refs_0_), channel_id=1, source_target_pairs={{0,2},{1,3},{2,0},{3,1},{4,6},{5,7},{6,4},{7,5},{8,10},{9,11},{10,... | collective-permute-start | bytes 1671176 | tf_op jit(solution)/shard_map/ppermute | solution.py:593
  60.4 1.8 %collective-permute-start.12 = (bf16[4,96,384]{2,1,0:T(8,128)(2,1)}, bf16[4,96,384]{2,1,0:T(8,128)(2,1)S(1)}, u32[]{:S(2)}, u32[]{:S(2)}) collective-permute-start(bf16[4,96,384]{2,1,0:T(8,128)(2,1)} %get-tuple-element.119), channel_id=1, source_target_pairs={{0,12},{1,13},{2,14},{3,15},{4,8},{5,9},{6,10},{7,11},{8,4},{9,5},... | collective-permute-start | bytes 884744 | tf_op jit(solution)/shard_map/ppermute | solution.py:593
  62.2 0.8 collective-permute-start.13
  63.0 0.7 slice.45
  63.8 3.7 %collective-permute-done.14.refs_3_ = bf16[64,2176]{1,0:T(8,128)(2,1)S(1)} collective-permute-done((bf16[64,2176]{1,0:T(8,128)(2,1)S(1)}, bf16[64,2176]{1,0:T(8,128)(2,1)S(1)}, u32[]{:S(2)}, u32[]{:S(2)}) %collective-permute-start.14) | collective-permute-done | bytes 278560 | tf_op jit(solution)/shard_map/ppermute | solution.py:593
  67.4 0.5 collective-permute-start.15
  68.0 6.8 %shard_map.127 = (bf16[384,2048]{1,0:T(8,128)(2,1)}, bf16[4,96,384]{2,1,0:T(8,128)(2,1)}) custom-call(s32[1]{0:T(128)} %bitcast.5.first, bf16[128,2176]{1,0:T(8,128)(2,1)} %copy-done.19, bf16[128,2176]{1,0:T(8,128)(2,1)} %copy-done.17, bf16[128,2176]{1,0:T(8,128)(2,1)} %copy-done.18, bf16[64,2176]{1,0:T(8,128)(2,1)} %copy-done.22, ...), custom_call_target="tpu_custom_call" | custom-call | flops 1409286144 | bytes 3670016 | tf_op jit(solution)/shard_map/pallas_call | solution.py:176
  74.8 0.6 collective-permute-done.15.refs_4_
  75.6 0.5 collective-permute-start.19
  76.0 1.0 slice.47
  77.1 0.7 collective-permute-start.20
  77.8 3.0 %collective-permute-start.18 = (bf16[4,96,384]{2,1,0:T(8,128)(2,1)S(1)}, bf16[4,96,384]{2,1,0:T(8,128)(2,1)S(1)}, u32[]{:S(2)}, u32[]{:S(2)}) collective-permute-start(bf16[4,96,384]{2,1,0:T(8,128)(2,1)S(1)} %copy-done.28), channel_id=1, source_target_pairs={{0,8},{1,9},{2,10},{3,11},{4,0},{5,1},{6,2},{7,3},{8,12},{9,13},{1... | collective-permute-start | bytes 884744 | tf_op jit(solution)/shard_map/ppermute | solution.py:593
  80.7 2.0 %shard_map.130 = (bf16[4,96,384]{2,1,0:T(8,128)(2,1)}, bf16[4,96,384]{2,1,0:T(8,128)(2,1)}, bf16[4,96,384]{2,1,0:T(8,128)(2,1)S(1)}) custom-call(bf16[4,96,384]{2,1,0:T(8,128)(2,1)S(1)} %get-tuple-element.132.refs_0_, bf16[4,96,384]{2,1,0:T(8,128)(2,1)S(1)} %collective-permute-done.6.refs_1_, bf16[4,96,384]{2,1,0:T(8,128)(2,1)S(1)} %collective-permute-done.12.refs_2_, ...), custom_call_target="tpu_custom_call" | custom-call | bytes 1769472 | tf_op jit(solution)/shard_map/pallas_call | solution.py:271
  82.7 1.6 %collective-permute-start.23 = (bf16[4,96,384]{2,1,0:T(8,128)(2,1)}, bf16[4,96,384]{2,1,0:T(8,128)(2,1)S(1)}, u32[]{:S(2)}, u32[]{:S(2)}) collective-permute-start(bf16[4,96,384]{2,1,0:T(8,128)(2,1)} %get-tuple-element.152), channel_id=1, source_target_pairs={{0,1},{1,0},{2,3},{3,2},{4,5},{5,4},{6,7},{7,6},{8,9},{9,8},{10,11... | collective-permute-start | bytes 884744 | tf_op jit(solution)/shard_map/ppermute | solution.py:593
  84.4 1.5 collective-permute-start.24
  85.9 6.7 %shard_map.128 = (bf16[384,2048]{1,0:T(8,128)(2,1)}, bf16[4,96,384]{2,1,0:T(8,128)(2,1)}) custom-call(s32[1]{0:T(128)} %bitcast.5.first, bf16[128,2176]{1,0:T(8,128)(2,1)} %copy-done.20, bf16[128,2176]{1,0:T(8,128)(2,1)} %copy-done.14, bf16[128,2176]{1,0:T(8,128)(2,1)} %copy-done.15, bf16[64,2176]{1,0:T(8,128)(2,1)} %copy-done.21, ...), custom_call_target="tpu_custom_call" | custom-call | flops 1409286144 | bytes 3670016 | tf_op jit(solution)/shard_map/pallas_call | solution.py:176
  93.1 2.7 %collective-permute-start.21 = (bf16[4,96,384]{2,1,0:T(8,128)(2,1)}, bf16[4,96,384]{2,1,0:T(8,128)(2,1)S(1)}, u32[]{:S(2)}, u32[]{:S(2)}) collective-permute-start(bf16[4,96,384]{2,1,0:T(8,128)(2,1)} %get-tuple-element.146), channel_id=1, source_target_pairs={{0,12},{1,13},{2,14},{3,15},{4,8},{5,9},{6,10},{7,11},{8,4},{9,5},... | collective-permute-start | bytes 884744 | tf_op jit(solution)/shard_map/ppermute | solution.py:593
  95.8 10.7 %shard_map.129 = (bf16[384,2048]{1,0:T(8,128)(2,1)}, bf16[4,96,384]{2,1,0:T(8,128)(2,1)}, bf16[384,2048]{1,0:T(8,128)(2,1)}, bf16[4,96,384]{2,1,0:T(8,128)(2,1)}) custom-call(s32[1]{0:T(128)} %bitcast.5.first, bf16[128,2176]{1,0:T(8,128)(2,1)} %collective-permute-done.9.refs_0_, bf16[128,2176]{1,0:T(8,128)(2,1)} %copy-done.16, ...), custom_call_target="tpu_custom_call" | custom-call | flops 2818572288 | bytes 7340032 | tf_op jit(solution)/shard_map/pallas_call | solution.py:176
  106.5 1.4 collective-permute-start.22
  107.9 2.5 %shard_map.131.weighted = bf16[4,384,384]{2,1,0:T(8,128)(2,1)S(1)} custom-call(bf16[4,96,384]{2,1,0:T(8,128)(2,1)S(1)} %get-tuple-element.132.refs_0_, bf16[4,96,384]{2,1,0:T(8,128)(2,1)S(1)} %collective-permute-done.6.refs_1_, bf16[4,96,384]{2,1,0:T(8,128)(2,1)S(1)} %collective-permute-done.12.refs_2_, ...), custom_call_target="tpu_custom_call" | custom-call | bytes 4718592 | tf_op jit(solution)/shard_map/pallas_call | solution.py:229
  110.5 1.4 copy-done.3
  111.9 1.4 copy-done.4
  113.3 4.5 %shard_map.132 = (bf16[2,192,2048]{2,1,0:T(8,128)(2,1)S(1)}, bf16[2,192,2048]{2,1,0:T(8,128)(2,1)S(1)}) custom-call(s32[2]{0:T(128)S(1)} %and_select_fusion.owners, bf16[4,384,384]{2,1,0:T(8,128)(2,1)S(1)} %shard_map.131.weighted, bf16[384,2048]{1,0:T(8,128)(2,1)S(1)} %copy-done.4, bf16[384,2048]{1,0:T(8,128)(2,1)S(1)} %copy-done.1, ...), custom_call_target="tpu_custom_call" | custom-call | flops 1207959552 | bytes 6291456 | tf_op jit(solution)/shard_map/pallas_call | solution.py:336
  117.9 4.5 %shard_map.133 = (bf16[2,192,2048]{2,1,0:T(8,128)(2,1)S(1)}, bf16[2,192,2048]{2,1,0:T(8,128)(2,1)S(1)}) custom-call(s32[2]{0:T(128)S(1)} %and_select_fusion.owners, bf16[4,384,384]{2,1,0:T(8,128)(2,1)S(1)} %shard_map.131.weighted, bf16[384,2048]{1,0:T(8,128)(2,1)S(1)} %copy-done.4, bf16[384,2048]{1,0:T(8,128)(2,1)S(1)} %copy-done.1, ...), custom_call_target="tpu_custom_call" | custom-call | flops 1207959552 | bytes 6291456 | tf_op jit(solution)/shard_map/pallas_call | solution.py:336
  122.4 0.5 collective-permute-start.27
  122.9 1.3 shard_map.134
  124.3 1.7 %collective-permute-done.27.refs_3_ = bf16[2,192,2048]{2,1,0:T(8,128)(2,1)S(1)} collective-permute-done((bf16[2,192,2048]{2,1,0:T(8,128)(2,1)S(1)}, bf16[2,192,2048]{2,1,0:T(8,128)(2,1)S(1)}, u32[]{:S(2)}, u32[]{:S(2)}) %collective-permute-start.27) | collective-permute-done | bytes 1572896 | tf_op jit(solution)/shard_map/ppermute | solution.py:695
  126.0 0.5 collective-permute-start.28
  126.5 1.5 collective-permute-start.29
  128.0 1.5 collective-permute-start.30
  129.5 2.8 %copy-done = f32[192,4,2048]{2,1,0:T(4,128)S(1)} copy-done((f32[192,4,2048]{2,1,0:T(4,128)S(1)}, f32[192,4,2048]{2,1,0:T(4,128)}, u32[]{:S(2)}) %copy-start) | copy-done | bytes 6291480
  132.3 9.7 %shard_map.136 = (f32[12288,128]{1,0:T(8,128)}, f32[12288,128]{1,0:T(8,128)}, f32[12288,128]{1,0:T(8,128)}, bf16[24576,128]{1,0:T(8,128)(2,1)}, bf16[12288,128]{1,0:T(8,128)(2,1)}) custom-call(s32[1]{0:T(128)} %bitcast.13.at, bf16[2,192,2048]{2,1,0:T(8,128)(2,1)S(1)} %get-tuple-element.178.refs_0_, ...), custom_call_target="tpu_custom_call" | custom-call | bytes 65536 | tf_op jit(solution)/shard_map/pallas_call | solution.py:420
  142.0 0.5 collective-permute-done.30.refs_6_
  142.5 2.6 %shard_map.137 = (f32[12288,128]{1,0:T(8,128)}, f32[12288,128]{1,0:T(8,128)}, f32[12288,128]{1,0:T(8,128)}, bf16[24576,128]{1,0:T(8,128)(2,1)}, bf16[12288,128]{1,0:T(8,128)(2,1)}) custom-call(s32[1]{0:T(128)} %bitcast.13.at, ...), custom_call_target="tpu_custom_call", output_to_operand_aliasing={{0}: (8, {}), {1}: (9, {}), {2}: (10, {}), {3}: (11, {}), {... | custom-call | bytes 65536 | tf_op jit(solution)/shard_map/pallas_call | solution.py:420
  145.2 6.7 %shard_map.135 = (bf16[1024,384]{1,0:T(8,128)(2,1)}, f32[8,128]{1,0:T(8,128)}) custom-call(f32[8,128]{1,0:T(8,128)} %fusion.27.target, f32[8,128]{1,0:T(8,128)} %reshape.249.probs, bf16[1024,384]{1,0:T(8,128)(2,1)} %bitcast.84, bf16[4,96,384]{2,1,0:T(8,128)(2,1)} %get-tuple-element.148.refs_0_, bf16[4,96,384]{2,1,0:T(8,128)(2,1)} %copy-done.5, ...), custom_call_target="tpu_custom_call" | custom-call | flops 1207959552 | bytes 3145728 | tf_op jit(solution)/shard_map/pallas_call | solution.py:527
  152.0 2.7 %shard_map.138 = bf16[24576,128]{1,0:T(8,128)(2,1)} custom-call(s32[1]{0:T(128)} %bitcast.38.at, bf16[12288,128]{1,0:T(8,128)(2,1)S(1)} %collective-permute-done.31.got, bf16[24576,128]{1,0:T(8,128)(2,1)} %get-tuple-element.191.full), custom_call_target="tpu_custom_call", output_to_operand_aliasing={{}: (2, {})} | custom-call | bytes 6291456 | tf_op jit(solution)/shard_map/pallas_call | solution.py:448
  (114 shorter events, 2.4 us)
Async XLA Ops:
  0.6 10.3 %copy-start.24 = (f32[128,8]{0,1:T(8,128)S(1)}, f32[128,8]{0,1:T(8,128)}, u32[]{:S(2)}) copy-start(f32[128,8]{0,1:T(8,128)} %param.10) | copy-start | bytes 12292
  2.6 12.4 %copy-start.11 = (bf16[128,2176]{1,0:T(8,128)(2,1)}, bf16[128,2176]{1,0:T(8,128)(2,1)S(1)}, u32[]{:S(2)}) copy-start(bf16[128,2176]{1,0:T(8,128)(2,1)S(1)} %fusion.9.refs_5_) | copy-start | bytes 1671172
  2.6 16.7 %collective-permute-start = (bf16[128,2176]{1,0:T(8,128)(2,1)S(1)}, bf16[128,2176]{1,0:T(8,128)(2,1)S(1)}, u32[]{:S(2)}, u32[]{:S(2)}) collective-permute-start(bf16[128,2176]{1,0:T(8,128)(2,1)S(1)} %fusion.9.refs_5_), channel_id=1, source_target_pairs={{0,4},{1,5},{2,6},{3,7},{4,12},{5,13},{6,14},{7,15},{8,0},{9,1},{1... | collective-permute-start | bytes 1671176 | tf_op jit(solution)/shard_map/ppermute | solution.py:593
  5.6 14.1 %collective-permute-start.1 = (bf16[128,2176]{1,0:T(8,128)(2,1)S(1)}, bf16[128,2176]{1,0:T(8,128)(2,1)S(1)}, u32[]{:S(2)}, u32[]{:S(2)}) collective-permute-start(bf16[128,2176]{1,0:T(8,128)(2,1)S(1)} %fusion.9.refs_5_), channel_id=1, source_target_pairs={{0,1},{1,0},{2,3},{3,2},{4,5},{5,4},{6,7},{7,6},{8,9},{9,8},{10,11... | collective-permute-start | bytes 1671176 | tf_op jit(solution)/shard_map/ppermute | solution.py:593
  7.1 13.8 %collective-permute-start.2 = (bf16[128,2176]{1,0:T(8,128)(2,1)S(1)}, bf16[128,2176]{1,0:T(8,128)(2,1)S(1)}, u32[]{:S(2)}, u32[]{:S(2)}) collective-permute-start(bf16[128,2176]{1,0:T(8,128)(2,1)S(1)} %fusion.9.refs_5_), channel_id=1, source_target_pairs={{0,2},{1,3},{2,0},{3,1},{4,6},{5,7},{6,4},{7,5},{8,10},{9,11},{10,... | collective-permute-start | bytes 1671176 | tf_op jit(solution)/shard_map/ppermute | solution.py:593
  11.7 36.2 %slice-start.4 = ((s8[6291456]{0:T(1024)(128)(4,1)}), s8[4194304]{0:T(1024)(128)(4,1)S(1)}, s32[]{:S(2)}) async-start(s8[6291456]{0:T(1024)(128)(4,1)} %bitcast.78), calls=%async_computation.4 | async-start | bytes 8388608
  11.7 36.2 %slice-start.5 = ((s8[6291456]{0:T(1024)(128)(4,1)}), s8[2097152]{0:T(1024)(128)(4,1)S(1)}, s32[]{:S(2)}) async-start(s8[6291456]{0:T(1024)(128)(4,1)} %bitcast.78), calls=%async_computation.5 | async-start | bytes 4194304
  19.3 7.3 %copy-start.19 = (bf16[128,2176]{1,0:T(8,128)(2,1)}, bf16[128,2176]{1,0:T(8,128)(2,1)S(1)}, u32[]{:S(2)}) copy-start(bf16[128,2176]{1,0:T(8,128)(2,1)S(1)} %collective-permute-done.refs_0_) | copy-start | bytes 1671172
  19.7 6.8 %copy-start.12 = (bf16[128,2176]{1,0:T(8,128)(2,1)}, bf16[128,2176]{1,0:T(8,128)(2,1)S(1)}, u32[]{:S(2)}) copy-start(bf16[128,2176]{1,0:T(8,128)(2,1)S(1)} %collective-permute-done.1.refs_6_) | copy-start | bytes 1671172
  20.9 5.6 %copy-start.13 = (bf16[128,2176]{1,0:T(8,128)(2,1)}, bf16[128,2176]{1,0:T(8,128)(2,1)S(1)}, u32[]{:S(2)}) copy-start(bf16[128,2176]{1,0:T(8,128)(2,1)S(1)} %collective-permute-done.2.refs_7_) | copy-start | bytes 1671172
  20.9 13.8 %collective-permute-start.3 = (bf16[128,2176]{1,0:T(8,128)(2,1)S(1)}, bf16[128,2176]{1,0:T(8,128)(2,1)S(1)}, u32[]{:S(2)}, u32[]{:S(2)}) collective-permute-start(bf16[128,2176]{1,0:T(8,128)(2,1)S(1)} %collective-permute-done.refs_0_), channel_id=1, source_target_pairs={{0,4},{1,5},{2,6},{3,7},{4,12},{5,13},{6,14},{7,15},{8,0},{9,1},{1... | collective-permute-start | bytes 1671176 | tf_op jit(solution)/shard_map/ppermute | solution.py:593
  23.5 12.6 %collective-permute-start.4 = (bf16[128,2176]{1,0:T(8,128)(2,1)S(1)}, bf16[128,2176]{1,0:T(8,128)(2,1)S(1)}, u32[]{:S(2)}, u32[]{:S(2)}) collective-permute-start(bf16[128,2176]{1,0:T(8,128)(2,1)S(1)} %collective-permute-done.refs_0_), channel_id=1, source_target_pairs={{0,1},{1,0},{2,3},{3,2},{4,5},{5,4},{6,7},{7,6},{8,9},{9,8},{10,11... | collective-permute-start | bytes 1671176 | tf_op jit(solution)/shard_map/ppermute | solution.py:593
  24.1 12.7 %collective-permute-start.5 = (bf16[128,2176]{1,0:T(8,128)(2,1)S(1)}, bf16[128,2176]{1,0:T(8,128)(2,1)S(1)}, u32[]{:S(2)}, u32[]{:S(2)}) collective-permute-start(bf16[128,2176]{1,0:T(8,128)(2,1)S(1)} %collective-permute-done.refs_0_), channel_id=1, source_target_pairs={{0,2},{1,3},{2,0},{3,1},{4,6},{5,7},{6,4},{7,5},{8,10},{9,11},{10,... | collective-permute-start | bytes 1671176 | tf_op jit(solution)/shard_map/ppermute | solution.py:593
  34.7 19.3 %copy-start.20 = (bf16[128,2176]{1,0:T(8,128)(2,1)}, bf16[128,2176]{1,0:T(8,128)(2,1)S(1)}, u32[]{:S(2)}) copy-start(bf16[128,2176]{1,0:T(8,128)(2,1)S(1)} %collective-permute-done.3.refs_0_) | copy-start | bytes 1671172
  36.1 4.0 %copy-start.17 = (bf16[128,2176]{1,0:T(8,128)(2,1)}, bf16[128,2176]{1,0:T(8,128)(2,1)S(1)}, u32[]{:S(2)}) copy-start(bf16[128,2176]{1,0:T(8,128)(2,1)S(1)} %collective-permute-done.4.refs_1_) | copy-start | bytes 1671172
  36.8 17.3 %copy-start.18 = (bf16[128,2176]{1,0:T(8,128)(2,1)}, bf16[128,2176]{1,0:T(8,128)(2,1)S(1)}, u32[]{:S(2)}) copy-start(bf16[128,2176]{1,0:T(8,128)(2,1)S(1)} %collective-permute-done.5.refs_2_) | copy-start | bytes 1671172
  36.8 9.7 %collective-permute-start.7 = (bf16[64,2176]{1,0:T(8,128)(2,1)S(1)}, bf16[64,2176]{1,0:T(8,128)(2,1)S(1)}, u32[]{:S(2)}, u32[]{:S(2)}) collective-permute-start(bf16[64,2176]{1,0:T(8,128)(2,1)S(1)} %slice.42), channel_id=1, source_target_pairs={{0,2},{1,3},{2,0},{3,1},{4,6},{5,7},{6,4},{7,5},{8,10},{9,11},{10,... | collective-permute-start | bytes 835592 | tf_op jit(solution)/shard_map/ppermute | solution.py:593
  38.4 19.3 %collective-permute-start.9 = (bf16[128,2176]{1,0:T(8,128)(2,1)S(1)}, bf16[128,2176]{1,0:T(8,128)(2,1)}, u32[]{:S(2)}, u32[]{:S(2)}) collective-permute-start(bf16[128,2176]{1,0:T(8,128)(2,1)S(1)} %collective-permute-done.3.refs_0_), channel_id=1, source_target_pairs={{0,4},{1,5},{2,6},{3,7},{4,12},{5,13},{6,14},{7,15},{8,0},{9,1},{1... | collective-permute-start | bytes 1671176 | tf_op jit(solution)/shard_map/ppermute | solution.py:593
  39.6 18.1 %collective-permute-start.10 = (bf16[128,2176]{1,0:T(8,128)(2,1)S(1)}, bf16[128,2176]{1,0:T(8,128)(2,1)S(1)}, u32[]{:S(2)}, u32[]{:S(2)}) collective-permute-start(bf16[128,2176]{1,0:T(8,128)(2,1)S(1)} %collective-permute-done.3.refs_0_), channel_id=1, source_target_pairs={{0,1},{1,0},{2,3},{3,2},{4,5},{5,4},{6,7},{7,6},{8,9},{9,8},{10,11... | collective-permute-start | bytes 1671176 | tf_op jit(solution)/shard_map/ppermute | solution.py:593
  40.1 17.6 %collective-permute-start.11 = (bf16[128,2176]{1,0:T(8,128)(2,1)S(1)}, bf16[128,2176]{1,0:T(8,128)(2,1)S(1)}, u32[]{:S(2)}, u32[]{:S(2)}) collective-permute-start(bf16[128,2176]{1,0:T(8,128)(2,1)S(1)} %collective-permute-done.3.refs_0_), channel_id=1, source_target_pairs={{0,2},{1,3},{2,0},{3,1},{4,6},{5,7},{6,4},{7,5},{8,10},{9,11},{10,... | collective-permute-start | bytes 1671176 | tf_op jit(solution)/shard_map/ppermute | solution.py:593
  40.7 17.0 %collective-permute-start.6 = (bf16[4,96,384]{2,1,0:T(8,128)(2,1)S(1)}, bf16[4,96,384]{2,1,0:T(8,128)(2,1)S(1)}, u32[]{:S(2)}, u32[]{:S(2)}) collective-permute-start(bf16[4,96,384]{2,1,0:T(8,128)(2,1)S(1)} %get-tuple-element.105), channel_id=1, source_target_pairs={{0,4},{1,5},{2,6},{3,7},{4,12},{5,13},{6,14},{7,15},{8,0},{9,1},{1... | collective-permute-start | bytes 884744 | tf_op jit(solution)/shard_map/ppermute | solution.py:593
  46.5 7.6 %copy-start.22 = (bf16[64,2176]{1,0:T(8,128)(2,1)}, bf16[64,2176]{1,0:T(8,128)(2,1)S(1)}, u32[]{:S(2)}) copy-start(bf16[64,2176]{1,0:T(8,128)(2,1)S(1)} %collective-permute-done.7.refs_3_) | copy-start | bytes 835588
  46.5 11.2 %collective-permute-start.8 = (bf16[64,2176]{1,0:T(8,128)(2,1)S(1)}, bf16[64,2176]{1,0:T(8,128)(2,1)S(1)}, u32[]{:S(2)}, u32[]{:S(2)}) collective-permute-start(bf16[64,2176]{1,0:T(8,128)(2,1)S(1)} %slice.43), channel_id=1, source_target_pairs={{0,1},{1,0},{2,3},{3,2},{4,5},{5,4},{6,7},{7,6},{8,9},{9,8},{10,11... | collective-permute-start | bytes 835592 | tf_op jit(solution)/shard_map/ppermute | solution.py:593
  57.7 9.7 %copy-start.23 = (bf16[64,2176]{1,0:T(8,128)(2,1)}, bf16[64,2176]{1,0:T(8,128)(2,1)S(1)}, u32[]{:S(2)}) copy-start(bf16[64,2176]{1,0:T(8,128)(2,1)S(1)} %collective-permute-done.8.refs_4_) | copy-start | bytes 835588
  57.7 17.1 %copy-start.14 = (bf16[128,2176]{1,0:T(8,128)(2,1)}, bf16[128,2176]{1,0:T(8,128)(2,1)S(1)}, u32[]{:S(2)}) copy-start(bf16[128,2176]{1,0:T(8,128)(2,1)S(1)} %collective-permute-done.10.refs_1_) | copy-start | bytes 1671172
  57.7 17.0 %copy-start.15 = (bf16[128,2176]{1,0:T(8,128)(2,1)}, bf16[128,2176]{1,0:T(8,128)(2,1)S(1)}, u32[]{:S(2)}) copy-start(bf16[128,2176]{1,0:T(8,128)(2,1)S(1)} %collective-permute-done.11.refs_2_) | copy-start | bytes 1671172
  57.8 9.7 %collective-permute-start.14 = (bf16[64,2176]{1,0:T(8,128)(2,1)S(1)}, bf16[64,2176]{1,0:T(8,128)(2,1)S(1)}, u32[]{:S(2)}, u32[]{:S(2)}) collective-permute-start(bf16[64,2176]{1,0:T(8,128)(2,1)S(1)} %slice.44), channel_id=1, source_target_pairs={{0,2},{1,3},{2,0},{3,1},{4,6},{5,7},{6,4},{7,5},{8,10},{9,11},{10,... | collective-permute-start | bytes 835592 | tf_op jit(solution)/shard_map/ppermute | solution.py:593
  57.8 17.6 %collective-permute-start.16 = (bf16[128,2176]{1,0:T(8,128)(2,1)}, bf16[128,2176]{1,0:T(8,128)(2,1)S(1)}, u32[]{:S(2)}, u32[]{:S(2)}) collective-permute-start(bf16[128,2176]{1,0:T(8,128)(2,1)} %collective-permute-done.9.refs_0_), channel_id=1, source_target_pairs={{0,1},{1,0},{2,3},{3,2},{4,5},{5,4},{6,7},{7,6},{8,9},{9,8},{10,11... | collective-permute-start | bytes 1671176 | tf_op jit(solution)/shard_map/ppermute | solution.py:593
  58.5 17.0 %collective-permute-start.17 = (bf16[128,2176]{1,0:T(8,128)(2,1)}, bf16[128,2176]{1,0:T(8,128)(2,1)}, u32[]{:S(2)}, u32[]{:S(2)}) collective-permute-start(bf16[128,2176]{1,0:T(8,128)(2,1)} %collective-permute-done.9.refs_0_), channel_id=1, source_target_pairs={{0,2},{1,3},{2,0},{3,1},{4,6},{5,7},{6,4},{7,5},{8,10},{9,11},{10,... | collective-permute-start | bytes 1671176 | tf_op jit(solution)/shard_map/ppermute | solution.py:593
  60.4 15.0 %collective-permute-start.12 = (bf16[4,96,384]{2,1,0:T(8,128)(2,1)}, bf16[4,96,384]{2,1,0:T(8,128)(2,1)S(1)}, u32[]{:S(2)}, u32[]{:S(2)}) collective-permute-start(bf16[4,96,384]{2,1,0:T(8,128)(2,1)} %get-tuple-element.119), channel_id=1, source_target_pairs={{0,12},{1,13},{2,14},{3,15},{4,8},{5,9},{6,10},{7,11},{8,4},{9,5},... | collective-permute-start | bytes 884744 | tf_op jit(solution)/shard_map/ppermute | solution.py:593
  62.2 13.2 %collective-permute-start.13 = (bf16[4,96,384]{2,1,0:T(8,128)(2,1)}, bf16[4,96,384]{2,1,0:T(8,128)(2,1)S(1)}, u32[]{:S(2)}, u32[]{:S(2)}) collective-permute-start(bf16[4,96,384]{2,1,0:T(8,128)(2,1)} %get-tuple-element.120), channel_id=1, source_target_pairs={{0,8},{1,9},{2,10},{3,11},{4,0},{5,1},{6,2},{7,3},{8,12},{9,13},{1... | collective-permute-start | bytes 884744 | tf_op jit(solution)/shard_map/ppermute | solution.py:593
  67.4 7.3 %copy-start.21 = (bf16[64,2176]{1,0:T(8,128)(2,1)}, bf16[64,2176]{1,0:T(8,128)(2,1)S(1)}, u32[]{:S(2)}) copy-start(bf16[64,2176]{1,0:T(8,128)(2,1)S(1)} %collective-permute-done.14.refs_3_) | copy-start | bytes 835588
  67.4 8.0 %collective-permute-start.15 = (bf16[64,2176]{1,0:T(8,128)(2,1)}, bf16[64,2176]{1,0:T(8,128)(2,1)}, u32[]{:S(2)}, u32[]{:S(2)}) collective-permute-start(bf16[64,2176]{1,0:T(8,128)(2,1)} %slice.45), channel_id=1, source_target_pairs={{0,1},{1,0},{2,3},{3,2},{4,5},{5,4},{6,7},{7,6},{8,9},{9,8},{10,11... | collective-permute-start | bytes 835592 | tf_op jit(solution)/shard_map/ppermute | solution.py:593
  68.0 7.6 %slice-start.6 = ((bf16[128,2176]{1,0:T(8,128)(2,1)}), bf16[64,2176]{1,0:T(8,128)(2,1)S(1)}, s32[]{:S(2)}) async-start(bf16[128,2176]{1,0:T(8,128)(2,1)} %copy-done.12), calls=%async_computation.6 | async-start | bytes 557056 | tf_op jit(solution)/shard_map/slice | solution.py:618
  75.6 17.5 %collective-permute-start.19 = (bf16[128,2176]{1,0:T(8,128)(2,1)S(1)}, bf16[128,2176]{1,0:T(8,128)(2,1)S(1)}, u32[]{:S(2)}, u32[]{:S(2)}) collective-permute-start(bf16[128,2176]{1,0:T(8,128)(2,1)S(1)} %pad_maximum_fusion), channel_id=1, source_target_pairs={{0,2},{1,3},{2,0},{3,1},{4,6},{5,7},{6,4},{7,5},{8,10},{9,11},{10,... | collective-permute-start | bytes 1671176 | tf_op jit(solution)/shard_map/ppermute | solution.py:593
  77.1 16.0 %collective-permute-start.20 = (bf16[128,2176]{1,0:T(8,128)(2,1)S(1)}, bf16[128,2176]{1,0:T(8,128)(2,1)S(1)}, u32[]{:S(2)}, u32[]{:S(2)}) collective-permute-start(bf16[128,2176]{1,0:T(8,128)(2,1)S(1)} %pad_maximum_fusion.1), channel_id=1, source_target_pairs={{0,1},{1,0},{2,3},{3,2},{4,5},{5,4},{6,7},{7,6},{8,9},{9,8},{10,11... | collective-permute-start | bytes 1671176 | tf_op jit(solution)/shard_map/ppermute | solution.py:593
  77.8 14.8 %collective-permute-start.18 = (bf16[4,96,384]{2,1,0:T(8,128)(2,1)S(1)}, bf16[4,96,384]{2,1,0:T(8,128)(2,1)S(1)}, u32[]{:S(2)}, u32[]{:S(2)}) collective-permute-start(bf16[4,96,384]{2,1,0:T(8,128)(2,1)S(1)} %copy-done.28), channel_id=1, source_target_pairs={{0,8},{1,9},{2,10},{3,11},{4,0},{5,1},{6,2},{7,3},{8,12},{9,13},{1... | collective-permute-start | bytes 884744 | tf_op jit(solution)/shard_map/ppermute | solution.py:593
  82.7 25.2 %collective-permute-start.23 = (bf16[4,96,384]{2,1,0:T(8,128)(2,1)}, bf16[4,96,384]{2,1,0:T(8,128)(2,1)S(1)}, u32[]{:S(2)}, u32[]{:S(2)}) collective-permute-start(bf16[4,96,384]{2,1,0:T(8,128)(2,1)} %get-tuple-element.152), channel_id=1, source_target_pairs={{0,1},{1,0},{2,3},{3,2},{4,5},{5,4},{6,7},{7,6},{8,9},{9,8},{10,11... | collective-permute-start | bytes 884744 | tf_op jit(solution)/shard_map/ppermute | solution.py:593
  84.4 23.6 %collective-permute-start.24 = (bf16[4,96,384]{2,1,0:T(8,128)(2,1)}, bf16[4,96,384]{2,1,0:T(8,128)(2,1)S(1)}, u32[]{:S(2)}, u32[]{:S(2)}) collective-permute-start(bf16[4,96,384]{2,1,0:T(8,128)(2,1)} %get-tuple-element.153), channel_id=1, source_target_pairs={{0,2},{1,3},{2,0},{3,1},{4,6},{5,7},{6,4},{7,5},{8,10},{9,11},{10,... | collective-permute-start | bytes 884744 | tf_op jit(solution)/shard_map/ppermute | solution.py:593
  92.6 30.3 %copy-start.5 = (bf16[4,96,384]{2,1,0:T(8,128)(2,1)}, bf16[4,96,384]{2,1,0:T(8,128)(2,1)S(1)}, u32[]{:S(2)}) copy-start(bf16[4,96,384]{2,1,0:T(8,128)(2,1)S(1)} %collective-permute-done.18.refs_1_) | copy-start | bytes 884740
  92.6 15.3 %collective-permute-start.25 = (bf16[4,96,384]{2,1,0:T(8,128)(2,1)S(1)}, bf16[4,96,384]{2,1,0:T(8,128)(2,1)S(1)}, u32[]{:S(2)}, u32[]{:S(2)}) collective-permute-start(bf16[4,96,384]{2,1,0:T(8,128)(2,1)S(1)} %get-tuple-element.154), channel_id=1, source_target_pairs={{0,3},{1,2},{2,1},{3,0},{4,7},{5,6},{6,5},{7,4},{8,11},{9,10},{10,... | collective-permute-start | bytes 884744 | tf_op jit(solution)/shard_map/ppermute | solution.py:593
  93.1 2.7 %copy-start.9 = (bf16[128,2176]{1,0:T(8,128)(2,1)}, bf16[128,2176]{1,0:T(8,128)(2,1)S(1)}, u32[]{:S(2)}) copy-start(bf16[128,2176]{1,0:T(8,128)(2,1)S(1)} %collective-permute-done.19.refs_3_.refs_8_) | copy-start | bytes 1671172
  93.1 2.7 %copy-start.10 = (bf16[128,2176]{1,0:T(8,128)(2,1)}, bf16[128,2176]{1,0:T(8,128)(2,1)S(1)}, u32[]{:S(2)}) copy-start(bf16[128,2176]{1,0:T(8,128)(2,1)S(1)} %collective-permute-done.20.refs_4_.refs_9_) | copy-start | bytes 1671172
  93.1 24.7 %collective-permute-start.21 = (bf16[4,96,384]{2,1,0:T(8,128)(2,1)}, bf16[4,96,384]{2,1,0:T(8,128)(2,1)S(1)}, u32[]{:S(2)}, u32[]{:S(2)}) collective-permute-start(bf16[4,96,384]{2,1,0:T(8,128)(2,1)} %get-tuple-element.146), channel_id=1, source_target_pairs={{0,12},{1,13},{2,14},{3,15},{4,8},{5,9},{6,10},{7,11},{8,4},{9,5},... | collective-permute-start | bytes 884744 | tf_op jit(solution)/shard_map/ppermute | solution.py:593
  106.5 11.4 %collective-permute-start.22 = (bf16[4,96,384]{2,1,0:T(8,128)(2,1)}, bf16[4,96,384]{2,1,0:T(8,128)(2,1)S(1)}, u32[]{:S(2)}, u32[]{:S(2)}) collective-permute-start(bf16[4,96,384]{2,1,0:T(8,128)(2,1)} %get-tuple-element.147), channel_id=1, source_target_pairs={{0,4},{1,5},{2,6},{3,7},{4,12},{5,13},{6,14},{7,15},{8,0},{9,1},{1... | collective-permute-start | bytes 884744 | tf_op jit(solution)/shard_map/ppermute | solution.py:593
  107.9 2.5 %copy-start.1 = (bf16[384,2048]{1,0:T(8,128)(2,1)S(1)}, bf16[384,2048]{1,0:T(8,128)(2,1)}, u32[]{:S(2)}) copy-start(bf16[384,2048]{1,0:T(8,128)(2,1)} %get-tuple-element.158.refs_1_) | copy-start | bytes 4718596
  107.9 2.5 %copy-start.2 = (bf16[384,2048]{1,0:T(8,128)(2,1)S(1)}, bf16[384,2048]{1,0:T(8,128)(2,1)}, u32[]{:S(2)}) copy-start(bf16[384,2048]{1,0:T(8,128)(2,1)} %get-tuple-element.159.refs_2_) | copy-start | bytes 4718596
  107.9 21.5 %slice-start.2 = ((s8[6291456]{0:T(1024)(128)(4,1)}), s8[4194304]{0:T(1024)(128)(4,1)S(1)}, s32[]{:S(2)}) async-start(s8[6291456]{0:T(1024)(128)(4,1)} %bitcast.68), calls=%async_computation.2 | async-start | bytes 8388608
  113.3 16.2 %slice-start = ((s8[6291456]{0:T(1024)(128)(4,1)}), s8[4194304]{0:T(1024)(128)(4,1)S(1)}, s32[]{:S(2)}) async-start(s8[6291456]{0:T(1024)(128)(4,1)} %bitcast.64), calls=%async_computation | async-start | bytes 8388608
  113.3 16.2 %slice-start.3 = ((s8[6291456]{0:T(1024)(128)(4,1)}), s8[2097152]{0:T(1024)(128)(4,1)S(1)}, s32[]{:S(2)}) async-start(s8[6291456]{0:T(1024)(128)(4,1)} %bitcast.68), calls=%async_computation.3 | async-start | bytes 4194304
  117.8 6.5 %collective-permute-start.26 = (bf16[2,192,2048]{2,1,0:T(8,128)(2,1)S(1)}, bf16[2,192,2048]{2,1,0:T(8,128)(2,1)S(1)}, u32[]{:S(2)}, u32[]{:S(2)}) collective-permute-start(bf16[2,192,2048]{2,1,0:T(8,128)(2,1)S(1)} %get-tuple-element.156), channel_id=1, source_target_pairs={{0,16},{16,0},{1,17},{17,1},{2,18},{18,2},{3,19},{19,3},{4,20},{20... | collective-permute-start | bytes 4718600 | tf_op jit(solution)/shard_map/ppermute | solution.py:695
  117.8 5.1 %copy-start.6 = (bf16[4,96,384]{2,1,0:T(8,128)(2,1)}, bf16[4,96,384]{2,1,0:T(8,128)(2,1)S(1)}, u32[]{:S(2)}) copy-start(bf16[4,96,384]{2,1,0:T(8,128)(2,1)S(1)} %collective-permute-done.21.refs_2_) | copy-start | bytes 884740
  117.9 5.1 %copy-start.8 = (bf16[4,96,384]{2,1,0:T(8,128)(2,1)}, bf16[4,96,384]{2,1,0:T(8,128)(2,1)S(1)}, u32[]{:S(2)}) copy-start(bf16[4,96,384]{2,1,0:T(8,128)(2,1)S(1)} %collective-permute-done.22.refs_3_) | copy-start | bytes 884740
  117.9 5.1 %copy-start.7 = (bf16[4,96,384]{2,1,0:T(8,128)(2,1)S(1)}, bf16[4,96,384]{2,1,0:T(8,128)(2,1)}, u32[]{:S(2)}) copy-start(bf16[4,96,384]{2,1,0:T(8,128)(2,1)} %get-tuple-element.148.refs_0_) | copy-start | bytes 884740
  117.9 11.6 %slice-start.1 = ((s8[6291456]{0:T(1024)(128)(4,1)}), s8[2097152]{0:T(1024)(128)(4,1)S(1)}, s32[]{:S(2)}) async-start(s8[6291456]{0:T(1024)(128)(4,1)} %bitcast.64), calls=%async_computation.1 | async-start | bytes 4194304
  122.4 3.6 %collective-permute-start.27 = (bf16[2,192,2048]{2,1,0:T(8,128)(2,1)S(1)}, bf16[2,192,2048]{2,1,0:T(8,128)(2,1)S(1)}, u32[]{:S(2)}, u32[]{:S(2)}) collective-permute-start(bf16[2,192,2048]{2,1,0:T(8,128)(2,1)S(1)} %get-tuple-element.162), channel_id=1, source_target_pairs={{0,16},{16,0},{1,17},{17,1},{2,18},{18,2},{3,19},{19,3},{4,20},{20... | collective-permute-start | bytes 4718600 | tf_op jit(solution)/shard_map/ppermute | solution.py:695
  126.0 16.0 %collective-permute-start.28 = (bf16[4,96,384]{2,1,0:T(8,128)(2,1)S(1)}, bf16[4,96,384]{2,1,0:T(8,128)(2,1)S(1)}, u32[]{:S(2)}, u32[]{:S(2)}) collective-permute-start(bf16[4,96,384]{2,1,0:T(8,128)(2,1)S(1)} %get-tuple-element.170), channel_id=1, source_target_pairs={{0,1},{1,0},{2,3},{3,2},{4,5},{5,4},{6,7},{7,6},{8,9},{9,8},{10,11... | collective-permute-start | bytes 884744 | tf_op jit(solution)/shard_map/ppermute | solution.py:593
  126.5 15.5 %collective-permute-start.29 = (bf16[4,96,384]{2,1,0:T(8,128)(2,1)S(1)}, bf16[4,96,384]{2,1,0:T(8,128)(2,1)S(1)}, u32[]{:S(2)}, u32[]{:S(2)}) collective-permute-start(bf16[4,96,384]{2,1,0:T(8,128)(2,1)S(1)} %get-tuple-element.171), channel_id=1, source_target_pairs={{0,2},{1,3},{2,0},{3,1},{4,6},{5,7},{6,4},{7,5},{8,10},{9,11},{10,... | collective-permute-start | bytes 884744 | tf_op jit(solution)/shard_map/ppermute | solution.py:593
  128.0 14.5 %collective-permute-start.30 = (bf16[4,96,384]{2,1,0:T(8,128)(2,1)S(1)}, bf16[4,96,384]{2,1,0:T(8,128)(2,1)S(1)}, u32[]{:S(2)}, u32[]{:S(2)}) collective-permute-start(bf16[4,96,384]{2,1,0:T(8,128)(2,1)S(1)} %get-tuple-element.172), channel_id=1, source_target_pairs={{0,3},{1,2},{2,1},{3,0},{4,7},{5,6},{6,5},{7,4},{8,11},{9,10},{10,... | collective-permute-start | bytes 884744 | tf_op jit(solution)/shard_map/ppermute | solution.py:593
  129.5 2.8 %copy-start = (f32[192,4,2048]{2,1,0:T(4,128)S(1)}, f32[192,4,2048]{2,1,0:T(4,128)}, u32[]{:S(2)}) copy-start(f32[192,4,2048]{2,1,0:T(4,128)} %param.15) | copy-start | bytes 18874372
  142.0 3.1 %copy-start.25 = (bf16[4,96,384]{2,1,0:T(8,128)(2,1)}, bf16[4,96,384]{2,1,0:T(8,128)(2,1)S(1)}, u32[]{:S(2)}) copy-start(bf16[4,96,384]{2,1,0:T(8,128)(2,1)S(1)} %collective-permute-done.28.refs_4_) | copy-start | bytes 884740
  142.0 3.1 %copy-start.26 = (bf16[4,96,384]{2,1,0:T(8,128)(2,1)}, bf16[4,96,384]{2,1,0:T(8,128)(2,1)S(1)}, u32[]{:S(2)}) copy-start(bf16[4,96,384]{2,1,0:T(8,128)(2,1)S(1)} %collective-permute-done.29.refs_5_) | copy-start | bytes 884740
  142.5 2.6 %copy-start.27 = (bf16[4,96,384]{2,1,0:T(8,128)(2,1)}, bf16[4,96,384]{2,1,0:T(8,128)(2,1)S(1)}, u32[]{:S(2)}) copy-start(bf16[4,96,384]{2,1,0:T(8,128)(2,1)S(1)} %collective-permute-done.30.refs_6_) | copy-start | bytes 884740
  145.1 6.8 %collective-permute-start.31 = (bf16[12288,128]{1,0:T(8,128)(2,1)}, bf16[12288,128]{1,0:T(8,128)(2,1)S(1)}, u32[]{:S(2)}, u32[]{:S(2)}) collective-permute-start(bf16[12288,128]{1,0:T(8,128)(2,1)} %get-tuple-element.190), channel_id=1, source_target_pairs={{0,16},{16,0},{1,17},{17,1},{2,18},{18,2},{3,19},{19,3},{4,20},{20... | collective-permute-start | bytes 9437192 | tf_op jit(solution)/shard_map/ppermute | solution.py:713
  (5 other events, 9.0 us)

commit v10 on v8

--- a/solution.py
+++ b/solution.py
@@ -107,7 +107,7 @@
     earlier = jnp.where(earlier, 1.0, 0.0).astype(jnp.bfloat16)
     stores = []
     for j in range(chunks):
-        rows, grads = all_rows.at[j], all_grads.at[j]
+        rows = all_rows.at[j]
         d_rows = outs[2 * j] if keep else all_d_rows[0].at[j]
         for load in loads[j]:
             load.wait()
@@ -141,21 +141,28 @@
         if not keep:
             stores.append(pltpu.make_async_copy(d_rows, outs[2 * j], sems.at[j, 5]))
             stores[-1].start()
-        count = 4 * CAP
-        found = []
-        for e in range(experts):
-            if j == 0:
-                weight_loads[e].wait()
-            found.append(
-                lax.dot_general(
-                    d_rows[e * count : (e + 1) * count, :],
-                    weights[e],
-                    (((1,), (1,)), ((), ())),
-                    preferred_element_type=jnp.float32,
-                )
+
+    count = 4 * CAP
+    found = []
+    for e in range(experts):
+        weight_loads[e].wait()
+        mine = [
+            (outs[2 * j] if keep else all_d_rows[0].at[j])[e * count : (e + 1) * count, :]
+            for j in range(chunks)
+        ]
+        found.append(
+            lax.dot_general(
+                mine[0] if chunks == 1 else jnp.concatenate(mine, axis=0),
+                weights[e],
+                (((1,), (1,)), ((), ())),
+                preferred_element_type=jnp.float32,
             )
+        )
+    for j in range(chunks):
+        grads = all_grads.at[j]
         for c in range(4):
-            mine = [f[c * CAP : (c + 1) * CAP] for f in found]
+            at = j * count + c * CAP
+            mine = [f[at : at + CAP] for f in found]
             grads[c] = jnp.concatenate(mine, axis=0).astype(jnp.bfloat16)
         stores.append(pltpu.make_async_copy(grads, outs[2 * j + 1], sems.at[j, 6]))
         stores[-1].start()

time: 154 us -> 152 us (0.987)
  Pallas kernels: 59.8 us -> 57.7 us
    pallas_call x3, Pallas kernels: 23.3 us -> 21.3 us  [chunk_grads(): pl.pallas_call(functools.partial(grads_kernel, spans, keep), out_shape=[j...]
where the time goes in v10:
time: 152 us
  Pallas kernels  57.7 us (38%)
  starting transfers between devices  38.8 us (26%)
  waiting for transfers between devices  31.2 us (21%)
  local copies, waits for them, and re-layouts  16.5 us (11%)
  matrix products  3.51 us (2%)
  other arithmetic  2.7 us (2%)
    ppermute x29, starting transfers between devices, move(): return lax.ppermute(block, 'inner', step_perm(size, steps, flip))  38.1 us
    ppermute x29, waiting for transfers between devices, move(): return lax.ppermute(block, 'inner', step_perm(size, steps, flip))  29.5 us
    pallas_call x3, Pallas kernels, chunk_grads(): pl.pallas_call(functools.partial(grads_kernel, spans, keep), out_shape=[j...  21.3 us
    unnamed x73, local copies, waits for them, and re-layouts  12.8 us
    pallas_call x2, Pallas kernels, adam_rows(): pl.pallas_call(functools.partial(adam_kernel, count, owners, kept, first)...  12.3 us
    pallas_call x2, Pallas kernels, partial_rows(): pl.pallas_call(functools.partial(partial_kernel, start, total), out_shape...  8.96 us
    pallas_call x1, Pallas kernels, finish(): pl.pallas_call(functools.partial(finish_kernel, pieces), out_shape=(jax.S...  6.75 us
    pallas_call x2, Pallas kernels, regroup(): pl.pallas_call(regroup_kernel, out_shape=[jax.ShapeDtypeStruct((count, sl...  3.29 us
  transfers between devices with their start and end apart: 32, of which 12 were waited for; matrix products, arithmetic and copies ran while one was open for 10% of the time, Pallas kernels for 35%

profile of v10, /device:TPU:0, one launch (start us, length us, event | category | flops | bytes accessed | tf_op | source)
XLA Modules:
  0.0 151.8 jit_solution(5125928539082319664)
XLA Ops:
  0.6 0.7 convert_element_type.46
  1.5 1.1 fusion.9.refs_5_
  2.6 3.1 %collective-permute-start = (bf16[128,2176]{1,0:T(8,128)(2,1)S(1)}, bf16[128,2176]{1,0:T(8,128)(2,1)S(1)}, u32[]{:S(2)}, u32[]{:S(2)}) collective-permute-start(bf16[128,2176]{1,0:T(8,128)(2,1)S(1)} %fusion.9.refs_5_), channel_id=1, source_target_pairs={{0,4},{1,5},{2,6},{3,7},{4,12},{5,13},{6,14},{7,15},{8,0},{9,1},{1... | collective-permute-start | bytes 1671176 | tf_op jit(solution)/shard_map/ppermute | solution.py:596
  5.6 1.5 collective-permute-start.1
  7.1 1.5 %collective-permute-start.2 = (bf16[128,2176]{1,0:T(8,128)(2,1)S(1)}, bf16[128,2176]{1,0:T(8,128)(2,1)S(1)}, u32[]{:S(2)}, u32[]{:S(2)}) collective-permute-start(bf16[128,2176]{1,0:T(8,128)(2,1)S(1)} %fusion.9.refs_5_), channel_id=1, source_target_pairs={{0,2},{1,3},{2,0},{3,1},{4,6},{5,7},{6,4},{7,5},{8,10},{9,11},{10,... | collective-permute-start | bytes 1671176 | tf_op jit(solution)/shard_map/ppermute | solution.py:596
  8.7 0.8 copy.47
  10.2 0.6 fusion.27.target
  11.0 0.7 reshape.249.probs
  11.7 3.2 %fusion.2 = bf16[1536,384]{1,0:T(8,128)(2,1)S(1)} fusion(s32[1024]{0:T(1024)S(1)} %fusion.41, bf16[128,8,384]{2,1,0:T(8,128)(2,1)} %param.9, f32[128,8]{1,0:T(8,128)S(1)} %copy.49), kind=kOutput, calls=%fused_computation.4 | convolution fusion | flops 1211301888 | bytes 1974272 | tf_op jit(solution)/shard_map/dot_general | solution.py:588
  14.9 4.4 %collective-permute-done.refs_0_ = bf16[128,2176]{1,0:T(8,128)(2,1)S(1)} collective-permute-done((bf16[128,2176]{1,0:T(8,128)(2,1)S(1)}, bf16[128,2176]{1,0:T(8,128)(2,1)S(1)}, u32[]{:S(2)}, u32[]{:S(2)}) %collective-permute-start) | collective-permute-done | bytes 557088 | tf_op jit(solution)/shard_map/ppermute | solution.py:596
  19.7 1.2 collective-permute-done.2.refs_7_
  20.9 2.6 %collective-permute-start.3 = (bf16[128,2176]{1,0:T(8,128)(2,1)S(1)}, bf16[128,2176]{1,0:T(8,128)(2,1)S(1)}, u32[]{:S(2)}, u32[]{:S(2)}) collective-permute-start(bf16[128,2176]{1,0:T(8,128)(2,1)S(1)} %collective-permute-done.refs_0_), channel_id=1, source_target_pairs={{0,4},{1,5},{2,6},{3,7},{4,12},{5,13},{6,14},{7,15},{8,0},{9,1},{1... | collective-permute-start | bytes 1671176 | tf_op jit(solution)/shard_map/ppermute | solution.py:596
  23.5 0.5 collective-permute-start.4
  24.1 1.5 %collective-permute-start.5 = (bf16[128,2176]{1,0:T(8,128)(2,1)S(1)}, bf16[128,2176]{1,0:T(8,128)(2,1)S(1)}, u32[]{:S(2)}, u32[]{:S(2)}) collective-permute-start(bf16[128,2176]{1,0:T(8,128)(2,1)S(1)} %collective-permute-done.refs_0_), channel_id=1, source_target_pairs={{0,2},{1,3},{2,0},{3,1},{4,6},{5,7},{6,4},{7,5},{8,10},{9,11},{10,... | collective-permute-start | bytes 1671176 | tf_op jit(solution)/shard_map/ppermute | solution.py:596
  25.6 1.0 slice_bitcast_fusion
  26.6 8.2 %collective-permute-done.3.refs_0_ = bf16[128,2176]{1,0:T(8,128)(2,1)S(1)} collective-permute-done((bf16[128,2176]{1,0:T(8,128)(2,1)S(1)}, bf16[128,2176]{1,0:T(8,128)(2,1)S(1)}, u32[]{:S(2)}, u32[]{:S(2)}) %collective-permute-start.3) | collective-permute-done | bytes 557088 | tf_op jit(solution)/shard_map/ppermute | solution.py:596
  34.7 1.4 collective-permute-done.4.refs_1_
  36.1 0.6 collective-permute-done.5.refs_2_
  36.8 1.6 %collective-permute-start.7 = (bf16[64,2176]{1,0:T(8,128)(2,1)S(1)}, bf16[64,2176]{1,0:T(8,128)(2,1)S(1)}, u32[]{:S(2)}, u32[]{:S(2)}) collective-permute-start(bf16[64,2176]{1,0:T(8,128)(2,1)S(1)} %slice.42), channel_id=1, source_target_pairs={{0,2},{1,3},{2,0},{3,1},{4,6},{5,7},{6,4},{7,5},{8,10},{9,11},{10,... | collective-permute-start | bytes 835592 | tf_op jit(solution)/shard_map/ppermute | solution.py:596
  38.4 1.2 collective-permute-start.9
  39.6 0.5 collective-permute-start.10
  40.1 0.5 collective-permute-start.11
  40.7 1.0 collective-permute-start.6
  41.6 4.8 %collective-permute-done.7.refs_3_ = bf16[64,2176]{1,0:T(8,128)(2,1)S(1)} collective-permute-done((bf16[64,2176]{1,0:T(8,128)(2,1)S(1)}, bf16[64,2176]{1,0:T(8,128)(2,1)S(1)}, u32[]{:S(2)}, u32[]{:S(2)}) %collective-permute-start.7) | collective-permute-done | bytes 278560 | tf_op jit(solution)/shard_map/ppermute | solution.py:596
  46.5 1.4 collective-permute-start.8
  47.9 6.2 %copy.63 = bf16[384,4,2048]{2,0,1:T(8,128)(2,1)} copy(bf16[384,4,2048]{2,1,0:T(4,128)(2,1)S(1)} %bitcast.79) | data formatting | bytes 12582912 | tf_op args[4]
  54.1 3.6 %collective-permute-done.8.refs_4_ = bf16[64,2176]{1,0:T(8,128)(2,1)S(1)} collective-permute-done((bf16[64,2176]{1,0:T(8,128)(2,1)S(1)}, bf16[64,2176]{1,0:T(8,128)(2,1)S(1)}, u32[]{:S(2)}, u32[]{:S(2)}) %collective-permute-start.8) | collective-permute-done | bytes 278560 | tf_op jit(solution)/shard_map/ppermute | solution.py:596
  57.8 0.6 collective-permute-start.16
  58.5 1.9 %collective-permute-start.17 = (bf16[128,2176]{1,0:T(8,128)(2,1)}, bf16[128,2176]{1,0:T(8,128)(2,1)}, u32[]{:S(2)}, u32[]{:S(2)}) collective-permute-start(bf16[128,2176]{1,0:T(8,128)(2,1)} %collective-permute-done.9.refs_0_), channel_id=1, source_target_pairs={{0,2},{1,3},{2,0},{3,1},{4,6},{5,7},{6,4},{7,5},{8,10},{9,11},{10,... | collective-permute-start | bytes 1671176 | tf_op jit(solution)/shard_map/ppermute | solution.py:596
  60.4 1.8 %collective-permute-start.12 = (bf16[4,96,384]{2,1,0:T(8,128)(2,1)}, bf16[4,96,384]{2,1,0:T(8,128)(2,1)S(1)}, u32[]{:S(2)}, u32[]{:S(2)}) collective-permute-start(bf16[4,96,384]{2,1,0:T(8,128)(2,1)} %get-tuple-element.119), channel_id=1, source_target_pairs={{0,12},{1,13},{2,14},{3,15},{4,8},{5,9},{6,10},{7,11},{8,4},{9,5},... | collective-permute-start | bytes 884744 | tf_op jit(solution)/shard_map/ppermute | solution.py:596
  62.2 0.8 collective-permute-start.13
  63.0 0.7 slice.45
  63.8 3.7 %collective-permute-done.14.refs_3_ = bf16[64,2176]{1,0:T(8,128)(2,1)S(1)} collective-permute-done((bf16[64,2176]{1,0:T(8,128)(2,1)S(1)}, bf16[64,2176]{1,0:T(8,128)(2,1)S(1)}, u32[]{:S(2)}, u32[]{:S(2)}) %collective-permute-start.14) | collective-permute-done | bytes 278560 | tf_op jit(solution)/shard_map/ppermute | solution.py:596
  67.4 0.5 collective-permute-start.15
  68.0 6.8 %shard_map.127 = (bf16[384,2048]{1,0:T(8,128)(2,1)}, bf16[4,96,384]{2,1,0:T(8,128)(2,1)}) custom-call(s32[1]{0:T(128)} %bitcast.5.first, bf16[128,2176]{1,0:T(8,128)(2,1)} %copy-done.19, bf16[128,2176]{1,0:T(8,128)(2,1)} %copy-done.17, bf16[128,2176]{1,0:T(8,128)(2,1)} %copy-done.18, bf16[64,2176]{1,0:T(8,128)(2,1)} %copy-done.22, ...), custom_call_target="tpu_custom_call" | custom-call | flops 1409286144 | bytes 3670016 | tf_op jit(solution)/shard_map/pallas_call | solution.py:179
  74.8 0.6 collective-permute-done.15.refs_4_
  75.6 0.5 collective-permute-start.19
  76.0 1.0 slice.47
  77.1 0.7 collective-permute-start.20
  77.8 3.0 %collective-permute-start.18 = (bf16[4,96,384]{2,1,0:T(8,128)(2,1)S(1)}, bf16[4,96,384]{2,1,0:T(8,128)(2,1)S(1)}, u32[]{:S(2)}, u32[]{:S(2)}) collective-permute-start(bf16[4,96,384]{2,1,0:T(8,128)(2,1)S(1)} %copy-done.28), channel_id=1, source_target_pairs={{0,8},{1,9},{2,10},{3,11},{4,0},{5,1},{6,2},{7,3},{8,12},{9,13},{1... | collective-permute-start | bytes 884744 | tf_op jit(solution)/shard_map/ppermute | solution.py:596
  80.7 2.0 %shard_map.130 = (bf16[4,96,384]{2,1,0:T(8,128)(2,1)}, bf16[4,96,384]{2,1,0:T(8,128)(2,1)}, bf16[4,96,384]{2,1,0:T(8,128)(2,1)S(1)}) custom-call(bf16[4,96,384]{2,1,0:T(8,128)(2,1)S(1)} %get-tuple-element.132.refs_0_, bf16[4,96,384]{2,1,0:T(8,128)(2,1)S(1)} %collective-permute-done.6.refs_1_, bf16[4,96,384]{2,1,0:T(8,128)(2,1)S(1)} %collective-permute-done.12.refs_2_, ...), custom_call_target="tpu_custom_call" | custom-call | bytes 1769472 | tf_op jit(solution)/shard_map/pallas_call | solution.py:274
  82.7 1.6 %collective-permute-start.23 = (bf16[4,96,384]{2,1,0:T(8,128)(2,1)}, bf16[4,96,384]{2,1,0:T(8,128)(2,1)S(1)}, u32[]{:S(2)}, u32[]{:S(2)}) collective-permute-start(bf16[4,96,384]{2,1,0:T(8,128)(2,1)} %get-tuple-element.152), channel_id=1, source_target_pairs={{0,1},{1,0},{2,3},{3,2},{4,5},{5,4},{6,7},{7,6},{8,9},{9,8},{10,11... | collective-permute-start | bytes 884744 | tf_op jit(solution)/shard_map/ppermute | solution.py:596
  84.4 1.5 %collective-permute-start.24 = (bf16[4,96,384]{2,1,0:T(8,128)(2,1)}, bf16[4,96,384]{2,1,0:T(8,128)(2,1)S(1)}, u32[]{:S(2)}, u32[]{:S(2)}) collective-permute-start(bf16[4,96,384]{2,1,0:T(8,128)(2,1)} %get-tuple-element.153), channel_id=1, source_target_pairs={{0,2},{1,3},{2,0},{3,1},{4,6},{5,7},{6,4},{7,5},{8,10},{9,11},{10,... | collective-permute-start | bytes 884744 | tf_op jit(solution)/shard_map/ppermute | solution.py:596
  85.9 6.7 %shard_map.128 = (bf16[384,2048]{1,0:T(8,128)(2,1)}, bf16[4,96,384]{2,1,0:T(8,128)(2,1)}) custom-call(s32[1]{0:T(128)} %bitcast.5.first, bf16[128,2176]{1,0:T(8,128)(2,1)} %copy-done.20, bf16[128,2176]{1,0:T(8,128)(2,1)} %copy-done.14, bf16[128,2176]{1,0:T(8,128)(2,1)} %copy-done.15, bf16[64,2176]{1,0:T(8,128)(2,1)} %copy-done.21, ...), custom_call_target="tpu_custom_call" | custom-call | flops 1409286144 | bytes 3670016 | tf_op jit(solution)/shard_map/pallas_call | solution.py:179
  93.1 2.7 %collective-permute-start.21 = (bf16[4,96,384]{2,1,0:T(8,128)(2,1)}, bf16[4,96,384]{2,1,0:T(8,128)(2,1)S(1)}, u32[]{:S(2)}, u32[]{:S(2)}) collective-permute-start(bf16[4,96,384]{2,1,0:T(8,128)(2,1)} %get-tuple-element.146), channel_id=1, source_target_pairs={{0,12},{1,13},{2,14},{3,15},{4,8},{5,9},{6,10},{7,11},{8,4},{9,5},... | collective-permute-start | bytes 884744 | tf_op jit(solution)/shard_map/ppermute | solution.py:596
  95.8 7.8 %shard_map.129 = (bf16[384,2048]{1,0:T(8,128)(2,1)}, bf16[4,96,384]{2,1,0:T(8,128)(2,1)}, bf16[384,2048]{1,0:T(8,128)(2,1)}, bf16[4,96,384]{2,1,0:T(8,128)(2,1)}) custom-call(s32[1]{0:T(128)} %bitcast.5.first, bf16[128,2176]{1,0:T(8,128)(2,1)} %collective-permute-done.9.refs_0_, bf16[128,2176]{1,0:T(8,128)(2,1)} %copy-done.16, ...), custom_call_target="tpu_custom_call" | custom-call | flops 2818572288 | bytes 7340032 | tf_op jit(solution)/shard_map/pallas_call | solution.py:179
  103.6 1.4 collective-permute-start.22
  105.0 2.5 %shard_map.131.weighted = bf16[4,384,384]{2,1,0:T(8,128)(2,1)S(1)} custom-call(bf16[4,96,384]{2,1,0:T(8,128)(2,1)S(1)} %get-tuple-element.132.refs_0_, bf16[4,96,384]{2,1,0:T(8,128)(2,1)S(1)} %collective-permute-done.6.refs_1_, bf16[4,96,384]{2,1,0:T(8,128)(2,1)S(1)} %collective-permute-done.12.refs_2_, ...), custom_call_target="tpu_custom_call" | custom-call | bytes 4718592 | tf_op jit(solution)/shard_map/pallas_call | solution.py:232
  107.6 1.4 copy-done.3
  109.0 1.4 copy-done.4
  110.4 4.5 %shard_map.132 = (bf16[2,192,2048]{2,1,0:T(8,128)(2,1)S(1)}, bf16[2,192,2048]{2,1,0:T(8,128)(2,1)S(1)}) custom-call(s32[2]{0:T(128)S(1)} %and_select_fusion.owners, bf16[4,384,384]{2,1,0:T(8,128)(2,1)S(1)} %shard_map.131.weighted, bf16[384,2048]{1,0:T(8,128)(2,1)S(1)} %copy-done.4, bf16[384,2048]{1,0:T(8,128)(2,1)S(1)} %copy-done.1, ...), custom_call_target="tpu_custom_call" | custom-call | flops 1207959552 | bytes 6291456 | tf_op jit(solution)/shard_map/pallas_call | solution.py:339
  115.0 4.5 %shard_map.133 = (bf16[2,192,2048]{2,1,0:T(8,128)(2,1)S(1)}, bf16[2,192,2048]{2,1,0:T(8,128)(2,1)S(1)}) custom-call(s32[2]{0:T(128)S(1)} %and_select_fusion.owners, bf16[4,384,384]{2,1,0:T(8,128)(2,1)S(1)} %shard_map.131.weighted, bf16[384,2048]{1,0:T(8,128)(2,1)S(1)} %copy-done.4, bf16[384,2048]{1,0:T(8,128)(2,1)S(1)} %copy-done.1, ...), custom_call_target="tpu_custom_call" | custom-call | flops 1207959552 | bytes 6291456 | tf_op jit(solution)/shard_map/pallas_call | solution.py:339
  119.5 0.5 collective-permute-start.27
  120.0 1.3 shard_map.134
  121.4 1.7 %collective-permute-done.27.refs_3_ = bf16[2,192,2048]{2,1,0:T(8,128)(2,1)S(1)} collective-permute-done((bf16[2,192,2048]{2,1,0:T(8,128)(2,1)S(1)}, bf16[2,192,2048]{2,1,0:T(8,128)(2,1)S(1)}, u32[]{:S(2)}, u32[]{:S(2)}) %collective-permute-start.27) | collective-permute-done | bytes 1572896 | tf_op jit(solution)/shard_map/ppermute | solution.py:698
  123.1 0.5 collective-permute-start.28
  123.6 1.5 %collective-permute-start.29 = (bf16[4,96,384]{2,1,0:T(8,128)(2,1)S(1)}, bf16[4,96,384]{2,1,0:T(8,128)(2,1)S(1)}, u32[]{:S(2)}, u32[]{:S(2)}) collective-permute-start(bf16[4,96,384]{2,1,0:T(8,128)(2,1)S(1)} %get-tuple-element.171), channel_id=1, source_target_pairs={{0,2},{1,3},{2,0},{3,1},{4,6},{5,7},{6,4},{7,5},{8,10},{9,11},{10,... | collective-permute-start | bytes 884744 | tf_op jit(solution)/shard_map/ppermute | solution.py:596
  125.1 1.5 collective-permute-start.30
  126.6 2.8 %copy-done = f32[192,4,2048]{2,1,0:T(4,128)S(1)} copy-done((f32[192,4,2048]{2,1,0:T(4,128)S(1)}, f32[192,4,2048]{2,1,0:T(4,128)}, u32[]{:S(2)}) %copy-start) | copy-done | bytes 6291480
  129.4 9.7 %shard_map.136 = (f32[12288,128]{1,0:T(8,128)}, f32[12288,128]{1,0:T(8,128)}, f32[12288,128]{1,0:T(8,128)}, bf16[24576,128]{1,0:T(8,128)(2,1)}, bf16[12288,128]{1,0:T(8,128)(2,1)}) custom-call(s32[1]{0:T(128)} %bitcast.13.at, bf16[2,192,2048]{2,1,0:T(8,128)(2,1)S(1)} %get-tuple-element.178.refs_0_, ...), custom_call_target="tpu_custom_call" | custom-call | bytes 65536 | tf_op jit(solution)/shard_map/pallas_call | solution.py:423
  139.1 0.5 collective-permute-done.30.refs_6_
  139.6 2.6 %shard_map.137 = (f32[12288,128]{1,0:T(8,128)}, f32[12288,128]{1,0:T(8,128)}, f32[12288,128]{1,0:T(8,128)}, bf16[24576,128]{1,0:T(8,128)(2,1)}, bf16[12288,128]{1,0:T(8,128)(2,1)}) custom-call(s32[1]{0:T(128)} %bitcast.13.at, ...), custom_call_target="tpu_custom_call", output_to_operand_aliasing={{0}: (8, {}), {1}: (9, {}), {2}: (10, {}), {3}: (11, {}), {... | custom-call | bytes 65536 | tf_op jit(solution)/shard_map/pallas_call | solution.py:423
  142.3 6.7 %shard_map.135 = (bf16[1024,384]{1,0:T(8,128)(2,1)}, f32[8,128]{1,0:T(8,128)}) custom-call(f32[8,128]{1,0:T(8,128)} %fusion.27.target, f32[8,128]{1,0:T(8,128)} %reshape.249.probs, bf16[1024,384]{1,0:T(8,128)(2,1)} %bitcast.84, bf16[4,96,384]{2,1,0:T(8,128)(2,1)} %get-tuple-element.148.refs_0_, bf16[4,96,384]{2,1,0:T(8,128)(2,1)} %copy-done.5, ...), custom_call_target="tpu_custom_call" | custom-call | flops 1207959552 | bytes 3145728 | tf_op jit(solution)/shard_map/pallas_call | solution.py:530
  149.1 2.7 %shard_map.138 = bf16[24576,128]{1,0:T(8,128)(2,1)} custom-call(s32[1]{0:T(128)} %bitcast.38.at, bf16[12288,128]{1,0:T(8,128)(2,1)S(1)} %collective-permute-done.31.got, bf16[24576,128]{1,0:T(8,128)(2,1)} %get-tuple-element.191.full), custom_call_target="tpu_custom_call", output_to_operand_aliasing={{}: (2, {})} | custom-call | bytes 6291456 | tf_op jit(solution)/shard_map/pallas_call | solution.py:451
  (114 shorter events, 2.4 us)
Async XLA Ops:
  0.6 10.3 %copy-start.24 = (f32[128,8]{0,1:T(8,128)S(1)}, f32[128,8]{0,1:T(8,128)}, u32[]{:S(2)}) copy-start(f32[128,8]{0,1:T(8,128)} %param.10) | copy-start | bytes 12292
  2.6 12.4 %copy-start.11 = (bf16[128,2176]{1,0:T(8,128)(2,1)}, bf16[128,2176]{1,0:T(8,128)(2,1)S(1)}, u32[]{:S(2)}) copy-start(bf16[128,2176]{1,0:T(8,128)(2,1)S(1)} %fusion.9.refs_5_) | copy-start | bytes 1671172
  2.6 16.7 %collective-permute-start = (bf16[128,2176]{1,0:T(8,128)(2,1)S(1)}, bf16[128,2176]{1,0:T(8,128)(2,1)S(1)}, u32[]{:S(2)}, u32[]{:S(2)}) collective-permute-start(bf16[128,2176]{1,0:T(8,128)(2,1)S(1)} %fusion.9.refs_5_), channel_id=1, source_target_pairs={{0,4},{1,5},{2,6},{3,7},{4,12},{5,13},{6,14},{7,15},{8,0},{9,1},{1... | collective-permute-start | bytes 1671176 | tf_op jit(solution)/shard_map/ppermute | solution.py:596
  5.6 14.1 %collective-permute-start.1 = (bf16[128,2176]{1,0:T(8,128)(2,1)S(1)}, bf16[128,2176]{1,0:T(8,128)(2,1)S(1)}, u32[]{:S(2)}, u32[]{:S(2)}) collective-permute-start(bf16[128,2176]{1,0:T(8,128)(2,1)S(1)} %fusion.9.refs_5_), channel_id=1, source_target_pairs={{0,1},{1,0},{2,3},{3,2},{4,5},{5,4},{6,7},{7,6},{8,9},{9,8},{10,11... | collective-permute-start | bytes 1671176 | tf_op jit(solution)/shard_map/ppermute | solution.py:596
  7.1 13.8 %collective-permute-start.2 = (bf16[128,2176]{1,0:T(8,128)(2,1)S(1)}, bf16[128,2176]{1,0:T(8,128)(2,1)S(1)}, u32[]{:S(2)}, u32[]{:S(2)}) collective-permute-start(bf16[128,2176]{1,0:T(8,128)(2,1)S(1)} %fusion.9.refs_5_), channel_id=1, source_target_pairs={{0,2},{1,3},{2,0},{3,1},{4,6},{5,7},{6,4},{7,5},{8,10},{9,11},{10,... | collective-permute-start | bytes 1671176 | tf_op jit(solution)/shard_map/ppermute | solution.py:596
  11.7 36.2 %slice-start.4 = ((s8[6291456]{0:T(1024)(128)(4,1)}), s8[4194304]{0:T(1024)(128)(4,1)S(1)}, s32[]{:S(2)}) async-start(s8[6291456]{0:T(1024)(128)(4,1)} %bitcast.78), calls=%async_computation.4 | async-start | bytes 8388608
  11.7 36.2 %slice-start.5 = ((s8[6291456]{0:T(1024)(128)(4,1)}), s8[2097152]{0:T(1024)(128)(4,1)S(1)}, s32[]{:S(2)}) async-start(s8[6291456]{0:T(1024)(128)(4,1)} %bitcast.78), calls=%async_computation.5 | async-start | bytes 4194304
  19.3 7.3 %copy-start.19 = (bf16[128,2176]{1,0:T(8,128)(2,1)}, bf16[128,2176]{1,0:T(8,128)(2,1)S(1)}, u32[]{:S(2)}) copy-start(bf16[128,2176]{1,0:T(8,128)(2,1)S(1)} %collective-permute-done.refs_0_) | copy-start | bytes 1671172
  19.7 6.8 %copy-start.12 = (bf16[128,2176]{1,0:T(8,128)(2,1)}, bf16[128,2176]{1,0:T(8,128)(2,1)S(1)}, u32[]{:S(2)}) copy-start(bf16[128,2176]{1,0:T(8,128)(2,1)S(1)} %collective-permute-done.1.refs_6_) | copy-start | bytes 1671172
  20.9 5.6 %copy-start.13 = (bf16[128,2176]{1,0:T(8,128)(2,1)}, bf16[128,2176]{1,0:T(8,128)(2,1)S(1)}, u32[]{:S(2)}) copy-start(bf16[128,2176]{1,0:T(8,128)(2,1)S(1)} %collective-permute-done.2.refs_7_) | copy-start | bytes 1671172
  20.9 13.8 %collective-permute-start.3 = (bf16[128,2176]{1,0:T(8,128)(2,1)S(1)}, bf16[128,2176]{1,0:T(8,128)(2,1)S(1)}, u32[]{:S(2)}, u32[]{:S(2)}) collective-permute-start(bf16[128,2176]{1,0:T(8,128)(2,1)S(1)} %collective-permute-done.refs_0_), channel_id=1, source_target_pairs={{0,4},{1,5},{2,6},{3,7},{4,12},{5,13},{6,14},{7,15},{8,0},{9,1},{1... | collective-permute-start | bytes 1671176 | tf_op jit(solution)/shard_map/ppermute | solution.py:596
  23.5 12.6 %collective-permute-start.4 = (bf16[128,2176]{1,0:T(8,128)(2,1)S(1)}, bf16[128,2176]{1,0:T(8,128)(2,1)S(1)}, u32[]{:S(2)}, u32[]{:S(2)}) collective-permute-start(bf16[128,2176]{1,0:T(8,128)(2,1)S(1)} %collective-permute-done.refs_0_), channel_id=1, source_target_pairs={{0,1},{1,0},{2,3},{3,2},{4,5},{5,4},{6,7},{7,6},{8,9},{9,8},{10,11... | collective-permute-start | bytes 1671176 | tf_op jit(solution)/shard_map/ppermute | solution.py:596
  24.1 12.7 %collective-permute-start.5 = (bf16[128,2176]{1,0:T(8,128)(2,1)S(1)}, bf16[128,2176]{1,0:T(8,128)(2,1)S(1)}, u32[]{:S(2)}, u32[]{:S(2)}) collective-permute-start(bf16[128,2176]{1,0:T(8,128)(2,1)S(1)} %collective-permute-done.refs_0_), channel_id=1, source_target_pairs={{0,2},{1,3},{2,0},{3,1},{4,6},{5,7},{6,4},{7,5},{8,10},{9,11},{10,... | collective-permute-start | bytes 1671176 | tf_op jit(solution)/shard_map/ppermute | solution.py:596
  34.7 19.3 %copy-start.20 = (bf16[128,2176]{1,0:T(8,128)(2,1)}, bf16[128,2176]{1,0:T(8,128)(2,1)S(1)}, u32[]{:S(2)}) copy-start(bf16[128,2176]{1,0:T(8,128)(2,1)S(1)} %collective-permute-done.3.refs_0_) | copy-start | bytes 1671172
  36.1 4.0 %copy-start.17 = (bf16[128,2176]{1,0:T(8,128)(2,1)}, bf16[128,2176]{1,0:T(8,128)(2,1)S(1)}, u32[]{:S(2)}) copy-start(bf16[128,2176]{1,0:T(8,128)(2,1)S(1)} %collective-permute-done.4.refs_1_) | copy-start | bytes 1671172
  36.8 17.3 %copy-start.18 = (bf16[128,2176]{1,0:T(8,128)(2,1)}, bf16[128,2176]{1,0:T(8,128)(2,1)S(1)}, u32[]{:S(2)}) copy-start(bf16[128,2176]{1,0:T(8,128)(2,1)S(1)} %collective-permute-done.5.refs_2_) | copy-start | bytes 1671172
  36.8 9.7 %collective-permute-start.7 = (bf16[64,2176]{1,0:T(8,128)(2,1)S(1)}, bf16[64,2176]{1,0:T(8,128)(2,1)S(1)}, u32[]{:S(2)}, u32[]{:S(2)}) collective-permute-start(bf16[64,2176]{1,0:T(8,128)(2,1)S(1)} %slice.42), channel_id=1, source_target_pairs={{0,2},{1,3},{2,0},{3,1},{4,6},{5,7},{6,4},{7,5},{8,10},{9,11},{10,... | collective-permute-start | bytes 835592 | tf_op jit(solution)/shard_map/ppermute | solution.py:596
  38.4 19.3 %collective-permute-start.9 = (bf16[128,2176]{1,0:T(8,128)(2,1)S(1)}, bf16[128,2176]{1,0:T(8,128)(2,1)}, u32[]{:S(2)}, u32[]{:S(2)}) collective-permute-start(bf16[128,2176]{1,0:T(8,128)(2,1)S(1)} %collective-permute-done.3.refs_0_), channel_id=1, source_target_pairs={{0,4},{1,5},{2,6},{3,7},{4,12},{5,13},{6,14},{7,15},{8,0},{9,1},{1... | collective-permute-start | bytes 1671176 | tf_op jit(solution)/shard_map/ppermute | solution.py:596
  39.6 18.1 %collective-permute-start.10 = (bf16[128,2176]{1,0:T(8,128)(2,1)S(1)}, bf16[128,2176]{1,0:T(8,128)(2,1)S(1)}, u32[]{:S(2)}, u32[]{:S(2)}) collective-permute-start(bf16[128,2176]{1,0:T(8,128)(2,1)S(1)} %collective-permute-done.3.refs_0_), channel_id=1, source_target_pairs={{0,1},{1,0},{2,3},{3,2},{4,5},{5,4},{6,7},{7,6},{8,9},{9,8},{10,11... | collective-permute-start | bytes 1671176 | tf_op jit(solution)/shard_map/ppermute | solution.py:596
  40.1 17.6 %collective-permute-start.11 = (bf16[128,2176]{1,0:T(8,128)(2,1)S(1)}, bf16[128,2176]{1,0:T(8,128)(2,1)S(1)}, u32[]{:S(2)}, u32[]{:S(2)}) collective-permute-start(bf16[128,2176]{1,0:T(8,128)(2,1)S(1)} %collective-permute-done.3.refs_0_), channel_id=1, source_target_pairs={{0,2},{1,3},{2,0},{3,1},{4,6},{5,7},{6,4},{7,5},{8,10},{9,11},{10,... | collective-permute-start | bytes 1671176 | tf_op jit(solution)/shard_map/ppermute | solution.py:596
  40.7 17.0 %collective-permute-start.6 = (bf16[4,96,384]{2,1,0:T(8,128)(2,1)S(1)}, bf16[4,96,384]{2,1,0:T(8,128)(2,1)S(1)}, u32[]{:S(2)}, u32[]{:S(2)}) collective-permute-start(bf16[4,96,384]{2,1,0:T(8,128)(2,1)S(1)} %get-tuple-element.105), channel_id=1, source_target_pairs={{0,4},{1,5},{2,6},{3,7},{4,12},{5,13},{6,14},{7,15},{8,0},{9,1},{1... | collective-permute-start | bytes 884744 | tf_op jit(solution)/shard_map/ppermute | solution.py:596
  46.5 7.6 %copy-start.22 = (bf16[64,2176]{1,0:T(8,128)(2,1)}, bf16[64,2176]{1,0:T(8,128)(2,1)S(1)}, u32[]{:S(2)}) copy-start(bf16[64,2176]{1,0:T(8,128)(2,1)S(1)} %collective-permute-done.7.refs_3_) | copy-start | bytes 835588
  46.5 11.2 %collective-permute-start.8 = (bf16[64,2176]{1,0:T(8,128)(2,1)S(1)}, bf16[64,2176]{1,0:T(8,128)(2,1)S(1)}, u32[]{:S(2)}, u32[]{:S(2)}) collective-permute-start(bf16[64,2176]{1,0:T(8,128)(2,1)S(1)} %slice.43), channel_id=1, source_target_pairs={{0,1},{1,0},{2,3},{3,2},{4,5},{5,4},{6,7},{7,6},{8,9},{9,8},{10,11... | collective-permute-start | bytes 835592 | tf_op jit(solution)/shard_map/ppermute | solution.py:596
  57.7 9.7 %copy-start.23 = (bf16[64,2176]{1,0:T(8,128)(2,1)}, bf16[64,2176]{1,0:T(8,128)(2,1)S(1)}, u32[]{:S(2)}) copy-start(bf16[64,2176]{1,0:T(8,128)(2,1)S(1)} %collective-permute-done.8.refs_4_) | copy-start | bytes 835588
  57.7 17.1 %copy-start.14 = (bf16[128,2176]{1,0:T(8,128)(2,1)}, bf16[128,2176]{1,0:T(8,128)(2,1)S(1)}, u32[]{:S(2)}) copy-start(bf16[128,2176]{1,0:T(8,128)(2,1)S(1)} %collective-permute-done.10.refs_1_) | copy-start | bytes 1671172
  57.7 17.0 %copy-start.15 = (bf16[128,2176]{1,0:T(8,128)(2,1)}, bf16[128,2176]{1,0:T(8,128)(2,1)S(1)}, u32[]{:S(2)}) copy-start(bf16[128,2176]{1,0:T(8,128)(2,1)S(1)} %collective-permute-done.11.refs_2_) | copy-start | bytes 1671172
  57.8 9.7 %collective-permute-start.14 = (bf16[64,2176]{1,0:T(8,128)(2,1)S(1)}, bf16[64,2176]{1,0:T(8,128)(2,1)S(1)}, u32[]{:S(2)}, u32[]{:S(2)}) collective-permute-start(bf16[64,2176]{1,0:T(8,128)(2,1)S(1)} %slice.44), channel_id=1, source_target_pairs={{0,2},{1,3},{2,0},{3,1},{4,6},{5,7},{6,4},{7,5},{8,10},{9,11},{10,... | collective-permute-start | bytes 835592 | tf_op jit(solution)/shard_map/ppermute | solution.py:596
  57.8 17.6 %collective-permute-start.16 = (bf16[128,2176]{1,0:T(8,128)(2,1)}, bf16[128,2176]{1,0:T(8,128)(2,1)S(1)}, u32[]{:S(2)}, u32[]{:S(2)}) collective-permute-start(bf16[128,2176]{1,0:T(8,128)(2,1)} %collective-permute-done.9.refs_0_), channel_id=1, source_target_pairs={{0,1},{1,0},{2,3},{3,2},{4,5},{5,4},{6,7},{7,6},{8,9},{9,8},{10,11... | collective-permute-start | bytes 1671176 | tf_op jit(solution)/shard_map/ppermute | solution.py:596
  58.5 17.0 %collective-permute-start.17 = (bf16[128,2176]{1,0:T(8,128)(2,1)}, bf16[128,2176]{1,0:T(8,128)(2,1)}, u32[]{:S(2)}, u32[]{:S(2)}) collective-permute-start(bf16[128,2176]{1,0:T(8,128)(2,1)} %collective-permute-done.9.refs_0_), channel_id=1, source_target_pairs={{0,2},{1,3},{2,0},{3,1},{4,6},{5,7},{6,4},{7,5},{8,10},{9,11},{10,... | collective-permute-start | bytes 1671176 | tf_op jit(solution)/shard_map/ppermute | solution.py:596
  60.4 15.0 %collective-permute-start.12 = (bf16[4,96,384]{2,1,0:T(8,128)(2,1)}, bf16[4,96,384]{2,1,0:T(8,128)(2,1)S(1)}, u32[]{:S(2)}, u32[]{:S(2)}) collective-permute-start(bf16[4,96,384]{2,1,0:T(8,128)(2,1)} %get-tuple-element.119), channel_id=1, source_target_pairs={{0,12},{1,13},{2,14},{3,15},{4,8},{5,9},{6,10},{7,11},{8,4},{9,5},... | collective-permute-start | bytes 884744 | tf_op jit(solution)/shard_map/ppermute | solution.py:596
  62.2 13.2 %collective-permute-start.13 = (bf16[4,96,384]{2,1,0:T(8,128)(2,1)}, bf16[4,96,384]{2,1,0:T(8,128)(2,1)S(1)}, u32[]{:S(2)}, u32[]{:S(2)}) collective-permute-start(bf16[4,96,384]{2,1,0:T(8,128)(2,1)} %get-tuple-element.120), channel_id=1, source_target_pairs={{0,8},{1,9},{2,10},{3,11},{4,0},{5,1},{6,2},{7,3},{8,12},{9,13},{1... | collective-permute-start | bytes 884744 | tf_op jit(solution)/shard_map/ppermute | solution.py:596
  67.4 7.3 %copy-start.21 = (bf16[64,2176]{1,0:T(8,128)(2,1)}, bf16[64,2176]{1,0:T(8,128)(2,1)S(1)}, u32[]{:S(2)}) copy-start(bf16[64,2176]{1,0:T(8,128)(2,1)S(1)} %collective-permute-done.14.refs_3_) | copy-start | bytes 835588
  67.4 8.0 %collective-permute-start.15 = (bf16[64,2176]{1,0:T(8,128)(2,1)}, bf16[64,2176]{1,0:T(8,128)(2,1)}, u32[]{:S(2)}, u32[]{:S(2)}) collective-permute-start(bf16[64,2176]{1,0:T(8,128)(2,1)} %slice.45), channel_id=1, source_target_pairs={{0,1},{1,0},{2,3},{3,2},{4,5},{5,4},{6,7},{7,6},{8,9},{9,8},{10,11... | collective-permute-start | bytes 835592 | tf_op jit(solution)/shard_map/ppermute | solution.py:596
  68.0 7.6 %slice-start.6 = ((bf16[128,2176]{1,0:T(8,128)(2,1)}), bf16[64,2176]{1,0:T(8,128)(2,1)S(1)}, s32[]{:S(2)}) async-start(bf16[128,2176]{1,0:T(8,128)(2,1)} %copy-done.12), calls=%async_computation.6 | async-start | bytes 557056 | tf_op jit(solution)/shard_map/slice | solution.py:621
  75.6 17.5 %collective-permute-start.19 = (bf16[128,2176]{1,0:T(8,128)(2,1)S(1)}, bf16[128,2176]{1,0:T(8,128)(2,1)S(1)}, u32[]{:S(2)}, u32[]{:S(2)}) collective-permute-start(bf16[128,2176]{1,0:T(8,128)(2,1)S(1)} %pad_maximum_fusion), channel_id=1, source_target_pairs={{0,2},{1,3},{2,0},{3,1},{4,6},{5,7},{6,4},{7,5},{8,10},{9,11},{10,... | collective-permute-start | bytes 1671176 | tf_op jit(solution)/shard_map/ppermute | solution.py:596
  77.1 16.0 %collective-permute-start.20 = (bf16[128,2176]{1,0:T(8,128)(2,1)S(1)}, bf16[128,2176]{1,0:T(8,128)(2,1)S(1)}, u32[]{:S(2)}, u32[]{:S(2)}) collective-permute-start(bf16[128,2176]{1,0:T(8,128)(2,1)S(1)} %pad_maximum_fusion.1), channel_id=1, source_target_pairs={{0,1},{1,0},{2,3},{3,2},{4,5},{5,4},{6,7},{7,6},{8,9},{9,8},{10,11... | collective-permute-start | bytes 1671176 | tf_op jit(solution)/shard_map/ppermute | solution.py:596
  77.8 14.8 %collective-permute-start.18 = (bf16[4,96,384]{2,1,0:T(8,128)(2,1)S(1)}, bf16[4,96,384]{2,1,0:T(8,128)(2,1)S(1)}, u32[]{:S(2)}, u32[]{:S(2)}) collective-permute-start(bf16[4,96,384]{2,1,0:T(8,128)(2,1)S(1)} %copy-done.28), channel_id=1, source_target_pairs={{0,8},{1,9},{2,10},{3,11},{4,0},{5,1},{6,2},{7,3},{8,12},{9,13},{1... | collective-permute-start | bytes 884744 | tf_op jit(solution)/shard_map/ppermute | solution.py:596
  82.7 22.3 %collective-permute-start.23 = (bf16[4,96,384]{2,1,0:T(8,128)(2,1)}, bf16[4,96,384]{2,1,0:T(8,128)(2,1)S(1)}, u32[]{:S(2)}, u32[]{:S(2)}) collective-permute-start(bf16[4,96,384]{2,1,0:T(8,128)(2,1)} %get-tuple-element.152), channel_id=1, source_target_pairs={{0,1},{1,0},{2,3},{3,2},{4,5},{5,4},{6,7},{7,6},{8,9},{9,8},{10,11... | collective-permute-start | bytes 884744 | tf_op jit(solution)/shard_map/ppermute | solution.py:596
  84.4 20.7 %collective-permute-start.24 = (bf16[4,96,384]{2,1,0:T(8,128)(2,1)}, bf16[4,96,384]{2,1,0:T(8,128)(2,1)S(1)}, u32[]{:S(2)}, u32[]{:S(2)}) collective-permute-start(bf16[4,96,384]{2,1,0:T(8,128)(2,1)} %get-tuple-element.153), channel_id=1, source_target_pairs={{0,2},{1,3},{2,0},{3,1},{4,6},{5,7},{6,4},{7,5},{8,10},{9,11},{10,... | collective-permute-start | bytes 884744 | tf_op jit(solution)/shard_map/ppermute | solution.py:596
  92.6 27.4 %copy-start.5 = (bf16[4,96,384]{2,1,0:T(8,128)(2,1)}, bf16[4,96,384]{2,1,0:T(8,128)(2,1)S(1)}, u32[]{:S(2)}) copy-start(bf16[4,96,384]{2,1,0:T(8,128)(2,1)S(1)} %collective-permute-done.18.refs_1_) | copy-start | bytes 884740
  92.6 12.4 %collective-permute-start.25 = (bf16[4,96,384]{2,1,0:T(8,128)(2,1)S(1)}, bf16[4,96,384]{2,1,0:T(8,128)(2,1)S(1)}, u32[]{:S(2)}, u32[]{:S(2)}) collective-permute-start(bf16[4,96,384]{2,1,0:T(8,128)(2,1)S(1)} %get-tuple-element.154), channel_id=1, source_target_pairs={{0,3},{1,2},{2,1},{3,0},{4,7},{5,6},{6,5},{7,4},{8,11},{9,10},{10,... | collective-permute-start | bytes 884744 | tf_op jit(solution)/shard_map/ppermute | solution.py:596
  93.1 2.7 %copy-start.9 = (bf16[128,2176]{1,0:T(8,128)(2,1)}, bf16[128,2176]{1,0:T(8,128)(2,1)S(1)}, u32[]{:S(2)}) copy-start(bf16[128,2176]{1,0:T(8,128)(2,1)S(1)} %collective-permute-done.19.refs_3_.refs_8_) | copy-start | bytes 1671172
  93.1 2.7 %copy-start.10 = (bf16[128,2176]{1,0:T(8,128)(2,1)}, bf16[128,2176]{1,0:T(8,128)(2,1)S(1)}, u32[]{:S(2)}) copy-start(bf16[128,2176]{1,0:T(8,128)(2,1)S(1)} %collective-permute-done.20.refs_4_.refs_9_) | copy-start | bytes 1671172
  93.1 21.8 %collective-permute-start.21 = (bf16[4,96,384]{2,1,0:T(8,128)(2,1)}, bf16[4,96,384]{2,1,0:T(8,128)(2,1)S(1)}, u32[]{:S(2)}, u32[]{:S(2)}) collective-permute-start(bf16[4,96,384]{2,1,0:T(8,128)(2,1)} %get-tuple-element.146), channel_id=1, source_target_pairs={{0,12},{1,13},{2,14},{3,15},{4,8},{5,9},{6,10},{7,11},{8,4},{9,5},... | collective-permute-start | bytes 884744 | tf_op jit(solution)/shard_map/ppermute | solution.py:596
  103.6 11.4 %collective-permute-start.22 = (bf16[4,96,384]{2,1,0:T(8,128)(2,1)}, bf16[4,96,384]{2,1,0:T(8,128)(2,1)S(1)}, u32[]{:S(2)}, u32[]{:S(2)}) collective-permute-start(bf16[4,96,384]{2,1,0:T(8,128)(2,1)} %get-tuple-element.147), channel_id=1, source_target_pairs={{0,4},{1,5},{2,6},{3,7},{4,12},{5,13},{6,14},{7,15},{8,0},{9,1},{1... | collective-permute-start | bytes 884744 | tf_op jit(solution)/shard_map/ppermute | solution.py:596
  105.0 2.5 %copy-start.1 = (bf16[384,2048]{1,0:T(8,128)(2,1)S(1)}, bf16[384,2048]{1,0:T(8,128)(2,1)}, u32[]{:S(2)}) copy-start(bf16[384,2048]{1,0:T(8,128)(2,1)} %get-tuple-element.158.refs_1_) | copy-start | bytes 4718596
  105.0 2.5 %copy-start.2 = (bf16[384,2048]{1,0:T(8,128)(2,1)S(1)}, bf16[384,2048]{1,0:T(8,128)(2,1)}, u32[]{:S(2)}) copy-start(bf16[384,2048]{1,0:T(8,128)(2,1)} %get-tuple-element.159.refs_2_) | copy-start | bytes 4718596
  105.0 21.5 %slice-start.2 = ((s8[6291456]{0:T(1024)(128)(4,1)}), s8[4194304]{0:T(1024)(128)(4,1)S(1)}, s32[]{:S(2)}) async-start(s8[6291456]{0:T(1024)(128)(4,1)} %bitcast.68), calls=%async_computation.2 | async-start | bytes 8388608
  110.4 16.2 %slice-start = ((s8[6291456]{0:T(1024)(128)(4,1)}), s8[4194304]{0:T(1024)(128)(4,1)S(1)}, s32[]{:S(2)}) async-start(s8[6291456]{0:T(1024)(128)(4,1)} %bitcast.64), calls=%async_computation | async-start | bytes 8388608
  110.4 16.2 %slice-start.3 = ((s8[6291456]{0:T(1024)(128)(4,1)}), s8[2097152]{0:T(1024)(128)(4,1)S(1)}, s32[]{:S(2)}) async-start(s8[6291456]{0:T(1024)(128)(4,1)} %bitcast.68), calls=%async_computation.3 | async-start | bytes 4194304
  114.9 6.5 %collective-permute-start.26 = (bf16[2,192,2048]{2,1,0:T(8,128)(2,1)S(1)}, bf16[2,192,2048]{2,1,0:T(8,128)(2,1)S(1)}, u32[]{:S(2)}, u32[]{:S(2)}) collective-permute-start(bf16[2,192,2048]{2,1,0:T(8,128)(2,1)S(1)} %get-tuple-element.156), channel_id=1, source_target_pairs={{0,16},{16,0},{1,17},{17,1},{2,18},{18,2},{3,19},{19,3},{4,20},{20... | collective-permute-start | bytes 4718600 | tf_op jit(solution)/shard_map/ppermute | solution.py:698
  114.9 5.1 %copy-start.6 = (bf16[4,96,384]{2,1,0:T(8,128)(2,1)}, bf16[4,96,384]{2,1,0:T(8,128)(2,1)S(1)}, u32[]{:S(2)}) copy-start(bf16[4,96,384]{2,1,0:T(8,128)(2,1)S(1)} %collective-permute-done.21.refs_2_) | copy-start | bytes 884740
  115.0 5.1 %copy-start.8 = (bf16[4,96,384]{2,1,0:T(8,128)(2,1)}, bf16[4,96,384]{2,1,0:T(8,128)(2,1)S(1)}, u32[]{:S(2)}) copy-start(bf16[4,96,384]{2,1,0:T(8,128)(2,1)S(1)} %collective-permute-done.22.refs_3_) | copy-start | bytes 884740
  115.0 5.1 %copy-start.7 = (bf16[4,96,384]{2,1,0:T(8,128)(2,1)S(1)}, bf16[4,96,384]{2,1,0:T(8,128)(2,1)}, u32[]{:S(2)}) copy-start(bf16[4,96,384]{2,1,0:T(8,128)(2,1)} %get-tuple-element.148.refs_0_) | copy-start | bytes 884740
  115.0 11.6 %slice-start.1 = ((s8[6291456]{0:T(1024)(128)(4,1)}), s8[2097152]{0:T(1024)(128)(4,1)S(1)}, s32[]{:S(2)}) async-start(s8[6291456]{0:T(1024)(128)(4,1)} %bitcast.64), calls=%async_computation.1 | async-start | bytes 4194304
  119.5 3.6 %collective-permute-start.27 = (bf16[2,192,2048]{2,1,0:T(8,128)(2,1)S(1)}, bf16[2,192,2048]{2,1,0:T(8,128)(2,1)S(1)}, u32[]{:S(2)}, u32[]{:S(2)}) collective-permute-start(bf16[2,192,2048]{2,1,0:T(8,128)(2,1)S(1)} %get-tuple-element.162), channel_id=1, source_target_pairs={{0,16},{16,0},{1,17},{17,1},{2,18},{18,2},{3,19},{19,3},{4,20},{20... | collective-permute-start | bytes 4718600 | tf_op jit(solution)/shard_map/ppermute | solution.py:698
  123.1 16.0 %collective-permute-start.28 = (bf16[4,96,384]{2,1,0:T(8,128)(2,1)S(1)}, bf16[4,96,384]{2,1,0:T(8,128)(2,1)S(1)}, u32[]{:S(2)}, u32[]{:S(2)}) collective-permute-start(bf16[4,96,384]{2,1,0:T(8,128)(2,1)S(1)} %get-tuple-element.170), channel_id=1, source_target_pairs={{0,1},{1,0},{2,3},{3,2},{4,5},{5,4},{6,7},{7,6},{8,9},{9,8},{10,11... | collective-permute-start | bytes 884744 | tf_op jit(solution)/shard_map/ppermute | solution.py:596
  123.6 15.5 %collective-permute-start.29 = (bf16[4,96,384]{2,1,0:T(8,128)(2,1)S(1)}, bf16[4,96,384]{2,1,0:T(8,128)(2,1)S(1)}, u32[]{:S(2)}, u32[]{:S(2)}) collective-permute-start(bf16[4,96,384]{2,1,0:T(8,128)(2,1)S(1)} %get-tuple-element.171), channel_id=1, source_target_pairs={{0,2},{1,3},{2,0},{3,1},{4,6},{5,7},{6,4},{7,5},{8,10},{9,11},{10,... | collective-permute-start | bytes 884744 | tf_op jit(solution)/shard_map/ppermute | solution.py:596
  125.1 14.5 %collective-permute-start.30 = (bf16[4,96,384]{2,1,0:T(8,128)(2,1)S(1)}, bf16[4,96,384]{2,1,0:T(8,128)(2,1)S(1)}, u32[]{:S(2)}, u32[]{:S(2)}) collective-permute-start(bf16[4,96,384]{2,1,0:T(8,128)(2,1)S(1)} %get-tuple-element.172), channel_id=1, source_target_pairs={{0,3},{1,2},{2,1},{3,0},{4,7},{5,6},{6,5},{7,4},{8,11},{9,10},{10,... | collective-permute-start | bytes 884744 | tf_op jit(solution)/shard_map/ppermute | solution.py:596
  126.6 2.8 %copy-start = (f32[192,4,2048]{2,1,0:T(4,128)S(1)}, f32[192,4,2048]{2,1,0:T(4,128)}, u32[]{:S(2)}) copy-start(f32[192,4,2048]{2,1,0:T(4,128)} %param.15) | copy-start | bytes 18874372
  139.1 3.1 %copy-start.25 = (bf16[4,96,384]{2,1,0:T(8,128)(2,1)}, bf16[4,96,384]{2,1,0:T(8,128)(2,1)S(1)}, u32[]{:S(2)}) copy-start(bf16[4,96,384]{2,1,0:T(8,128)(2,1)S(1)} %collective-permute-done.28.refs_4_) | copy-start | bytes 884740
  139.1 3.1 %copy-start.26 = (bf16[4,96,384]{2,1,0:T(8,128)(2,1)}, bf16[4,96,384]{2,1,0:T(8,128)(2,1)S(1)}, u32[]{:S(2)}) copy-start(bf16[4,96,384]{2,1,0:T(8,128)(2,1)S(1)} %collective-permute-done.29.refs_5_) | copy-start | bytes 884740
  139.6 2.6 %copy-start.27 = (bf16[4,96,384]{2,1,0:T(8,128)(2,1)}, bf16[4,96,384]{2,1,0:T(8,128)(2,1)S(1)}, u32[]{:S(2)}) copy-start(bf16[4,96,384]{2,1,0:T(8,128)(2,1)S(1)} %collective-permute-done.30.refs_6_) | copy-start | bytes 884740
  142.2 6.8 %collective-permute-start.31 = (bf16[12288,128]{1,0:T(8,128)(2,1)}, bf16[12288,128]{1,0:T(8,128)(2,1)S(1)}, u32[]{:S(2)}, u32[]{:S(2)}) collective-permute-start(bf16[12288,128]{1,0:T(8,128)(2,1)} %get-tuple-element.190), channel_id=1, source_target_pairs={{0,16},{16,0},{1,17},{17,1},{2,18},{18,2},{3,19},{19,3},{4,20},{20... | collective-permute-start | bytes 9437192 | tf_op jit(solution)/shard_map/ppermute | solution.py:716
  (5 other events, 9.0 us)
